TPU v7x, 32 devices: a whole 2x2x4 slice. The times are simulated.
32 devices in a mesh: seq: 8 (over z, x), fsdp: 4 (over y, core).
Axes of the slice: x: 2, y: 2, z: 4, core: 2. Of those that a mesh axis runs over, the one named last changes fastest.
Arguments:
- tokens: bfloat16 [4, 2048, 768], P('fsdp', 'seq'), may hold values from -6 to 6
- block_order: int32 [16], replicated, may hold values from 0 to 15, as said below
- doc_lengths: int32 [4, 4], P('fsdp'), may hold values from 1 to 1024, 2048 in all within a row
- norm_one_gain: bfloat16 [768], P('fsdp'), may hold values from 0.099609375 to 1.8984375
- norm_one_bias: bfloat16 [768], P('fsdp'), may hold values from -4 to 4
- query_weight: bfloat16 [768, 768], P('fsdp'), may hold values from -0.21875 to 0.21875
- query_bias: bfloat16 [768], P('fsdp'), may hold values from -6 to 6
- key_weight: bfloat16 [768, 64], P('fsdp'), may hold values from -0.21875 to 0.21875
- key_bias: bfloat16 [16], P('fsdp'), may hold values from -6 to 6
- value_weight: bfloat16 [768, 64], P('fsdp'), may hold values from -0.21875 to 0.21875
- value_bias: bfloat16 [64], P('fsdp'), may hold values from -6 to 6
- out_weight: bfloat16 [768, 768], P('fsdp'), may hold values from -1.75 to 1.75
- out_bias: bfloat16 [768], P('fsdp'), may hold values from -6 to 6
- norm_two_gain: bfloat16 [768], P('fsdp'), may hold values from 0.099609375 to 1.8984375
- norm_two_bias: bfloat16 [768], P('fsdp'), may hold values from -4 to 4
- up_weight: bfloat16 [3072, 768], P('fsdp'), may hold values from -0.21875 to 0.21875
- up_bias: bfloat16 [3072], P('fsdp'), may hold values from -6 to 6
- down_weight: bfloat16 [3072, 768], P('fsdp'), may hold values from -0.109375 to 0.109375
- down_bias: bfloat16 [768], P('fsdp'), may hold values from -6 to 6
- cotangent: bfloat16 [4, 2048, 768], P('fsdp', 'seq'), may hold values from -6 to 6
Outputs:
- layer_out: bfloat16 [4, 2048, 768], P('fsdp', 'seq')
- grad_tokens: bfloat16 [4, 2048, 768], P('fsdp', 'seq')
- grad_norm_one_gain: float32 [768], P('fsdp')
- grad_norm_one_bias: float32 [768], P('fsdp')
- grad_query_weight: float32 [768, 768], P('fsdp')
- grad_query_bias: float32 [768], P('fsdp')
- grad_key_weight: float32 [768, 64], P('fsdp')
- grad_key_bias: float32 [16], P('fsdp')
- grad_value_weight: float32 [768, 64], P('fsdp')
- grad_value_bias: float32 [64], P('fsdp')
- grad_out_weight: float32 [768, 768], P('fsdp')
- grad_out_bias: float32 [768], P('fsdp')
- grad_norm_two_gain: float32 [768], P('fsdp')
- grad_norm_two_bias: float32 [768], P('fsdp')
- grad_up_weight: float32 [3072, 768], P('fsdp')
- grad_up_bias: float32 [3072], P('fsdp')
- grad_down_weight: float32 [3072, 768], P('fsdp')
- grad_down_bias: float32 [768], P('fsdp')
Inputs may be any that keep to these rules, and one draw needn't show every extreme that they name: `block_order`: for every index i of seq, entries 2i and 2i+1 are two blocks b and 15 - b; every block appears once. `doc_lengths`: each sequence's lengths sum to 2048.
All inputs are finite; a program needn't handle non-finite values.
Results may differ from a plain program's by a relative error of at most 0.012.
The roundings to bfloat16 on the way count: a program that leaves them out, or rounds other values in their place, can miss the bound.
Values may be sent and summed in bfloat16 or wider, within the bound.
No kernel may reach another device: no remote copies, remote signals or barrier semaphores. Data moves between devices by JAX's collectives and lax.ppermute only.
A program may use at most 128 MiB of HBM per device.

v0:
```python
import jax
import jax.numpy as jnp
from jax import lax
from jax.sharding import PartitionSpec as P

HEADS = 12
HDIM = 64
ROT = 16


NEGATIVE = -1e30
EPSILON = 1e-05
SQRT_HALF = 0.7071067811865476
GAUSS_FACTOR = 0.3989422804014327
HIGHEST = lax.Precision.HIGHEST


def norm_forward(values, gain_vector, shift_vector):
    center = values - jnp.mean(values, -1, keepdims=True)
    inverse_std = lax.rsqrt(jnp.mean(center * center, -1, keepdims=True) + EPSILON)
    normal = center * inverse_std
    return (normal * gain_vector + shift_vector, normal, inverse_std)


def norm_backward(gradient, normal, inverse_std, gain_vector):
    scaled = gradient * gain_vector
    return inverse_std * (
        scaled
        - jnp.mean(scaled, -1, keepdims=True)
        - normal * jnp.mean(scaled * normal, -1, keepdims=True)
    )


def rotary_tables(positions):
    half_rot = ROT // 2
    frequencies = 10000.0 ** (-2.0 * jnp.arange(half_rot, dtype=jnp.float32) / ROT)
    angles = positions.astype(jnp.float32)[:, None] * frequencies[None, :]
    return (jnp.cos(angles), jnp.sin(angles))


def rotate(values, cosine_table, sine_table):
    half_rot = ROT // 2
    first_half = values[..., :half_rot]
    second_half = values[..., half_rot:ROT]
    return jnp.concatenate(
        [
            first_half * cosine_table - second_half * sine_table,
            second_half * cosine_table + first_half * sine_table,
            values[..., ROT:],
        ],
        -1,
    )


def rotate_back(gradient, cosine_table, sine_table):
    half_rot = ROT // 2
    first_half = gradient[..., :half_rot]
    second_half = gradient[..., half_rot:ROT]
    return jnp.concatenate(
        [
            first_half * cosine_table + second_half * sine_table,
            second_half * cosine_table - first_half * sine_table,
            gradient[..., ROT:],
        ],
        -1,
    )


def gelu_slope(values):
    return (
        0.5 * (1.0 + jax.scipy.special.erf(values * SQRT_HALF))
        + values * jnp.exp(-0.5 * values * values) * GAUSS_FACTOR
    )


def contract(left_array, right_array, left_dim, right_dim):
    return lax.dot_general(
        left_array,
        right_array,
        (((left_dim,), (right_dim,)), ((), ())),
        preferred_element_type=jnp.float32,
    )


def on_device(
    tokens,
    block_order,
    doc_lengths,
    norm_one_gain,
    norm_one_bias,
    query_weight,
    query_bias,
    key_weight,
    key_bias,
    value_weight,
    value_bias,
    out_weight,
    out_bias,
    norm_two_gain,
    norm_two_bias,
    up_weight,
    up_bias,
    down_weight,
    down_bias,
    cotangent,
):
    seq_count, local_len, model_width = tokens.shape
    block_len = local_len // 2
    cycle_size = lax.axis_size("seq")
    slot_count = 2 * cycle_size
    length = slot_count * block_len
    row_count = seq_count * local_len
    pair_width = 2 * HDIM
    score_scale = HDIM ** (-0.5)
    (
        query_full,
        key_full,
        value_full,
        out_full,
        gain_one,
        shift_one,
        gain_two,
        shift_two,
        query_bias_full,
        key_bias_full,
        value_bias_full,
        out_bias_full,
        down_bias_full,
    ) = (
        lax.all_gather(query_weight, "fsdp", axis=0, tiled=True),
        lax.all_gather(key_weight, "fsdp", axis=0, tiled=True),
        lax.all_gather(value_weight, "fsdp", axis=0, tiled=True),
        lax.all_gather(out_weight, "fsdp", axis=0, tiled=True),
        lax.all_gather(norm_one_gain, "fsdp", axis=0, tiled=True),
        lax.all_gather(norm_one_bias, "fsdp", axis=0, tiled=True),
        lax.all_gather(norm_two_gain, "fsdp", axis=0, tiled=True),
        lax.all_gather(norm_two_bias, "fsdp", axis=0, tiled=True),
        lax.all_gather(query_bias, "fsdp", axis=0, tiled=True),
        lax.all_gather(key_bias, "fsdp", axis=0, tiled=True),
        lax.all_gather(value_bias, "fsdp", axis=0, tiled=True),
        lax.all_gather(out_bias, "fsdp", axis=0, tiled=True),
        lax.all_gather(down_bias, "fsdp", axis=0, tiled=True),
    )
    gain_one = gain_one.astype(jnp.float32)
    gain_two = gain_two.astype(jnp.float32)
    device = lax.axis_index("seq")
    own_blocks = lax.dynamic_slice_in_dim(block_order, 2 * device, 2)
    offsets = jnp.arange(block_len, dtype=jnp.int32)
    own_pos = (own_blocks[:, None] * block_len + offsets[None, :]).reshape(local_len)
    doc_ends = jnp.cumsum(doc_lengths, axis=1)[:, :-1]

    def doc_index(positions):
        return jnp.sum((positions[None, :, None] >= doc_ends[:, None, :]).astype(jnp.int32), axis=2)

    own_docs = doc_index(own_pos)
    slot_docs = doc_index(
        (block_order[:, None] * block_len + offsets[None, :]).reshape(length)
    ).reshape(seq_count, slot_count, block_len)
    token_rows = tokens.reshape(row_count, model_width).astype(jnp.float32)
    normed_one, normal_one, inverse_std_one = norm_forward(
        token_rows, gain_one, shift_one.astype(jnp.float32)
    )
    normed_two, normal_two, inverse_std_two = norm_forward(
        token_rows, gain_two, shift_two.astype(jnp.float32)
    )
    input_one = normed_one.astype(jnp.bfloat16)
    input_two = normed_two.astype(jnp.bfloat16)
    projection_weight = jnp.concatenate([query_full, key_full, value_full], axis=1)
    projection_bias = jnp.concatenate(
        [query_bias_full, key_bias_full, jnp.zeros((HDIM - ROT,), jnp.bfloat16), value_bias_full]
    ).astype(jnp.float32)
    projected = (
        jnp.dot(input_one, projection_weight, preferred_element_type=jnp.float32) + projection_bias
    )
    cosine_table, sine_table = rotary_tables(own_pos)
    query_rot = rotate(
        projected[:, :model_width].reshape(seq_count, local_len, HEADS, HDIM),
        cosine_table[:, None, :],
        sine_table[:, None, :],
    ).astype(jnp.bfloat16)
    key_rot = rotate(
        projected[:, model_width : model_width + HDIM].reshape(seq_count, local_len, HDIM),
        cosine_table,
        sine_table,
    ).astype(jnp.bfloat16)
    value_low = (
        projected[:, model_width + HDIM :].reshape(seq_count, local_len, HDIM).astype(jnp.bfloat16)
    )
    own_keyvals = jnp.concatenate([key_rot, value_low], axis=2)
    gathered_keyvals = lax.all_gather(own_keyvals, "seq", axis=1, tiled=True).reshape(
        seq_count, slot_count, block_len, pair_width
    )
    swapped = own_blocks[0] > own_blocks[1]
    low_block = jnp.minimum(own_blocks[0], own_blocks[1])
    high_block = jnp.maximum(own_blocks[0], own_blocks[1])

    def to_pair(tensor_in):
        paired = jnp.moveaxis(
            tensor_in.reshape((seq_count, 2, block_len) + tensor_in.shape[2:]), 1, 0
        )
        return jnp.where(swapped, paired[::-1], paired)

    def from_pair(paired):
        ordered = jnp.where(swapped, paired[::-1], paired)
        return jnp.moveaxis(ordered, 0, 1).reshape((seq_count, local_len) + paired.shape[3:])

    group_size = 8
    entry_total = slot_count + 1
    step_count = -(-entry_total // group_size)
    entry_index = jnp.arange(step_count * group_size, dtype=jnp.int32)
    upper_side = entry_index > low_block
    side_index = upper_side.astype(jnp.int32)
    alive_flag = entry_index < entry_total
    key_block = jnp.where(
        alive_flag, jnp.where(upper_side, entry_index - low_block - 1, entry_index), 0
    )
    query_block = jnp.where(upper_side, high_block, low_block)
    slot_index = jnp.arange(slot_count, dtype=jnp.int32)
    key_slot = jnp.sum(
        jnp.where(block_order[None, :] == key_block[:, None], slot_index[None, :], 0), axis=1
    )
    plan = (
        side_index.reshape(step_count, group_size),
        key_slot.reshape(step_count, group_size),
        key_block.reshape(step_count, group_size),
        query_block.reshape(step_count, group_size),
        alive_flag.reshape(step_count, group_size),
    )
    query_pair = to_pair(query_rot)
    query_doc_pair = to_pair(own_docs)
    pick_two = jnp.arange(2, dtype=jnp.int32)

    def block_scores(step_items):
        side_now, slot_now, key_now, query_now, alive_now = step_items
        queries = jnp.take(query_pair, side_now, axis=0)
        key_values = jnp.take(gathered_keyvals, slot_now, axis=1)
        keys_now = key_values[..., :HDIM]
        values_now = key_values[..., HDIM:]
        scores = (
            jnp.einsum("gsqhd,sgkd->gshqk", queries, keys_now, preferred_element_type=jnp.float32)
            * score_scale
        )
        query_pos = query_now[:, None] * block_len + offsets[None, :]
        key_pos = key_now[:, None] * block_len + offsets[None, :]
        query_docs = jnp.take(query_doc_pair, side_now, axis=0)
        key_docs = jnp.moveaxis(jnp.take(slot_docs, slot_now, axis=1), 1, 0)
        allowed = (
            (key_pos[:, None, None, :] <= query_pos[:, None, :, None])
            & (key_docs[:, :, None, :] == query_docs[:, :, :, None])
            & alive_now[:, None, None, None]
        )
        side_hot = (side_now[:, None] == pick_two[None, :]).astype(jnp.float32)
        return (queries, keys_now, values_now, scores, allowed[:, :, None], side_hot)

    def statistic_step(carry_state, step_items):
        running_top, running_total = carry_state
        queries, keys_now, values_now, scores, allowed, side_hot = block_scores(step_items)
        scores = jnp.where(allowed, scores, NEGATIVE)
        block_top = jnp.max(scores, axis=-1)
        step_top = jnp.max(
            jnp.where(side_hot[:, :, None, None, None] > 0.5, block_top[:, None], NEGATIVE), axis=0
        )
        new_top = jnp.maximum(running_top, step_top)
        row_top = jnp.take(new_top, step_items[0], axis=0)
        weights = jnp.where(allowed, jnp.exp(scores - row_top[..., None]), 0.0)
        shrink = jnp.exp(running_top - new_top)
        running_total = running_total * shrink + jnp.einsum(
            "gr,gshq->rshq", side_hot, jnp.sum(weights, axis=-1), precision=HIGHEST
        )
        return ((new_top, running_total), None)

    start_top = jnp.full((2, seq_count, HEADS, block_len), NEGATIVE, jnp.float32)
    start_total = jnp.zeros((2, seq_count, HEADS, block_len), jnp.float32)
    stat_state = lax.scan(statistic_step, (start_top, start_total), plan)[0]
    logsum_pair = stat_state[0] + jnp.log(stat_state[1])
    cotangent_rows = cotangent.reshape(row_count, model_width)
    grad_attn = contract(cotangent_rows, out_full, 1, 1).astype(jnp.bfloat16)
    grad_pair = to_pair(grad_attn.reshape(seq_count, local_len, HEADS, HDIM))

    def value_step(carry_state, step_items):
        out_sum, delta_sum = carry_state
        queries, keys_now, values_now, scores, allowed, side_hot = block_scores(step_items)
        side_now = step_items[0]
        probabilities = jnp.where(
            allowed, jnp.exp(scores - jnp.take(logsum_pair, side_now, axis=0)[..., None]), 0.0
        )
        part_out = jnp.einsum(
            "gshqk,sgkd->gsqhd",
            probabilities.astype(jnp.bfloat16),
            values_now,
            preferred_element_type=jnp.float32,
        )
        grads_now = jnp.take(grad_pair, side_now, axis=0)
        prob_grad = jnp.einsum(
            "gsqhd,sgkd->gshqk", grads_now, values_now, preferred_element_type=jnp.float32
        )
        delta_part = jnp.sum(probabilities * prob_grad, axis=-1)
        out_sum = out_sum + jnp.einsum("gr,gsqhd->rsqhd", side_hot, part_out, precision=HIGHEST)
        delta_sum = delta_sum + jnp.einsum("gr,gshq->rshq", side_hot, delta_part, precision=HIGHEST)
        return ((out_sum, delta_sum), None)

    start_sum = jnp.zeros((2, seq_count, block_len, HEADS, HDIM), jnp.float32)
    start_delta = jnp.zeros((2, seq_count, HEADS, block_len), jnp.float32)
    attn_pair, delta_pair = lax.scan(value_step, (start_sum, start_delta), plan)[0]
    attn_low = from_pair(attn_pair).reshape(row_count, model_width).astype(jnp.bfloat16)
    attention = jnp.dot(
        attn_low, out_full, preferred_element_type=jnp.float32
    ) + out_bias_full.astype(jnp.float32)
    up_full, up_bias_full, down_full = (
        lax.all_gather(up_weight, "fsdp", axis=0, tiled=True),
        lax.all_gather(up_bias, "fsdp", axis=0, tiled=True),
        lax.all_gather(down_weight, "fsdp", axis=0, tiled=True),
    )
    pre_act = contract(input_two, up_full, 1, 1) + up_bias_full.astype(jnp.float32)
    hidden = jax.nn.gelu(pre_act, approximate=False).astype(jnp.bfloat16)
    mlp_out = jnp.dot(hidden, down_full, preferred_element_type=jnp.float32)
    layer_out = (
        (token_rows + attention + mlp_out + down_bias_full.astype(jnp.float32))
        .astype(jnp.bfloat16)
        .reshape(seq_count, local_len, model_width)
    )
    cotangent_float = cotangent_rows.astype(jnp.float32)
    grad_bias_out = jnp.sum(cotangent_float, axis=0)
    grad_out_weight = contract(attn_low, cotangent_rows, 0, 0)
    grad_pre = (contract(cotangent_rows, down_full, 1, 1) * gelu_slope(pre_act)).astype(
        jnp.bfloat16
    )
    grad_down_weight = contract(hidden, cotangent_rows, 0, 0)
    grad_up_weight = contract(grad_pre, input_two, 0, 0)
    grad_up_bias = jnp.sum(grad_pre.astype(jnp.float32), axis=0)
    grad_norm_two = jnp.dot(grad_pre, up_full, preferred_element_type=jnp.float32)

    def backward_step(carry_state, step_items):
        query_grad, keyval_grad = carry_state
        queries, keys_now, values_now, scores, allowed, side_hot = block_scores(step_items)
        side_now = step_items[0]
        slot_now = step_items[1]
        probabilities = jnp.where(
            allowed, jnp.exp(scores - jnp.take(logsum_pair, side_now, axis=0)[..., None]), 0.0
        )
        grads_now = jnp.take(grad_pair, side_now, axis=0)
        value_grad = jnp.einsum(
            "gshqk,gsqhd->sgkd",
            probabilities.astype(jnp.bfloat16),
            grads_now,
            preferred_element_type=jnp.float32,
        )
        prob_grad = jnp.einsum(
            "gsqhd,sgkd->gshqk", grads_now, values_now, preferred_element_type=jnp.float32
        )
        score_grad = (
            probabilities * (prob_grad - jnp.take(delta_pair, side_now, axis=0)[..., None])
        ).astype(jnp.bfloat16)
        query_part = (
            jnp.einsum(
                "gshqk,sgkd->gsqhd", score_grad, keys_now, preferred_element_type=jnp.float32
            )
            * score_scale
        )
        key_part = (
            jnp.einsum("gshqk,gsqhd->sgkd", score_grad, queries, preferred_element_type=jnp.float32)
            * score_scale
        )
        query_grad = query_grad + jnp.einsum(
            "gr,gsqhd->rsqhd", side_hot, query_part, precision=HIGHEST
        )
        keyval_grad = keyval_grad.at[:, slot_now].add(
            jnp.concatenate([key_part, value_grad], axis=3)
        )
        return ((query_grad, keyval_grad), None)

    start_query = jnp.zeros((2, seq_count, block_len, HEADS, HDIM), jnp.float32)
    start_keyval = jnp.zeros((seq_count, slot_count, block_len, pair_width), jnp.float32)
    back_state = lax.scan(backward_step, (start_query, start_keyval), plan)[0]
    own_keyval_grad = lax.psum_scatter(
        back_state[1].reshape(seq_count, length, pair_width), "seq", scatter_dimension=1, tiled=True
    )
    query_pre_grad = (
        rotate_back(from_pair(back_state[0]), cosine_table[:, None, :], sine_table[:, None, :])
        .astype(jnp.bfloat16)
        .reshape(row_count, model_width)
    )
    key_pre_grad = (
        rotate_back(own_keyval_grad[..., :HDIM], cosine_table, sine_table)
        .astype(jnp.bfloat16)
        .reshape(row_count, HDIM)
    )
    value_pre_grad = own_keyval_grad[..., HDIM:].astype(jnp.bfloat16).reshape(row_count, HDIM)
    projection_grad = jnp.concatenate([query_pre_grad, key_pre_grad, value_pre_grad], axis=1)
    projection_weight_grad = contract(input_one, projection_grad, 0, 0)
    projection_bias_grad = jnp.sum(projection_grad.astype(jnp.float32), axis=0)
    grad_norm_one = contract(projection_grad, projection_weight, 1, 1)
    grad_query_weight = projection_weight_grad[:, :model_width]
    grad_key_weight = projection_weight_grad[:, model_width : model_width + HDIM]
    grad_value_weight = projection_weight_grad[:, model_width + HDIM :]
    grad_query_bias = projection_bias_grad[:model_width]
    grad_key_bias = projection_bias_grad[model_width : model_width + ROT]
    grad_value_bias = projection_bias_grad[model_width + HDIM :]
    grad_one_gain = jnp.sum(grad_norm_one * normal_one, axis=0)
    grad_one_bias = jnp.sum(grad_norm_one, axis=0)
    grad_two_gain = jnp.sum(grad_norm_two * normal_two, axis=0)
    grad_two_bias = jnp.sum(grad_norm_two, axis=0)
    grad_tokens = (
        (
            cotangent_float
            + norm_backward(grad_norm_one, normal_one, inverse_std_one, gain_one)
            + norm_backward(grad_norm_two, normal_two, inverse_std_two, gain_two)
        )
        .astype(jnp.bfloat16)
        .reshape(seq_count, local_len, model_width)
    )
    (
        grad_one_gain,
        grad_one_bias,
        grad_query_weight,
        grad_query_bias,
        grad_key_weight,
        grad_key_bias,
        grad_value_weight,
        grad_value_bias,
        grad_out_weight,
        grad_bias_out,
        grad_two_gain,
        grad_two_bias,
        grad_up_weight,
        grad_up_bias,
        grad_down_weight,
    ) = (
        lax.psum_scatter(grad_one_gain, "fsdp", scatter_dimension=0, tiled=True),
        lax.psum_scatter(grad_one_bias, "fsdp", scatter_dimension=0, tiled=True),
        lax.psum_scatter(grad_query_weight, "fsdp", scatter_dimension=0, tiled=True),
        lax.psum_scatter(grad_query_bias, "fsdp", scatter_dimension=0, tiled=True),
        lax.psum_scatter(grad_key_weight, "fsdp", scatter_dimension=0, tiled=True),
        lax.psum_scatter(grad_key_bias, "fsdp", scatter_dimension=0, tiled=True),
        lax.psum_scatter(grad_value_weight, "fsdp", scatter_dimension=0, tiled=True),
        lax.psum_scatter(grad_value_bias, "fsdp", scatter_dimension=0, tiled=True),
        lax.psum_scatter(grad_out_weight, "fsdp", scatter_dimension=0, tiled=True),
        lax.psum_scatter(grad_bias_out, "fsdp", scatter_dimension=0, tiled=True),
        lax.psum_scatter(grad_two_gain, "fsdp", scatter_dimension=0, tiled=True),
        lax.psum_scatter(grad_two_bias, "fsdp", scatter_dimension=0, tiled=True),
        lax.psum_scatter(grad_up_weight, "fsdp", scatter_dimension=0, tiled=True),
        lax.psum_scatter(grad_up_bias, "fsdp", scatter_dimension=0, tiled=True),
        lax.psum_scatter(grad_down_weight, "fsdp", scatter_dimension=0, tiled=True),
    )
    (
        grad_one_gain,
        grad_one_bias,
        grad_query_weight,
        grad_query_bias,
        grad_key_weight,
        grad_key_bias,
        grad_value_weight,
        grad_value_bias,
        grad_out_weight,
        grad_bias_out,
        grad_two_gain,
        grad_two_bias,
        grad_up_weight,
        grad_up_bias,
        grad_down_weight,
    ) = lax.psum(
        (
            grad_one_gain,
            grad_one_bias,
            grad_query_weight,
            grad_query_bias,
            grad_key_weight,
            grad_key_bias,
            grad_value_weight,
            grad_value_bias,
            grad_out_weight,
            grad_bias_out,
            grad_two_gain,
            grad_two_bias,
            grad_up_weight,
            grad_up_bias,
            grad_down_weight,
        ),
        "seq",
    )
    return (
        layer_out,
        grad_tokens,
        grad_one_gain,
        grad_one_bias,
        grad_query_weight,
        grad_query_bias,
        grad_key_weight,
        grad_key_bias,
        grad_value_weight,
        grad_value_bias,
        grad_out_weight,
        grad_bias_out,
        grad_two_gain,
        grad_two_bias,
        grad_up_weight,
        grad_up_bias,
        grad_down_weight,
        grad_bias_out,
    )


def solution(mesh):
    return jax.shard_map(
        on_device,
        mesh=mesh,
        in_specs=(
            P("fsdp", "seq", None),
            P(),
            P("fsdp", None),
            P("fsdp"),
            P("fsdp"),
            P("fsdp", None),
            P("fsdp"),
            P("fsdp", None),
            P("fsdp"),
            P("fsdp", None),
            P("fsdp"),
            P("fsdp", None),
            P("fsdp"),
            P("fsdp"),
            P("fsdp"),
            P("fsdp", None),
            P("fsdp"),
            P("fsdp", None),
            P("fsdp"),
            P("fsdp", "seq", None),
        ),
        out_specs=(
            P("fsdp", "seq", None),
            P("fsdp", "seq", None),
            P("fsdp"),
            P("fsdp"),
            P("fsdp", None),
            P("fsdp"),
            P("fsdp", None),
            P("fsdp"),
            P("fsdp", None),
            P("fsdp"),
            P("fsdp", None),
            P("fsdp"),
            P("fsdp"),
            P("fsdp"),
            P("fsdp", None),
            P("fsdp"),
            P("fsdp", None),
            P("fsdp"),
        ),
        check_vma=False,
    )
```

profile of v0, /device:TPU:0, one launch (start us, length us, event | category | flops | bytes accessed | tf_op | source)
XLA Modules:
  0.0 1135.1 jit_solution(1980284133374254844)
XLA Ops:
  20.2 7.6 all-gather
  35.3 12.8 %all-reduce.21 = (bf16[768]{0:T(1024)(128)(2,1)}, bf16[768]{0:T(1024)(128)(2,1)}, bf16[768]{0:T(1024)(128)(2,1)}, bf16[768]{0:T(1024)(128)(2,1)}, bf16[64]{0:T(2...) all-reduce(bf16[768]{0:T(1024)(128)(2,1)S(1)} %dynamic-update-slice, ...), channel_id=1, replica_groups=mesh['seq'=8,'fsdp'=4] {'fsdp'}, use_global_device_ids=true, to_apply=%add.7 | all-reduce | flops 5456 | bytes 21824
  48.2 5.6 all-gather.1
  62.1 3.6 rev.17
  66.3 3.6 rev.16
  69.9 32.1 %all_gather.59 = bf16[1,2048,128]{1,2,0:T(8,128)(2,1)S(1)} all-gather(bf16[1,256,128]{1,2,0:T(8,128)(2,1)S(1)} %pad_maximum_fusion.4), channel_id=1, replica_groups=mesh['seq'=8,'fsdp'=4] {'seq'}, dimensions={1}, use_global_device_ids=true | all-gather | bytes 589824 | tf_op jit(solution)/shard_map/all_gather | solution.py:190
  106.8 58.6 %while.42 = (s32[]{:T(128)}, f32[2,1,12,128]{3,0,2,1:T(2,128)S(1)}, f32[2,1,12,128]{3,0,2,1:T(2,128)S(1)}, s32[3,8]{1,0:T(4,128)S(1)}, s32[3,8]{1,0:T(4,128)S(1)...) while((s32[]{:T(128)}, f32[2,1,12,128]{3,0,2,1:T(2,128)S(1)}, ...), condition=%wide.region_10.16_spmd.clone.clone, body=%wide.region_6.15_spmd.clone.clone.sunk | while | flops 215642320 | bytes 25396648 | solution.py:274
  110.5 3.0 gather_fusion.2
  116.2 4.3 fusion.297
  121.3 4.8 select_reduce_fusion.6
  130.0 3.0 gather_fusion.2
  135.7 4.3 fusion.297
  140.8 4.8 select_reduce_fusion.6
  149.5 3.0 gather_fusion.2
  155.2 4.3 fusion.297
  160.4 4.8 select_reduce_fusion.6
  167.8 81.4 %while.43 = (s32[]{:T(128)}, f32[2,1,128,12,64]{2,0,4,3,1:T(2,128)S(1)}, f32[2,1,12,128]{3,0,2,1:T(2,128)}, s32[3,8]{1,0:T(4,128)}, s32[3,8]{1,0:T(4,128)S(1)}, ...) while((s32[]{:T(128)}, ...), condition=%wide.region_13.19_spmd.clone.clone, body=%wide.region_11.18_spmd.clone.clone.sunk | while | flops 639938688 | bytes 51209236 | solution.py:304
  175.2 3.1 gather_fusion.6
  181.3 4.3 fusion.308
  190.5 3.9 fusion.315
  202.2 3.1 gather_fusion.6
  208.3 4.3 fusion.308
  217.5 3.9 fusion.315
  229.2 3.1 gather_fusion.6
  235.3 4.3 fusion.308
  244.4 3.9 fusion.315
  251.1 145.6 %while.44 = (s32[]{:T(128)}, f32[2,1,128,12,64]{2,0,4,3,1:T(2,128)}, f32[1,16,128,128]{3,2,1,0:T(8,128)}, s32[3,8]{1,0:T(4,128)}, s32[3,8]{1,0:T(4,128)S(1)}, /*...) while((s32[]{:T(128)}, ...), condition=%wide.region_16.22_spmd.clone.clone, body=%wide.region_14.21_spmd.clone.clone.sunk | while | flops 1045002368 | bytes 81839256 | solution.py:374
  259.4 3.0 gather_fusion.12
  262.5 3.1 gather_fusion.11
  265.6 7.5 fusion.327
  273.1 5.2 copy.383
  278.3 5.2 copy.385
  291.5 4.5 fusion.334
  307.1 3.0 gather_fusion.12
  310.1 3.1 gather_fusion.11
  313.2 7.5 fusion.327
  320.8 5.2 copy.383
  326.0 5.2 copy.385
  339.1 5.6 fusion.334
  355.9 3.0 gather_fusion.12
  358.9 3.1 gather_fusion.11
  362.0 7.5 fusion.327
  369.5 5.2 copy.383
  374.7 5.2 copy.385
  387.9 5.6 fusion.334
  400.4 4.7 rev.19
  406.2 57.1 %reduce-scatter.8.cloned.1.call-done = f32[1,256,128]{1,2,0:T(8,128)} async-done(((f32[1,2048,128]{1,2,0:T(8,128)}), f32[1,256,128]{1,2,0:T(8,128)}) %reduce-scatter.8.cloned.1.call-update) | async-done | bytes 131088 | tf_op jit(solution)/shard_map/reduce_scatter | solution.py:375
  473.8 3.2 slice.196
  477.2 5.2 all-gather.2
  482.4 18.9 %all-gather.12.cloned.1.call-done = bf16[3072,768]{1,0:T(8,128)(2,1)} async-done(((bf16[768,768]{1,0:T(8,128)(2,1)}), bf16[3072,768]{1,0:T(8,128)(2,1)}) %all-gather.12.cloned.1.call-update) | async-done | bytes 4718608 | tf_op jit(solution)/shard_map/all_gather | solution.py:310
  501.3 11.1 fusion.128
  512.5 27.9 %all-gather.14.cloned.1.call-done = bf16[3072,768]{1,0:T(8,128)(2,1)} async-done(((bf16[768,768]{1,0:T(8,128)(2,1)}), bf16[3072,768]{1,0:T(8,128)(2,1)}) %all-gather.14.cloned.1.call-update) | async-done | bytes 4718608 | tf_op jit(solution)/shard_map/all_gather | solution.py:312
  540.3 6.3 convert_reduce_fusion
  547.8 5.3 fusion.212
  553.4 6.5 fusion.175
  562.8 4.3 fusion.225
  569.6 10.8 all-reduce.20
  588.4 36.3 %reduce-scatter.16.cloned.1.call-done = f32[192,768]{1,0:T(8,128)} async-done(((f32[768,768]{1,0:T(8,128)}), f32[192,768]{1,0:T(8,128)}) %reduce-scatter.16.cloned.1.call-update) | async-done | bytes 589840 | tf_op jit(solution)/shard_map/reduce_scatter | solution.py:437
  624.8 36.2 %reduce-scatter.10.cloned.1.call-done = f32[192,768]{1,0:T(8,128)} async-done(((f32[768,768]{1,0:T(8,128)}), f32[192,768]{1,0:T(8,128)}) %reduce-scatter.10.cloned.1.call-update) | async-done | bytes 589840 | tf_op jit(solution)/shard_map/reduce_scatter | solution.py:431
  661.0 81.1 %reduce-scatter.18.cloned.1.call-done = f32[768,768]{1,0:T(8,128)} async-done(((f32[3072,768]{1,0:T(8,128)}), f32[768,768]{1,0:T(8,128)}) %reduce-scatter.18.cloned.1.call-update) | async-done | bytes 2359312 | tf_op jit(solution)/shard_map/reduce_scatter | solution.py:441
  742.1 81.2 %reduce-scatter.20.cloned.1.call-done = f32[768,768]{1,0:T(8,128)} async-done(((f32[3072,768]{1,0:T(8,128)}), f32[768,768]{1,0:T(8,128)}) %reduce-scatter.20.cloned.1.call-update) | async-done | bytes 2359312 | tf_op jit(solution)/shard_map/reduce_scatter | solution.py:443
  823.4 3.8 fusion.224
  828.5 74.6 %all-reduce.25.cloned.1.call-done = (f32[192]{0:T(256)}, f32[192]{0:T(256)}, f32[192]{0:T(256)}, f32[192,64]{1,0:T(8,128)}, f32[4]{0:T(128)}, /*index=5*/f32[192...) async-done(((f32[192]{0:T(256)}, f32[192]{0:T(256)}, f32[192]{0:T(256)}, f32[192,64]{1,0:T(8,128)}, f32[4]{0:T(128)}, ...) | async-done | bytes 106080 | tf_op jit(solution)/shard_map/psum | solution.py:461
  906.4 203.5 %all-reduce.27.cloned.1.call-done = (f32[192,768]{1,0:T(8,128)}, f32[192,768]{1,0:T(8,128)}, f32[768,768]{1,0:T(8,128)}, f32[768,768]{1,0:T(8,128)}) async-done(((f32[192,768]{1,0:T(8,128)}, f32[192,768]{1,0:T(8,128)}, f32[768,768]{1,0:T(8,128)}, f32[768,768]{1,0:T(8,128)}), (f32[192,768]{1,0:T(8,128)}, f32[192,768]{1,0:T(8,128)}, f32[768,768]{1,0:T(8,128)}, ...) | async-done | bytes 5898256 | tf_op jit(solution)/shard_map/psum | solution.py:461
  (523 shorter events, 207.5 us)
Async XLA Ops:
  7.2 50.0 %all-gather.8.cloned.1.call-start = ((), (), s32[]{:S(2)}) async-start(), calls=%async_computation.7 | async-start | bytes 1474560 | tf_op jit(solution)/shard_map/all_gather | solution.py:130
  7.9 52.1 %all-gather.10.cloned.1.call-start = ((), (), s32[]{:S(2)}) async-start(), calls=%async_computation.8 | async-start | bytes 1474560 | tf_op jit(solution)/shard_map/all_gather | solution.py:133
  8.7 454.6 %reduce-scatter.8.cloned.1.call-start = ((), (), s32[]{:S(2)}) async-start(), calls=%async_computation.11 | async-start | bytes 1179648 | tf_op jit(solution)/shard_map/reduce_scatter | solution.py:375
  8.7 51.1 %copy-start.42 = (f32[8]{0:T(128)}, f32[8]{0:T(128)S(1)}, u32[]{:S(2)}) copy-start(f32[8]{0:T(128)S(1)} %multiply_power_fusion) | copy-start | bytes 100
  19.1 40.6 %copy-start.33 = (f32[256]{0:T(256)}, f32[256]{0:T(256)S(1)}, u32[]{:S(2)}) copy-start(f32[256]{0:T(256)S(1)} %broadcast_multiply_fusion.4) | copy-start | bytes 3076
  19.9 39.9 %copy-start.35 = (f32[256]{0:T(256)}, f32[256]{0:T(256)S(1)}, u32[]{:S(2)}) copy-start(f32[256]{0:T(256)S(1)} %get-tuple-element.1062) | copy-start | bytes 3076
  55.3 4.5 copy-start.31
  55.3 4.4 copy-start.39
  55.5 4.3 copy-start.20
  55.6 4.2 copy-start.22
  57.0 2.9 copy-start.37
  57.1 8.8 copy-start.24
  57.1 8.8 copy-start.26
  57.2 2.9 copy-start.7
  65.9 37.1 %copy-start.15 = (bf16[2,1,128,12,64]{2,0,4,3,1:T(2,128)(2,1)S(1)}, bf16[2,1,128,12,64]{2,0,4,3,1:T(2,128)(2,1)}, u32[]{:S(2)}) copy-start(bf16[2,1,128,12,64]{2,0,4,3,1:T(2,128)(2,1)} %rev.17) | copy-start | bytes 1179652
  66.3 40.5 %copy-start.50 = (pred[3,8]{1,0:T(4,128)(4,1)S(1)}, pred[3,8]{1,0:T(4,128)(4,1)}, u32[]{:S(2)}) copy-start(pred[3,8]{1,0:T(4,128)(4,1)} %get-tuple-element.1479) | copy-start | bytes 76
  190.5 3.9 copy-start.17
  217.4 3.9 copy-start.17
  244.4 3.9 copy-start.17
  249.2 1.9 copy-start.2
  283.5 2.6 copy-start.1
  283.5 2.6 copy-start.9
  287.5 2.2 copy-start
  331.2 2.6 copy-start.1
  331.2 2.6 copy-start.9
  335.1 2.2 copy-start
  379.9 2.6 copy-start.1
  379.9 2.6 copy-start.9
  383.9 2.2 copy-start
  399.2 102.1 %all-gather.12.cloned.1.call-start = ((), (), s32[]{:S(2)}) async-start(), calls=%async_computation.9 | async-start | bytes 5898240 | tf_op jit(solution)/shard_map/all_gather | solution.py:310
  399.8 140.5 %all-gather.14.cloned.1.call-start = ((), (), s32[]{:S(2)}) async-start(), calls=%async_computation.10 | async-start | bytes 5898240 | tf_op jit(solution)/shard_map/all_gather | solution.py:312
  400.4 5.7 copy-start.25
  400.4 5.7 copy-start.27
  400.4 185.7 %reduce-scatter.14.cloned.1.call-start = ((), (), s32[]{:S(2)}) async-start(), calls=%async_computation.14 | async-start | bytes 491520 | tf_op jit(solution)/shard_map/reduce_scatter | solution.py:435
  405.2 59.0 %copy-start.36 = (f32[256]{0:T(256)S(1)}, f32[256]{0:T(256)}, u32[]{:S(2)}) copy-start(f32[256]{0:T(256)} %copy-done.35) | copy-start | bytes 3076
  405.2 59.0 %copy-start.43 = (f32[8]{0:T(128)S(1)}, f32[8]{0:T(128)}, u32[]{:S(2)}) copy-start(f32[8]{0:T(128)} %copy-done.42) | copy-start | bytes 100
  405.2 60.7 %copy-start.6 = (bf16[1,256,768]{2,1,0:T(8,128)(2,1)S(1)}, bf16[1,256,768]{2,1,0:T(8,128)(2,1)}, u32[]{:S(2)}) copy-start(bf16[1,256,768]{2,1,0:T(8,128)(2,1)} %param.36) | copy-start | bytes 1179652
  405.2 60.7 %copy-start.32 = (f32[768]{0:T(1024)S(1)}, f32[768]{0:T(1024)}, u32[]{:S(2)}) copy-start(f32[768]{0:T(1024)} %copy-done.31) | copy-start | bytes 9220
  405.2 60.7 %copy-start.34 = (f32[256]{0:T(256)S(1)}, f32[256]{0:T(256)}, u32[]{:S(2)}) copy-start(f32[256]{0:T(256)} %copy-done.33) | copy-start | bytes 3076
  405.2 60.7 %copy-start.38 = (f32[256]{0:T(256)S(1)}, f32[256]{0:T(256)}, u32[]{:S(2)}) copy-start(f32[256]{0:T(256)} %copy-done.37) | copy-start | bytes 3076
  405.2 60.7 %copy-start.40 = (f32[768]{0:T(1024)S(1)}, f32[768]{0:T(1024)}, u32[]{:S(2)}) copy-start(f32[768]{0:T(1024)} %copy-done.39) | copy-start | bytes 9220
  406.2 63.1 %copy-start.3 = (f32[2,1,128,12,64]{2,0,4,3,1:T(2,128)S(1)}, f32[2,1,128,12,64]{2,0,4,3,1:T(2,128)}, u32[]{:S(2)}) copy-start(f32[2,1,128,12,64]{2,0,4,3,1:T(2,128)} %copy-done.2) | copy-start | bytes 2359300
  466.7 1.5 copy-start.5
  468.2 3.6 copy-start.8
  469.3 119.1 %reduce-scatter.12.cloned.1.call-start = ((), (), s32[]{:S(2)}) async-start(), calls=%async_computation.13 | async-start | bytes 491520 | tf_op jit(solution)/shard_map/reduce_scatter | solution.py:433
  471.7 153.1 %reduce-scatter.16.cloned.1.call-start = ((), (), s32[]{:S(2)}) async-start(), calls=%async_computation.15 | async-start | bytes 2949120 | tf_op jit(solution)/shard_map/reduce_scatter | solution.py:437
  473.7 3.4 copy-start.48
  473.8 3.4 copy-start.49
  473.8 3.4 copy-start.47
  473.8 187.2 %reduce-scatter.10.cloned.1.call-start = ((), (), s32[]{:S(2)}) async-start(), calls=%async_computation.12 | async-start | bytes 2949120 | tf_op jit(solution)/shard_map/reduce_scatter | solution.py:431
  477.1 265.0 %reduce-scatter.18.cloned.1.call-start = ((), (), s32[]{:S(2)}) async-start(), calls=%async_computation.16 | async-start | bytes 11796480 | tf_op jit(solution)/shard_map/reduce_scatter | solution.py:441
  553.1 270.3 %reduce-scatter.20.cloned.1.call-start = ((), (), s32[]{:S(2)}) async-start(), calls=%async_computation.17 | async-start | bytes 11796480 | tf_op jit(solution)/shard_map/reduce_scatter | solution.py:443
  559.9 343.3 %all-reduce.25.cloned.1.call-start = ((), (), s32[]{:S(2)}) async-start(), calls=%async_computation.18 | async-start | bytes 415744 | tf_op jit(solution)/shard_map/psum | solution.py:461
  562.8 4.4 copy-start.21
  562.8 4.4 copy-start.23
  562.8 4.4 copy-start.51
  569.6 253.7 %copy-start.46 = (bf16[768]{0:T(1024)(128)(2,1)S(1)}, bf16[768]{0:T(1024)(128)(2,1)}, u32[]{:S(2)}) copy-start(bf16[768]{0:T(1024)(128)(2,1)} %get-tuple-element.1006) | copy-start | bytes 4612
  569.6 253.8 %copy-start.45 = (bf16[768]{0:T(1024)(128)(2,1)S(1)}, bf16[768]{0:T(1024)(128)(2,1)}, u32[]{:S(2)}) copy-start(bf16[768]{0:T(1024)(128)(2,1)} %get-tuple-element.1007) | copy-start | bytes 4612
  569.6 253.8 %copy-start.10 = (bf16[256,3072]{1,0:T(8,128)(2,1)S(1)}, bf16[256,3072]{1,0:T(8,128)(2,1)}, u32[]{:S(2)}) copy-start(bf16[256,3072]{1,0:T(8,128)(2,1)} %get-tuple-element.1065) | copy-start | bytes 4718596
  588.4 521.5 %all-reduce.27.cloned.1.call-start = ((), (), s32[]{:S(2)}) async-start(), calls=%async_computation.19 | async-start | bytes 11796480 | tf_op jit(solution)/shard_map/psum | solution.py:461
  823.4 3.8 copy-start.16
  1109.9 14.9 %copy-start.12 = (f32[768,768]{1,0:T(8,128)S(1)}, f32[768,768]{1,0:T(8,128)}, u32[]{:S(2)}) copy-start(f32[768,768]{1,0:T(8,128)} %get-tuple-element.1570) | copy-start | bytes 7077892
  1115.6 10.6 copy-start.44
  1115.6 11.2 copy-start.11
  (15 other events, 13.2 us)
Sparse Core Ops, SparseCore 0:
  9.6 20.8 all-gather.7
  32.0 17.6 all-gather.9
  399.3 63.8 reduce-scatter.7
  464.8 36.5 all-gather.11
  502.8 37.4 all-gather.13
  543.4 20.8 reduce-scatter.13
  567.5 20.8 reduce-scatter.11
  591.6 33.0 reduce-scatter.15
  627.9 33.0 reduce-scatter.9
  663.6 78.4 reduce-scatter.17
  744.8 78.4 reduce-scatter.19
  830.3 72.7 all-reduce.24
  907.2 202.6 all-reduce.26
where the time goes:
time: 1140 us
  waiting for transfers between devices  622 us (55%)
  local copies, waits for them, and re-layouts  185 us (16%)
  matrix products  126 us (11%)
  other arithmetic  101 us (9%)
  blocking collectives  74.1 us (6%)
  between operations  23.8 us (2%)
    psum x2, waiting for transfers between devices, on_device(): lax.psum((grad_one_gain, grad_one_bias, grad_query_weight, grad_query_bia...  278 us
    reduce_scatter x1, waiting for transfers between devices, on_device(): lax.psum_scatter(grad_down_weight, 'fsdp', scatter_dimension=0, tiled=True)  81.2 us
    reduce_scatter x1, waiting for transfers between devices, on_device(): lax.psum_scatter(grad_up_weight, 'fsdp', scatter_dimension=0, tiled=True)  81.1 us
    reduce_scatter x1, waiting for transfers between devices, on_device(): lax.psum_scatter(back_state[1].reshape(seq_count, length, pair_width), 's...  57.1 us
    another operation x12, other arithmetic  44.5 us
    unnamed x145, local copies, waits for them, and re-layouts  44.5 us
    reduce_scatter x1, waiting for transfers between devices, on_device(): lax.psum_scatter(grad_out_weight, 'fsdp', scatter_dimension=0, tiled=True)  36.3 us
    reduce_scatter x1, waiting for transfers between devices, on_device(): lax.psum_scatter(grad_query_weight, 'fsdp', scatter_dimension=0, tiled=True)  36.2 us
  transfers between devices with their start and end apart: 13, of which 10 were waited for; matrix products, arithmetic and copies ran while one was open for 8% of the time, Pallas kernels for 0%

commit v1 on v0

v1 whole, which is shorter than its diff:
```python
import functools

import jax
import jax.numpy as jnp
from jax import lax
from jax.experimental import pallas as pl
from jax.experimental.pallas import tpu as pltpu
from jax.sharding import PartitionSpec as P

HEADS = 12
HDIM = 64
ROT = 16
HALF = ROT // 2
BLOCK = 128

NEGATIVE = -1e30
EPSILON = 1e-05
SQRT_HALF = 0.7071067811865476
GAUSS_FACTOR = 0.3989422804014327
SCALE = HDIM ** (-0.5)
BF = jnp.bfloat16
F32 = jnp.float32
MIB = 1024 * 1024
VMEM = pl.BlockSpec(memory_space=pltpu.VMEM)
SMEM = pl.BlockSpec(memory_space=pltpu.SMEM)

NN = (((1,), (0,)), ((), ()))
NT = (((1,), (1,)), ((), ()))
TN = (((0,), (0,)), ((), ()))


def dot(left, right, dims=NN):
    return lax.dot_general(left, right, dims, preferred_element_type=F32)


def shape(dims, dtype):
    return jax.ShapeDtypeStruct(dims, dtype)


def params(limit=48):
    return pltpu.CompilerParams(vmem_limit_bytes=limit * MIB)


def cost(flops, data, special=0):
    return pl.CostEstimate(flops=flops, bytes_accessed=data, transcendentals=special)


def swap(value, axis, bit):
    size = lax.axis_size(axis)
    return lax.ppermute(value, axis, [(i, i ^ bit) for i in range(size)])


def bits_of(size):
    return [1 << i for i in range(size.bit_length() - 1)]


def normalize(values):
    center = values - jnp.mean(values, -1, keepdims=True)
    inverse_std = lax.rsqrt(jnp.mean(center * center, -1, keepdims=True) + EPSILON)
    return (center * inverse_std, inverse_std)


def pick(pieces, index):
    result = pieces[-1]
    for i in range(len(pieces) - 2, -1, -1):
        result = jnp.where(index == i, pieces[i], result)
    return result


def rel_order(size):
    order = [0]
    for bit in reversed(bits_of(size)):
        order = order + [r ^ bit for r in order]
    return order


def front_kernel(rels, x_ref, *refs):
    count = len(rels)
    packs = refs[:count]
    cs_ref, n1_ref, kv_ref, vec_ref, wkv_ref, pieces = refs[count:]
    me = lax.axis_index("fsdp")
    part = packs[0].shape[0] - 16
    for rel, pack in zip(rels, packs):
        wkv_ref[pl.ds((rel ^ me) * part, part), :] = pack[:part, : 2 * HDIM]
        pieces[rel ^ me] = pack[part:, :].astype(F32)
    vec = jnp.concatenate([pieces[p] for p in range(count)], axis=1)
    vec_ref[...] = vec
    normal, _ = normalize(x_ref[...].astype(F32))
    n1 = (normal * vec[0:1] + vec[1:2]).astype(BF)
    n1_ref[...] = n1
    key_part, value_part = ROT // count, HDIM // count
    key_bias = jnp.concatenate([pieces[p][7:8, :key_part] for p in range(count)], axis=1)
    value_bias = jnp.concatenate(
        [pieces[p][7:8, key_part : key_part + value_part] for p in range(count)], axis=1
    )
    bias = jnp.concatenate([key_bias, jnp.zeros((1, HDIM - ROT), F32), value_bias], axis=1)
    turned = (dot(n1, wkv_ref[...]) + bias).T
    cosine, sine = cs_ref[:HALF], cs_ref[HALF:]
    first, second = turned[:HALF], turned[HALF:ROT]
    turned = jnp.concatenate(
        [first * cosine - second * sine, second * cosine + first * sine, turned[ROT:]], axis=0
    )
    kv_ref[...] = turned.T.astype(BF)


def query_kernel(n1_ref, dy_ref, wq_ref, wo_ref, vec_ref, cs_ref, qt_ref, dot_ref):
    width = wq_ref.shape[1]
    turned = (dot(n1_ref[...], wq_ref[...]) + vec_ref[4:5]).T
    cosine, sine = cs_ref[:HALF], cs_ref[HALF:]
    for h in range(HEADS):
        base = h * HDIM
        first, second = turned[base : base + HALF], turned[base + HALF : base + ROT]
        head = jnp.concatenate(
            [
                first * cosine - second * sine,
                second * cosine + first * sine,
                turned[base + ROT : base + HDIM],
            ],
            axis=0,
        )
        qt_ref[base : base + HDIM, :] = (head.astype(BF).astype(F32) * SCALE).astype(BF)
    dot_ref[...] = dot(dy_ref[...], wo_ref[...], NT).T.astype(BF)


def mlp_kernel(rels, seq_orders, shards, *refs):
    count = len(rels)
    xs = refs[:count]
    dys = refs[count : 2 * count]
    (
        up_ref,
        down_ref,
        ub_ref,
        vec_ref,
        keep_ref,
        send_ref,
        n1c_ref,
        upk_ref,
        ups_ref,
        dnk_ref,
        dns_ref,
        sums_ref,
        x_s,
        dy_s,
        acc_up,
        acc_dn,
        acc_v,
    ) = refs[2 * count :]
    step = pl.program_id(0)
    me = lax.axis_index("fsdp")
    seq_me = lax.axis_index("seq")
    width = up_ref.shape[1]
    hidden = up_ref.shape[0]
    sequence = rels[count // 2 :] + rels[: count // 2]
    for g, rel in enumerate(sequence):
        index = rels.index(rel)

        @pl.when(step == g)
        def _():
            x_s[...] = xs[index][...].astype(F32)
            dy_s[...] = dys[index][...]

    @pl.when(step == 0)
    def _():
        acc_up[...] = jnp.zeros_like(acc_up)
        acc_dn[...] = jnp.zeros_like(acc_dn)
        acc_v[...] = jnp.zeros_like(acc_v)

    rel_now = pick([jnp.int32(r) for r in sequence], step)
    normal, _ = normalize(x_s[...])
    part = width // count
    n1 = (normal * vec_ref[0:1] + vec_ref[1:2])
    n1c_ref[rel_now ^ me] = pick(
        [n1[:, p * part : (p + 1) * part] for p in range(count)], me
    ).astype(BF)
    n2 = (normal * vec_ref[2:3] + vec_ref[3:4]).astype(BF)
    dy = dy_s[...]
    out = None
    dn2 = None
    tile = 256
    for c in range(hidden // tile):
        rows = slice(c * tile, (c + 1) * tile)
        up_c, down_c = up_ref[rows, :], down_ref[rows, :]
        u = dot(n2, up_c, NT) + ub_ref[:, rows].astype(F32)
        dg = dot(dy, down_c, NT)
        phi = 0.5 * (1.0 + lax.erf(u * SQRT_HALF))
        g = (u * phi).astype(BF)
        du = (dg * (phi + u * jnp.exp(-0.5 * u * u) * GAUSS_FACTOR)).astype(BF)
        out_c = dot(g, down_c)
        dn2_c = dot(du, up_c)
        out = out_c if out is None else out + out_c
        dn2 = dn2_c if dn2 is None else dn2 + dn2_c
        acc_dn[rows, :] += dot(g, dy, TN)
        acc_up[rows, :] += dot(du, n2, TN)
        acc_v[2:3, rows] += jnp.sum(du.astype(F32), axis=0, keepdims=True)
    acc_v[0:1, :width] += jnp.sum(dn2 * normal, axis=0, keepdims=True)
    acc_v[1:2, :width] += jnp.sum(dn2, axis=0, keepdims=True)
    out_low = out.astype(BF)
    h_low = (dn2 * vec_ref[2:3]).astype(BF)

    @pl.when(step < count // 2)
    def _():
        send_ref[0, 0] = out_low
        send_ref[0, 1] = h_low

    @pl.when(step >= count // 2)
    def _():
        keep_ref[0, 0] = out_low
        keep_ref[0, 1] = h_low

    @pl.when(step == count - 1)
    def _():
        sums_ref[...] = acc_v[...]
        rows = hidden // shards
        for acc, order, near, far in (
            (acc_up, seq_orders[0], upk_ref, ups_ref),
            (acc_dn, seq_orders[1], dnk_ref, dns_ref),
        ):
            for m in range(shards):
                source = (order[m] ^ seq_me) & (shards - 1)
                value = acc[pl.ds(pl.multiple_of(source * rows, rows), rows), :].astype(BF)
                half = shards // 2
                target = near if m < half else far
                target[(m % half) * rows : (m % half + 1) * rows, :] = value


def attend_kernel(
    per_group,
    chunk_blocks,
    most,
    order_ref,
    len_ref,
    qt_ref,
    dot_ref,
    kv_ref,
    cs_ref,
    o_ref,
    dq_ref,
    dkv_ref,
    s_scr,
    p_scr,
    pb_scr,
    ds_scr,
    bias_scr,
    kv_scr,
    dkv_scr,
    qs,
    dos,
    ot,
    dqt,
    inverse,
):
    side, group = pl.program_id(0), pl.program_id(1)
    seq_me = lax.axis_index("seq")
    slots = kv_ref.shape[0] // BLOCK
    chunk = chunk_blocks * BLOCK
    lanes = per_group * BLOCK
    first_step = jnp.logical_and(side == 0, group == 0)
    last_step = jnp.logical_and(
        side == pl.num_programs(0) - 1, group == pl.num_programs(1) - 1
    )

    @pl.when(first_step)
    def _():
        dkv_scr[...] = jnp.zeros_like(dkv_scr)

        @pl.loop(0, slots)
        def _(i):
            rel = (i // 2) ^ seq_me
            place = jnp.int32(0)
            for bit in bits_of(slots // 2):
                place = place * 2 + (rel // bit) % 2
            inverse[order_ref[i]] = place * 2 + i % 2

    block = order_ref[2 * seq_me + side]
    base = block * BLOCK
    end_1 = len_ref[0, 0]
    end_2 = end_1 + len_ref[0, 1]
    end_3 = end_2 + len_ref[0, 2]

    def start_of(position):
        low = jnp.where(position >= end_1, end_1, 0)
        low = jnp.where(position >= end_2, end_2, low)
        return jnp.where(position >= end_3, end_3, low)

    q_pos = base + lax.broadcasted_iota(jnp.int32, (1, BLOCK), 1)
    q_start = start_of(q_pos)
    low_block = jnp.maximum(start_of(base) // BLOCK, block - (most - 1))
    chunks = (block - low_block + chunk_blocks) // chunk_blocks

    def slot_of(j):
        return inverse[jnp.minimum(low_block + j, block)]

    @pl.loop(0, chunks * chunk_blocks)
    def _(j):
        kv_scr[pl.ds(j * BLOCK, BLOCK), :] = kv_ref[pl.ds(slot_of(j) * BLOCK, BLOCK), :]

    for h in range(per_group):
        cols = slice(h * BLOCK, (h + 1) * BLOCK)
        qs[:, cols] = qt_ref[h * HDIM : (h + 1) * HDIM, :]
        dos[:, cols] = dot_ref[h * HDIM : (h + 1) * HDIM, :]

    def score_step(c, top):
        kv = kv_scr[pl.ds(c * chunk, chunk), :]
        s_scr[c] = dot(kv[:, :HDIM], qs[...])
        p_scr[c] = dot(kv[:, HDIM:], dos[...])
        k_pos = (low_block + c * chunk_blocks) * BLOCK + lax.broadcasted_iota(
            jnp.int32, (chunk, BLOCK), 0
        )
        allowed = jnp.logical_and(k_pos <= q_pos, k_pos >= q_start)
        bias_scr[...] = jnp.where(allowed, 0.0, NEGATIVE)
        tops = []
        for h in range(per_group):
            cols = slice(h * BLOCK, (h + 1) * BLOCK)
            s = s_scr[c, :, cols] + bias_scr[...]
            s_scr[c, :, cols] = s
            tops.append(jnp.max(s, axis=0, keepdims=True))
        return jnp.maximum(top, jnp.concatenate(tops, axis=1))

    top = lax.fori_loop(0, chunks, score_step, jnp.full((1, lanes), NEGATIVE, F32))

    def weight_step(c, carry):
        total, delta = carry
        totals, deltas = [], []
        for h in range(per_group):
            cols = slice(h * BLOCK, (h + 1) * BLOCK)
            e = jnp.exp(s_scr[c, :, cols] - top[:, cols])
            s_scr[c, :, cols] = e
            totals.append(jnp.sum(e, axis=0, keepdims=True))
            deltas.append(jnp.sum(e * p_scr[c, :, cols], axis=0, keepdims=True))
        return (
            total + jnp.concatenate(totals, axis=1),
            delta + jnp.concatenate(deltas, axis=1),
        )

    zero = jnp.zeros((1, lanes), F32)
    total, delta = lax.fori_loop(0, chunks, weight_step, (zero, zero))
    shrink = 1.0 / total
    delta = delta * shrink
    ot[...] = jnp.zeros_like(ot)
    dqt[...] = jnp.zeros_like(dqt)

    def grad_step(c, _):
        for h in range(per_group):
            cols = slice(h * BLOCK, (h + 1) * BLOCK)
            p = s_scr[c, :, cols] * shrink[:, cols]
            pb_scr[:, cols] = p.astype(BF)
            ds_scr[:, cols] = (p * (p_scr[c, :, cols] - delta[:, cols])).astype(BF)
        kv = kv_scr[pl.ds(c * chunk, chunk), :]
        ot[...] += dot(kv[:, HDIM:], pb_scr[...], TN)
        dqt[...] += dot(kv[:, :HDIM], ds_scr[...], TN)
        dk = dot(ds_scr[...], qs[...], NT)
        dv = dot(pb_scr[...], dos[...], NT)
        both = jnp.concatenate([dk, dv], axis=1)
        for b in range(chunk_blocks):

            @pl.when(low_block + c * chunk_blocks + b <= block)
            def _():
                place = slot_of(c * chunk_blocks + b) * BLOCK
                dkv_scr[pl.ds(pl.multiple_of(place, BLOCK), BLOCK), :] += both[
                    b * BLOCK : (b + 1) * BLOCK
                ]

        return 0

    lax.fori_loop(0, chunks, grad_step, 0)
    cosine, sine = cs_ref[:HALF], cs_ref[HALF:]
    outs, grads = [], []
    for h in range(per_group):
        cols = slice(h * BLOCK, (h + 1) * BLOCK)
        outs.append(ot[:, cols])
        grad = dqt[:, cols] * SCALE
        first, second = grad[:HALF], grad[HALF:ROT]
        grads.append(first * cosine + second * sine)
        grads.append(second * cosine - first * sine)
        grads.append(grad[ROT:])
    o_ref[...] = jnp.concatenate(outs, axis=0).T.astype(BF)
    dq_ref[...] = jnp.concatenate(grads, axis=0).T.astype(BF)

    @pl.when(last_step)
    def _():
        dkv_ref[...] = dkv_scr[...].astype(dkv_ref.dtype)


def output_kernel(x_ref, o_ref, wo_ref, vec_ref, near_ref, far_ref, layer_ref):
    mlp = near_ref[...].astype(F32) + far_ref[...].astype(F32)
    attention = dot(o_ref[...], wo_ref[...]) + vec_ref[5:6]
    layer_ref[...] = (x_ref[...].astype(F32) + attention + mlp + vec_ref[6:7]).astype(BF)


def weight_kernel(rels, n1c_ref, dq_ref, o_ref, *refs):
    count = len(rels)
    dys = refs[:count]
    (grad_ref,) = refs[count:]
    me = lax.axis_index("fsdp")
    part = n1c_ref.shape[2]
    rows = dys[0].shape[0]
    grad_q = None
    grad_o = None
    for p in range(count):
        term = dot(n1c_ref[p], dq_ref[p * rows : (p + 1) * rows, :], TN)
        grad_q = term if grad_q is None else grad_q + term
    for rel, dy_ref in zip(rels, dys):
        start = pl.multiple_of((rel ^ me) * rows, rows)
        o = o_ref[pl.ds(start, rows), :]
        cols = pick([o[:, p * part : (p + 1) * part] for p in range(count)], me)
        term = dot(cols, dy_ref[...], TN)
        grad_o = term if grad_o is None else grad_o + term
    grad_ref[:part] = grad_q.astype(BF)
    grad_ref[part:] = grad_o.astype(BF)


def tail_kernel(
    rels,
    x_ref,
    dy_ref,
    n1_ref,
    dq_ref,
    wq_ref,
    wkv_ref,
    vec_ref,
    cs_ref,
    near_ref,
    far_ref,
    dkvn_ref,
    dkvf_ref,
    sums_ref,
    grad_ref,
    keep_ref,
    send_ref,
    wg_s,
    vs,
):
    count = len(rels)
    me = lax.axis_index("fsdp")
    dkv = (dkvn_ref[...].astype(F32) + dkvf_ref[...].astype(F32)).T
    cosine, sine = cs_ref[:HALF], cs_ref[HALF:]
    first, second = dkv[:HALF], dkv[HALF:ROT]
    dkv = jnp.concatenate(
        [first * cosine + second * sine, second * cosine - first * sine, dkv[ROT:]], axis=0
    )
    dkv = dkv.T.astype(BF)
    dq = dq_ref[...]
    dn1 = dot(dq, wq_ref[...], NT) + dot(dkv, wkv_ref[...], NT)
    normal, inverse_std = normalize(x_ref[...].astype(F32))
    dy = dy_ref[...].astype(F32)
    total = near_ref[...].astype(F32) + far_ref[...].astype(F32) + dn1 * vec_ref[0:1]
    grad_ref[...] = (
        dy
        + inverse_std
        * (
            total
            - jnp.mean(total, -1, keepdims=True)
            - normal * jnp.mean(total * normal, -1, keepdims=True)
        )
    ).astype(BF)
    wg_s[...] = dot(n1_ref[...], dkv, TN)
    width = x_ref.shape[1]
    part = width // count
    dkv_sum = jnp.sum(dkv.astype(F32), axis=0, keepdims=True)
    vec = jnp.concatenate(
        [
            jnp.sum(dn1 * normal, axis=0, keepdims=True),
            jnp.sum(dn1, axis=0, keepdims=True),
            sums_ref[0:1, :width],
            sums_ref[1:2, :width],
            jnp.sum(dq.astype(F32), axis=0, keepdims=True),
            jnp.sum(dy, axis=0, keepdims=True),
        ],
        axis=0,
    )
    lanes = 128
    chunks = -(-part // lanes)
    for p in range(count):
        piece = vec[:, p * part : (p + 1) * part]
        piece = jnp.concatenate([piece, jnp.zeros((6, chunks * lanes - part), F32)], axis=1)
        for c in range(chunks):
            vs[p, c * 8 : c * 8 + 6, :] = piece[:, c * lanes : (c + 1) * lanes]
            vs[p, c * 8 + 6 : c * 8 + 7, :] = dkv_sum
            vs[p, c * 8 + 7 : c * 8 + 8, :] = jnp.zeros((1, lanes), F32)
    half = count // 2
    extra = sums_ref.shape[1] // lanes
    top = part + 8 * chunks
    for m, rel in enumerate(rels):
        target = keep_ref if m < half else send_ref
        place = m % half
        target[place, :part] = wg_s[pl.ds(pl.multiple_of((rel ^ me) * part, part), part), :]
        target[place, part:top] = vs[rel ^ me]
        for e in range(target.shape[1] - top):
            if rel == 0 and e < extra:
                row = sums_ref[2:3, e * lanes : (e + 1) * lanes]
            else:
                row = jnp.zeros((1, lanes), F32)
            target[place, top + e : top + e + 1] = row


def final_kernel(seq_orders, shards, upn, upf, dnn, dnf, gup_ref, gdn_ref):
    step = pl.program_id(0)
    seq_me = lax.axis_index("seq")
    rows = gup_ref.shape[0]
    half = shards // 2
    for order, near, far, target in (
        (seq_orders[0], upn, upf, gup_ref),
        (seq_orders[1], dnn, dnf, gdn_ref),
    ):
        wanted = (step ^ seq_me) & (shards - 1)
        place = jnp.int32(0)
        for m, rel in enumerate(order):
            place = jnp.where(wanted == rel, m, place)

        @pl.when(place < half)
        def _():
            start = pl.multiple_of(place * rows, rows)
            target[...] = near[pl.ds(start, rows), :].astype(F32)

        @pl.when(place >= half)
        def _():
            start = pl.multiple_of((place - half) * rows, rows)
            target[...] = far[pl.ds(start, rows), :].astype(F32)


def shard_order(bits):
    order = [0]
    for bit in reversed(bits):
        order = order + [r ^ bit for r in order]
    return order


def reduce_shards(near, far, bits, rest):
    for index, bit in enumerate(bits):
        value = near + swap(far, "seq", bit)
        if index + 1 < len(bits):
            half = value.shape[0] // 2
            near, far = value[:half], value[half:]
    for bit in rest:
        value = value + swap(value, "seq", bit)
    for index, bit in enumerate(reversed(bits)):
        other = swap(value, "seq", bit)
        if index + 1 < len(bits):
            value = jnp.concatenate([value, other], axis=0)
    return (value, other)


def on_device(
    tokens,
    block_order,
    doc_lengths,
    norm_one_gain,
    norm_one_bias,
    query_weight,
    query_bias,
    key_weight,
    key_bias,
    value_weight,
    value_bias,
    out_weight,
    out_bias,
    norm_two_gain,
    norm_two_bias,
    up_weight,
    up_bias,
    down_weight,
    down_bias,
    cotangent,
):
    _, rows, width = tokens.shape
    hidden = up_weight.shape[0]
    part = query_weight.shape[0]
    fsdp = lax.axis_size("fsdp")
    seqs = lax.axis_size("seq")
    slots = 2 * seqs
    fbits = bits_of(fsdp)
    sbits = bits_of(seqs)
    rels = rel_order(fsdp)
    fsdp_me = lax.axis_index("fsdp")
    seq_me = lax.axis_index("seq")
    x_own = tokens.reshape(rows, width)
    dy_own = cotangent.reshape(rows, width)

    def spread(value):
        parts = [value]
        for bit in reversed(fbits):
            parts = parts + [swap(v, "fsdp", bit) for v in parts]
        return parts

    small = jnp.concatenate(
        [key_bias, value_bias, jnp.zeros((part - key_bias.shape[0] - value_bias.shape[0],), BF)]
    )
    vectors = jnp.stack(
        [
            norm_one_gain,
            norm_one_bias,
            norm_two_gain,
            norm_two_bias,
            query_bias,
            out_bias,
            down_bias,
            small,
        ]
        + [jnp.zeros((part,), BF)] * 8
    )
    weights = jnp.concatenate(
        [key_weight, value_weight, jnp.zeros((part, part - 2 * HDIM), BF)], axis=1
    )
    packs = spread(jnp.concatenate([weights, vectors], axis=0))
    xs = spread(x_own)
    dys = spread(dy_own)
    wq = lax.all_gather(query_weight, "fsdp", axis=0, tiled=True)
    wo = lax.all_gather(out_weight, "fsdp", axis=0, tiled=True)

    own_blocks = lax.dynamic_slice_in_dim(block_order, 2 * seq_me, 2)
    offsets = jnp.arange(BLOCK, dtype=jnp.int32)
    own_pos = (own_blocks[:, None] * BLOCK + offsets[None, :]).reshape(rows)
    frequencies = 10000.0 ** (-2.0 * jnp.arange(HALF, dtype=F32) / ROT)
    angles = own_pos.astype(F32)[None, :] * frequencies[:, None]
    cs = jnp.concatenate([jnp.cos(angles), jnp.sin(angles)], axis=0)

    n1, kv_own, vec, wkv = pl.pallas_call(
        functools.partial(front_kernel, rels),
        out_shape=(
            shape((rows, width), BF),
            shape((rows, 2 * HDIM), BF),
            shape((16, width), F32),
            shape((width, 2 * HDIM), BF),
        ),
        in_specs=[VMEM] * (2 + fsdp),
        out_specs=(VMEM,) * 4,
        scratch_shapes=[pltpu.VMEM((fsdp, 16, part), F32)],
        compiler_params=params(),
        cost_estimate=cost(2 * rows * width * 128, 3 * MIB // 2),
        name="front",
    )(x_own, *packs, cs)

    kv = kv_own[None]
    for bit in reversed(sbits):
        kv = jnp.concatenate([kv, swap(kv, "seq", bit)], axis=0)
    kv_all = kv.reshape(seqs * rows, 2 * HDIM)

    shards = seqs
    while (hidden // shards) % 16:
        shards //= 2
    low_bits = [b for b in sbits if b < shards]
    rest_bits = [b for b in sbits if b >= shards]
    up_bits = low_bits
    down_bits = low_bits[1:] + low_bits[:1]
    seq_orders = (shard_order(up_bits), shard_order(down_bits))
    half = fsdp // 2
    mlp_flops = 12 * fsdp * rows * width * hidden
    keep, send, n1c, upk, ups, dnk, dns, sums = pl.pallas_call(
        functools.partial(mlp_kernel, rels, seq_orders, shards),
        grid=(fsdp,),
        out_shape=(
            shape((half, 2, rows, width), BF),
            shape((half, 2, rows, width), BF),
            shape((fsdp, rows, part), BF),
            shape((hidden // 2, width), BF),
            shape((hidden // 2, width), BF),
            shape((hidden // 2, width), BF),
            shape((hidden // 2, width), BF),
            shape((8, max(hidden, width)), F32),
        ),
        in_specs=[VMEM] * (2 * fsdp + 4),
        out_specs=(
            pl.BlockSpec((1, 2, rows, width), lambda g: (jnp.maximum(g - half, 0), 0, 0, 0)),
            pl.BlockSpec((1, 2, rows, width), lambda g: (jnp.minimum(g, half - 1), 0, 0, 0)),
        )
        + (VMEM,) * 6,
        scratch_shapes=[
            pltpu.VMEM((rows, width), F32),
            pltpu.VMEM((rows, width), BF),
            pltpu.VMEM((hidden, width), F32),
            pltpu.VMEM((hidden, width), F32),
            pltpu.VMEM((8, max(hidden, width)), F32),
        ],
        compiler_params=params(),
        cost_estimate=cost(mlp_flops, 12 * MIB, 2 * fsdp * rows * hidden),
        name="mlp",
    )(*xs, *dys, up_weight, down_weight, up_bias.reshape(1, hidden), vec)

    qt, do_t = pl.pallas_call(
        query_kernel,
        out_shape=(shape((width, rows), BF), shape((width, rows), BF)),
        in_specs=[VMEM] * 6,
        out_specs=(VMEM, VMEM),
        compiler_params=params(),
        cost_estimate=cost(4 * rows * width * width, 4 * MIB),
        name="query",
    )(n1, dy_own, wq, wo, vec, cs)

    most = min(slots, slots // 2 + 1)
    chunk_blocks = 2
    most_chunks = -(-most // chunk_blocks)
    chunk = chunk_blocks * BLOCK
    per_group = HEADS
    while most_chunks * chunk * per_group * BLOCK * 8 > 20 * MIB and per_group > 2:
        per_group = {12: 6, 6: 4, 4: 2}[per_group]
    lanes = per_group * BLOCK
    span = per_group * HDIM
    own, dq, dkv = pl.pallas_call(
        functools.partial(attend_kernel, per_group, chunk_blocks, most),
        grid=(2, HEADS // per_group),
        out_shape=(
            shape((rows, width), BF),
            shape((rows, width), BF),
            shape((slots * BLOCK, 2 * HDIM), BF),
        ),
        in_specs=[
            SMEM,
            SMEM,
            pl.BlockSpec((span, BLOCK), lambda i, g: (g, i)),
            pl.BlockSpec((span, BLOCK), lambda i, g: (g, i)),
            VMEM,
            pl.BlockSpec((ROT, BLOCK), lambda i, g: (0, i)),
        ],
        out_specs=(
            pl.BlockSpec((BLOCK, span), lambda i, g: (i, g)),
            pl.BlockSpec((BLOCK, span), lambda i, g: (i, g)),
            VMEM,
        ),
        scratch_shapes=[
            pltpu.VMEM((most_chunks, chunk, lanes), F32),
            pltpu.VMEM((most_chunks, chunk, lanes), F32),
            pltpu.VMEM((chunk, lanes), BF),
            pltpu.VMEM((chunk, lanes), BF),
            pltpu.VMEM((chunk, BLOCK), F32),
            pltpu.VMEM((most_chunks * chunk, 2 * HDIM), BF),
            pltpu.VMEM((slots * BLOCK, 2 * HDIM), F32),
            pltpu.VMEM((HDIM, lanes), BF),
            pltpu.VMEM((HDIM, lanes), BF),
            pltpu.VMEM((HDIM, lanes), F32),
            pltpu.VMEM((HDIM, lanes), F32),
            pltpu.SMEM((slots,), jnp.int32),
        ],
        compiler_params=params(56),
        cost_estimate=cost(24 * slots * BLOCK * BLOCK * width, 8 * MIB, slots * BLOCK * BLOCK * 12),
        name="attend",
    )(block_order, doc_lengths, qt, do_t, kv_all, cs)

    near, far = keep, send
    for index, bit in enumerate(fbits):
        if index + 1 < len(fbits):
            value = near + swap(far, "fsdp", bit)
            near, far = value[: value.shape[0] // 2], value[value.shape[0] // 2 :]
        else:
            far = swap(far, "fsdp", bit)
    near, far = near[0], far[0]

    layer_out = pl.pallas_call(
        output_kernel,
        out_shape=shape((rows, width), BF),
        in_specs=[VMEM] * 6,
        out_specs=VMEM,
        compiler_params=params(),
        cost_estimate=cost(2 * rows * width * width, 3 * MIB),
        name="output",
    )(x_own, own, wo, vec, near[0], far[0])

    gup = reduce_shards(upk, ups, up_bits, rest_bits)
    gdn = reduce_shards(dnk, dns, down_bits, rest_bits)

    o_all = lax.all_gather(own, "fsdp", axis=0, tiled=True)
    dq_all = lax.all_gather(dq, "fsdp", axis=0, tiled=True)
    gqo = pl.pallas_call(
        functools.partial(weight_kernel, rels),
        out_shape=shape((2 * part, width), BF),
        in_specs=[VMEM] * (3 + fsdp),
        out_specs=VMEM,
        compiler_params=params(),
        cost_estimate=cost(4 * fsdp * rows * part * width, 6 * MIB),
        name="weight",
    )(n1c, dq_all, o_all, *dys)
    gqo = lax.psum(gqo, "seq").astype(F32)

    value = dkv
    for index, bit in enumerate(sbits):
        split = value.shape[0] // 2
        near_kv, far_kv = value[:split], swap(value[split:], "seq", bit)
        if index + 1 < len(sbits):
            value = near_kv + far_kv

    extra = -(-hidden // 128)
    chunks = -(-part // 128)
    height = part + 8 * chunks + -(-extra // 8) * 8
    grad_tokens, keep_t, send_t = pl.pallas_call(
        functools.partial(tail_kernel, rels),
        out_shape=(
            shape((rows, width), BF),
            shape((half, height, 128), F32),
            shape((half, height, 128), F32),
        ),
        in_specs=[VMEM] * 13,
        out_specs=(VMEM, VMEM, VMEM),
        scratch_shapes=[
            pltpu.VMEM((width, 2 * HDIM), F32),
            pltpu.VMEM((fsdp, 8 * chunks, 128), F32),
        ],
        compiler_params=params(),
        cost_estimate=cost(2 * rows * width * (width + 256), 5 * MIB),
        name="tail",
    )(x_own, dy_own, n1, dq, wq, wkv, vec, cs, near[1], far[1], near_kv, far_kv, sums)

    near_t, far_t = keep_t, send_t
    for index, bit in enumerate(fbits):
        value = near_t + swap(far_t, "fsdp", bit)
        near_t, far_t = value[: value.shape[0] // 2], value[value.shape[0] // 2 :]
    value = value[0]
    for bit in sbits:
        value = value + swap(value, "seq", bit)

    shard_rows = hidden // shards
    grad_up, grad_down = pl.pallas_call(
        functools.partial(final_kernel, seq_orders, shards),
        grid=(shards,),
        out_shape=(shape((hidden, width), F32), shape((hidden, width), F32)),
        in_specs=[VMEM] * 4,
        out_specs=(
            pl.BlockSpec((shard_rows, width), lambda g: (g, 0)),
            pl.BlockSpec((shard_rows, width), lambda g: (g, 0)),
        ),
        compiler_params=params(),
        cost_estimate=cost(0, 8 * MIB),
        name="final",
    )(*gup, *gdn)

    kv_grad = value[:part]
    lines = value[part : part + 8 * chunks].reshape(chunks, 8, 128)
    lines = jnp.moveaxis(lines, 0, 1).reshape(8, chunks * 128)
    dkv_line = value[part + 6]
    key_part, value_part = key_bias.shape[0], value_bias.shape[0]
    grad_up_bias = value[part + 8 * chunks :].reshape(-1)[:hidden]
    vec_out = [lines[i, :part] for i in range(6)]
    grad_key_bias = lax.dynamic_slice_in_dim(dkv_line, fsdp_me * key_part, key_part)
    grad_value_bias = lax.dynamic_slice_in_dim(dkv_line, HDIM + fsdp_me * value_part, value_part)
    return (
        layer_out.reshape(1, rows, width),
        grad_tokens.reshape(1, rows, width),
        vec_out[0],
        vec_out[1],
        gqo[:part],
        vec_out[4],
        kv_grad[:, :HDIM],
        grad_key_bias,
        kv_grad[:, HDIM:],
        grad_value_bias,
        gqo[part:],
        vec_out[5],
        vec_out[2],
        vec_out[3],
        grad_up,
        grad_up_bias,
        grad_down,
        vec_out[5],
    )


def solution(mesh):
    split = P("fsdp")
    matrix = P("fsdp", None)
    stream = P("fsdp", "seq", None)
    return jax.shard_map(
        on_device,
        mesh=mesh,
        in_specs=(
            stream,
            P(),
            matrix,
            split,
            split,
            matrix,
            split,
            matrix,
            split,
            matrix,
            split,
            matrix,
            split,
            split,
            split,
            matrix,
            split,
            matrix,
            split,
            stream,
        ),
        out_specs=(
            stream,
            stream,
            split,
            split,
            matrix,
            split,
            matrix,
            split,
            matrix,
            split,
            matrix,
            split,
            split,
            split,
            matrix,
            split,
            matrix,
            split,
        ),
        check_vma=False,
    )
```

time: 1140 us -> 295 us (0.26)
  waiting for transfers between devices: 622 us -> 163 us
  local copies, waits for them, and re-layouts: 185 us -> 22.2 us
  matrix products: 126 us -> 0 us
  other arithmetic: 101 us -> 6.44 us
  blocking collectives: 74.1 us -> 0 us
  starting transfers between devices: 0.77 us -> 46.8 us
  Pallas kernels: 0 us -> 39.6 us
    reduce_scatter x7 -> x0, waiting for transfers between devices: 294 us -> none  [the longest x1 81.2 us: on_device(): lax.psum_scatter(grad_down_weight, 'fsdp', scatter_dimension=0, tiled=True)]
    psum x2 -> x1, waiting for transfers between devices: 278 us -> 69.1 us  [on_device(): gqo = lax.psum(gqo, 'seq').astype(F32)]
    dot_general x51 -> x0, matrix products: 126 us -> none  [the longest x8 34.7 us: contract(): lax.dot_general(left_array, right_array, (((left_dim,), (right_dim,)), ((...]
    ppermute x0 -> x34, waiting for transfers between devices: none -> 92.8 us  [swap(): return lax.ppermute(value, axis, [(i, i ^ bit) for i in range(size)])]
    gather x63 -> x0, local copies, waits for them, and re-layouts: 78.9 us -> none  [the longest x9 27.5 us: block_scores(): queries = jnp.take(query_pair, side_now, axis=0)]
    all_gather x4 -> x0, blocking collectives: 50.5 us -> none  [the longest x1 32.1 us: on_device(): lax.all_gather(own_keyvals, 'seq', axis=1, tiled=True)]
    all_gather x4, waiting for transfers between devices: 46.8 us -> 0.01 us  [the longest x1 0.01 us: on_device(): wq = lax.all_gather(query_weight, 'fsdp', axis=0, tiled=True)]
    ppermute x0 -> x34, starting transfers between devices: none -> 46.5 us  [swap(): return lax.ppermute(value, axis, [(i, i ^ bit) for i in range(size)])]
  transfers between devices with their start and end apart: 13 -> 39, of which waited for: 10 -> 16; matrix products, arithmetic and copies ran while one was open for 8% -> 6% of each run, Pallas kernels for 0% -> 13%
where the time goes in v1:
time: 295 us; the launch traced here: 293 us
  waiting for transfers between devices  163 us (55%)
  starting transfers between devices  46.8 us (16%)
  Pallas kernels  39.6 us (13%)
  local copies, waits for them, and re-layouts  22.2 us (8%)
  between operations  14.4 us (5%)
  other arithmetic  6.44 us (2%)
    ppermute x34, waiting for transfers between devices, swap(): return lax.ppermute(value, axis, [(i, i ^ bit) for i in range(size)])  92.8 us
    psum x1, waiting for transfers between devices, on_device(): gqo = lax.psum(gqo, 'seq').astype(F32)  69.1 us
    ppermute x34, starting transfers between devices, swap(): return lax.ppermute(value, axis, [(i, i ^ bit) for i in range(size)])  46.5 us
    pallas_call x1, Pallas kernels, on_device(): pl.pallas_call(functools.partial(mlp_kernel, rels, seq_orders, shards), g...  15.8 us
    pallas_call x1, Pallas kernels, on_device(): pl.pallas_call(functools.partial(attend_kernel, per_group, chunk_blocks,...  12.1 us
    unnamed x71, local copies, waits for them, and re-layouts  10.7 us
  transfers between devices with their start and end apart: 39, of which 16 were waited for; matrix products, arithmetic and copies ran while one was open for 6% of the time, Pallas kernels for 13%

profile of v1, /device:TPU:0, one launch (start us, length us, event | category | flops | bytes accessed | tf_op | source)
XLA Modules:
  0.0 292.9 jit_solution(3437667887117348914)
XLA Ops:
  7.3 0.7 all-gather.5.cloned.1.call-update
  8.0 0.7 all-gather.7.cloned.1.call-update
  8.8 0.9 copy.39
  9.6 0.9 copy.38
  15.1 0.7 pad_maximum_fusion.8
  16.1 3.0 %collective-permute-start = (bf16[208,192]{1,0:T(8,128)(2,1)S(1)}, bf16[208,192]{1,0:T(8,128)(2,1)S(1)}, u32[]{:S(2)}, u32[]{:S(2)}) collective-permute-start(bf16[208,192]{1,0:T(8,128)(2,1)S(1)} %concatenate.43.refs_0_), channel_id=1, source_target_pairs={{0,2},{1,3},{2,0},{3,1},{4,6},{5,7},{6,4},{7,5},{8,10},{9,11},{10,... | collective-permute-start | bytes 239624 | tf_op jit(solution)/shard_map/ppermute | solution.py:50
  19.4 4.2 %collective-permute-done.refs_1_ = bf16[208,192]{1,0:T(8,128)(2,1)S(1)} collective-permute-done((bf16[208,192]{1,0:T(8,128)(2,1)S(1)}, bf16[208,192]{1,0:T(8,128)(2,1)S(1)}, u32[]{:S(2)}, u32[]{:S(2)}) %collective-permute-start) | collective-permute-done | bytes 79904 | tf_op jit(solution)/shard_map/ppermute | solution.py:50
  23.6 1.3 collective-permute-done.2.refs_3_
  25.6 2.6 collective-permute-start.3
  28.2 4.0 %collective-permute-done.3 = bf16[1,256,128]{2,1,0:T(8,128)(2,1)S(1)} collective-permute-done((bf16[1,256,128]{2,1,0:T(8,128)(2,1)S(1)}, bf16[1,256,128]{2,1,0:T(8,128)(2,1)S(1)}, u32[]{:S(2)}, u32[]{:S(2)}) %collective-permute-start.3) | collective-permute-done | bytes 65568 | tf_op jit(solution)/shard_map/ppermute | solution.py:50
  32.8 2.5 collective-permute-start.6
  35.4 1.9 collective-permute-done.4
  37.3 1.6 collective-permute-start.5
  39.4 9.8 %collective-permute-done.6.refs_1_ = bf16[256,768]{1,0:T(8,128)(2,1)S(1)} collective-permute-done((bf16[256,768]{1,0:T(8,128)(2,1)S(1)}, bf16[256,768]{1,0:T(8,128)(2,1)S(1)}, u32[]{:S(2)}, u32[]{:S(2)}) %collective-permute-start.6) | collective-permute-done | bytes 393248 | tf_op jit(solution)/shard_map/ppermute | solution.py:50
  49.2 9.9 %collective-permute-done.9.refs_5_.refs_1_ = bf16[256,768]{1,0:T(8,128)(2,1)S(1)} collective-permute-done((bf16[256,768]{1,0:T(8,128)(2,1)S(1)}, bf16[256,768]{1,0:T(8,128)(2,1)S(1)}, u32[]{:S(2)}, u32[]{:S(2)}) %collective-permute-start.9) | collective-permute-done | bytes 393248 | tf_op jit(solution)/shard_map/ppermute | solution.py:50
  59.1 0.9 pad_maximum_fusion.2
  60.0 1.3 copy-done
  61.3 1.3 copy-done.2
  62.6 0.8 query.1
  63.4 0.7 copy-done.26
  64.2 0.7 copy-done.27
  64.9 12.1 %attend.1 = (bf16[256,768]{1,0:T(8,128)(2,1)}, bf16[256,768]{1,0:T(8,128)(2,1)}, bf16[2048,128]{1,0:T(8,128)(2,1)}) custom-call(s32[16]{0:T(128)} %order_ref.1, s32[1,4]{1,0:T(1,128)} %len_ref.1, bf16[768,256]{1,0:T(8,128)(2,1)} %copy-done.26, bf16[768,256]{1,0:T(8,128)(2,1)} %copy-done.27, bf16[2048,128]{1,0:T(8,128)(2,1)} %bitcast.52, f32[16,256]{1,0:T(8,128)} %copy-done.20), custom_call_target="tpu_custom_call" | custom-call | flops 4831838208 | bytes 8388608 | tf_op jit(solution)/shard_map/attend/pallas_call | solution.py:698
  77.1 15.8 %mlp.1 = (bf16[2,2,256,768]{3,2,1,0:T(8,128)(2,1)}, bf16[2,2,256,768]{3,2,1,0:T(8,128)(2,1)}, bf16[4,256,192]{2,1,0:T(8,128)(2,1)S(1)}, bf16[384,768]{1,0:T(8,12...) custom-call(bf16[256,768]{1,0:T(8,128)(2,1)S(1)} %bitcast.45, ...), custom_call_target="tpu_custom_call" | custom-call | flops 7247757312 | bytes 12582912 | tf_op jit(solution)/shard_map/mlp/pallas_call | solution.py:648
  93.0 1.6 collective-permute-start.22
  94.5 13.3 %collective-permute-done.22 = bf16[384,768]{1,0:T(8,128)(2,1)S(1)} collective-permute-done((bf16[384,768]{1,0:T(8,128)(2,1)S(1)}, bf16[384,768]{1,0:T(8,128)(2,1)S(1)}, u32[]{:S(2)}, u32[]{:S(2)}) %collective-permute-start.22) | collective-permute-done | bytes 589856 | tf_op jit(solution)/shard_map/ppermute | solution.py:50
  108.2 1.5 collective-permute-start.12
  109.9 8.4 %collective-permute-start.29 = (bf16[192,768]{1,0:T(8,128)(2,1)S(1)}, bf16[192,768]{1,0:T(8,128)(2,1)S(1)}, u32[]{:S(2)}, u32[]{:S(2)}) collective-permute-start(bf16[192,768]{1,0:T(8,128)(2,1)S(1)} %slice.180), channel_id=1, source_target_pairs={{0,16},{4,20},{8,24},{12,28},{16,0},{20,4},{24,8},{28,12},{1,17},{... | collective-permute-start | bytes 884744 | tf_op jit(solution)/shard_map/ppermute | solution.py:50
  118.3 1.4 collective-permute-done.23
  119.8 0.7 slice.178
  120.4 4.6 %collective-permute-start.24 = (bf16[96,768]{1,0:T(8,128)(2,1)}, bf16[96,768]{1,0:T(8,128)(2,1)S(1)}, u32[]{:S(2)}, u32[]{:S(2)}) collective-permute-start(bf16[96,768]{1,0:T(8,128)(2,1)} %slice.178), channel_id=1, source_target_pairs={{0,16},{4,20},{8,24},{12,28},{16,0},{20,4},{24,8},{28,12},{1,17},{... | collective-permute-start | bytes 442376 | tf_op jit(solution)/shard_map/ppermute | solution.py:50
  125.0 8.9 %collective-permute-done.29 = bf16[192,768]{1,0:T(8,128)(2,1)S(1)} collective-permute-done((bf16[192,768]{1,0:T(8,128)(2,1)S(1)}, bf16[192,768]{1,0:T(8,128)(2,1)S(1)}, u32[]{:S(2)}, u32[]{:S(2)}) %collective-permute-start.29) | collective-permute-done | bytes 294944 | tf_op jit(solution)/shard_map/ppermute | solution.py:50
  133.9 0.7 slice.182
  134.6 2.0 collective-permute-start.30
  136.6 0.7 slice.123
  137.7 4.0 %collective-permute-done.30 = bf16[96,768]{1,0:T(8,128)(2,1)} collective-permute-done((bf16[96,768]{1,0:T(8,128)(2,1)}, bf16[96,768]{1,0:T(8,128)(2,1)}, u32[]{:S(2)}, u32[]{:S(2)}) %collective-permute-start.30) | collective-permute-done | bytes 147488 | tf_op jit(solution)/shard_map/ppermute | solution.py:50
  141.7 0.9 slice_add_fusion.3
  142.6 1.3 collective-permute-start.31
  143.9 1.4 collective-permute-done.14
  145.3 1.1 slice_add_fusion.2
  146.4 1.1 collective-permute-start.15
  147.6 1.0 collective-permute-start.26
  148.6 1.8 add.78
  150.4 1.3 collective-permute-start.13
  151.8 2.4 collective-permute-start.32
  154.2 1.1 collective-permute-start.16
  155.4 16.4 %collective-permute-done.13 = bf16[1,2,256,768]{3,2,1,0:T(8,128)(2,1)S(1)} collective-permute-done((bf16[1,2,256,768]{3,2,1,0:T(8,128)(2,1)S(1)}, bf16[1,2,256,768]{3,2,1,0:T(8,128)(2,1)S(1)}, u32[]{:S(2)}, u32[]{:S(2)}) %collective-permute-start.13) | collective-permute-done | bytes 786464 | tf_op jit(solution)/shard_map/ppermute | solution.py:50
  171.9 2.0 tail.1
  173.9 1.5 collective-permute-start.27
  176.1 1.6 collective-permute-start.33
  177.7 3.0 %collective-permute-done.18 = f32[1,216,128]{2,1,0:T(8,128)S(1)} collective-permute-done((f32[1,216,128]{2,1,0:T(8,128)S(1)}, f32[1,216,128]{2,1,0:T(8,128)S(1)}, u32[]{:S(2)}, u32[]{:S(2)}) %collective-permute-start.18) | collective-permute-done | bytes 110624 | tf_op jit(solution)/shard_map/ppermute | solution.py:50
  180.7 1.3 collective-permute-start.19
  182.1 10.0 %collective-permute-done.19 = f32[216,128]{1,0:T(8,128)S(1)} collective-permute-done((f32[216,128]{1,0:T(8,128)S(1)}, f32[216,128]{1,0:T(8,128)S(1)}, u32[]{:S(2)}, u32[]{:S(2)}) %collective-permute-start.19) | collective-permute-done | bytes 110624 | tf_op jit(solution)/shard_map/ppermute | solution.py:50
  192.1 1.6 collective-permute-start.20
  193.6 3.3 %collective-permute-done.20 = f32[216,128]{1,0:T(8,128)S(1)} collective-permute-done((f32[216,128]{1,0:T(8,128)S(1)}, f32[216,128]{1,0:T(8,128)S(1)}, u32[]{:S(2)}, u32[]{:S(2)}) %collective-permute-start.20) | collective-permute-done | bytes 110624 | tf_op jit(solution)/shard_map/ppermute | solution.py:50
  196.9 2.5 collective-permute-start.21
  199.4 5.0 %final.1 = (f32[768,768]{1,0:T(8,128)}, f32[768,768]{1,0:T(8,128)}) custom-call(bf16[384,768]{1,0:T(8,128)(2,1)S(1)} %pad_maximum_fusion.upn, bf16[384,768]{1,0:T(8,128)(2,1)} %collective-permute-done.27.upf, bf16[384,768]{1,0:T(8,128)(2,1)S(1)} %pad_maximum_fusion.1.dnn, bf16[384,768]{1,0:T(8,128)(2,1)} %collective-permute-done.33.dnf), custom_call_target="tpu_custom_call" | custom-call | bytes 8388608 | tf_op jit(solution)/shard_map/final/pallas_call | solution.py:810
  204.5 1.3 output.1
  205.9 0.7 copy.40
  206.6 0.7 copy.41
  207.4 1.4 copy-done.7
  208.8 1.4 copy-done.8
  210.2 2.0 weight.1
  214.5 69.1 %all-reduce.2.cloned.1.call-done = bf16[384,768]{1,0:T(8,128)(2,1)} async-done(((bf16[384,768]{1,0:T(8,128)(2,1)}), bf16[384,768]{1,0:T(8,128)(2,1)}) %all-reduce.2.cloned.1.call-update) | async-done | bytes 589840 | tf_op jit(solution)/shard_map/psum | solution.py:771
  283.6 2.1 fusion.1
  (159 shorter events, 12.2 us)
Async XLA Ops:
  7.2 11.9 %copy-start.32 = (s32[16]{0:T(128)S(1)}, s32[16]{0:T(128)}, u32[]{:S(2)}) copy-start(s32[16]{0:T(128)} %order_ref.1) | copy-start | bytes 196
  7.2 17.7 %copy-start.5 = (bf16[1,256,768]{2,1,0:T(8,128)(2,1)S(1)}, bf16[1,256,768]{2,1,0:T(8,128)(2,1)}, u32[]{:S(2)}) copy-start(bf16[1,256,768]{2,1,0:T(8,128)(2,1)} %param.20) | copy-start | bytes 1179652
  7.2 28.1 %copy-start.4 = (bf16[1,256,768]{2,1,0:T(8,128)(2,1)S(1)}, bf16[1,256,768]{2,1,0:T(8,128)(2,1)}, u32[]{:S(2)}) copy-start(bf16[1,256,768]{2,1,0:T(8,128)(2,1)} %param.39) | copy-start | bytes 1179652
  7.2 52.8 %all-gather.5.cloned.1.call-start = ((), (), s32[]{:S(2)}) async-start(), calls=%async_computation | async-start | bytes 1474560 | tf_op jit(solution)/shard_map/all_gather | solution.py:607
  8.0 52.0 %all-gather.7.cloned.1.call-start = ((), (), s32[]{:S(2)}) async-start(), calls=%async_computation.1 | async-start | bytes 1474560 | tf_op jit(solution)/shard_map/all_gather | solution.py:608
  8.7 198.6 %all-gather.9.cloned.1.call-start = ((), (), s32[]{:S(2)}) async-start(), calls=%async_computation.2 | async-start | bytes 1966080 | tf_op jit(solution)/shard_map/all_gather | solution.py:761
  16.1 7.5 %collective-permute-start = (bf16[208,192]{1,0:T(8,128)(2,1)S(1)}, bf16[208,192]{1,0:T(8,128)(2,1)S(1)}, u32[]{:S(2)}, u32[]{:S(2)}) collective-permute-start(bf16[208,192]{1,0:T(8,128)(2,1)S(1)} %concatenate.43.refs_0_), channel_id=1, source_target_pairs={{0,2},{1,3},{2,0},{3,1},{4,6},{5,7},{6,4},{7,5},{8,10},{9,11},{10,... | collective-permute-start | bytes 239624 | tf_op jit(solution)/shard_map/ppermute | solution.py:50
  19.1 4.5 %collective-permute-start.1 = (bf16[208,192]{1,0:T(8,128)(2,1)S(1)}, bf16[208,192]{1,0:T(8,128)(2,1)S(1)}, u32[]{:S(2)}, u32[]{:S(2)}) collective-permute-start(bf16[208,192]{1,0:T(8,128)(2,1)S(1)} %concatenate.43.refs_0_), channel_id=1, source_target_pairs={{0,1},{1,0},{2,3},{3,2},{4,5},{5,4},{6,7},{7,6},{8,9},{9,8},{10,11... | collective-permute-start | bytes 239624 | tf_op jit(solution)/shard_map/ppermute | solution.py:50
  23.6 1.3 collective-permute-start.2
  23.6 36.4 %copy-start.20 = (f32[16,256]{1,0:T(8,128)}, f32[16,256]{1,0:T(8,128)S(1)}, u32[]{:S(2)}) copy-start(f32[16,256]{1,0:T(8,128)S(1)} %pad_maximum_fusion.7.refs_4_.cs_ref) | copy-start | bytes 49156
  25.6 33.5 %copy-start.22 = (bf16[768,128]{1,0:T(8,128)(2,1)}, bf16[768,128]{1,0:T(8,128)(2,1)S(1)}, u32[]{:S(2)}) copy-start(bf16[768,128]{1,0:T(8,128)(2,1)S(1)} %get-tuple-element.49.wkv_ref) | copy-start | bytes 589828
  25.6 146.3 %copy-start.12 = (f32[16,768]{1,0:T(8,128)}, f32[16,768]{1,0:T(8,128)S(1)}, u32[]{:S(2)}) copy-start(f32[16,768]{1,0:T(8,128)S(1)} %get-tuple-element.41.vec_ref.refs_11_) | copy-start | bytes 147460
  25.6 6.6 %collective-permute-start.3 = (bf16[1,256,128]{2,1,0:T(8,128)(2,1)S(1)}, bf16[1,256,128]{2,1,0:T(8,128)(2,1)S(1)}, u32[]{:S(2)}, u32[]{:S(2)}) collective-permute-start(bf16[1,256,128]{2,1,0:T(8,128)(2,1)S(1)} %bitcast.48), channel_id=1, source_target_pairs={{0,16},{4,20},{8,24},{12,28},{16,0},{20,4},{24,8},{28,12},{1,17},{... | collective-permute-start | bytes 196616 | tf_op jit(solution)/shard_map/ppermute | solution.py:50
  32.2 5.0 %collective-permute-start.4 = (bf16[2,256,128]{2,1,0:T(8,128)(2,1)S(1)}, bf16[2,256,128]{2,1,0:T(8,128)(2,1)S(1)}, u32[]{:S(2)}, u32[]{:S(2)}) collective-permute-start(bf16[2,256,128]{2,1,0:T(8,128)(2,1)S(1)} %pad_maximum_fusion.6), channel_id=1, source_target_pairs={{0,8},{4,12},{8,0},{12,4},{16,24},{20,28},{24,16},{28,20},{1,9},{5... | collective-permute-start | bytes 393224 | tf_op jit(solution)/shard_map/ppermute | solution.py:50
  32.8 16.4 %collective-permute-start.6 = (bf16[256,768]{1,0:T(8,128)(2,1)S(1)}, bf16[256,768]{1,0:T(8,128)(2,1)S(1)}, u32[]{:S(2)}, u32[]{:S(2)}) collective-permute-start(bf16[256,768]{1,0:T(8,128)(2,1)S(1)} %bitcast.43), channel_id=1, source_target_pairs={{0,2},{1,3},{2,0},{3,1},{4,6},{5,7},{6,4},{7,5},{8,10},{9,11},{10,... | collective-permute-start | bytes 1179656 | tf_op jit(solution)/shard_map/ppermute | solution.py:50
  35.3 23.7 %collective-permute-start.9 = (bf16[256,768]{1,0:T(8,128)(2,1)S(1)}, bf16[256,768]{1,0:T(8,128)(2,1)S(1)}, u32[]{:S(2)}, u32[]{:S(2)}) collective-permute-start(bf16[256,768]{1,0:T(8,128)(2,1)S(1)} %bitcast.36), channel_id=1, source_target_pairs={{0,2},{1,3},{2,0},{3,1},{4,6},{5,7},{6,4},{7,5},{8,10},{9,11},{10,... | collective-permute-start | bytes 1179656 | tf_op jit(solution)/shard_map/ppermute | solution.py:50
  37.3 21.8 %collective-permute-start.5 = (bf16[4,256,128]{2,1,0:T(8,128)(2,1)S(1)}, bf16[4,256,128]{2,1,0:T(8,128)(2,1)S(1)}, u32[]{:S(2)}, u32[]{:S(2)}) collective-permute-start(bf16[4,256,128]{2,1,0:T(8,128)(2,1)S(1)} %pad_maximum_fusion.5), channel_id=1, source_target_pairs={{0,4},{4,0},{8,12},{12,8},{16,20},{20,16},{24,28},{28,24},{1,5},{5... | collective-permute-start | bytes 786440 | tf_op jit(solution)/shard_map/ppermute | solution.py:50
  38.9 38.2 %collective-permute-start.7 = (bf16[256,768]{1,0:T(8,128)(2,1)S(1)}, bf16[256,768]{1,0:T(8,128)(2,1)S(1)}, u32[]{:S(2)}, u32[]{:S(2)}) collective-permute-start(bf16[256,768]{1,0:T(8,128)(2,1)S(1)} %bitcast.44), channel_id=1, source_target_pairs={{0,1},{1,0},{2,3},{3,2},{4,5},{5,4},{6,7},{7,6},{8,9},{9,8},{10,11... | collective-permute-start | bytes 1179656 | tf_op jit(solution)/shard_map/ppermute | solution.py:50
  38.9 38.2 %collective-permute-start.10 = (bf16[256,768]{1,0:T(8,128)(2,1)S(1)}, bf16[256,768]{1,0:T(8,128)(2,1)S(1)}, u32[]{:S(2)}, u32[]{:S(2)}) collective-permute-start(bf16[256,768]{1,0:T(8,128)(2,1)S(1)} %bitcast.37), channel_id=1, source_target_pairs={{0,1},{1,0},{2,3},{3,2},{4,5},{5,4},{6,7},{7,6},{8,9},{9,8},{10,11... | collective-permute-start | bytes 1179656 | tf_op jit(solution)/shard_map/ppermute | solution.py:50
  49.2 27.9 %collective-permute-start.8 = (bf16[256,768]{1,0:T(8,128)(2,1)S(1)}, bf16[256,768]{1,0:T(8,128)(2,1)}, u32[]{:S(2)}, u32[]{:S(2)}) collective-permute-start(bf16[256,768]{1,0:T(8,128)(2,1)S(1)} %collective-permute-done.6.refs_1_), channel_id=1, source_target_pairs={{0,1},{1,0},{2,3},{3,2},{4,5},{5,4},{6,7},{7,6},{8,9},{9,8},{10,11... | collective-permute-start | bytes 1179656 | tf_op jit(solution)/shard_map/ppermute | solution.py:50
  59.1 18.0 %copy-start.14 = (bf16[256,768]{1,0:T(8,128)(2,1)}, bf16[256,768]{1,0:T(8,128)(2,1)S(1)}, u32[]{:S(2)}) copy-start(bf16[256,768]{1,0:T(8,128)(2,1)S(1)} %collective-permute-done.9.refs_5_.refs_1_) | copy-start | bytes 1179652
  59.1 18.0 %collective-permute-start.11 = (bf16[256,768]{1,0:T(8,128)(2,1)S(1)}, bf16[256,768]{1,0:T(8,128)(2,1)S(1)}, u32[]{:S(2)}, u32[]{:S(2)}) collective-permute-start(bf16[256,768]{1,0:T(8,128)(2,1)S(1)} %collective-permute-done.9.refs_5_.refs_1_), channel_id=1, source_target_pairs={{0,1},{1,0},{2,3},{3,2},{4,5},{5,4},{6,7},{7,6},{8,9},{9,8},{10,11... | collective-permute-start | bytes 1179656 | tf_op jit(solution)/shard_map/ppermute | solution.py:50
  64.9 12.1 %copy-start.31 = (bf16[768]{0:T(1024)(128)(2,1)S(1)}, bf16[768]{0:T(1024)(128)(2,1)}, u32[]{:S(2)}) copy-start(bf16[768]{0:T(1024)(128)(2,1)} %param.36) | copy-start | bytes 4612
  77.0 130.3 %all-gather.11.cloned.1.call-start = ((), (), s32[]{:S(2)}) async-start(), calls=%async_computation.3 | async-start | bytes 1966080 | tf_op jit(solution)/shard_map/all_gather | solution.py:760
  77.1 15.9 %copy-start.16 = (bf16[256,768]{1,0:T(8,128)(2,1)}, bf16[256,768]{1,0:T(8,128)(2,1)S(1)}, u32[]{:S(2)}) copy-start(bf16[256,768]{1,0:T(8,128)(2,1)S(1)} %collective-permute-done.10.refs_6_.refs_2_) | copy-start | bytes 1179652
  77.1 15.8 %copy-start.18 = (bf16[256,768]{1,0:T(8,128)(2,1)}, bf16[256,768]{1,0:T(8,128)(2,1)S(1)}, u32[]{:S(2)}) copy-start(bf16[256,768]{1,0:T(8,128)(2,1)S(1)} %collective-permute-done.11.refs_7_.refs_3_) | copy-start | bytes 1179652
  92.9 15.1 %copy-start.10 = (bf16[4,256,192]{2,1,0:T(8,128)(2,1)}, bf16[4,256,192]{2,1,0:T(8,128)(2,1)S(1)}, u32[]{:S(2)}) copy-start(bf16[4,256,192]{2,1,0:T(8,128)(2,1)S(1)} %get-tuple-element.55.n1c_ref) | copy-start | bytes 1179652
  92.9 15.1 %copy-start.24 = (f32[8,768]{1,0:T(8,128)}, f32[8,768]{1,0:T(8,128)S(1)}, u32[]{:S(2)}) copy-start(f32[8,768]{1,0:T(8,128)S(1)} %get-tuple-element.51.sums_ref) | copy-start | bytes 73732
  93.0 14.9 %collective-permute-start.22 = (bf16[384,768]{1,0:T(8,128)(2,1)S(1)}, bf16[384,768]{1,0:T(8,128)(2,1)S(1)}, u32[]{:S(2)}, u32[]{:S(2)}) collective-permute-start(bf16[384,768]{1,0:T(8,128)(2,1)S(1)} %get-tuple-element.57), channel_id=1, source_target_pairs={{0,4},{4,0},{8,12},{12,8},{16,20},{20,16},{24,28},{28,24},{1,5},{5... | collective-permute-start | bytes 1769480 | tf_op jit(solution)/shard_map/ppermute | solution.py:50
  94.5 15.2 %collective-permute-start.28 = (bf16[384,768]{1,0:T(8,128)(2,1)S(1)}, bf16[384,768]{1,0:T(8,128)(2,1)S(1)}, u32[]{:S(2)}, u32[]{:S(2)}) collective-permute-start(bf16[384,768]{1,0:T(8,128)(2,1)S(1)} %get-tuple-element.59), channel_id=1, source_target_pairs={{0,8},{4,12},{8,0},{12,4},{16,24},{20,28},{24,16},{28,20},{1,9},{5... | collective-permute-start | bytes 1769480 | tf_op jit(solution)/shard_map/ppermute | solution.py:50
  108.1 11.7 %collective-permute-start.23 = (bf16[192,768]{1,0:T(8,128)(2,1)S(1)}, bf16[192,768]{1,0:T(8,128)(2,1)S(1)}, u32[]{:S(2)}, u32[]{:S(2)}) collective-permute-start(bf16[192,768]{1,0:T(8,128)(2,1)S(1)} %slice.176), channel_id=1, source_target_pairs={{0,8},{4,12},{8,0},{12,4},{16,24},{20,28},{24,16},{28,20},{1,9},{5... | collective-permute-start | bytes 884744 | tf_op jit(solution)/shard_map/ppermute | solution.py:50
  108.2 40.4 %collective-permute-start.12 = (bf16[2,2,256,768]{3,2,1,0:T(8,128)(2,1)}, bf16[2,2,256,768]{3,2,1,0:T(8,128)(2,1)}, u32[]{:S(2)}, u32[]{:S(2)}) collective-permute-start(bf16[2,2,256,768]{3,2,1,0:T(8,128)(2,1)} %get-tuple-element.47), channel_id=1, source_target_pairs={{0,1},{1,0},{2,3},{3,2},{4,5},{5,4},{6,7},{7,6},{8,9},{9,8},{10,11... | collective-permute-start | bytes 4718600 | tf_op jit(solution)/shard_map/ppermute | solution.py:50
  109.9 26.8 %copy-start.29 = (bf16[2048,128]{1,0:T(8,128)(2,1)S(1)}, bf16[2048,128]{1,0:T(8,128)(2,1)}, u32[]{:S(2)}) copy-start(bf16[2048,128]{1,0:T(8,128)(2,1)} %get-tuple-element.50) | copy-start | bytes 1572868
  109.9 24.0 %collective-permute-start.29 = (bf16[192,768]{1,0:T(8,128)(2,1)S(1)}, bf16[192,768]{1,0:T(8,128)(2,1)S(1)}, u32[]{:S(2)}, u32[]{:S(2)}) collective-permute-start(bf16[192,768]{1,0:T(8,128)(2,1)S(1)} %slice.180), channel_id=1, source_target_pairs={{0,16},{4,20},{8,24},{12,28},{16,0},{20,4},{24,8},{28,12},{1,17},{... | collective-permute-start | bytes 884744 | tf_op jit(solution)/shard_map/ppermute | solution.py:50
  120.4 17.2 %collective-permute-start.24 = (bf16[96,768]{1,0:T(8,128)(2,1)}, bf16[96,768]{1,0:T(8,128)(2,1)S(1)}, u32[]{:S(2)}, u32[]{:S(2)}) collective-permute-start(bf16[96,768]{1,0:T(8,128)(2,1)} %slice.178), channel_id=1, source_target_pairs={{0,16},{4,20},{8,24},{12,28},{16,0},{20,4},{24,8},{28,12},{1,17},{... | collective-permute-start | bytes 442376 | tf_op jit(solution)/shard_map/ppermute | solution.py:50
  134.6 7.1 %collective-permute-start.30 = (bf16[96,768]{1,0:T(8,128)(2,1)}, bf16[96,768]{1,0:T(8,128)(2,1)}, u32[]{:S(2)}, u32[]{:S(2)}) collective-permute-start(bf16[96,768]{1,0:T(8,128)(2,1)} %slice.182), channel_id=1, source_target_pairs={{0,4},{4,0},{8,12},{12,8},{16,20},{20,16},{24,28},{28,24},{1,5},{5... | collective-permute-start | bytes 442376 | tf_op jit(solution)/shard_map/ppermute | solution.py:50
  137.3 8.0 %collective-permute-start.14 = (bf16[1024,128]{1,0:T(8,128)(2,1)}, bf16[1024,128]{1,0:T(8,128)(2,1)}, u32[]{:S(2)}, u32[]{:S(2)}) collective-permute-start(bf16[1024,128]{1,0:T(8,128)(2,1)} %slice.123), channel_id=1, source_target_pairs={{0,4},{4,0},{8,12},{12,8},{16,20},{20,16},{24,28},{28,24},{1,5},{5... | collective-permute-start | bytes 786440 | tf_op jit(solution)/shard_map/ppermute | solution.py:50
  137.4 11.2 %copy-start.28 = (bf16[2,2,256,768]{3,2,1,0:T(8,128)(2,1)S(1)}, bf16[2,2,256,768]{3,2,1,0:T(8,128)(2,1)}, u32[]{:S(2)}) copy-start(bf16[2,2,256,768]{3,2,1,0:T(8,128)(2,1)} %get-tuple-element.46) | copy-start | bytes 4718596
  137.4 146.3 %all-reduce.2.cloned.1.call-start = ((), (), s32[]{:S(2)}) async-start(), calls=%async_computation.4 | async-start | bytes 1179648 | tf_op jit(solution)/shard_map/psum | solution.py:771
  137.6 9.9 %collective-permute-start.25 = (bf16[96,768]{1,0:T(8,128)(2,1)S(1)}, bf16[96,768]{1,0:T(8,128)(2,1)S(1)}, u32[]{:S(2)}, u32[]{:S(2)}) collective-permute-start(bf16[96,768]{1,0:T(8,128)(2,1)S(1)} %slice_add_fusion.4), channel_id=1, source_target_pairs={{0,16},{4,20},{8,24},{12,28},{16,0},{20,4},{24,8},{28,12},{1,17},{... | collective-permute-start | bytes 442376 | tf_op jit(solution)/shard_map/ppermute | solution.py:50
  142.6 9.1 %collective-permute-start.31 = (bf16[96,768]{1,0:T(8,128)(2,1)S(1)}, bf16[96,768]{1,0:T(8,128)(2,1)S(1)}, u32[]{:S(2)}, u32[]{:S(2)}) collective-permute-start(bf16[96,768]{1,0:T(8,128)(2,1)S(1)} %slice_add_fusion.3), channel_id=1, source_target_pairs={{0,4},{4,0},{8,12},{12,8},{16,20},{20,16},{24,28},{28,24},{1,5},{5... | collective-permute-start | bytes 442376 | tf_op jit(solution)/shard_map/ppermute | solution.py:50
  146.4 7.7 %collective-permute-start.15 = (bf16[512,128]{1,0:T(8,128)(2,1)S(1)}, bf16[512,128]{1,0:T(8,128)(2,1)S(1)}, u32[]{:S(2)}, u32[]{:S(2)}) collective-permute-start(bf16[512,128]{1,0:T(8,128)(2,1)S(1)} %slice.158), channel_id=1, source_target_pairs={{0,8},{4,12},{8,0},{12,4},{16,24},{20,28},{24,16},{28,20},{1,9},{5... | collective-permute-start | bytes 393224 | tf_op jit(solution)/shard_map/ppermute | solution.py:50
  147.6 26.3 %collective-permute-start.26 = (bf16[192,768]{1,0:T(8,128)(2,1)S(1)}, bf16[192,768]{1,0:T(8,128)(2,1)S(1)}, u32[]{:S(2)}, u32[]{:S(2)}) collective-permute-start(bf16[192,768]{1,0:T(8,128)(2,1)S(1)} %pad_maximum_fusion.3), channel_id=1, source_target_pairs={{0,8},{4,12},{8,0},{12,4},{16,24},{20,28},{24,16},{28,20},{1,9},{5... | collective-permute-start | bytes 884744 | tf_op jit(solution)/shard_map/ppermute | solution.py:50
  150.4 21.3 %collective-permute-start.13 = (bf16[1,2,256,768]{3,2,1,0:T(8,128)(2,1)S(1)}, bf16[1,2,256,768]{3,2,1,0:T(8,128)(2,1)S(1)}, u32[]{:S(2)}, u32[]{:S(2)}) collective-permute-start(bf16[1,2,256,768]{3,2,1,0:T(8,128)(2,1)S(1)} %slice.153), channel_id=1, source_target_pairs={{0,2},{1,3},{2,0},{3,1},{4,6},{5,7},{6,4},{7,5},{8,10},{9,11},{10,... | collective-permute-start | bytes 2359304 | tf_op jit(solution)/shard_map/ppermute | solution.py:50
  151.8 24.3 %collective-permute-start.32 = (bf16[192,768]{1,0:T(8,128)(2,1)S(1)}, bf16[192,768]{1,0:T(8,128)(2,1)S(1)}, u32[]{:S(2)}, u32[]{:S(2)}) collective-permute-start(bf16[192,768]{1,0:T(8,128)(2,1)S(1)} %pad_maximum_fusion.4), channel_id=1, source_target_pairs={{0,16},{4,20},{8,24},{12,28},{16,0},{20,4},{24,8},{28,12},{1,17},{... | collective-permute-start | bytes 884744 | tf_op jit(solution)/shard_map/ppermute | solution.py:50
  154.2 17.6 %collective-permute-start.16 = (bf16[256,128]{1,0:T(8,128)(2,1)S(1)}, bf16[256,128]{1,0:T(8,128)(2,1)S(1)}, u32[]{:S(2)}, u32[]{:S(2)}) collective-permute-start(bf16[256,128]{1,0:T(8,128)(2,1)S(1)} %get-tuple-element.86), channel_id=1, source_target_pairs={{0,16},{4,20},{8,24},{12,28},{16,0},{20,4},{24,8},{28,12},{1,17},{... | collective-permute-start | bytes 196616 | tf_op jit(solution)/shard_map/ppermute | solution.py:50
  155.3 16.5 %copy-start.21 = (f32[16,256]{1,0:T(8,128)S(1)}, f32[16,256]{1,0:T(8,128)}, u32[]{:S(2)}) copy-start(f32[16,256]{1,0:T(8,128)} %copy-done.20) | copy-start | bytes 49156
  155.3 16.5 %copy-start.23 = (bf16[768,128]{1,0:T(8,128)(2,1)S(1)}, bf16[768,128]{1,0:T(8,128)(2,1)}, u32[]{:S(2)}) copy-start(bf16[768,128]{1,0:T(8,128)(2,1)} %copy-done.22) | copy-start | bytes 589828
  155.3 16.6 %copy-start.25 = (f32[8,768]{1,0:T(8,128)S(1)}, f32[8,768]{1,0:T(8,128)}, u32[]{:S(2)}) copy-start(f32[8,768]{1,0:T(8,128)} %copy-done.24) | copy-start | bytes 73732
  155.4 16.5 %copy-start.3 = (bf16[768,768]{1,0:T(8,128)(2,1)S(1)}, bf16[768,768]{1,0:T(8,128)(2,1)}, u32[]{:S(2)}) copy-start(bf16[768,768]{1,0:T(8,128)(2,1)} %all-gather.5.cloned.1.call-done.wq_ref) | copy-start | bytes 3538948
  155.4 16.5 %copy-start.9 = (bf16[256,768]{1,0:T(8,128)(2,1)S(1)}, bf16[256,768]{1,0:T(8,128)(2,1)}, u32[]{:S(2)}) copy-start(bf16[256,768]{1,0:T(8,128)(2,1)} %get-tuple-element.48.dq_ref) | copy-start | bytes 1179652
  173.8 1.6 collective-permute-start.17
  173.9 25.5 %collective-permute-start.27 = (bf16[384,768]{1,0:T(8,128)(2,1)S(1)}, bf16[384,768]{1,0:T(8,128)(2,1)}, u32[]{:S(2)}, u32[]{:S(2)}) collective-permute-start(bf16[384,768]{1,0:T(8,128)(2,1)S(1)} %pad_maximum_fusion.upn), channel_id=1, source_target_pairs={{0,4},{4,0},{8,12},{12,8},{16,20},{20,16},{24,28},{28,24},{1,5},{5... | collective-permute-start | bytes 1769480 | tf_op jit(solution)/shard_map/ppermute | solution.py:50
  175.5 5.3 %collective-permute-start.18 = (f32[1,216,128]{2,1,0:T(8,128)S(1)}, f32[1,216,128]{2,1,0:T(8,128)S(1)}, u32[]{:S(2)}, u32[]{:S(2)}) collective-permute-start(f32[1,216,128]{2,1,0:T(8,128)S(1)} %slice.162), channel_id=1, source_target_pairs={{0,2},{1,3},{2,0},{3,1},{4,6},{5,7},{6,4},{7,5},{8,10},{9,11},{10,... | collective-permute-start | bytes 331784 | tf_op jit(solution)/shard_map/ppermute | solution.py:50
  176.1 23.3 %collective-permute-start.33 = (bf16[384,768]{1,0:T(8,128)(2,1)S(1)}, bf16[384,768]{1,0:T(8,128)(2,1)}, u32[]{:S(2)}, u32[]{:S(2)}) collective-permute-start(bf16[384,768]{1,0:T(8,128)(2,1)S(1)} %pad_maximum_fusion.1.dnn), channel_id=1, source_target_pairs={{0,8},{4,12},{8,0},{12,4},{16,24},{20,28},{24,16},{28,20},{1,9},{5... | collective-permute-start | bytes 1769480 | tf_op jit(solution)/shard_map/ppermute | solution.py:50
  180.7 11.3 %collective-permute-start.19 = (f32[216,128]{1,0:T(8,128)S(1)}, f32[216,128]{1,0:T(8,128)S(1)}, u32[]{:S(2)}, u32[]{:S(2)}) collective-permute-start(f32[216,128]{1,0:T(8,128)S(1)} %fusion), channel_id=1, source_target_pairs={{0,4},{4,0},{8,12},{12,8},{16,20},{20,16},{24,28},{28,24},{1,5},{5... | collective-permute-start | bytes 331784 | tf_op jit(solution)/shard_map/ppermute | solution.py:50
  192.1 4.8 %collective-permute-start.20 = (f32[216,128]{1,0:T(8,128)S(1)}, f32[216,128]{1,0:T(8,128)S(1)}, u32[]{:S(2)}, u32[]{:S(2)}) collective-permute-start(f32[216,128]{1,0:T(8,128)S(1)} %add.83), channel_id=1, source_target_pairs={{0,8},{4,12},{8,0},{12,4},{16,24},{20,28},{24,16},{28,20},{1,9},{5... | collective-permute-start | bytes 331784 | tf_op jit(solution)/shard_map/ppermute | solution.py:50
  196.9 8.8 %collective-permute-start.21 = (f32[216,128]{1,0:T(8,128)S(1)}, f32[216,128]{1,0:T(8,128)S(1)}, u32[]{:S(2)}, u32[]{:S(2)}) collective-permute-start(f32[216,128]{1,0:T(8,128)S(1)} %add.84), channel_id=1, source_target_pairs={{0,16},{4,20},{8,24},{12,28},{16,0},{20,4},{24,8},{28,12},{1,17},{... | collective-permute-start | bytes 331784 | tf_op jit(solution)/shard_map/ppermute | solution.py:50
  199.4 5.1 %copy-start.1 = (bf16[768,768]{1,0:T(8,128)(2,1)S(1)}, bf16[768,768]{1,0:T(8,128)(2,1)}, u32[]{:S(2)}) copy-start(bf16[768,768]{1,0:T(8,128)(2,1)} %all-gather.7.cloned.1.call-done.wo_ref) | copy-start | bytes 3538948
  199.4 5.1 %copy-start.6 = (bf16[256,768]{1,0:T(8,128)(2,1)S(1)}, bf16[256,768]{1,0:T(8,128)(2,1)}, u32[]{:S(2)}) copy-start(bf16[256,768]{1,0:T(8,128)(2,1)} %get-tuple-element.45.o_ref) | copy-start | bytes 1179652
  199.4 5.1 %copy-start.13 = (f32[16,768]{1,0:T(8,128)S(1)}, f32[16,768]{1,0:T(8,128)}, u32[]{:S(2)}) copy-start(f32[16,768]{1,0:T(8,128)} %copy-done.12) | copy-start | bytes 147460
  204.5 2.9 copy-start.17
  204.5 2.8 copy-start.19
  212.8 73.0 %copy-start.30 = (f32[1,192]{1,0:T(1,128)}, f32[1,192]{1,0:T(1,128)S(1)}, u32[]{:S(2)}) copy-start(f32[1,192]{1,0:T(1,128)S(1)} %get-tuple-element.92) | copy-start | bytes 2308
  (8 other events, 10.0 us)
Sparse Core Ops, SparseCore 0:
  9.6 20.1 all-gather.4
  31.4 25.3 all-gather.6
  77.1 28.1 all-gather.8
  137.5 20.7 all-gather.10
  212.3 71.2 all-reduce.1

commit v2 on v1

v2 whole, which is shorter than its diff:
```python
import functools

import jax
import jax.numpy as jnp
from jax import lax
from jax.experimental import pallas as pl
from jax.experimental.pallas import tpu as pltpu
from jax.sharding import PartitionSpec as P

HEADS = 12
HDIM = 64
ROT = 16
HALF = ROT // 2
BLOCK = 128

NEGATIVE = -1e30
EPSILON = 1e-05
SQRT_HALF = 0.7071067811865476
GAUSS_FACTOR = 0.3989422804014327
SCALE = HDIM ** (-0.5)
BF = jnp.bfloat16
F32 = jnp.float32
MIB = 1024 * 1024
VMEM = pl.BlockSpec(memory_space=pltpu.VMEM)
SMEM = pl.BlockSpec(memory_space=pltpu.SMEM)
ANY = pl.BlockSpec(memory_space=pl.ANY)
HBM = pl.BlockSpec(memory_space=pltpu.HBM)

NN = (((1,), (0,)), ((), ()))
NT = (((1,), (1,)), ((), ()))
TN = (((0,), (0,)), ((), ()))


def dot(left, right, dims=NN):
    return lax.dot_general(left, right, dims, preferred_element_type=F32)


def shape(dims, dtype):
    return jax.ShapeDtypeStruct(dims, dtype)


def params(limit=48):
    return pltpu.CompilerParams(vmem_limit_bytes=limit * MIB)


def micros(time):
    return pl.CostEstimate(flops=time * 1000000000, bytes_accessed=1000, transcendentals=0)


class Sequence:
    def __init__(self):
        self.last = ()

    def run(self, kernel, outs, ins, scratch=(), limit=16, name=None, after=(), time=1, **specs):
        single = isinstance(outs, jax.ShapeDtypeStruct)
        self.last = self.last + tuple(after)
        count, extra = len(ins), len(self.last)

        def body(*refs):
            kernel(*refs[:count], *refs[count + extra :])

        results = pl.pallas_call(
            body,
            out_shape=outs,
            in_specs=list(specs.get("in_specs", [VMEM] * count)) + [ANY] * extra,
            out_specs=specs.get("out_specs", VMEM if single else (VMEM,) * len(outs)),
            grid=specs.get("grid", ()),
            scratch_shapes=list(scratch),
            compiler_params=params(limit),
            cost_estimate=micros(time),
            name=name,
        )(*ins, *self.last)
        self.last = (min((results,) if single else results, key=lambda v: v.size),)
        return results

    def stage(self, *tasks):
        ins, outs, plan = [], [], []
        for kind, arrays, parts in tasks:
            rows = arrays[0].shape[0] if kind is not join_step else sum(v.shape[0] for v in arrays)
            plan.append((kind, len(arrays), parts))
            ins.extend(arrays)
            outs.extend([shape((rows // parts,) + arrays[0].shape[1:], BF)] * parts)

        def kernel(*refs):
            sources, targets = refs[: len(ins)], refs[len(ins) :]
            for kind, count, parts in plan:
                kind(sources[:count], targets[:parts])
                sources, targets = sources[count:], targets[parts:]

        results = list(self.run(kernel, tuple(outs), ins, name="stage"))
        grouped = []
        for _, _, parts in plan:
            grouped.append(results[:parts])
            results = results[parts:]
        return grouped


class Sum:
    def __init__(self, near, far, bits, rest):
        self.near, self.coming = near, swap(far, "seq", bits[0])
        self.plan = [(bit, 2) for bit in bits[1:]] + [(bit, 1) for bit in rest]
        self.plan += [(bits[-1], 0)] + [(bit, -1) for bit in reversed(bits[:-1])]

    def left(self):
        return len(self.plan)

    def task(self):
        parts = self.plan[0][1]
        if parts == -1:
            return (join_step, [self.near, self.coming], 1)
        return (merge_step, [self.near, self.coming], max(parts, 1))

    def give(self, results):
        bit = self.plan.pop(0)[0]
        self.near = results[0]
        self.coming = swap(results[-1], "seq", bit)

    def pair(self):
        return (self.near, self.coming)


class Reduce(Sum):
    def __init__(self, near, far, bits):
        Sum.__init__(self, near, far, bits, [])
        self.plan = self.plan[: len(bits) - 1]


class Mix(Sum):
    def __init__(self, near, far, fbits, sbits):
        self.near, self.coming = near, swap(far, "fsdp", fbits[0])
        self.plan = [("fsdp", bit, 2) for bit in fbits[1:]] + [("seq", bit, 1) for bit in sbits]

    def task(self):
        return (mix_step, [self.near, self.coming], self.plan[0][2])

    def give(self, results):
        axis, bit, _ = self.plan.pop(0)
        self.near = results[0]
        self.coming = swap(results[-1], axis, bit)


def advance(sequence, *items, extra=()):
    results = sequence.stage(*[item.task() for item in items], *extra)
    for item, result in zip(items, results):
        item.give(result)
    return [result[0] for result in results[len(items) :]]


def swap(value, axis, bit):
    size = lax.axis_size(axis)
    return lax.ppermute(value, axis, [(i, i ^ bit) for i in range(size)])


def bits_of(size):
    return [1 << i for i in range(size.bit_length() - 1)]


def normalize(values):
    center = values - jnp.mean(values, -1, keepdims=True)
    inverse_std = lax.rsqrt(jnp.mean(center * center, -1, keepdims=True) + EPSILON)
    return (center * inverse_std, inverse_std)


def pick(pieces, index):
    result = pieces[-1]
    for i in range(len(pieces) - 2, -1, -1):
        result = jnp.where(index == i, pieces[i], result)
    return result


def rel_order(size):
    order = [0]
    for bit in reversed(bits_of(size)):
        order = order + [r ^ bit for r in order]
    return order


def pack_kernel(*refs):
    count = len(refs) // 2
    pack_ref, both_ref, sems = refs[count], refs[count + 1], refs[-1]
    rows = refs[0].shape[0]
    held = (both_ref.at[:rows], both_ref.at[rows:]) + refs[count + 2 : -1]
    copies = [
        pltpu.make_async_copy(refs[i], held[i], sems.at[i]) for i in range(count)
    ]
    for copy in copies:
        copy.start()
    for copy in copies:
        copy.wait()
    g1, b1, g2, b2, qb, ob, db, kb, vb, wk_ref, wv_ref = held[2:]
    part = g1.shape[0]
    small = jnp.concatenate(
        [
            kb[...].astype(F32).reshape(1, kb.shape[0]),
            vb[...].astype(F32).reshape(1, vb.shape[0]),
            jnp.zeros((1, part - kb.shape[0] - vb.shape[0]), F32),
        ],
        axis=1,
    )
    lines = [ref[...].astype(F32).reshape(1, part) for ref in (g1, b1, g2, b2, qb, ob, db)]
    lines = jnp.concatenate(lines + [small, jnp.zeros((8, part), F32)], axis=0)
    pack_ref[:HDIM] = wk_ref[...]
    pack_ref[HDIM : 2 * HDIM] = wv_ref[...]
    pack_ref[2 * HDIM :] = lines.astype(BF)


def front_kernel(rels, x_ref, *refs):
    count = len(rels)
    packs = refs[:count]
    cs_ref, n1_ref, kv_ref, vec_ref, wkv_ref, pieces, weights = refs[count:]
    me = lax.axis_index("fsdp")
    for rel, pack in zip(rels, packs):
        weights[rel ^ me] = pack[: 2 * HDIM, :]
        pieces[rel ^ me] = pack[2 * HDIM :, :].astype(F32)
    wkv = jnp.concatenate([weights[p] for p in range(count)], axis=1)
    wkv_ref[...] = wkv
    vec = jnp.concatenate([pieces[p] for p in range(count)], axis=1)
    vec_ref[...] = vec
    normal, _ = normalize(x_ref[...].astype(F32))
    n1 = (normal * vec[0:1] + vec[1:2]).astype(BF)
    n1_ref[...] = n1
    key_part, value_part = ROT // count, HDIM // count
    key_bias = jnp.concatenate([pieces[p][7:8, :key_part] for p in range(count)], axis=1)
    value_bias = jnp.concatenate(
        [pieces[p][7:8, key_part : key_part + value_part] for p in range(count)], axis=1
    )
    bias = jnp.concatenate([key_bias, jnp.zeros((1, HDIM - ROT), F32), value_bias], axis=1)
    turned = (dot(n1, wkv, NT) + bias).T
    cosine, sine = cs_ref[:HALF], cs_ref[HALF:]
    first, second = turned[:HALF], turned[HALF:ROT]
    turned = jnp.concatenate(
        [first * cosine - second * sine, second * cosine + first * sine, turned[ROT:]], axis=0
    )
    kv_ref[...] = turned.T.astype(BF)


def query_kernel(rels, n1_ref, dy_ref, vec_ref, cs_ref, *refs):
    count = len(rels)
    packs = refs[:count]
    qt_ref, dot_ref, wq_ref, wo_ref = refs[count:]
    me = lax.axis_index("fsdp")
    part = packs[0].shape[0] // 2
    for rel, pack in zip(rels, packs):
        start = pl.multiple_of((rel ^ me) * part, part)
        wq_ref[pl.ds(start, part), :] = pack[:part]
        wo_ref[pl.ds(start, part), :] = pack[part:]
    turned = (dot(n1_ref[...], wq_ref[...]) + vec_ref[4:5]).T
    cosine, sine = cs_ref[:HALF], cs_ref[HALF:]
    for h in range(HEADS):
        base = h * HDIM
        first, second = turned[base : base + HALF], turned[base + HALF : base + ROT]
        head = jnp.concatenate(
            [
                first * cosine - second * sine,
                second * cosine + first * sine,
                turned[base + ROT : base + HDIM],
            ],
            axis=0,
        )
        qt_ref[base : base + HDIM, :] = (head.astype(BF).astype(F32) * SCALE).astype(BF)
    dot_ref[...] = dot(dy_ref[...], wo_ref[...], NT).T.astype(BF)


def mlp_kernel(seq_orders, last, *refs):
    both, refs = refs[:2], refs[2:]
    if last:
        up_ref, down_ref, ub_ref, vec_ref, early_up, early_dn, early_sums = refs[:7]
        keep_ref, send_ref, n1c_ref, upk_ref, ups_ref, dnk_ref, dns_ref, sums_ref = refs[7:15]
        normal_s, n2_s, dy_s, acc_up, acc_dn = refs[15:]
    else:
        up_ref, down_ref, ub_ref, vec_ref, wq_ref, wo_ref = refs[:6]
        keep_ref, send_ref, n1c_ref, acc_up, acc_dn, sums_ref, pack_ref = refs[6:13]
        normal_s, n2_s, dy_s = refs[13:]
        half = pack_ref.shape[0] // 2
        pack_ref[:half] = wq_ref[...]
        pack_ref[half:] = wo_ref[...]
    me = lax.axis_index("fsdp")
    seq_me = lax.axis_index("seq")
    hidden, width = up_ref.shape
    part = n1c_ref.shape[2]
    rows = n1c_ref.shape[1]
    for i in range(2):
        here = slice(i * rows, (i + 1) * rows)
        x, dy = both[i][:rows], both[i][rows:]
        dy_s[here] = dy
        normal, _ = normalize(x.astype(F32))
        normal_s[here] = normal
        n1 = normal * vec_ref[0:1] + vec_ref[1:2]
        n1c_ref[i] = pick(
            [n1[:, p * part : (p + 1) * part] for p in range(width // part)], me
        ).astype(BF)
        n2_s[here] = (normal * vec_ref[2:3] + vec_ref[3:4]).astype(BF)
    n2, dy = n2_s[...], dy_s[...]
    out = None
    dn2 = None
    tile = 256
    bias = ub_ref[...].astype(F32).reshape(1, hidden)
    sums = []
    for c in range(hidden // tile):
        here = slice(c * tile, (c + 1) * tile)
        up_c, down_c = up_ref[here, :], down_ref[here, :]
        u = dot(n2, up_c, NT) + bias[:, here]
        dg = dot(dy, down_c, NT)
        phi = 0.5 * (1.0 + lax.erf(u * SQRT_HALF))
        g = (u * phi).astype(BF)
        du = (dg * (phi + u * jnp.exp(-0.5 * u * u) * GAUSS_FACTOR)).astype(BF)
        out_c = dot(g, down_c)
        dn2_c = dot(du, up_c)
        out = out_c if out is None else out + out_c
        dn2 = dn2_c if dn2 is None else dn2 + dn2_c
        grad_down, grad_up = dot(g, dy, TN), dot(du, n2, TN)
        if last:
            grad_down, grad_up = grad_down + early_dn[here, :], grad_up + early_up[here, :]
        acc_dn[here, :] = grad_down
        acc_up[here, :] = grad_up
        sums.append(jnp.sum(du.astype(F32), axis=0, keepdims=True))
    lines = [
        jnp.sum(dn2 * normal_s[...], axis=0, keepdims=True),
        jnp.sum(dn2, axis=0, keepdims=True),
        jnp.concatenate(sums, axis=1),
    ]
    for i, line in enumerate(lines):
        size = line.shape[1]
        if last:
            line = line + early_sums[i : i + 1, :size]
        sums_ref[i : i + 1, :size] = line
    for i, target in enumerate((keep_ref, send_ref)):
        here = slice(i * rows, (i + 1) * rows)
        target[0] = out[here].astype(BF)
        target[1] = (dn2[here] * vec_ref[2:3]).astype(BF)
    if last:
        spread_shards(acc_up, seq_orders[0], seq_me, upk_ref, ups_ref)
        spread_shards(acc_dn, seq_orders[1], seq_me, dnk_ref, dns_ref)


def attend_kernel(
    per_group,
    chunk_blocks,
    most,
    order_ref,
    len_ref,
    qt_ref,
    dot_ref,
    kv_near,
    kv_far,
    cs_ref,
    o_ref,
    far_ref,
    near_ref,
    dkvn_ref,
    dkvf_ref,
    s_scr,
    p_scr,
    pb_scr,
    ds_scr,
    bias_scr,
    kv_scr,
    dkv_scr,
    qs,
    dos,
    ot,
    dqt,
    inverse,
):
    side, group = pl.program_id(0), pl.program_id(1)
    seq_me = lax.axis_index("seq")
    half = kv_near.shape[0]
    slots = 2 * half // BLOCK
    chunk = chunk_blocks * BLOCK
    lanes = per_group * BLOCK
    first_step = jnp.logical_and(side == 0, group == 0)
    last_step = jnp.logical_and(
        side == pl.num_programs(0) - 1, group == pl.num_programs(1) - 1
    )

    @pl.when(first_step)
    def _():
        dkv_scr[...] = jnp.zeros_like(dkv_scr)

        @pl.loop(0, slots)
        def _(i):
            rel = (i // 2) ^ seq_me
            place = jnp.int32(0)
            for bit in bits_of(slots // 2):
                place = place * 2 + (rel // bit) % 2
            inverse[order_ref[i]] = place * 2 + i % 2

    block = order_ref[2 * seq_me + side]
    base = block * BLOCK
    end_1 = len_ref[0, 0]
    end_2 = end_1 + len_ref[0, 1]
    end_3 = end_2 + len_ref[0, 2]

    def start_of(position):
        low = jnp.where(position >= end_1, end_1, 0)
        low = jnp.where(position >= end_2, end_2, low)
        return jnp.where(position >= end_3, end_3, low)

    q_pos = base + lax.broadcasted_iota(jnp.int32, (1, BLOCK), 1)
    q_start = start_of(q_pos)
    low_block = jnp.maximum(start_of(base) // BLOCK, block - (most - 1))
    chunks = (block - low_block + chunk_blocks) // chunk_blocks

    def slot_of(j):
        return inverse[jnp.minimum(low_block + j, block)]

    @pl.loop(0, chunks * chunk_blocks)
    def _(j):
        start = slot_of(j) * BLOCK
        here = pl.ds(pl.multiple_of(j * BLOCK, BLOCK), BLOCK)

        @pl.when(start < half)
        def _():
            kv_scr[here, :] = kv_near[pl.ds(pl.multiple_of(start, BLOCK), BLOCK), :]

        @pl.when(start >= half)
        def _():
            kv_scr[here, :] = kv_far[pl.ds(pl.multiple_of(start - half, BLOCK), BLOCK), :]

    for h in range(per_group):
        cols = slice(h * BLOCK, (h + 1) * BLOCK)
        qs[:, cols] = qt_ref[h * HDIM : (h + 1) * HDIM, :]
        dos[:, cols] = dot_ref[h * HDIM : (h + 1) * HDIM, :]

    def score_step(c, top):
        kv = kv_scr[pl.ds(c * chunk, chunk), :]
        s_scr[c] = dot(kv[:, :HDIM], qs[...])
        p_scr[c] = dot(kv[:, HDIM:], dos[...])
        k_pos = (low_block + c * chunk_blocks) * BLOCK + lax.broadcasted_iota(
            jnp.int32, (chunk, BLOCK), 0
        )
        allowed = jnp.logical_and(k_pos <= q_pos, k_pos >= q_start)
        bias_scr[...] = jnp.where(allowed, 0.0, NEGATIVE)
        tops = []
        for h in range(per_group):
            cols = slice(h * BLOCK, (h + 1) * BLOCK)
            s = s_scr[c, :, cols] + bias_scr[...]
            s_scr[c, :, cols] = s
            tops.append(jnp.max(s, axis=0, keepdims=True))
        return jnp.maximum(top, jnp.concatenate(tops, axis=1))

    top = lax.fori_loop(0, chunks, score_step, jnp.full((1, lanes), NEGATIVE, F32))

    def weight_step(c, carry):
        total, delta = carry
        totals, deltas = [], []
        for h in range(per_group):
            cols = slice(h * BLOCK, (h + 1) * BLOCK)
            e = jnp.exp(s_scr[c, :, cols] - top[:, cols])
            s_scr[c, :, cols] = e
            totals.append(jnp.sum(e, axis=0, keepdims=True))
            deltas.append(jnp.sum(e * p_scr[c, :, cols], axis=0, keepdims=True))
        return (
            total + jnp.concatenate(totals, axis=1),
            delta + jnp.concatenate(deltas, axis=1),
        )

    zero = jnp.zeros((1, lanes), F32)
    total, delta = lax.fori_loop(0, chunks, weight_step, (zero, zero))
    shrink = 1.0 / total
    delta = delta * shrink
    ot[...] = jnp.zeros_like(ot)
    dqt[...] = jnp.zeros_like(dqt)

    def grad_step(c, _):
        for h in range(per_group):
            cols = slice(h * BLOCK, (h + 1) * BLOCK)
            p = s_scr[c, :, cols] * shrink[:, cols]
            pb_scr[:, cols] = p.astype(BF)
            ds_scr[:, cols] = (p * (p_scr[c, :, cols] - delta[:, cols])).astype(BF)
        kv = kv_scr[pl.ds(c * chunk, chunk), :]
        ot[...] += dot(kv[:, HDIM:], pb_scr[...], TN)
        dqt[...] += dot(kv[:, :HDIM], ds_scr[...], TN)
        dk = dot(ds_scr[...], qs[...], NT)
        dv = dot(pb_scr[...], dos[...], NT)
        both = jnp.concatenate([dk, dv], axis=1)
        for b in range(chunk_blocks):

            @pl.when(low_block + c * chunk_blocks + b <= block)
            def _():
                place = slot_of(c * chunk_blocks + b) * BLOCK
                dkv_scr[pl.ds(pl.multiple_of(place, BLOCK), BLOCK), :] += both[
                    b * BLOCK : (b + 1) * BLOCK
                ]

        return 0

    lax.fori_loop(0, chunks, grad_step, 0)
    cosine, sine = cs_ref[:HALF], cs_ref[HALF:]
    outs, grads = [], []
    for h in range(per_group):
        cols = slice(h * BLOCK, (h + 1) * BLOCK)
        outs.append(ot[:, cols])
        grad = dqt[:, cols] * SCALE
        first, second = grad[:HALF], grad[HALF:ROT]
        grads.append(first * cosine + second * sine)
        grads.append(second * cosine - first * sine)
        grads.append(grad[ROT:])
    width = o_ref.shape[1]
    here = pl.ds(pl.multiple_of(side * BLOCK, BLOCK), BLOCK)
    span = per_group * HDIM
    across = pl.ds(0 if span == width else pl.multiple_of(group * span, span), span)
    o_ref[here, across] = jnp.concatenate(outs, axis=0).T.astype(BF)
    grad = jnp.concatenate(grads, axis=0).T.astype(BF)
    far_ref[here, across] = grad
    near_ref[here, across] = grad

    @pl.when(group == pl.num_programs(1) - 1)
    def _():
        me = lax.axis_index("fsdp")
        part = near_ref.shape[1] - width
        count = width // part
        o = o_ref[here, :].astype(F32)
        pieces = [o[:, p * part : (p + 1) * part] for p in range(count)]
        near_ref[here, width:] = pick(pieces, me ^ 1).astype(BF)
        far_ref[here, width:] = jnp.concatenate(
            [pick(pieces, me ^ 2), pick(pieces, me ^ 3)], axis=1
        ).astype(BF)

    @pl.when(last_step)
    def _():
        dkvn_ref[...] = dkv_scr[:half].astype(dkvn_ref.dtype)
        dkvf_ref[...] = dkv_scr[half:].astype(dkvf_ref.dtype)


def output_kernel(x_ref, o_ref, wo_ref, vec_ref, a_ref, b_ref, c_ref, layer_ref):
    mlp = a_ref[0].astype(F32) + b_ref[0].astype(F32) + c_ref[0].astype(F32)
    attention = dot(o_ref[...], wo_ref[...]) + vec_ref[5:6]
    layer_ref[...] = (x_ref[...].astype(F32) + attention + mlp + vec_ref[6:7]).astype(BF)


def spread_shards(source, order, seq_me, near, far):
    shards = len(order)
    rows = source.shape[0] // shards
    half = shards // 2
    for m in range(shards):
        start = pl.multiple_of(((order[m] ^ seq_me) & (shards - 1)) * rows, rows)
        target = near if m < half else far
        target[(m % half) * rows : (m % half + 1) * rows, :] = source[pl.ds(start, rows), :].astype(
            BF
        )


def weight_kernel(order, n1a_ref, n1b_ref, o_ref, own_ref, z1_ref, z2_ref, z3_ref, *refs):
    me = lax.axis_index("fsdp")
    rows, part = n1a_ref.shape[1:]
    dys = [ref.at[rows:] for ref in refs[:4]]
    near_ref, far_ref, grad = refs[4:]
    width = dys[0].shape[1]
    o = o_ref[...].astype(F32)
    own = pick([o[:, p * part : (p + 1) * part] for p in range(width // part)], me).astype(BF)
    items = (
        (n1a_ref[0], own_ref[:, :width], own, dys[0][...]),
        (n1a_ref[1], z1_ref[:, :width], z1_ref[:, width:], dys[1][...]),
        (n1b_ref[0], z2_ref[:, :width], z2_ref[:, width : width + part], dys[2][...]),
        (n1b_ref[1], z3_ref[:, :width], z3_ref[:, width + part :], dys[3][...]),
    )
    grad_q = None
    grad_o = None
    for n1, dq, cols, dy in items:
        term_q, term_o = dot(n1, dq, TN), dot(cols, dy, TN)
        grad_q = term_q if grad_q is None else grad_q + term_q
        grad_o = term_o if grad_o is None else grad_o + term_o
    grad[:part] = grad_q
    grad[part:] = grad_o
    spread_shards(grad, order, lax.axis_index("seq"), near_ref, far_ref)


def tail_kernel(
    rels,
    x_ref,
    dy_ref,
    n1_ref,
    dq_ref,
    wq_ref,
    wkv_ref,
    vec_ref,
    cs_ref,
    a_ref,
    b_ref,
    c_ref,
    dkvn_ref,
    dkvf_ref,
    sums_ref,
    grad_ref,
    keep_ref,
    send_ref,
    vs,
):
    count = len(rels)
    me = lax.axis_index("fsdp")
    width = x_ref.shape[1]
    part = width // count
    dkv = (dkvn_ref[...].astype(F32) + dkvf_ref[...].astype(F32)).T
    cosine, sine = cs_ref[:HALF], cs_ref[HALF:]
    first, second = dkv[:HALF], dkv[HALF:ROT]
    dkv = jnp.concatenate(
        [first * cosine + second * sine, second * cosine - first * sine, dkv[ROT:]], axis=0
    )
    dkv_sum = jnp.sum(dkv.astype(BF).T.astype(F32), axis=0, keepdims=True)
    dkv_t = dkv.astype(BF)
    dq = dq_ref[:, :width]
    dn1 = dot(dq, wq_ref[...], NT) + dot(dkv_t, wkv_ref[...], TN)
    normal, inverse_std = normalize(x_ref[...].astype(F32))
    dy = dy_ref[...].astype(F32)
    total = a_ref[1].astype(F32) + b_ref[1].astype(F32) + c_ref[1].astype(F32)
    total = total + dn1 * vec_ref[0:1]
    grad_ref[...] = (
        dy
        + inverse_std
        * (
            total
            - jnp.mean(total, -1, keepdims=True)
            - normal * jnp.mean(total * normal, -1, keepdims=True)
        )
    ).astype(BF)
    grad_kv = dot(dkv_t, n1_ref[...])
    lines = jnp.concatenate(
        [
            jnp.sum(dn1 * normal, axis=0, keepdims=True),
            jnp.sum(dn1, axis=0, keepdims=True),
            sums_ref[0:1, :width],
            sums_ref[1:2, :width],
            jnp.sum(dq.astype(F32), axis=0, keepdims=True),
            jnp.sum(dy, axis=0, keepdims=True),
            jnp.concatenate(
                [jnp.concatenate([dkv_sum, jnp.zeros((1, part - 2 * HDIM), F32)], axis=1)] * count,
                axis=1,
            ),
            jnp.zeros((1, width), F32),
        ],
        axis=0,
    )
    for p in range(count):
        cols = slice(p * part, (p + 1) * part)
        vs[p, : 2 * HDIM, :] = grad_kv[:, cols]
        vs[p, 2 * HDIM :, :] = lines[:, cols]
    half = count // 2
    extra = sums_ref.shape[1] // part
    up_bias = jnp.concatenate(
        [sums_ref[2:3, e * part : (e + 1) * part] for e in range(extra)]
        + [jnp.zeros((8 - extra, part), F32)],
        axis=0,
    )
    for m, rel in enumerate(rels):
        target = keep_ref if m < half else send_ref
        piece = vs[rel ^ me]
        last = up_bias if rel == 0 else jnp.zeros_like(up_bias)
        store_split(
            target, m % half, piece[: 2 * HDIM], jnp.concatenate([piece[2 * HDIM :], last], axis=0)
        )


def store_split(target, index, matrix, lines):
    top = matrix.shape[0]
    high = lines.astype(BF)
    target[index, :top] = matrix.astype(BF)
    target[index, top : top + 16] = high
    target[index, top + 16 : top + 32] = (lines - high.astype(F32)).astype(BF)


def load_split(value):
    top = 2 * HDIM
    value = value.astype(F32)
    return (value[:top], value[top : top + 16] + value[top + 16 : top + 32])


def mix_step(sources, targets):
    a_ref, b_ref = sources
    each = a_ref.shape[0] // len(targets)
    for i, target in enumerate(targets):
        for j in range(each):
            first, second = load_split(a_ref[i * each + j]), load_split(b_ref[i * each + j])
            store_split(target, j, first[0] + second[0], first[1] + second[1])


def merge_step(sources, targets):
    a_ref, b_ref = sources
    rows = a_ref.shape[0] // len(targets)
    for i, target in enumerate(targets):
        here = slice(i * rows, (i + 1) * rows)
        target[...] = (a_ref[here].astype(F32) + b_ref[here].astype(F32)).astype(BF)


def join_step(sources, targets):
    rows = 0
    for source in sources:
        targets[0][rows : rows + source.shape[0]] = source[...]
        rows += source.shape[0]


def matrix_kernel(order, near_ref, far_ref, *refs):
    outs, (held, sems) = refs[:-2], refs[-2:]
    seq_me = lax.axis_index("seq")
    shards = len(order)
    half = shards // 2
    rows = near_ref.shape[0] // half
    each = shards // len(outs)
    copies = []
    for t in range(shards):
        wanted = (t ^ seq_me) & (shards - 1)
        place = jnp.int32(0)
        for m, rel in enumerate(order):
            place = jnp.where(wanted == rel, m, place)
        start = pl.multiple_of((place & (half - 1)) * rows, rows)

        @pl.when(place < half)
        def _():
            held[t] = near_ref[pl.ds(start, rows), :].astype(F32)

        @pl.when(place >= half)
        def _():
            held[t] = far_ref[pl.ds(start, rows), :].astype(F32)

        first = (t % each) * rows
        copy = pltpu.make_async_copy(
            held.at[t], outs[t // each].at[first : first + rows, :], sems.at[t]
        )
        copy.start()
        copies.append(copy)
    for copy in copies:
        copy.wait()


def vector_kernel(a_ref, b_ref, g1, b1, qb, kb, vb, ob, g2, b2, ub, db, wk_ref, wv_ref):
    me = lax.axis_index("fsdp")
    first, second = load_split(a_ref[0]), load_split(b_ref[0])
    total, lines = first[0] + second[0], first[1] + second[1]
    part = total.shape[1]
    wk_ref[...] = total[:HDIM]
    wv_ref[...] = total[HDIM:]
    for i, targets in enumerate(((g1,), (b1,), (g2,), (b2,), (qb,), (ob, db))):
        for target in targets:
            target[...] = lines[i : i + 1].reshape(part)
    kp, vp = kb.shape[0], vb.shape[0]
    line = lines[6:7]
    count = HDIM // vp
    kb[...] = pick([line[:, p * kp : (p + 1) * kp] for p in range(count)], me).reshape(kp)
    vb[...] = pick(
        [line[:, HDIM + p * vp : HDIM + (p + 1) * vp] for p in range(count)], me
    ).reshape(vp)
    extra = ub.shape[0] // part
    ub[...] = jnp.concatenate([lines[8 + e : 9 + e] for e in range(extra)], axis=1).reshape(
        ub.shape[0]
    )


def shard_count(rows, devices):
    shards = devices
    while shards > 2 and (rows % shards or (rows // shards) % 16):
        shards //= 2
    return shards


def shard_order(bits):
    order = [0]
    for bit in reversed(bits):
        order = order + [r ^ bit for r in order]
    return order


def on_device(
    tokens,
    block_order,
    doc_lengths,
    norm_one_gain,
    norm_one_bias,
    query_weight,
    query_bias,
    key_weight,
    key_bias,
    value_weight,
    value_bias,
    out_weight,
    out_bias,
    norm_two_gain,
    norm_two_bias,
    up_weight,
    up_bias,
    down_weight,
    down_bias,
    cotangent,
):
    _, rows, width = tokens.shape
    hidden = up_weight.shape[0]
    part = query_weight.shape[0]
    fsdp = lax.axis_size("fsdp")
    seqs = lax.axis_size("seq")
    slots = 2 * seqs
    fbits = bits_of(fsdp)
    sbits = bits_of(seqs)
    rels = rel_order(fsdp)
    fsdp_me = lax.axis_index("fsdp")
    seq_me = lax.axis_index("seq")
    x_own = tokens.reshape(rows, width)
    dy_own = cotangent.reshape(rows, width)

    def spread(value):
        parts = [value]
        for bit in reversed(fbits):
            parts = parts + [swap(v, "fsdp", bit) for v in parts]
        return parts

    pieces = (
        x_own,
        dy_own,
        norm_one_gain,
        norm_one_bias,
        norm_two_gain,
        norm_two_bias,
        query_bias,
        out_bias,
        down_bias,
        key_bias,
        value_bias,
        key_weight.T,
        value_weight.T,
    )
    sequence = Sequence()
    run = sequence.run
    pack, both_0 = run(
        pack_kernel,
        (shape((2 * HDIM + 16, part), BF), shape((2 * rows, width), BF)),
        pieces,
        [pltpu.VMEM(v.shape, BF) for v in pieces[2:]] + [pltpu.SemaphoreType.DMA((len(pieces),))],
        limit=60,
        name="pack",
        time=2,
        in_specs=[HBM] * len(pieces),
    )
    packs = spread(pack)
    both_2 = swap(both_0, "fsdp", 2)
    both_1 = swap(both_0, "fsdp", 1)

    own_blocks = lax.dynamic_slice_in_dim(block_order, 2 * seq_me, 2)
    offsets = jnp.arange(BLOCK, dtype=jnp.int32)
    own_pos = (own_blocks[:, None] * BLOCK + offsets[None, :]).reshape(rows)
    frequencies = 10000.0 ** (-2.0 * jnp.arange(HALF, dtype=F32) / ROT)
    angles = own_pos.astype(F32)[None, :] * frequencies[:, None]
    cs = jnp.concatenate([jnp.cos(angles), jnp.sin(angles)], axis=0)

    n1, kv_own, vec, wkv = run(
        functools.partial(front_kernel, rels),
        (
            shape((rows, width), BF),
            shape((rows, 2 * HDIM), BF),
            shape((16, width), F32),
            shape((2 * HDIM, width), BF),
        ),
        (x_own, *packs, cs),
        [pltpu.VMEM((fsdp, 16, part), F32), pltpu.VMEM((fsdp, 2 * HDIM, part), BF)],
        name="front",
    )

    kv = kv_own
    for bit in reversed(sbits[3:]):
        ((kv,),) = sequence.stage((join_step, [kv, swap(kv, "seq", bit)], 1))
    kv_parts = [kv] + [swap(kv, "seq", bit) for bit in (sbits[2], sbits[1], sbits[1] + sbits[2])]

    shards = shard_count(hidden, seqs)
    low_bits = [b for b in sbits if b < shards]
    rest_bits = [b for b in sbits if b >= shards]
    up_bits = low_bits
    dn_bits = low_bits[1:] + low_bits[:1]
    seq_orders = (shard_order(up_bits), shard_order(dn_bits))
    chunk_out = shape((2, rows, width), BF)
    n1c_out = shape((2, rows, part), BF)
    sums_out = shape((8, max(hidden, width)), F32)
    mlp_scratch = [
        pltpu.VMEM((2 * rows, width), F32),
        pltpu.VMEM((2 * rows, width), BF),
        pltpu.VMEM((2 * rows, width), BF),
    ]
    keep_a, send_a, n1a, early_up, early_dn, early_sums, pack_qo = run(
        functools.partial(mlp_kernel, None, False),
        (
            chunk_out,
            chunk_out,
            n1c_out,
            shape((hidden, width), F32),
            shape((hidden, width), F32),
            sums_out,
            shape((2 * part, width), BF),
        ),
        (both_0, both_1, up_weight, down_weight, up_bias, vec, query_weight, out_weight),
        mlp_scratch,
        limit=24,
        name="mlp_near",
        time=7,
    )
    (kv_near,), (relay,) = sequence.stage((join_step, kv_parts, 1), (join_step, [both_2], 1))
    both_3 = swap(relay, "fsdp", 1)
    qo_1 = swap(pack_qo, "fsdp", 1)
    back_a = swap(send_a, "fsdp", 1)
    kv_far = swap(kv_near, "seq", sbits[0])
    qo_2 = swap(pack_qo, "fsdp", 2)
    keep_b, send_b, n1b, upk, ups, dnk, dns, sums = run(
        functools.partial(mlp_kernel, seq_orders, True),
        (chunk_out, chunk_out, n1c_out)
        + (shape((hidden // 2, width), BF),) * 4
        + (sums_out,),
        (both_2, both_3, up_weight, down_weight, up_bias, vec, early_up, early_dn, early_sums),
        mlp_scratch + [pltpu.VMEM((hidden, width), F32)] * 2,
        limit=28,
        name="mlp_far",
        time=8,
        after=(qo_1, back_a, kv_far),
    )
    up = Sum(upk, ups, up_bits, rest_bits)
    dn = Sum(dnk, dns, dn_bits, rest_bits)
    ((relay_qo,),) = sequence.stage((join_step, [qo_2], 1))
    qo_3 = swap(relay_qo, "fsdp", 1)
    back_b = swap(send_b, "fsdp", 1)
    qt, do_t, wq, wo = run(
        functools.partial(query_kernel, rels),
        (
            shape((width, rows), BF),
            shape((width, rows), BF),
            shape((width, width), BF),
            shape((width, width), BF),
        ),
        (n1, dy_own, vec, cs, pack_qo, qo_2, qo_1, qo_3),
        name="query",
    )
    ((back,),) = sequence.stage((merge_step, [keep_b, back_b], 1))
    back = swap(back, "fsdp", 2)
    mlp_parts = (keep_a, back_a, back)

    most = min(slots, slots // 2 + 1)
    chunk_blocks = 2
    most_chunks = -(-most // chunk_blocks)
    chunk = chunk_blocks * BLOCK
    per_group = HEADS
    while most_chunks * chunk * per_group * BLOCK * 8 > 20 * MIB and per_group > 2:
        per_group = {12: 6, 6: 4, 4: 2}[per_group]
    lanes = per_group * BLOCK
    span = per_group * HDIM
    own, z_far, z_near, dkv_near, dkv_far = run(
        functools.partial(attend_kernel, per_group, chunk_blocks, most),
        (
            shape((rows, width), BF),
            shape((rows, width + 2 * part), BF),
            shape((rows, width + part), BF),
            shape((seqs * BLOCK, 2 * HDIM), BF),
            shape((seqs * BLOCK, 2 * HDIM), BF),
        ),
        (block_order, doc_lengths, qt, do_t, kv_near, kv_far, cs),
        [
            pltpu.VMEM((most_chunks, chunk, lanes), F32),
            pltpu.VMEM((most_chunks, chunk, lanes), F32),
            pltpu.VMEM((chunk, lanes), BF),
            pltpu.VMEM((chunk, lanes), BF),
            pltpu.VMEM((chunk, BLOCK), F32),
            pltpu.VMEM((most_chunks * chunk, 2 * HDIM), BF),
            pltpu.VMEM((slots * BLOCK, 2 * HDIM), F32),
            pltpu.VMEM((HDIM, lanes), BF),
            pltpu.VMEM((HDIM, lanes), BF),
            pltpu.VMEM((HDIM, lanes), F32),
            pltpu.VMEM((HDIM, lanes), F32),
            pltpu.SMEM((slots,), jnp.int32),
        ],
        limit=40,
        name="attend",
        time=13,
        grid=(2, HEADS // per_group),
        in_specs=[
            SMEM,
            SMEM,
            pl.BlockSpec((span, BLOCK), lambda i, g: (g, i)),
            pl.BlockSpec((span, BLOCK), lambda i, g: (g, i)),
            VMEM,
            VMEM,
            pl.BlockSpec((ROT, BLOCK), lambda i, g: (0, i)),
        ],
    )

    dkv = Reduce(dkv_near, dkv_far, sbits)
    z2 = swap(z_far, "fsdp", 2)
    advance(sequence, up, dn)
    layer_out = run(
        output_kernel,
        shape((rows, width), BF),
        (x_own, own, wo, vec, *mlp_parts),
        name="output",
    )
    while dkv.left() > 1:
        advance(sequence, dkv)
    z1 = swap(z_near, "fsdp", 1)
    (relay_z,) = advance(sequence, dkv, up, dn, extra=[(join_step, [z2], 1)])
    z3 = swap(relay_z, "fsdp", 1)

    qo_shards = shard_count(2 * part, seqs)
    qo_bits = [b for b in sbits if b < qo_shards]
    qo_rest = [b for b in sbits if b >= qo_shards]
    qo_order = shard_order(qo_bits)
    qok, qos = run(
        functools.partial(weight_kernel, qo_order),
        (shape((part, width), BF), shape((part, width), BF)),
        (n1a, n1b, own, z_near, z1, z2, z3, both_0, both_1, both_2, both_3),
        [pltpu.VMEM((2 * part, width), F32)],
        name="weight",
    )
    qo = Sum(qok, qos, qo_bits, qo_rest)
    height = 2 * HDIM + 32
    half = fsdp // 2
    mixed = shape((half, height, part), BF)
    grad_tokens, near_t, far_t = run(
        functools.partial(tail_kernel, rels),
        (shape((rows, width), BF), mixed, mixed),
        (x_own, dy_own, n1, z_near, wq, wkv, vec, cs, *mlp_parts, *dkv.pair(), sums),
        [pltpu.VMEM((fsdp, 2 * HDIM + 8, part), F32)],
        name="tail",
        time=2,
    )
    mix = Mix(near_t, far_t, fbits, sbits)
    advance(sequence, up, dn, mix, qo)
    advance(sequence, up, dn, mix, qo)
    advance(sequence, mix, qo)
    advance(sequence, up, dn, mix, qo)
    while up.left() + dn.left() + mix.left() + qo.left():
        advance(sequence, *[item for item in (mix, qo, up, dn) if item.left()])

    def matrix(pair, order, count):
        each = 2 * pair[0].shape[0] // len(order)
        return run(
            functools.partial(matrix_kernel, order),
            (shape((2 * pair[0].shape[0] // count, width), F32),) * count,
            pair,
            [
                pltpu.VMEM((len(order), each, width), F32),
                pltpu.SemaphoreType.DMA((len(order),)),
            ],
            limit=16,
            name="matrix",
            out_specs=(ANY,) * count,
        )

    vector = shape((part,), F32)
    g1, b1, qb, kb, vb, ob, g2, b2, ub, db, wk, wv = run(
        vector_kernel,
        (
            vector,
            vector,
            vector,
            shape(key_bias.shape, F32),
            shape(value_bias.shape, F32),
            vector,
            vector,
            vector,
            shape((hidden,), F32),
            vector,
            shape((HDIM, part), F32),
            shape((HDIM, part), F32),
        ),
        mix.pair(),
        limit=16,
        name="vector",
    )
    grad_query, grad_out = matrix(qo.pair(), qo_order, 2)
    (grad_up,) = matrix(up.pair(), seq_orders[0], 1)
    (grad_down,) = matrix(dn.pair(), seq_orders[1], 1)
    return (
        layer_out.reshape(1, rows, width),
        grad_tokens.reshape(1, rows, width),
        g1,
        b1,
        grad_query,
        qb,
        wk.T,
        kb,
        wv.T,
        vb,
        grad_out,
        ob,
        g2,
        b2,
        grad_up,
        ub,
        grad_down,
        db,
    )


def solution(mesh):
    split = P("fsdp")
    matrix = P("fsdp", None)
    stream = P("fsdp", "seq", None)
    return jax.shard_map(
        on_device,
        mesh=mesh,
        in_specs=(
            stream,
            P(),
            matrix,
            split,
            split,
            matrix,
            split,
            matrix,
            split,
            matrix,
            split,
            matrix,
            split,
            split,
            split,
            matrix,
            split,
            matrix,
            split,
            stream,
        ),
        out_specs=(
            stream,
            stream,
            split,
            split,
            matrix,
            split,
            matrix,
            split,
            matrix,
            split,
            matrix,
            split,
            split,
            split,
            matrix,
            split,
            matrix,
            split,
        ),
        check_vma=False,
    )
```

time: 295 us -> 164 us (0.56)
  waiting for transfers between devices: 163 us -> 66.7 us
  local copies, waits for them, and re-layouts: 22.2 us -> 5.31 us
  between operations: 14.4 us -> 1.21 us
  other arithmetic: 6.44 us -> 0.28 us
  starting transfers between devices: 46.8 us -> 52.3 us
    psum x1 -> x0, waiting for transfers between devices: 69.1 us -> none  [on_device(): gqo = lax.psum(gqo, 'seq').astype(F32)]
    ppermute x34 -> x45, waiting for transfers between devices: 92.8 us -> 66.7 us  [swap(): return lax.ppermute(value, axis, [(i, i ^ bit) for i in range(size)])]
    ppermute x34 -> x45, starting transfers between devices: 46.5 us -> 52.3 us  [swap(): return lax.ppermute(value, axis, [(i, i ^ bit) for i in range(size)])]
    slice x14 -> x0, local copies, waits for them, and re-layouts: 5.6 us -> none  [the longest x1 2.14 us: on_device(): gqo[part:]]
    unnamed x71 -> x30, local copies, waits for them, and re-layouts: 10.7 us -> 5.31 us
    another operation x8 -> x0, local copies, waits for them, and re-layouts: 4.62 us -> none  [on_device(): jnp.stack([norm_one_gain, norm_one_bias, norm_two_gain, norm_two_bias, qu...]
    add x13 -> x0, other arithmetic: 4.22 us -> none  [the longest x1 1.77 us: on_device(): value = near + swap(far, 'fsdp', bit)]
    pallas_call x8 -> x24, Pallas kernels: 39.6 us -> 38.6 us  [run(): pl.pallas_call(body, out_shape=outs, in_specs=list(specs.get('in_specs',...]
  transfers between devices with their start and end apart: 39 -> 45, of which waited for: 16 -> 24; matrix products, arithmetic and copies ran while one was open for 6% -> 0% of each run, Pallas kernels for 13% -> 21%
where the time goes in v2:
time: 164 us
  waiting for transfers between devices  66.7 us (41%)
  starting transfers between devices  52.3 us (32%)
  Pallas kernels  38.6 us (24%)
  local copies, waits for them, and re-layouts  5.31 us (3%)
    ppermute x45, waiting for transfers between devices, swap(): return lax.ppermute(value, axis, [(i, i ^ bit) for i in range(size)])  66.7 us
    ppermute x45, starting transfers between devices, swap(): return lax.ppermute(value, axis, [(i, i ^ bit) for i in range(size)])  52.3 us
    pallas_call x24, Pallas kernels, run(): pl.pallas_call(body, out_shape=outs, in_specs=list(specs.get('in_specs',...  38.6 us
    unnamed x30, local copies, waits for them, and re-layouts  5.31 us
  transfers between devices with their start and end apart: 45, of which 24 were waited for; matrix products, arithmetic and copies ran while one was open for 0% of the time, Pallas kernels for 21%

profile of v2, /device:TPU:0, one launch (start us, length us, event | category | flops | bytes accessed | tf_op | source)
XLA Modules:
  0.0 164.3 jit_solution(17849238892514615702)
XLA Ops:
  0.7 2.2 %pack.1 = (bf16[144,192]{1,0:T(8,128)(2,1)}, bf16[512,768]{1,0:T(8,128)(2,1)}) custom-call(bf16[256,768]{1,0:T(8,128)(2,1)} %bitcast.10, bf16[256,768]{1,0:T(8,128)(2,1)} %bitcast.14, bf16[192]{0:T(256)(128)(2,1)} %refs_2_.3, bf16[192]{0:T(256)(128)(2,1)} %refs_3_.3, bf16[192]{0:T(256)(128)(2,1)} %refs_4_.3, bf16[192]{0:T(256)(128)(2,1)} %refs_5_.1, ...), custom_call_target="tpu_custom_call" | custom-call | flops 2000000000 | bytes 1000 | tf_op jit(solution)/shard_map/pack/pallas_call | solution.py:62
  2.9 3.0 %collective-permute-start = (bf16[144,192]{1,0:T(8,128)(2,1)}, bf16[144,192]{1,0:T(8,128)(2,1)S(1)}, u32[]{:S(2)}, u32[]{:S(2)}) collective-permute-start(bf16[144,192]{1,0:T(8,128)(2,1)} %get-tuple-element.99.refs_1_.refs_6_), channel_id=1, source_target_pairs={{0,2},{1,3},{2,0},{3,1},{4,6},{5,7},{6,4},{7,5},{8,10},{9,11},{10,... | collective-permute-start | bytes 165896 | tf_op jit(solution)/shard_map/ppermute | solution.py:151
  6.9 2.1 %collective-permute-done.refs_2_ = bf16[144,192]{1,0:T(8,128)(2,1)S(1)} collective-permute-done((bf16[144,192]{1,0:T(8,128)(2,1)}, bf16[144,192]{1,0:T(8,128)(2,1)S(1)}, u32[]{:S(2)}, u32[]{:S(2)}) %collective-permute-start) | collective-permute-done | bytes 55328 | tf_op jit(solution)/shard_map/ppermute | solution.py:151
  8.9 1.3 collective-permute-done.2.refs_4_
  10.2 0.9 copy-done.10
  11.1 0.9 front.1
  12.0 2.7 %collective-permute-start.7 = (bf16[256,128]{1,0:T(8,128)(2,1)S(1)}, bf16[256,128]{1,0:T(8,128)(2,1)S(1)}, u32[]{:S(2)}, u32[]{:S(2)}) collective-permute-start(bf16[256,128]{1,0:T(8,128)(2,1)S(1)} %get-tuple-element.104.refs_0_), channel_id=1, source_target_pairs={{0,16},{4,20},{8,24},{12,28},{16,0},{20,4},{24,8},{28,12},{1,17},{... | collective-permute-start | bytes 196616 | tf_op jit(solution)/shard_map/ppermute | solution.py:151
  14.7 1.6 collective-permute-start.8
  16.5 4.9 %mlp_near.1 = (bf16[2,256,768]{2,1,0:T(8,128)(2,1)S(1)}, bf16[2,256,768]{2,1,0:T(8,128)(2,1)S(1)}, bf16[2,256,192]{2,1,0:T(8,128)(2,1)S(1)}, f32[768,768]{1,0:T(...) custom-call(bf16[512,768]{1,0:T(8,128)(2,1)S(1)} %copy-done.1, ...), custom_call_target="tpu_custom_call" | custom-call | flops 7000000000 | bytes 1000 | tf_op jit(solution)/shard_map/mlp_near/pallas_call | solution.py:62
  21.4 0.9 collective-permute-done.9.refs_3_
  22.3 3.8 %collective-permute-done.6.refs_4_.refs_0_.refs_9_ = bf16[512,768]{1,0:T(8,128)(2,1)S(1)} collective-permute-done((bf16[512,768]{1,0:T(8,128)(2,1)}, bf16[512,768]{1,0:T(8,128)(2,1)S(1)}, u32[]{:S(2)}, u32[]{:S(2)}) %collective-permute-start.6) | collective-permute-done | bytes 786464 | tf_op jit(solution)/shard_map/ppermute | solution.py:151
  26.9 1.5 collective-permute-start.12
  28.4 1.2 collective-permute-start.4
  29.6 5.9 %collective-permute-done.12.refs_12_.refs_5_ = bf16[1024,128]{1,0:T(8,128)(2,1)S(1)} collective-permute-done((bf16[1024,128]{1,0:T(8,128)(2,1)S(1)}, bf16[1024,128]{1,0:T(8,128)(2,1)S(1)}, u32[]{:S(2)}, u32[]{:S(2)}) %collective-permute-start.12) | collective-permute-done | bytes 262176 | tf_op jit(solution)/shard_map/ppermute | solution.py:151
  35.5 5.3 %mlp_far.1 = (bf16[2,256,768]{2,1,0:T(8,128)(2,1)S(1)}, bf16[2,256,768]{2,1,0:T(8,128)(2,1)S(1)}, bf16[2,256,192]{2,1,0:T(8,128)(2,1)S(1)}, bf16[384,768]{1,0:T(...) custom-call(bf16[512,768]{1,0:T(8,128)(2,1)S(1)} %collective-permute, ...), custom_call_target="tpu_custom_call" | custom-call | flops 8000000000 | bytes 1000 | tf_op jit(solution)/shard_map/mlp_far/pallas_call | solution.py:62
  40.9 2.8 %collective-permute-done.4.refs_0_.refs_5_ = bf16[384,768]{1,0:T(8,128)(2,1)S(1)} collective-permute-done((bf16[384,768]{1,0:T(8,128)(2,1)S(1)}, bf16[384,768]{1,0:T(8,128)(2,1)S(1)}, u32[]{:S(2)}, u32[]{:S(2)}) %collective-permute-start.4) | collective-permute-done | bytes 589856 | tf_op jit(solution)/shard_map/ppermute | solution.py:151
  44.5 1.6 collective-permute-start.17
  46.1 1.0 query.1
  47.4 1.3 collective-permute-start.15
  48.8 13.2 %attend.1 = (bf16[256,768]{1,0:T(8,128)(2,1)S(1)}, bf16[256,1152]{1,0:T(8,128)(2,1)S(1)}, bf16[256,960]{1,0:T(8,128)(2,1)S(1)}, bf16[1024,128]{1,0:T(8,128)(2,1)S(1)}, bf16[1024,128]{1,0:T(8,128)(2,1)S(1)}) custom-call(s32[16]{0:T(128)S(1)} %copy-done.12, s32[1,4]{1,0:T(1,128)S(1)} %copy-done.13, bf16[768,256]{1,0:T(8,128)(2,1)S(1)} %get-tuple-element.112.refs_2_, ...), custom_call_target="tpu_custom_call" | custom-call | flops 12999999488 | bytes 1000 | tf_op jit(solution)/shard_map/attend/pallas_call | solution.py:62
  62.0 3.0 %collective-permute-start.22 = (bf16[256,1152]{1,0:T(8,128)(2,1)S(1)}, bf16[256,1152]{1,0:T(8,128)(2,1)S(1)}, u32[]{:S(2)}, u32[]{:S(2)}) collective-permute-start(bf16[256,1152]{1,0:T(8,128)(2,1)S(1)} %get-tuple-element.134), channel_id=1, source_target_pairs={{0,2},{1,3},{2,0},{3,1},{4,6},{5,7},{6,4},{7,5},{8,10},{9,11},{10,... | collective-permute-start | bytes 1769480 | tf_op jit(solution)/shard_map/ppermute | solution.py:151
  65.3 3.5 %collective-permute-start.20 = (bf16[192,768]{1,0:T(8,128)(2,1)S(1)}, bf16[192,768]{1,0:T(8,128)(2,1)S(1)}, u32[]{:S(2)}, u32[]{:S(2)}) collective-permute-start(bf16[192,768]{1,0:T(8,128)(2,1)S(1)} %get-tuple-element.131), channel_id=1, source_target_pairs={{0,8},{4,12},{8,0},{12,4},{16,24},{20,28},{24,16},{28,20},{1,9},{5... | collective-permute-start | bytes 884744 | tf_op jit(solution)/shard_map/ppermute | solution.py:151
  68.8 1.3 collective-permute-start.21
  70.1 1.3 output.1.refs_2_
  71.4 0.7 collective-permute-done.18.refs_1_
  72.2 1.0 copy-done.5
  73.2 2.7 %collective-permute-start.19 = (bf16[512,128]{1,0:T(8,128)(2,1)S(1)}, bf16[512,128]{1,0:T(8,128)(2,1)S(1)}, u32[]{:S(2)}, u32[]{:S(2)}) collective-permute-start(bf16[512,128]{1,0:T(8,128)(2,1)S(1)} %get-tuple-element.130), channel_id=1, source_target_pairs={{0,8},{4,12},{8,0},{12,4},{16,24},{20,28},{24,16},{28,20},{1,9},{5... | collective-permute-start | bytes 393224 | tf_op jit(solution)/shard_map/ppermute | solution.py:151
  76.0 4.9 %collective-permute-done.20.refs_3_ = bf16[192,768]{1,0:T(8,128)(2,1)S(1)} collective-permute-done((bf16[192,768]{1,0:T(8,128)(2,1)S(1)}, bf16[192,768]{1,0:T(8,128)(2,1)S(1)}, u32[]{:S(2)}, u32[]{:S(2)}) %collective-permute-start.20) | collective-permute-done | bytes 294944 | tf_op jit(solution)/shard_map/ppermute | solution.py:151
  80.8 1.6 collective-permute-done.21.refs_5_
  82.4 2.8 %collective-permute-done.19.refs_1_ = bf16[512,128]{1,0:T(8,128)(2,1)S(1)} collective-permute-done((bf16[512,128]{1,0:T(8,128)(2,1)S(1)}, bf16[512,128]{1,0:T(8,128)(2,1)S(1)}, u32[]{:S(2)}, u32[]{:S(2)}) %collective-permute-start.19) | collective-permute-done | bytes 131104 | tf_op jit(solution)/shard_map/ppermute | solution.py:151
  85.4 0.7 collective-permute-start.25
  86.1 3.6 %collective-permute-start.23 = (bf16[256,128]{1,0:T(8,128)(2,1)S(1)}, bf16[256,128]{1,0:T(8,128)(2,1)S(1)}, u32[]{:S(2)}, u32[]{:S(2)}) collective-permute-start(bf16[256,128]{1,0:T(8,128)(2,1)S(1)} %get-tuple-element.136), channel_id=1, source_target_pairs={{0,16},{4,20},{8,24},{12,28},{16,0},{20,4},{24,8},{28,12},{1,17},{... | collective-permute-start | bytes 196616 | tf_op jit(solution)/shard_map/ppermute | solution.py:151
  89.7 1.6 collective-permute-start.27
  91.3 1.1 weight.1
  92.9 4.1 %collective-permute-done.23.refs_12_ = bf16[256,128]{1,0:T(8,128)(2,1)S(1)} collective-permute-done((bf16[256,128]{1,0:T(8,128)(2,1)S(1)}, bf16[256,128]{1,0:T(8,128)(2,1)S(1)}, u32[]{:S(2)}, u32[]{:S(2)}) %collective-permute-start.23) | collective-permute-done | bytes 65568 | tf_op jit(solution)/shard_map/ppermute | solution.py:151
  97.0 2.2 %tail.1 = (bf16[256,768]{1,0:T(8,128)(2,1)}, bf16[2,160,192]{2,1,0:T(8,128)(2,1)S(1)}, bf16[2,160,192]{2,1,0:T(8,128)(2,1)S(1)}) custom-call(bf16[256,768]{1,0:T(8,128)(2,1)S(1)} %bitcast.13, bf16[256,768]{1,0:T(8,128)(2,1)S(1)} %bitcast.16, bf16[256,768]{1,0:T(8,128)(2,1)S(1)} %get-tuple-element.100.refs_0_.refs_2_, ...), custom_call_target="tpu_custom_call" | custom-call | flops 2000000000 | bytes 1000 | tf_op jit(solution)/shard_map/tail/pallas_call | solution.py:62
  99.8 0.9 collective-permute-done.28.refs_5_
  100.7 1.0 collective-permute-done.29.refs_7_
  101.8 2.7 %collective-permute-start.30 = (bf16[96,768]{1,0:T(8,128)(2,1)S(1)}, bf16[96,768]{1,0:T(8,128)(2,1)S(1)}, u32[]{:S(2)}, u32[]{:S(2)}) collective-permute-start(bf16[96,768]{1,0:T(8,128)(2,1)S(1)} %get-tuple-element.149.refs_0_), channel_id=1, source_target_pairs={{0,16},{4,20},{8,24},{12,28},{16,0},{20,4},{24,8},{28,12},{1,17},{... | collective-permute-start | bytes 442376 | tf_op jit(solution)/shard_map/ppermute | solution.py:151
  104.5 0.7 collective-permute-start.31
  105.2 1.3 collective-permute-start.33
  106.7 4.2 %collective-permute-done.32.refs_5_ = bf16[1,160,192]{2,1,0:T(8,128)(2,1)S(1)} collective-permute-done((bf16[1,160,192]{2,1,0:T(8,128)(2,1)S(1)}, bf16[1,160,192]{2,1,0:T(8,128)(2,1)S(1)}, u32[]{:S(2)}, u32[]{:S(2)}) %collective-permute-start.32) | collective-permute-done | bytes 61472 | tf_op jit(solution)/shard_map/ppermute | solution.py:151
  110.9 1.4 collective-permute-done.33.refs_7_
  112.5 1.7 %collective-permute-start.35 = (bf16[192,768]{1,0:T(8,128)(2,1)S(1)}, bf16[192,768]{1,0:T(8,128)(2,1)S(1)}, u32[]{:S(2)}, u32[]{:S(2)}) collective-permute-start(bf16[192,768]{1,0:T(8,128)(2,1)S(1)} %get-tuple-element.156.refs_2_), channel_id=1, source_target_pairs={{0,16},{4,20},{8,24},{12,28},{16,0},{20,4},{24,8},{28,12},{1,17},{... | collective-permute-start | bytes 884744 | tf_op jit(solution)/shard_map/ppermute | solution.py:151
  114.2 1.3 collective-permute-start.37
  115.5 0.9 collective-permute-start.36
  116.4 3.6 %collective-permute-done.36.refs_1_ = bf16[1,160,192]{2,1,0:T(8,128)(2,1)S(1)} collective-permute-done((bf16[1,160,192]{2,1,0:T(8,128)(2,1)S(1)}, bf16[1,160,192]{2,1,0:T(8,128)(2,1)S(1)}, u32[]{:S(2)}, u32[]{:S(2)}) %collective-permute-start.36) | collective-permute-done | bytes 61472 | tf_op jit(solution)/shard_map/ppermute | solution.py:151
  119.9 11.1 %collective-permute-done.37.refs_3_ = bf16[48,768]{1,0:T(8,128)(2,1)S(1)} collective-permute-done((bf16[48,768]{1,0:T(8,128)(2,1)S(1)}, bf16[48,768]{1,0:T(8,128)(2,1)S(1)}, u32[]{:S(2)}, u32[]{:S(2)}) %collective-permute-start.37) | collective-permute-done | bytes 73760 | tf_op jit(solution)/shard_map/ppermute | solution.py:151
  131.1 2.1 %collective-permute-start.38 = (bf16[1,160,192]{2,1,0:T(8,128)(2,1)S(1)}, bf16[1,160,192]{2,1,0:T(8,128)(2,1)S(1)}, u32[]{:S(2)}, u32[]{:S(2)}) collective-permute-start(bf16[1,160,192]{2,1,0:T(8,128)(2,1)S(1)} %get-tuple-element.160.refs_4_.refs_8_), channel_id=1, source_target_pairs={{0,8},{4,12},{8,0},{12,4},{16,24},{20,28},{24,16},{28,20},{1,9},{5... | collective-permute-start | bytes 184328 | tf_op jit(solution)/shard_map/ppermute | solution.py:151
  133.3 2.4 %collective-permute-done.38.refs_5_ = bf16[1,160,192]{2,1,0:T(8,128)(2,1)S(1)} collective-permute-done((bf16[1,160,192]{2,1,0:T(8,128)(2,1)S(1)}, bf16[1,160,192]{2,1,0:T(8,128)(2,1)S(1)}, u32[]{:S(2)}, u32[]{:S(2)}) %collective-permute-start.38) | collective-permute-done | bytes 61472 | tf_op jit(solution)/shard_map/ppermute | solution.py:151
  135.7 0.8 collective-permute-done.39.refs_7_
  136.6 1.3 collective-permute-start.41
  137.9 2.8 %collective-permute-start.43 = (bf16[384,768]{1,0:T(8,128)(2,1)S(1)}, bf16[384,768]{1,0:T(8,128)(2,1)S(1)}, u32[]{:S(2)}, u32[]{:S(2)}) collective-permute-start(bf16[384,768]{1,0:T(8,128)(2,1)S(1)} %get-tuple-element.176.refs_0_), channel_id=1, source_target_pairs={{0,4},{4,0},{8,12},{12,8},{16,20},{20,16},{24,28},{28,24},{1,5},{5... | collective-permute-start | bytes 1769480 | tf_op jit(solution)/shard_map/ppermute | solution.py:151
  140.7 0.8 collective-permute-start.44
  141.5 2.0 %collective-permute-done.41.refs_1_ = bf16[96,768]{1,0:T(8,128)(2,1)S(1)} collective-permute-done((bf16[96,768]{1,0:T(8,128)(2,1)S(1)}, bf16[96,768]{1,0:T(8,128)(2,1)S(1)}, u32[]{:S(2)}, u32[]{:S(2)}) %collective-permute-start.41) | collective-permute-done | bytes 147488 | tf_op jit(solution)/shard_map/ppermute | solution.py:151
  143.5 3.7 %collective-permute-start.42 = (bf16[192,768]{1,0:T(8,128)(2,1)S(1)}, bf16[192,768]{1,0:T(8,128)(2,1)S(1)}, u32[]{:S(2)}, u32[]{:S(2)}) collective-permute-start(bf16[192,768]{1,0:T(8,128)(2,1)S(1)} %stage.21.refs_2_.refs_0_), channel_id=1, source_target_pairs={{0,4},{4,0},{8,12},{12,8},{16,20},{20,16},{24,28},{28,24},{1,5},{5... | collective-permute-start | bytes 884744 | tf_op jit(solution)/shard_map/ppermute | solution.py:151
  147.7 5.4 %collective-permute-done.40.refs_1_ = bf16[1,160,192]{2,1,0:T(8,128)(2,1)S(1)} collective-permute-done((bf16[1,160,192]{2,1,0:T(8,128)(2,1)S(1)}, bf16[1,160,192]{2,1,0:T(8,128)(2,1)S(1)}, u32[]{:S(2)}, u32[]{:S(2)}) %collective-permute-start.40) | collective-permute-done | bytes 61472 | tf_op jit(solution)/shard_map/ppermute | solution.py:151
  153.1 0.9 vector.1
  154.0 2.7 %collective-permute-done.42.refs_1_ = bf16[192,768]{1,0:T(8,128)(2,1)S(1)} collective-permute-done((bf16[192,768]{1,0:T(8,128)(2,1)S(1)}, bf16[192,768]{1,0:T(8,128)(2,1)S(1)}, u32[]{:S(2)}, u32[]{:S(2)}) %collective-permute-start.42) | collective-permute-done | bytes 294944 | tf_op jit(solution)/shard_map/ppermute | solution.py:151
  157.3 1.1 matrix.3
  158.4 1.1 copy-done.2
  159.5 1.5 matrix.4.refs_2_
  161.0 1.7 %copy-done = f32[768,768]{1,0:T(8,128)S(1)} copy-done((f32[768,768]{1,0:T(8,128)S(1)}, f32[768,768]{1,0:T(8,128)}, u32[]{:S(2)}) %copy-start) | copy-done | bytes 2359320
  162.7 1.5 matrix.5
  (85 shorter events, 6.8 us)
Async XLA Ops:
  0.7 5.9 %copy-start.12 = (s32[16]{0:T(128)S(1)}, s32[16]{0:T(128)}, u32[]{:S(2)}) copy-start(s32[16]{0:T(128)} %refs_0_.1) | copy-start | bytes 196
  0.7 9.5 %copy-start.3 = (bf16[1,256,768]{2,1,0:T(8,128)(2,1)S(1)}, bf16[1,256,768]{2,1,0:T(8,128)(2,1)}, u32[]{:S(2)}) copy-start(bf16[1,256,768]{2,1,0:T(8,128)(2,1)} %param.20) | copy-start | bytes 1179652
  0.7 15.8 %copy-start.11 = (bf16[768]{0:T(1024)(128)(2,1)S(1)}, bf16[768]{0:T(1024)(128)(2,1)}, u32[]{:S(2)}) copy-start(bf16[768]{0:T(1024)(128)(2,1)} %refs_4_.5) | copy-start | bytes 4612
  2.9 13.6 %copy-start.1 = (bf16[512,768]{1,0:T(8,128)(2,1)S(1)}, bf16[512,768]{1,0:T(8,128)(2,1)}, u32[]{:S(2)}) copy-start(bf16[512,768]{1,0:T(8,128)(2,1)} %get-tuple-element.102.refs_0_.refs_7_) | copy-start | bytes 2359300
  2.9 13.5 %copy-start.8 = (bf16[192,768]{1,0:T(8,128)(2,1)S(1)}, bf16[192,768]{1,0:T(8,128)(2,1)}, u32[]{:S(2)}) copy-start(bf16[192,768]{1,0:T(8,128)(2,1)} %refs_6_.3) | copy-start | bytes 884740
  2.9 13.5 %copy-start.9 = (bf16[192,768]{1,0:T(8,128)(2,1)S(1)}, bf16[192,768]{1,0:T(8,128)(2,1)}, u32[]{:S(2)}) copy-start(bf16[192,768]{1,0:T(8,128)(2,1)} %refs_7_.3) | copy-start | bytes 884740
  2.9 6.0 %collective-permute-start = (bf16[144,192]{1,0:T(8,128)(2,1)}, bf16[144,192]{1,0:T(8,128)(2,1)S(1)}, u32[]{:S(2)}, u32[]{:S(2)}) collective-permute-start(bf16[144,192]{1,0:T(8,128)(2,1)} %get-tuple-element.99.refs_1_.refs_6_), channel_id=1, source_target_pairs={{0,2},{1,3},{2,0},{3,1},{4,6},{5,7},{6,4},{7,5},{8,10},{9,11},{10,... | collective-permute-start | bytes 165896 | tf_op jit(solution)/shard_map/ppermute | solution.py:151
  6.0 3.0 %collective-permute-start.1 = (bf16[144,192]{1,0:T(8,128)(2,1)}, bf16[144,192]{1,0:T(8,128)(2,1)S(1)}, u32[]{:S(2)}, u32[]{:S(2)}) collective-permute-start(bf16[144,192]{1,0:T(8,128)(2,1)} %get-tuple-element.99.refs_1_.refs_6_), channel_id=1, source_target_pairs={{0,1},{1,0},{2,3},{3,2},{4,5},{5,4},{6,7},{7,6},{8,9},{9,8},{10,11... | collective-permute-start | bytes 165896 | tf_op jit(solution)/shard_map/ppermute | solution.py:151
  6.0 10.5 %collective-permute-start.3 = (bf16[512,768]{1,0:T(8,128)(2,1)}, bf16[512,768]{1,0:T(8,128)(2,1)S(1)}, u32[]{:S(2)}, u32[]{:S(2)}) collective-permute-start(bf16[512,768]{1,0:T(8,128)(2,1)} %get-tuple-element.102.refs_0_.refs_7_), channel_id=1, source_target_pairs={{0,1},{1,0},{2,3},{3,2},{4,5},{5,4},{6,7},{7,6},{8,9},{9,8},{10,11... | collective-permute-start | bytes 2359304 | tf_op jit(solution)/shard_map/ppermute | solution.py:151
  6.5 19.7 %collective-permute-start.6 = (bf16[512,768]{1,0:T(8,128)(2,1)}, bf16[512,768]{1,0:T(8,128)(2,1)S(1)}, u32[]{:S(2)}, u32[]{:S(2)}) collective-permute-start(bf16[512,768]{1,0:T(8,128)(2,1)} %get-tuple-element.102.refs_0_.refs_7_), channel_id=1, source_target_pairs={{0,2},{1,3},{2,0},{3,1},{4,6},{5,7},{6,4},{7,5},{8,10},{9,11},{10,... | collective-permute-start | bytes 2359304 | tf_op jit(solution)/shard_map/ppermute | solution.py:151
  6.6 9.9 %copy-start.6 = (bf16[768,768]{1,0:T(8,128)(2,1)S(1)}, bf16[768,768]{1,0:T(8,128)(2,1)}, u32[]{:S(2)}) copy-start(bf16[768,768]{1,0:T(8,128)(2,1)} %refs_2_.5) | copy-start | bytes 3538948
  6.6 9.9 %copy-start.7 = (bf16[768,768]{1,0:T(8,128)(2,1)S(1)}, bf16[768,768]{1,0:T(8,128)(2,1)}, u32[]{:S(2)}) copy-start(bf16[768,768]{1,0:T(8,128)(2,1)} %refs_3_.5) | copy-start | bytes 3538948
  8.9 1.3 collective-permute-start.2
  10.2 0.9 copy-start.10
  12.0 9.4 %collective-permute-start.7 = (bf16[256,128]{1,0:T(8,128)(2,1)S(1)}, bf16[256,128]{1,0:T(8,128)(2,1)S(1)}, u32[]{:S(2)}, u32[]{:S(2)}) collective-permute-start(bf16[256,128]{1,0:T(8,128)(2,1)S(1)} %get-tuple-element.104.refs_0_), channel_id=1, source_target_pairs={{0,16},{4,20},{8,24},{12,28},{16,0},{20,4},{24,8},{28,12},{1,17},{... | collective-permute-start | bytes 196616 | tf_op jit(solution)/shard_map/ppermute | solution.py:151
  14.7 6.7 %collective-permute-start.8 = (bf16[256,128]{1,0:T(8,128)(2,1)S(1)}, bf16[256,128]{1,0:T(8,128)(2,1)S(1)}, u32[]{:S(2)}, u32[]{:S(2)}) collective-permute-start(bf16[256,128]{1,0:T(8,128)(2,1)S(1)} %get-tuple-element.104.refs_0_), channel_id=1, source_target_pairs={{0,8},{4,12},{8,0},{12,4},{16,24},{20,28},{24,16},{28,20},{1,9},{5... | collective-permute-start | bytes 196616 | tf_op jit(solution)/shard_map/ppermute | solution.py:151
  16.3 6.1 %collective-permute-start.9 = (bf16[256,128]{1,0:T(8,128)(2,1)S(1)}, bf16[256,128]{1,0:T(8,128)(2,1)S(1)}, u32[]{:S(2)}, u32[]{:S(2)}) collective-permute-start(bf16[256,128]{1,0:T(8,128)(2,1)S(1)} %get-tuple-element.104.refs_0_), channel_id=1, source_target_pairs={{0,24},{4,28},{8,16},{12,20},{16,8},{20,12},{24,0},{28,4},{1,25},{... | collective-permute-start | bytes 196616 | tf_op jit(solution)/shard_map/ppermute | solution.py:151
  26.2 9.3 %collective-permute-start.10 = (bf16[512,768]{1,0:T(8,128)(2,1)S(1)}, bf16[512,768]{1,0:T(8,128)(2,1)S(1)}, u32[]{:S(2)}, u32[]{:S(2)}) collective-permute-start(bf16[512,768]{1,0:T(8,128)(2,1)S(1)} %get-tuple-element.106), channel_id=1, source_target_pairs={{0,1},{1,0},{2,3},{3,2},{4,5},{5,4},{6,7},{7,6},{8,9},{9,8},{10,11... | collective-permute-start | bytes 2359304 | tf_op jit(solution)/shard_map/ppermute | solution.py:151
  26.3 9.2 %collective-permute-start.11 = (bf16[2,256,768]{2,1,0:T(8,128)(2,1)S(1)}, bf16[2,256,768]{2,1,0:T(8,128)(2,1)S(1)}, u32[]{:S(2)}, u32[]{:S(2)}) collective-permute-start(bf16[2,256,768]{2,1,0:T(8,128)(2,1)S(1)} %get-tuple-element.110), channel_id=1, source_target_pairs={{0,1},{1,0},{2,3},{3,2},{4,5},{5,4},{6,7},{7,6},{8,9},{9,8},{10,11... | collective-permute-start | bytes 2359304 | tf_op jit(solution)/shard_map/ppermute | solution.py:151
  26.8 8.7 %collective-permute-start.5 = (bf16[384,768]{1,0:T(8,128)(2,1)S(1)}, bf16[384,768]{1,0:T(8,128)(2,1)S(1)}, u32[]{:S(2)}, u32[]{:S(2)}) collective-permute-start(bf16[384,768]{1,0:T(8,128)(2,1)S(1)} %get-tuple-element.103.refs_4_), channel_id=1, source_target_pairs={{0,1},{1,0},{2,3},{3,2},{4,5},{5,4},{6,7},{7,6},{8,9},{9,8},{10,11... | collective-permute-start | bytes 1769480 | tf_op jit(solution)/shard_map/ppermute | solution.py:151
  26.9 8.7 %collective-permute-start.12 = (bf16[1024,128]{1,0:T(8,128)(2,1)S(1)}, bf16[1024,128]{1,0:T(8,128)(2,1)S(1)}, u32[]{:S(2)}, u32[]{:S(2)}) collective-permute-start(bf16[1024,128]{1,0:T(8,128)(2,1)S(1)} %get-tuple-element.109.refs_9_.refs_4_), channel_id=1, source_target_pairs={{0,4},{4,0},{8,12},{12,8},{16,20},{20,16},{24,28},{28,24},{1,5},{5... | collective-permute-start | bytes 786440 | tf_op jit(solution)/shard_map/ppermute | solution.py:151
  28.4 15.4 %collective-permute-start.4 = (bf16[384,768]{1,0:T(8,128)(2,1)S(1)}, bf16[384,768]{1,0:T(8,128)(2,1)S(1)}, u32[]{:S(2)}, u32[]{:S(2)}) collective-permute-start(bf16[384,768]{1,0:T(8,128)(2,1)S(1)} %get-tuple-element.103.refs_4_), channel_id=1, source_target_pairs={{0,2},{1,3},{2,0},{3,1},{4,6},{5,7},{6,4},{7,5},{8,10},{9,11},{10,... | collective-permute-start | bytes 1769480 | tf_op jit(solution)/shard_map/ppermute | solution.py:151
  40.8 5.2 %copy-start.4 = (bf16[1,256,768]{2,1,0:T(8,128)(2,1)S(1)}, bf16[1,256,768]{2,1,0:T(8,128)(2,1)}, u32[]{:S(2)}) copy-start(bf16[1,256,768]{2,1,0:T(8,128)(2,1)} %param.39) | copy-start | bytes 1179652
  40.9 6.2 %collective-permute-start.14 = (bf16[2,256,768]{2,1,0:T(8,128)(2,1)S(1)}, bf16[2,256,768]{2,1,0:T(8,128)(2,1)S(1)}, u32[]{:S(2)}, u32[]{:S(2)}) collective-permute-start(bf16[2,256,768]{2,1,0:T(8,128)(2,1)S(1)} %get-tuple-element.115), channel_id=1, source_target_pairs={{0,1},{1,0},{2,3},{3,2},{4,5},{5,4},{6,7},{7,6},{8,9},{9,8},{10,11... | collective-permute-start | bytes 2359304 | tf_op jit(solution)/shard_map/ppermute | solution.py:151
  43.8 2.3 %collective-permute-start.13 = (bf16[384,768]{1,0:T(8,128)(2,1)S(1)}, bf16[384,768]{1,0:T(8,128)(2,1)S(1)}, u32[]{:S(2)}, u32[]{:S(2)}) collective-permute-start(bf16[384,768]{1,0:T(8,128)(2,1)S(1)} %stage.12.refs_8_), channel_id=1, source_target_pairs={{0,1},{1,0},{2,3},{3,2},{4,5},{5,4},{6,7},{7,6},{8,9},{9,8},{10,11... | collective-permute-start | bytes 1769480 | tf_op jit(solution)/shard_map/ppermute | solution.py:151
  43.9 21.1 %collective-permute-start.16 = (bf16[384,768]{1,0:T(8,128)(2,1)S(1)}, bf16[384,768]{1,0:T(8,128)(2,1)S(1)}, u32[]{:S(2)}, u32[]{:S(2)}) collective-permute-start(bf16[384,768]{1,0:T(8,128)(2,1)S(1)} %get-tuple-element.120), channel_id=1, source_target_pairs={{0,4},{4,0},{8,12},{12,8},{16,20},{20,16},{24,28},{28,24},{1,5},{5... | collective-permute-start | bytes 1769480 | tf_op jit(solution)/shard_map/ppermute | solution.py:151
  44.5 20.5 %collective-permute-start.17 = (bf16[384,768]{1,0:T(8,128)(2,1)S(1)}, bf16[384,768]{1,0:T(8,128)(2,1)S(1)}, u32[]{:S(2)}, u32[]{:S(2)}) collective-permute-start(bf16[384,768]{1,0:T(8,128)(2,1)S(1)} %get-tuple-element.122), channel_id=1, source_target_pairs={{0,8},{4,12},{8,0},{12,4},{16,24},{20,28},{24,16},{28,20},{1,9},{5... | collective-permute-start | bytes 1769480 | tf_op jit(solution)/shard_map/ppermute | solution.py:151
  47.0 1.7 %copy-start.13 = (s32[1,4]{1,0:T(1,128)S(1)}, s32[1,4]{1,0:T(1,128)}, u32[]{:S(2)}) copy-start(s32[1,4]{1,0:T(1,128)} %refs_1_.1) | copy-start | bytes 52
  47.4 22.7 %collective-permute-start.15 = (bf16[2,256,768]{2,1,0:T(8,128)(2,1)S(1)}, bf16[2,256,768]{2,1,0:T(8,128)(2,1)S(1)}, u32[]{:S(2)}, u32[]{:S(2)}) collective-permute-start(bf16[2,256,768]{2,1,0:T(8,128)(2,1)S(1)} %stage.13.refs_7_), channel_id=1, source_target_pairs={{0,2},{1,3},{2,0},{3,1},{4,6},{5,7},{6,4},{7,5},{8,10},{9,11},{10,... | collective-permute-start | bytes 2359304 | tf_op jit(solution)/shard_map/ppermute | solution.py:151
  62.0 20.4 %collective-permute-start.22 = (bf16[256,1152]{1,0:T(8,128)(2,1)S(1)}, bf16[256,1152]{1,0:T(8,128)(2,1)S(1)}, u32[]{:S(2)}, u32[]{:S(2)}) collective-permute-start(bf16[256,1152]{1,0:T(8,128)(2,1)S(1)} %get-tuple-element.134), channel_id=1, source_target_pairs={{0,2},{1,3},{2,0},{3,1},{4,6},{5,7},{6,4},{7,5},{8,10},{9,11},{10,... | collective-permute-start | bytes 1769480 | tf_op jit(solution)/shard_map/ppermute | solution.py:151
  65.0 7.2 %collective-permute-start.18 = (bf16[1024,128]{1,0:T(8,128)(2,1)S(1)}, bf16[1024,128]{1,0:T(8,128)(2,1)S(1)}, u32[]{:S(2)}, u32[]{:S(2)}) collective-permute-start(bf16[1024,128]{1,0:T(8,128)(2,1)S(1)} %get-tuple-element.128), channel_id=1, source_target_pairs={{0,4},{4,0},{8,12},{12,8},{16,20},{20,16},{24,28},{28,24},{1,5},{5... | collective-permute-start | bytes 786440 | tf_op jit(solution)/shard_map/ppermute | solution.py:151
  65.3 15.6 %collective-permute-start.20 = (bf16[192,768]{1,0:T(8,128)(2,1)S(1)}, bf16[192,768]{1,0:T(8,128)(2,1)S(1)}, u32[]{:S(2)}, u32[]{:S(2)}) collective-permute-start(bf16[192,768]{1,0:T(8,128)(2,1)S(1)} %get-tuple-element.131), channel_id=1, source_target_pairs={{0,8},{4,12},{8,0},{12,4},{16,24},{20,28},{24,16},{28,20},{1,9},{5... | collective-permute-start | bytes 884744 | tf_op jit(solution)/shard_map/ppermute | solution.py:151
  68.8 13.6 %collective-permute-start.21 = (bf16[192,768]{1,0:T(8,128)(2,1)S(1)}, bf16[192,768]{1,0:T(8,128)(2,1)S(1)}, u32[]{:S(2)}, u32[]{:S(2)}) collective-permute-start(bf16[192,768]{1,0:T(8,128)(2,1)S(1)} %get-tuple-element.133), channel_id=1, source_target_pairs={{0,16},{4,20},{8,24},{12,28},{16,0},{20,4},{24,8},{28,12},{1,17},{... | collective-permute-start | bytes 884744 | tf_op jit(solution)/shard_map/ppermute | solution.py:151
  72.2 1.0 copy-start.5
  73.2 12.0 %collective-permute-start.19 = (bf16[512,128]{1,0:T(8,128)(2,1)S(1)}, bf16[512,128]{1,0:T(8,128)(2,1)S(1)}, u32[]{:S(2)}, u32[]{:S(2)}) collective-permute-start(bf16[512,128]{1,0:T(8,128)(2,1)S(1)} %get-tuple-element.130), channel_id=1, source_target_pairs={{0,8},{4,12},{8,0},{12,4},{16,24},{20,28},{24,16},{28,20},{1,9},{5... | collective-permute-start | bytes 393224 | tf_op jit(solution)/shard_map/ppermute | solution.py:151
  85.4 5.9 %collective-permute-start.25 = (bf16[256,1152]{1,0:T(8,128)(2,1)S(1)}, bf16[256,1152]{1,0:T(8,128)(2,1)S(1)}, u32[]{:S(2)}, u32[]{:S(2)}) collective-permute-start(bf16[256,1152]{1,0:T(8,128)(2,1)S(1)} %get-tuple-element.139), channel_id=1, source_target_pairs={{0,1},{1,0},{2,3},{3,2},{4,5},{5,4},{6,7},{7,6},{8,9},{9,8},{10,11... | collective-permute-start | bytes 1769480 | tf_op jit(solution)/shard_map/ppermute | solution.py:151
  86.1 5.2 %collective-permute-start.24 = (bf16[256,960]{1,0:T(8,128)(2,1)S(1)}, bf16[256,960]{1,0:T(8,128)(2,1)S(1)}, u32[]{:S(2)}, u32[]{:S(2)}) collective-permute-start(bf16[256,960]{1,0:T(8,128)(2,1)S(1)} %get-tuple-element.125.refs_3_), channel_id=1, source_target_pairs={{0,1},{1,0},{2,3},{3,2},{4,5},{5,4},{6,7},{7,6},{8,9},{9,8},{10,11... | collective-permute-start | bytes 1474568 | tf_op jit(solution)/shard_map/ppermute | solution.py:151
  86.1 10.9 %collective-permute-start.23 = (bf16[256,128]{1,0:T(8,128)(2,1)S(1)}, bf16[256,128]{1,0:T(8,128)(2,1)S(1)}, u32[]{:S(2)}, u32[]{:S(2)}) collective-permute-start(bf16[256,128]{1,0:T(8,128)(2,1)S(1)} %get-tuple-element.136), channel_id=1, source_target_pairs={{0,16},{4,20},{8,24},{12,28},{16,0},{20,4},{24,8},{28,12},{1,17},{... | collective-permute-start | bytes 196616 | tf_op jit(solution)/shard_map/ppermute | solution.py:151
  89.7 10.1 %collective-permute-start.26 = (bf16[96,768]{1,0:T(8,128)(2,1)S(1)}, bf16[96,768]{1,0:T(8,128)(2,1)S(1)}, u32[]{:S(2)}, u32[]{:S(2)}) collective-permute-start(bf16[96,768]{1,0:T(8,128)(2,1)S(1)} %get-tuple-element.143), channel_id=1, source_target_pairs={{0,16},{4,20},{8,24},{12,28},{16,0},{20,4},{24,8},{28,12},{1,17},{... | collective-permute-start | bytes 442376 | tf_op jit(solution)/shard_map/ppermute | solution.py:151
  89.7 10.1 %collective-permute-start.27 = (bf16[96,768]{1,0:T(8,128)(2,1)S(1)}, bf16[96,768]{1,0:T(8,128)(2,1)S(1)}, u32[]{:S(2)}, u32[]{:S(2)}) collective-permute-start(bf16[96,768]{1,0:T(8,128)(2,1)S(1)} %get-tuple-element.145), channel_id=1, source_target_pairs={{0,4},{4,0},{8,12},{12,8},{16,20},{20,16},{24,28},{28,24},{1,5},{5... | collective-permute-start | bytes 442376 | tf_op jit(solution)/shard_map/ppermute | solution.py:151
  92.4 9.2 %collective-permute-start.29 = (bf16[192,768]{1,0:T(8,128)(2,1)S(1)}, bf16[192,768]{1,0:T(8,128)(2,1)S(1)}, u32[]{:S(2)}, u32[]{:S(2)}) collective-permute-start(bf16[192,768]{1,0:T(8,128)(2,1)S(1)} %get-tuple-element.148), channel_id=1, source_target_pairs={{0,4},{4,0},{8,12},{12,8},{16,20},{20,16},{24,28},{28,24},{1,5},{5... | collective-permute-start | bytes 884744 | tf_op jit(solution)/shard_map/ppermute | solution.py:151
  99.3 1.4 collective-permute-start.28
  101.8 9.1 %collective-permute-start.30 = (bf16[96,768]{1,0:T(8,128)(2,1)S(1)}, bf16[96,768]{1,0:T(8,128)(2,1)S(1)}, u32[]{:S(2)}, u32[]{:S(2)}) collective-permute-start(bf16[96,768]{1,0:T(8,128)(2,1)S(1)} %get-tuple-element.149.refs_0_), channel_id=1, source_target_pairs={{0,16},{4,20},{8,24},{12,28},{16,0},{20,4},{24,8},{28,12},{1,17},{... | collective-permute-start | bytes 442376 | tf_op jit(solution)/shard_map/ppermute | solution.py:151
  104.5 6.5 %collective-permute-start.31 = (bf16[96,768]{1,0:T(8,128)(2,1)S(1)}, bf16[96,768]{1,0:T(8,128)(2,1)S(1)}, u32[]{:S(2)}, u32[]{:S(2)}) collective-permute-start(bf16[96,768]{1,0:T(8,128)(2,1)S(1)} %get-tuple-element.150.refs_2_), channel_id=1, source_target_pairs={{0,4},{4,0},{8,12},{12,8},{16,20},{20,16},{24,28},{28,24},{1,5},{5... | collective-permute-start | bytes 442376 | tf_op jit(solution)/shard_map/ppermute | solution.py:151
  105.2 7.2 %collective-permute-start.33 = (bf16[96,768]{1,0:T(8,128)(2,1)S(1)}, bf16[96,768]{1,0:T(8,128)(2,1)S(1)}, u32[]{:S(2)}, u32[]{:S(2)}) collective-permute-start(bf16[96,768]{1,0:T(8,128)(2,1)S(1)} %get-tuple-element.154), channel_id=1, source_target_pairs={{0,8},{4,12},{8,0},{12,4},{16,24},{20,28},{24,16},{28,20},{1,9},{5... | collective-permute-start | bytes 442376 | tf_op jit(solution)/shard_map/ppermute | solution.py:151
  106.4 4.4 %collective-permute-start.32 = (bf16[1,160,192]{2,1,0:T(8,128)(2,1)S(1)}, bf16[1,160,192]{2,1,0:T(8,128)(2,1)S(1)}, u32[]{:S(2)}, u32[]{:S(2)}) collective-permute-start(bf16[1,160,192]{2,1,0:T(8,128)(2,1)S(1)} %get-tuple-element.152), channel_id=1, source_target_pairs={{0,2},{1,3},{2,0},{3,1},{4,6},{5,7},{6,4},{7,5},{8,10},{9,11},{10,... | collective-permute-start | bytes 184328 | tf_op jit(solution)/shard_map/ppermute | solution.py:151
  112.4 24.0 %collective-permute-start.34 = (bf16[192,768]{1,0:T(8,128)(2,1)S(1)}, bf16[192,768]{1,0:T(8,128)(2,1)S(1)}, u32[]{:S(2)}, u32[]{:S(2)}) collective-permute-start(bf16[192,768]{1,0:T(8,128)(2,1)S(1)} %get-tuple-element.155.refs_0_), channel_id=1, source_target_pairs={{0,8},{4,12},{8,0},{12,4},{16,24},{20,28},{24,16},{28,20},{1,9},{5... | collective-permute-start | bytes 884744 | tf_op jit(solution)/shard_map/ppermute | solution.py:151
  112.5 24.0 %collective-permute-start.35 = (bf16[192,768]{1,0:T(8,128)(2,1)S(1)}, bf16[192,768]{1,0:T(8,128)(2,1)S(1)}, u32[]{:S(2)}, u32[]{:S(2)}) collective-permute-start(bf16[192,768]{1,0:T(8,128)(2,1)S(1)} %get-tuple-element.156.refs_2_), channel_id=1, source_target_pairs={{0,16},{4,20},{8,24},{12,28},{16,0},{20,4},{24,8},{28,12},{1,17},{... | collective-permute-start | bytes 884744 | tf_op jit(solution)/shard_map/ppermute | solution.py:151
  114.2 16.8 %collective-permute-start.37 = (bf16[48,768]{1,0:T(8,128)(2,1)S(1)}, bf16[48,768]{1,0:T(8,128)(2,1)S(1)}, u32[]{:S(2)}, u32[]{:S(2)}) collective-permute-start(bf16[48,768]{1,0:T(8,128)(2,1)S(1)} %get-tuple-element.159), channel_id=1, source_target_pairs={{0,16},{4,20},{8,24},{12,28},{16,0},{20,4},{24,8},{28,12},{1,17},{... | collective-permute-start | bytes 221192 | tf_op jit(solution)/shard_map/ppermute | solution.py:151
  115.5 4.4 %collective-permute-start.36 = (bf16[1,160,192]{2,1,0:T(8,128)(2,1)S(1)}, bf16[1,160,192]{2,1,0:T(8,128)(2,1)S(1)}, u32[]{:S(2)}, u32[]{:S(2)}) collective-permute-start(bf16[1,160,192]{2,1,0:T(8,128)(2,1)S(1)} %get-tuple-element.157.refs_0_.refs_4_), channel_id=1, source_target_pairs={{0,4},{4,0},{8,12},{12,8},{16,20},{20,16},{24,28},{28,24},{1,5},{5... | collective-permute-start | bytes 184328 | tf_op jit(solution)/shard_map/ppermute | solution.py:151
  131.0 5.4 %collective-permute-start.39 = (bf16[48,768]{1,0:T(8,128)(2,1)S(1)}, bf16[48,768]{1,0:T(8,128)(2,1)S(1)}, u32[]{:S(2)}, u32[]{:S(2)}) collective-permute-start(bf16[48,768]{1,0:T(8,128)(2,1)S(1)} %get-tuple-element.161.refs_6_), channel_id=1, source_target_pairs={{0,16},{4,20},{8,24},{12,28},{16,0},{20,4},{24,8},{28,12},{1,17},{... | collective-permute-start | bytes 221192 | tf_op jit(solution)/shard_map/ppermute | solution.py:151
  131.1 4.6 %collective-permute-start.38 = (bf16[1,160,192]{2,1,0:T(8,128)(2,1)S(1)}, bf16[1,160,192]{2,1,0:T(8,128)(2,1)S(1)}, u32[]{:S(2)}, u32[]{:S(2)}) collective-permute-start(bf16[1,160,192]{2,1,0:T(8,128)(2,1)S(1)} %get-tuple-element.160.refs_4_.refs_8_), channel_id=1, source_target_pairs={{0,8},{4,12},{8,0},{12,4},{16,24},{20,28},{24,16},{28,20},{1,9},{5... | collective-permute-start | bytes 184328 | tf_op jit(solution)/shard_map/ppermute | solution.py:151
  136.6 6.8 %collective-permute-start.41 = (bf16[96,768]{1,0:T(8,128)(2,1)S(1)}, bf16[96,768]{1,0:T(8,128)(2,1)S(1)}, u32[]{:S(2)}, u32[]{:S(2)}) collective-permute-start(bf16[96,768]{1,0:T(8,128)(2,1)S(1)} %get-tuple-element.163.refs_0_), channel_id=1, source_target_pairs={{0,8},{4,12},{8,0},{12,4},{16,24},{20,28},{24,16},{28,20},{1,9},{5... | collective-permute-start | bytes 442376 | tf_op jit(solution)/shard_map/ppermute | solution.py:151
  137.9 20.5 %collective-permute-start.43 = (bf16[384,768]{1,0:T(8,128)(2,1)S(1)}, bf16[384,768]{1,0:T(8,128)(2,1)S(1)}, u32[]{:S(2)}, u32[]{:S(2)}) collective-permute-start(bf16[384,768]{1,0:T(8,128)(2,1)S(1)} %get-tuple-element.176.refs_0_), channel_id=1, source_target_pairs={{0,4},{4,0},{8,12},{12,8},{16,20},{20,16},{24,28},{28,24},{1,5},{5... | collective-permute-start | bytes 1769480 | tf_op jit(solution)/shard_map/ppermute | solution.py:151
  140.7 20.3 %collective-permute-start.44 = (bf16[384,768]{1,0:T(8,128)(2,1)S(1)}, bf16[384,768]{1,0:T(8,128)(2,1)S(1)}, u32[]{:S(2)}, u32[]{:S(2)}) collective-permute-start(bf16[384,768]{1,0:T(8,128)(2,1)S(1)} %get-tuple-element.178.refs_0_), channel_id=1, source_target_pairs={{0,8},{4,12},{8,0},{12,4},{16,24},{20,28},{24,16},{28,20},{1,9},{5... | collective-permute-start | bytes 1769480 | tf_op jit(solution)/shard_map/ppermute | solution.py:151
  143.5 13.2 %collective-permute-start.42 = (bf16[192,768]{1,0:T(8,128)(2,1)S(1)}, bf16[192,768]{1,0:T(8,128)(2,1)S(1)}, u32[]{:S(2)}, u32[]{:S(2)}) collective-permute-start(bf16[192,768]{1,0:T(8,128)(2,1)S(1)} %stage.21.refs_2_.refs_0_), channel_id=1, source_target_pairs={{0,4},{4,0},{8,12},{12,8},{16,20},{20,16},{24,28},{28,24},{1,5},{5... | collective-permute-start | bytes 884744 | tf_op jit(solution)/shard_map/ppermute | solution.py:151
  147.2 5.9 %collective-permute-start.40 = (bf16[1,160,192]{2,1,0:T(8,128)(2,1)S(1)}, bf16[1,160,192]{2,1,0:T(8,128)(2,1)S(1)}, u32[]{:S(2)}, u32[]{:S(2)}) collective-permute-start(bf16[1,160,192]{2,1,0:T(8,128)(2,1)S(1)} %get-tuple-element.162.refs_2_.refs_0_), channel_id=1, source_target_pairs={{0,16},{4,20},{8,24},{12,28},{16,0},{20,4},{24,8},{28,12},{1,17},{... | collective-permute-start | bytes 184328 | tf_op jit(solution)/shard_map/ppermute | solution.py:151
  156.7 0.7 copy-start.14
  158.4 1.1 copy-start.2
  161.0 1.7 %copy-start = (f32[768,768]{1,0:T(8,128)S(1)}, f32[768,768]{1,0:T(8,128)}, u32[]{:S(2)}) copy-start(f32[768,768]{1,0:T(8,128)} %matrix.4.refs_2_) | copy-start | bytes 7077892

commit v3 on v2

v3 whole, which is shorter than its diff:
```python
import functools

import jax
import jax.numpy as jnp
from jax import lax
from jax.experimental import pallas as pl
from jax.experimental.pallas import tpu as pltpu
from jax.sharding import PartitionSpec as P

HEADS = 12
HDIM = 64
ROT = 16
HALF = ROT // 2
BLOCK = 128

NEGATIVE = -1e30
EPSILON = 1e-05
SQRT_HALF = 0.7071067811865476
GAUSS_FACTOR = 0.3989422804014327
SCALE = HDIM ** (-0.5)
BF = jnp.bfloat16
F32 = jnp.float32
MIB = 1024 * 1024
VMEM = pl.BlockSpec(memory_space=pltpu.VMEM)
SMEM = pl.BlockSpec(memory_space=pltpu.SMEM)
ANY = pl.BlockSpec(memory_space=pl.ANY)
HBM = pl.BlockSpec(memory_space=pltpu.HBM)

NN = (((1,), (0,)), ((), ()))
NT = (((1,), (1,)), ((), ()))
TN = (((0,), (0,)), ((), ()))


def dot(left, right, dims=NN):
    return lax.dot_general(left, right, dims, preferred_element_type=F32)


def shape(dims, dtype):
    return jax.ShapeDtypeStruct(dims, dtype)


def params(limit=48):
    return pltpu.CompilerParams(vmem_limit_bytes=limit * MIB)


def micros(time):
    return pl.CostEstimate(flops=max(1, time * 1000000000), bytes_accessed=1000, transcendentals=0)


class Sequence:
    def __init__(self):
        self.last = ()

    def run(self, kernel, outs, ins, scratch=(), limit=16, name=None, after=(), time=0, token=True, **specs):
        single = isinstance(outs, jax.ShapeDtypeStruct)
        self.last = self.last + tuple(after)
        count, extra = len(ins), len(self.last)

        def body(*refs):
            kernel(*refs[:count], *refs[count + extra :])

        results = pl.pallas_call(
            body,
            out_shape=outs,
            in_specs=list(specs.get("in_specs", [VMEM] * count)) + [ANY] * extra,
            out_specs=specs.get("out_specs", VMEM if single else (VMEM,) * len(outs)),
            grid=specs.get("grid", ()),
            scratch_shapes=list(scratch),
            compiler_params=params(limit),
            cost_estimate=micros(time),
            name=name,
        )(*ins, *self.last)
        if token:
            self.last = (min((results,) if single else results, key=lambda v: v.size),)
        return results

    def stage(self, tasks, bundles=(), after=()):
        bundles = [list(bundle) for bundle in bundles]
        placed = {key for bundle in bundles for key in bundle}
        for t, (_, _, parts) in enumerate(tasks):
            bundles += [[(t, p)] for p in range(parts) if (t, p) not in placed]
        sizes = {}
        for t, (kind, views, parts) in enumerate(tasks):
            rows = sum(v.rows for v in views) if kind is join_step else views[0].rows
            for p in range(parts):
                sizes[t, p] = rows // parts
        ins, outs, spots = [], [], {}
        for index, bundle in enumerate(bundles):
            start = 0
            for key in bundle:
                spots[key] = (index, start, sizes[key])
                start += sizes[key]
            like = tasks[bundle[0][0]][1][0].array
            outs.append(shape((start,) + like.shape[1:], BF))
        plan = []
        for t, (kind, views, parts) in enumerate(tasks):
            sources = []
            for view in views:
                at = next((i for i, v in enumerate(ins) if v is view.array), len(ins))
                if at == len(ins):
                    ins.append(view.array)
                sources.append((at, view.start, view.rows))
            plan.append((kind, sources, [spots[t, p] for p in range(parts)]))

        def kernel(*refs):
            def pieces(found, offset):
                return [refs[offset + i].at[start : start + size] for i, start, size in found]

            for kind, sources, targets in plan:
                kind(pieces(sources, 0), pieces(targets, len(ins)))

        results = self.run(kernel, tuple(outs), ins, name="stage", after=after)
        return {key: View(results[i], start, rows) for key, (i, start, rows) in spots.items()}


class View:
    def __init__(self, array, start=0, rows=None):
        self.array, self.start = array, start
        self.rows = array.shape[0] if rows is None else rows


class Sum:
    def __init__(self, near, far, bits, rest, small=False):
        self.small = small
        self.near, self.coming = View(near), View(swap(far, "seq", bits[0]))
        plan = [(bit, 2) for bit in bits[1:]] + [(bit, 1) for bit in rest]
        plan += [(bits[-1], 1)] + [(bit, -1) for bit in reversed(bits[:-1])]
        self.plan = [("seq", bit, parts) for bit, parts in plan]

    def left(self):
        return len(self.plan)

    def task(self):
        parts = self.plan[0][2]
        if parts == -1:
            return (join_step, [self.near, self.coming], 1)
        return (merge_step, [self.near, self.coming], parts)

    def pair(self):
        return (self.near, self.coming)


class Reduce(Sum):
    def __init__(self, near, far, bits):
        Sum.__init__(self, near, far, bits, [])
        self.plan = self.plan[: len(bits) - 1]


class Mix(Sum):
    def __init__(self, near, far, fbits, sbits):
        self.small = True
        self.near, self.coming = View(near), View(swap(far, "fsdp", fbits[0]))
        self.plan = [("fsdp", bit, 2) for bit in fbits[1:]] + [("seq", bit, 1) for bit in sbits]

    def task(self):
        return (mix_step, [self.near, self.coming], self.plan[0][2])


def join_all(sequence, *arrays, after=()):
    task = (join_step, [View(v) for v in arrays], 1)
    return sequence.stage([task], after=after)[0, 0].array


def flow(sequence, *items, extra=(), after=(), together=False):
    tasks = [item.task() for item in items] + list(extra)
    groups = {}
    for t, item in enumerate(items):
        axis, bit, _ = item.plan[0]
        key = (axis, bit, 0 if item.small or together else 1 + t)
        groups.setdefault(key, []).append((t, tasks[t][2] - 1))
    views = sequence.stage(tasks, groups.values(), after)
    for (axis, bit, _), keys in groups.items():
        sent = swap(views[keys[0]].array, axis, bit)
        for t, part in keys:
            view = views[t, part]
            items[t].near = views[t, 0]
            items[t].coming = View(sent, view.start, view.rows)
            items[t].plan.pop(0)
    return [views[len(items) + i, 0].array for i in range(len(extra))]


def swap(value, axis, bit):
    size = lax.axis_size(axis)
    return lax.ppermute(value, axis, [(i, i ^ bit) for i in range(size)])


def bits_of(size):
    return [1 << i for i in range(size.bit_length() - 1)]


def normalize(values):
    center = values - jnp.mean(values, -1, keepdims=True)
    inverse_std = lax.rsqrt(jnp.mean(center * center, -1, keepdims=True) + EPSILON)
    return (center * inverse_std, inverse_std)


def pick(pieces, index):
    result = pieces[-1]
    for i in range(len(pieces) - 2, -1, -1):
        result = jnp.where(index == i, pieces[i], result)
    return result


def rel_order(size):
    order = [0]
    for bit in reversed(bits_of(size)):
        order = order + [r ^ bit for r in order]
    return order


def pack_kernel(*refs):
    count = len(refs) // 2
    pack_ref, both_ref, qo_ref, bulk_ref = refs[count : count + 4]
    sems = refs[-1]
    rows, part = refs[0].shape[0], refs[2].shape[0]
    held = (both_ref.at[:rows], both_ref.at[rows:], qo_ref.at[:part], qo_ref.at[part:])
    held += refs[count + 4 : -1]
    start = 0
    pairs = [(refs[i], held[i]) for i in range(count)]
    for ref in refs[:4]:
        size = ref.shape[0]
        pairs.append((ref, bulk_ref.at[start : start + size]))
        start += size
    copies = [pltpu.make_async_copy(*pair, sems.at[i]) for i, pair in enumerate(pairs)]
    for copy in copies:
        copy.start()
    for copy in copies:
        copy.wait()
    g1, b1, g2, b2, qb, ob, db, kb, vb, wk_ref, wv_ref = held[4:]
    small = jnp.concatenate(
        [
            kb[...].astype(F32).reshape(1, kb.shape[0]),
            vb[...].astype(F32).reshape(1, vb.shape[0]),
            jnp.zeros((1, part - kb.shape[0] - vb.shape[0]), F32),
        ],
        axis=1,
    )
    lines = [ref[...].astype(F32).reshape(1, part) for ref in (g1, b1, g2, b2, qb, ob, db)]
    lines = jnp.concatenate(lines + [small, jnp.zeros((8, part), F32)], axis=0)
    pack_ref[:HDIM] = wk_ref[...]
    pack_ref[HDIM : 2 * HDIM] = wv_ref[...]
    pack_ref[2 * HDIM :] = lines.astype(BF)


def table_kernel(cosine, sine, out):
    out[:HALF] = cosine[...]
    out[HALF:] = sine[...]


def front_kernel(rels, x_ref, *refs):
    count = len(rels)
    packs = refs[:count]
    cs_ref, n1_ref, kv_ref, vec_ref, wkv_ref, pieces, weights = refs[count:]
    me = lax.axis_index("fsdp")
    for rel, pack in zip(rels, packs):
        weights[rel ^ me] = pack[: 2 * HDIM, :]
        pieces[rel ^ me] = pack[2 * HDIM :, :].astype(F32)
    wkv = jnp.concatenate([weights[p] for p in range(count)], axis=1)
    wkv_ref[...] = wkv
    vec = jnp.concatenate([pieces[p] for p in range(count)], axis=1)
    vec_ref[...] = vec
    normal, _ = normalize(x_ref[...].astype(F32))
    n1 = (normal * vec[0:1] + vec[1:2]).astype(BF)
    n1_ref[...] = n1
    key_part, value_part = ROT // count, HDIM // count
    key_bias = jnp.concatenate([pieces[p][7:8, :key_part] for p in range(count)], axis=1)
    value_bias = jnp.concatenate(
        [pieces[p][7:8, key_part : key_part + value_part] for p in range(count)], axis=1
    )
    bias = jnp.concatenate([key_bias, jnp.zeros((1, HDIM - ROT), F32), value_bias], axis=1)
    turned = (dot(n1, wkv, NT) + bias).T
    cosine, sine = cs_ref[:HALF], cs_ref[HALF:]
    first, second = turned[:HALF], turned[HALF:ROT]
    turned = jnp.concatenate(
        [first * cosine - second * sine, second * cosine + first * sine, turned[ROT:]], axis=0
    )
    kv_ref[...] = turned.T.astype(BF)


def query_kernel(rels, n1_ref, both_ref, vec_ref, cs_ref, *refs):
    count = len(rels) - 1
    part = refs[0].shape[0] // 2
    tops = [pack.shape[0] - 2 * part for pack in refs[:count]]
    pairs = [
        (pack.at[top : top + part], pack.at[top + part : top + 2 * part])
        for pack, top in zip(refs[:count], tops)
    ]
    pairs.append(refs[count : count + 2])
    qt_ref, dot_ref, wq_ref, wo_ref = refs[count + 2 :]
    me = lax.axis_index("fsdp")
    for rel, (near, far) in zip(rels, pairs):
        start = pl.multiple_of((rel ^ me) * part, part)
        wq_ref[pl.ds(start, part), :] = near[...]
        wo_ref[pl.ds(start, part), :] = far[...]
    turned = (dot(n1_ref[...], wq_ref[...]) + vec_ref[4:5]).T
    cosine, sine = cs_ref[:HALF], cs_ref[HALF:]
    for h in range(HEADS):
        base = h * HDIM
        first, second = turned[base : base + HALF], turned[base + HALF : base + ROT]
        head = jnp.concatenate(
            [
                first * cosine - second * sine,
                second * cosine + first * sine,
                turned[base + ROT : base + HDIM],
            ],
            axis=0,
        )
        qt_ref[base : base + HDIM, :] = (head.astype(BF).astype(F32) * SCALE).astype(BF)
    dy = both_ref[n1_ref.shape[0] :]
    dot_ref[...] = dot(dy, wo_ref[...], NT).T.astype(BF)


def mlp_kernel(seq_orders, last, *refs):
    both, refs = refs[:2], refs[2:]
    if last:
        up_ref, down_ref, ub_ref, vec_ref, early_up, early_dn, early_sums = refs[:7]
        keep_ref, send_ref, n1c_ref, upk_ref, ups_ref, dnk_ref, dns_ref, sums_ref = refs[7:15]
        normal_s, n2_s, dy_s, acc_up, acc_dn = refs[15:]
    else:
        up_ref, down_ref, ub_ref, vec_ref = refs[:4]
        keep_ref, send_ref, n1c_ref, acc_up, acc_dn, sums_ref = refs[4:10]
        normal_s, n2_s, dy_s = refs[10:]
    me = lax.axis_index("fsdp")
    seq_me = lax.axis_index("seq")
    hidden, width = up_ref.shape
    part = n1c_ref.shape[2]
    rows = n1c_ref.shape[1]
    for i in range(2):
        here = slice(i * rows, (i + 1) * rows)
        x, dy = both[i][:rows], both[i][rows : 2 * rows]
        dy_s[here] = dy
        normal, _ = normalize(x.astype(F32))
        normal_s[here] = normal
        n1 = normal * vec_ref[0:1] + vec_ref[1:2]
        n1c_ref[i] = pick(
            [n1[:, p * part : (p + 1) * part] for p in range(width // part)], me
        ).astype(BF)
        n2_s[here] = (normal * vec_ref[2:3] + vec_ref[3:4]).astype(BF)
    n2, dy = n2_s[...], dy_s[...]
    out = None
    dn2 = None
    tile = 256
    bias = ub_ref[...].astype(F32).reshape(1, hidden)
    sums = []
    for c in range(hidden // tile):
        here = slice(c * tile, (c + 1) * tile)
        up_c, down_c = up_ref[here, :], down_ref[here, :]
        u = dot(n2, up_c, NT) + bias[:, here]
        dg = dot(dy, down_c, NT)
        phi = 0.5 * (1.0 + lax.erf(u * SQRT_HALF))
        g = (u * phi).astype(BF)
        du = (dg * (phi + u * jnp.exp(-0.5 * u * u) * GAUSS_FACTOR)).astype(BF)
        out_c = dot(g, down_c)
        dn2_c = dot(du, up_c)
        out = out_c if out is None else out + out_c
        dn2 = dn2_c if dn2 is None else dn2 + dn2_c
        grad_down, grad_up = dot(g, dy, TN), dot(du, n2, TN)
        if last:
            grad_down, grad_up = grad_down + early_dn[here, :], grad_up + early_up[here, :]
        acc_dn[here, :] = grad_down
        acc_up[here, :] = grad_up
        sums.append(jnp.sum(du.astype(F32), axis=0, keepdims=True))
    lines = [
        jnp.sum(dn2 * normal_s[...], axis=0, keepdims=True),
        jnp.sum(dn2, axis=0, keepdims=True),
        jnp.concatenate(sums, axis=1),
    ]
    for i, line in enumerate(lines):
        size = line.shape[1]
        if last:
            line = line + early_sums[i : i + 1, :size]
        sums_ref[i : i + 1, :size] = line
    for i, target in enumerate((keep_ref, send_ref)):
        here = slice(i * rows, (i + 1) * rows)
        target[0] = out[here].astype(BF)
        target[1] = (dn2[here] * vec_ref[2:3]).astype(BF)
    if last:
        spread_shards(acc_up, seq_orders[0], seq_me, upk_ref, ups_ref)
        spread_shards(acc_dn, seq_orders[1], seq_me, dnk_ref, dns_ref)


def attend_kernel(kv_bits, dkv_bits, side, per_group, chunk_blocks, most, order_ref, len_ref, *refs):
    qt_ref, dot_ref, *kv_refs, cs_ref = refs[:5]
    refs = refs[5:]
    if side == 1:
        early, refs = refs[:3], refs[3:]
    else:
        early = ()
    count = 4 if side == 0 else 5
    attend_side(
        (kv_bits, dkv_bits),
        side,
        per_group,
        chunk_blocks,
        most,
        order_ref,
        len_ref,
        qt_ref,
        dot_ref,
        kv_refs,
        cs_ref,
        early,
        refs[:count],
        *refs[count:],
    )


def attend_side(
    orders,
    side,
    per_group,
    chunk_blocks,
    most,
    order_ref,
    len_ref,
    qt_ref,
    dot_ref,
    kv_refs,
    cs_ref,
    early,
    outs_refs,
    s_scr,
    p_scr,
    pb_scr,
    ds_scr,
    bias_scr,
    kv_scr,
    kvt_scr,
    dkv_scr,
    qs,
    dos,
    ot,
    dqt,
    inverse,
):
    group = pl.program_id(0)
    o_ref, far_ref, near_ref = outs_refs[:3]
    seq_me = lax.axis_index("seq")
    half = held = kv_refs[0].shape[0]
    slots = 2 * held // BLOCK
    chunk = chunk_blocks * BLOCK
    lanes = per_group * BLOCK
    @pl.when(group == 0)
    def _():
        if side == 0:
            dkv_scr[...] = jnp.zeros_like(dkv_scr)
        else:
            dkv_scr[...] = early[2][...]
            for source, target in zip(early[:2], (o_ref, near_ref)):
                target[:BLOCK] = source[...]

        @pl.loop(0, slots)
        def _(i):
            rel = (i // 2) ^ seq_me
            for at, bits in enumerate(orders):
                place = jnp.int32(0)
                for bit in bits:
                    place = place * 2 + (rel // bit) % 2
                inverse[at, order_ref[i]] = place * 2 + i % 2

    block = order_ref[2 * seq_me + side]
    base = block * BLOCK
    end_1 = len_ref[0, 0]
    end_2 = end_1 + len_ref[0, 1]
    end_3 = end_2 + len_ref[0, 2]

    def start_of(position):
        low = jnp.where(position >= end_1, end_1, 0)
        low = jnp.where(position >= end_2, end_2, low)
        return jnp.where(position >= end_3, end_3, low)

    q_pos = base + lax.broadcasted_iota(jnp.int32, (1, BLOCK), 1)
    q_start = start_of(q_pos)
    low_block = jnp.maximum(start_of(base) // BLOCK, block - (most - 1))
    chunks = (block - low_block + chunk_blocks) // chunk_blocks

    def slot_of(j, at):
        return inverse[at, jnp.minimum(low_block + j, block)]

    @pl.loop(0, chunks * chunk_blocks)
    def _(j):
        start = slot_of(j, 0) * BLOCK
        here = pl.ds(pl.multiple_of(j * BLOCK, BLOCK), BLOCK)
        for i, kv_ref in enumerate(kv_refs):

            @pl.when(start // held == i)
            def _():
                there = pl.multiple_of(start - i * held, BLOCK)
                kv_scr[here, :] = kv_ref[pl.ds(there, BLOCK), :]

    for h in range(per_group):
        cols = slice(h * BLOCK, (h + 1) * BLOCK)
        qs[:, cols] = qt_ref[h * HDIM : (h + 1) * HDIM, :]
        dos[:, cols] = dot_ref[h * HDIM : (h + 1) * HDIM, :]

    pairs = per_group // 2

    def columns(h):
        return slice(h * BLOCK, (h + 1) * BLOCK)

    def score_step(c, top):
        keys = kv_scr[pl.ds(c * chunk, chunk), :HDIM]
        k_pos = (low_block + c * chunk_blocks) * BLOCK + lax.broadcasted_iota(
            jnp.int32, (chunk, BLOCK), 0
        )
        allowed = jnp.logical_and(k_pos <= q_pos, k_pos >= q_start)
        bias_scr[c] = jnp.where(allowed, 0.0, NEGATIVE)
        tops = []
        for pair in range(pairs):
            s = dot(keys, qs[:, pair * 2 * BLOCK : (pair + 1) * 2 * BLOCK])
            for half_at in range(2):
                part = s[:, columns(half_at)] + bias_scr[c]
                s_scr[c, :, columns(2 * pair + half_at)] = part
                tops.append(jnp.max(part, axis=0, keepdims=True))
        return jnp.maximum(top, jnp.concatenate(tops, axis=1))

    top = lax.fori_loop(0, chunks, score_step, jnp.full((1, lanes), NEGATIVE, F32))

    def weight_step(c, carry):
        total, delta = carry
        totals, deltas = [], []
        values = kv_scr[pl.ds(c * chunk, chunk), HDIM:]
        for pair in range(pairs):
            dp = dot(values, dos[:, pair * 2 * BLOCK : (pair + 1) * 2 * BLOCK])
            for half_at in range(2):
                cols = columns(2 * pair + half_at)
                part = dp[:, columns(half_at)]
                p_scr[c, :, cols] = part
                e = jnp.exp(s_scr[c, :, cols] - top[:, cols])
                s_scr[c, :, cols] = e
                totals.append(jnp.sum(e, axis=0, keepdims=True))
                deltas.append(jnp.sum(e * part, axis=0, keepdims=True))
        return (
            total + jnp.concatenate(totals, axis=1),
            delta + jnp.concatenate(deltas, axis=1),
        )

    zero = jnp.zeros((1, lanes), F32)
    total, delta = lax.fori_loop(0, chunks, weight_step, (zero, zero))
    shrink = 1.0 / total
    delta = delta * shrink
    ot[...] = jnp.zeros_like(ot)
    dqt[...] = jnp.zeros_like(dqt)

    def grad_step(c, _):
        kvt = kvt_scr[c]
        for pair in range(pairs):
            both = slice(pair * 2 * BLOCK, (pair + 1) * 2 * BLOCK)
            for half_at in range(2):
                cols = columns(2 * pair + half_at)
                p = s_scr[c, :, cols] * shrink[:, cols]
                pb_scr[:, cols] = p.astype(BF)
                ds_scr[:, cols] = (p * (p_scr[c, :, cols] - delta[:, cols])).astype(BF)
            ot[:, both] += dot(kvt[HDIM:], pb_scr[:, both])
            dqt[:, both] += dot(kvt[:HDIM], ds_scr[:, both])
        dk = dot(ds_scr[...], qs[...], NT)
        dv = dot(pb_scr[...], dos[...], NT)
        both = jnp.concatenate([dk, dv], axis=1)
        for b in range(chunk_blocks):

            @pl.when(low_block + c * chunk_blocks + b <= block)
            def _():
                place = slot_of(c * chunk_blocks + b, 1) * BLOCK
                dkv_scr[pl.ds(pl.multiple_of(place, BLOCK), BLOCK), :] += both[
                    b * BLOCK : (b + 1) * BLOCK
                ]

        return 0

    @pl.loop(0, chunks)
    def _(c):
        kvt_scr[c] = kv_scr[pl.ds(c * chunk, chunk), :].astype(F32).T.astype(BF)

    lax.fori_loop(0, chunks, grad_step, 0)
    cosine, sine = cs_ref[:HALF], cs_ref[HALF:]
    outs, grads = [], []
    for h in range(per_group):
        cols = slice(h * BLOCK, (h + 1) * BLOCK)
        outs.append(ot[:, cols])
        grad = dqt[:, cols] * SCALE
        first, second = grad[:HALF], grad[HALF:ROT]
        grads.append(first * cosine + second * sine)
        grads.append(second * cosine - first * sine)
        grads.append(grad[ROT:])
    width = o_ref.shape[1]
    here = slice(side * BLOCK, (side + 1) * BLOCK)
    span = per_group * HDIM
    across = pl.ds(0 if span == width else pl.multiple_of(group * span, span), span)
    o_ref[here, across] = jnp.concatenate(outs, axis=0).T.astype(BF)
    grad = jnp.concatenate(grads, axis=0).T.astype(BF)
    far_ref[:, across] = grad
    near_ref[here, across] = grad

    @pl.when(group == pl.num_programs(0) - 1)
    def _():
        me = lax.axis_index("fsdp")
        part = near_ref.shape[1] - width
        count = width // part
        o = o_ref[here, :].astype(F32)
        pieces = [o[:, p * part : (p + 1) * part] for p in range(count)]
        near_ref[here, width:] = pick(pieces, me ^ 1).astype(BF)
        far_ref[:, width:] = jnp.concatenate(
            [pick(pieces, me ^ 2), pick(pieces, me ^ 3)], axis=1
        ).astype(BF)

        if side == 0:
            outs_refs[3][...] = dkv_scr[...]
        else:
            outs_refs[3][...] = dkv_scr[:half].astype(BF)
            outs_refs[4][...] = dkv_scr[half:].astype(BF)


def output_kernel(both_ref, o_ref, wo_ref, vec_ref, dn1_ref, a_ref, b_ref, c_ref, *outs):
    layer_ref, grad_ref = outs
    rows = o_ref.shape[0]
    x, dy = both_ref[:rows].astype(F32), both_ref[rows:].astype(F32)
    mlp = a_ref[0].astype(F32) + b_ref[0].astype(F32) + c_ref[0].astype(F32)
    attention = dot(o_ref[...], wo_ref[...]) + vec_ref[5:6]
    layer_ref[...] = (x + attention + mlp + vec_ref[6:7]).astype(BF)
    normal, inverse_std = normalize(x)
    total = a_ref[1].astype(F32) + b_ref[1].astype(F32) + c_ref[1].astype(F32)
    total = total + dn1_ref[...] * vec_ref[0:1]
    grad_ref[...] = (
        dy
        + inverse_std
        * (
            total
            - jnp.mean(total, -1, keepdims=True)
            - normal * jnp.mean(total * normal, -1, keepdims=True)
        )
    ).astype(BF)


def shard_at(order, m, seq_me):
    return (order[m] ^ seq_me) & order[-1]


def spread_shards(source, order, seq_me, near, far):
    shards = len(order)
    rows = source.shape[0] // shards
    half = shards // 2
    for m in range(shards):
        start = pl.multiple_of(shard_at(order, m, seq_me) * rows, rows)
        target = near if m < half else far
        target[(m % half) * rows : (m % half + 1) * rows, :] = source[pl.ds(start, rows), :].astype(
            BF
        )


def weight_kernel(order, n1a_ref, n1b_ref, o_ref, own_ref, z1_ref, z2_ref, z3_ref, *refs):
    me = lax.axis_index("fsdp")
    rows, part = n1a_ref.shape[1:]
    dys = [ref.at[rows : 2 * rows] for ref in refs[:4]]
    near_ref, far_ref, grad = refs[4:]
    width = dys[0].shape[1]
    o = o_ref[...].astype(F32)
    own = pick([o[:, p * part : (p + 1) * part] for p in range(width // part)], me).astype(BF)
    items = (
        (n1a_ref[0], own_ref[:, :width], own, dys[0][...]),
        (n1a_ref[1], z1_ref[:, :width], z1_ref[:, width:], dys[1][...]),
        (n1b_ref[0], z2_ref[:, :width], z2_ref[:, width:], dys[2][...]),
        (n1b_ref[1], z3_ref[:, :width], z3_ref[:, width:], dys[3][...]),
    )
    grad_q = None
    grad_o = None
    for n1, dq, cols, dy in items:
        term_q, term_o = dot(n1, dq, TN), dot(cols, dy, TN)
        grad_q = term_q if grad_q is None else grad_q + term_q
        grad_o = term_o if grad_o is None else grad_o + term_o
    grad[:part] = grad_q
    grad[part:] = grad_o
    spread_shards(grad, order, lax.axis_index("seq"), near_ref, far_ref)


def tail_kernel(
    rels,
    both_ref,
    n1_ref,
    dq_ref,
    wq_ref,
    wkv_ref,
    vec_ref,
    cs_ref,
    dkvn_ref,
    dkvf_ref,
    sums_ref,
    dn1_ref,
    keep_ref,
    send_ref,
    vs,
):
    count = len(rels)
    me = lax.axis_index("fsdp")
    rows, width = n1_ref.shape
    part = width // count
    dkv = (dkvn_ref[...].astype(F32) + dkvf_ref[...].astype(F32)).T
    cosine, sine = cs_ref[:HALF], cs_ref[HALF:]
    first, second = dkv[:HALF], dkv[HALF:ROT]
    dkv = jnp.concatenate(
        [first * cosine + second * sine, second * cosine - first * sine, dkv[ROT:]], axis=0
    )
    dkv_sum = jnp.sum(dkv.astype(BF).T.astype(F32), axis=0, keepdims=True)
    dkv_t = dkv.astype(BF)
    dq = dq_ref[:, :width]
    dn1 = dot(dq, wq_ref[...], NT) + dot(dkv_t, wkv_ref[...], TN)
    dn1_ref[...] = dn1
    normal, _ = normalize(both_ref[:rows].astype(F32))
    dy = both_ref[rows:].astype(F32)
    grad_kv = dot(dkv_t, n1_ref[...])
    lines = jnp.concatenate(
        [
            jnp.sum(dn1 * normal, axis=0, keepdims=True),
            jnp.sum(dn1, axis=0, keepdims=True),
            sums_ref[0:1, :width],
            sums_ref[1:2, :width],
            jnp.sum(dq.astype(F32), axis=0, keepdims=True),
            jnp.sum(dy, axis=0, keepdims=True),
            jnp.concatenate(
                [jnp.concatenate([dkv_sum, jnp.zeros((1, part - 2 * HDIM), F32)], axis=1)] * count,
                axis=1,
            ),
            jnp.zeros((1, width), F32),
        ],
        axis=0,
    )
    for p in range(count):
        cols = slice(p * part, (p + 1) * part)
        vs[p, : 2 * HDIM, :] = grad_kv[:, cols]
        vs[p, 2 * HDIM :, :] = lines[:, cols]
    half = count // 2
    extra = sums_ref.shape[1] // part
    up_bias = jnp.concatenate(
        [sums_ref[2:3, e * part : (e + 1) * part] for e in range(extra)]
        + [jnp.zeros((8 - extra, part), F32)],
        axis=0,
    )
    size = keep_ref.shape[0] // half
    for m, rel in enumerate(rels):
        target = keep_ref if m < half else send_ref
        piece = vs[rel ^ me]
        last = up_bias if rel == 0 else jnp.zeros_like(up_bias)
        lines = jnp.concatenate([piece[2 * HDIM :], last], axis=0)
        target[(m % half) * size : (m % half + 1) * size] = join_split(
            fold(piece[: 2 * HDIM], count), fold(lines, count)
        )


def join_split(matrix, lines):
    high = lines.astype(BF).astype(F32)
    rest = jnp.zeros((8, matrix.shape[1]), F32)
    return jnp.concatenate([matrix, high, lines - high, rest], axis=0).astype(BF)


def load_split(value):
    value = value.astype(F32)
    return (value[:32], value[32:36] + value[36:40])


def fold(value, count):
    rows = value.shape[0] // count
    return jnp.concatenate([value[i * rows : (i + 1) * rows] for i in range(count)], axis=1)


def unfold(value, part):
    return jnp.concatenate(
        [value[:, i : i + part] for i in range(0, value.shape[1], part)], axis=0
    )


def mix_step(sources, targets):
    each = sources[0].shape[0] // len(targets)
    for i, target in enumerate(targets):
        here = slice(i * each, (i + 1) * each)
        first, second = load_split(sources[0][here]), load_split(sources[1][here])
        target[...] = join_split(first[0] + second[0], first[1] + second[1])


def merge_step(sources, targets):
    a_ref, b_ref = sources
    rows = a_ref.shape[0] // len(targets)
    for i, target in enumerate(targets):
        here = slice(i * rows, (i + 1) * rows)
        target[...] = (a_ref[here].astype(F32) + b_ref[here].astype(F32)).astype(BF)


def relay_kernel(part, first_ref, second_ref, own_ref, next_ref):
    width = own_ref.shape[1] - part
    for i, ref in enumerate((first_ref, second_ref)):
        here = slice(i * BLOCK, (i + 1) * BLOCK)
        own_ref[here] = ref[:, : width + part]
        next_ref[here, :width] = ref[:, :width]
        next_ref[here, width:] = ref[:, width + part :]


def join_step(sources, targets):
    rows = 0
    for source in sources:
        targets[0][rows : rows + source.shape[0]] = source[...]
        rows += source.shape[0]


def matrix_kernel(order, near_view, far_view, near_ref, far_ref, *refs):
    outs, (held, sems) = refs[:-2], refs[-2:]
    seq_me = lax.axis_index("seq")
    shards = len(order)
    half = shards // 2
    near_ref = near_ref.at[near_view[0] : near_view[0] + near_view[1]]
    far_ref = far_ref.at[far_view[0] : far_view[0] + far_view[1]]
    rows = near_ref.shape[0] // half
    each = shards // len(outs)
    copies = []
    for t in range(shards):
        place = jnp.int32(0)
        for m in range(shards):
            place = jnp.where(shard_at(order, m, seq_me) == t, m, place)
        start = pl.multiple_of((place & (half - 1)) * rows, rows)

        @pl.when(place < half)
        def _():
            held[t] = near_ref[pl.ds(start, rows), :].astype(F32)

        @pl.when(place >= half)
        def _():
            held[t] = far_ref[pl.ds(start, rows), :].astype(F32)

        first = (t % each) * rows
        copy = pltpu.make_async_copy(
            held.at[t], outs[t // each].at[first : first + rows, :], sems.at[t]
        )
        copy.start()
        copies.append(copy)
    for copy in copies:
        copy.wait()


def vector_kernel(a_at, b_at, a_ref, b_ref, g1, b1, qb, kb, vb, ob, g2, b2, ub, db, wk_ref, wv_ref):
    me = lax.axis_index("fsdp")
    first, second = load_split(a_ref[a_at : a_at + 48]), load_split(b_ref[b_at : b_at + 48])
    part = g1.shape[0]
    total = unfold(first[0] + second[0], part)
    lines = unfold(first[1] + second[1], part)
    wk_ref[...] = total[:HDIM]
    wv_ref[...] = total[HDIM:]
    for i, targets in enumerate(((g1,), (b1,), (g2,), (b2,), (qb,), (ob, db))):
        for target in targets:
            target[...] = lines[i : i + 1].reshape(part)
    kp, vp = kb.shape[0], vb.shape[0]
    line = lines[6:7]
    count = HDIM // vp
    kb[...] = pick([line[:, p * kp : (p + 1) * kp] for p in range(count)], me).reshape(kp)
    vb[...] = pick(
        [line[:, HDIM + p * vp : HDIM + (p + 1) * vp] for p in range(count)], me
    ).reshape(vp)
    extra = ub.shape[0] // part
    ub[...] = jnp.concatenate([lines[8 + e : 9 + e] for e in range(extra)], axis=1).reshape(
        ub.shape[0]
    )


def shard_count(rows, devices):
    shards = devices
    while shards > 2 and (rows % shards or (rows // shards) % 16):
        shards //= 2
    return shards


def shard_order(bits):
    order = [0]
    for bit in reversed(bits):
        order = order + [r ^ bit for r in order]
    return order


def on_device(
    tokens,
    block_order,
    doc_lengths,
    norm_one_gain,
    norm_one_bias,
    query_weight,
    query_bias,
    key_weight,
    key_bias,
    value_weight,
    value_bias,
    out_weight,
    out_bias,
    norm_two_gain,
    norm_two_bias,
    up_weight,
    up_bias,
    down_weight,
    down_bias,
    cotangent,
):
    _, rows, width = tokens.shape
    hidden = up_weight.shape[0]
    part = query_weight.shape[0]
    fsdp = lax.axis_size("fsdp")
    seqs = lax.axis_size("seq")
    slots = 2 * seqs
    fbits = bits_of(fsdp)
    sbits = bits_of(seqs)
    rels = rel_order(fsdp)
    fsdp_me = lax.axis_index("fsdp")
    seq_me = lax.axis_index("seq")
    x_own = tokens.reshape(rows, width)
    dy_own = cotangent.reshape(rows, width)

    def spread(value):
        parts = [value]
        for bit in reversed(fbits):
            parts = parts + [swap(v, "fsdp", bit) for v in parts]
        return parts

    pieces = (
        x_own,
        dy_own,
        query_weight,
        out_weight,
        norm_one_gain,
        norm_one_bias,
        norm_two_gain,
        norm_two_bias,
        query_bias,
        out_bias,
        down_bias,
        key_bias,
        value_bias,
        key_weight.T,
        value_weight.T,
    )
    sequence = Sequence()
    run = sequence.run
    pack, both_0, qo_0, bulk_0 = run(
        pack_kernel,
        (
            shape((2 * HDIM + 16, part), BF),
            shape((2 * rows, width), BF),
            shape((2 * part, width), BF),
            shape((2 * rows + 2 * part, width), BF),
        ),
        pieces,
        [pltpu.VMEM(v.shape, BF) for v in pieces[4:]] + [pltpu.SemaphoreType.DMA((len(pieces) + 4,))],
        limit=60,
        name="pack",
        time=2,
        in_specs=[HBM] * len(pieces),
    )
    packs = spread(pack)
    qo_2 = swap(qo_0, "fsdp", 2)
    both_2 = swap(both_0, "fsdp", 2)
    bulk_1 = swap(bulk_0, "fsdp", 1)

    own_blocks = lax.dynamic_slice_in_dim(block_order, 2 * seq_me, 2)
    offsets = jnp.arange(BLOCK, dtype=jnp.int32)
    own_pos = (own_blocks[:, None] * BLOCK + offsets[None, :]).reshape(rows)
    frequencies = 10000.0 ** (-2.0 * jnp.arange(HALF, dtype=F32) / ROT)
    angles = own_pos.astype(F32)[None, :] * frequencies[:, None]
    cs = run(
        table_kernel,
        shape((ROT, rows), F32),
        (jnp.cos(angles), jnp.sin(angles)),
        name="tables",
        time=5,
    )

    n1, kv_own, vec, wkv = run(
        functools.partial(front_kernel, rels),
        (
            shape((rows, width), BF),
            shape((rows, 2 * HDIM), BF),
            shape((16, width), F32),
            shape((2 * HDIM, width), BF),
        ),
        (x_own, *packs, cs),
        [pltpu.VMEM((fsdp, 16, part), F32), pltpu.VMEM((fsdp, 2 * HDIM, part), BF)],
        name="front",
        time=1,
    )

    kv = kv_own
    for bit in reversed(sbits[3:]):
        kv = join_all(sequence, kv, swap(kv, "seq", bit))
    kv_parts = [kv] + [swap(kv, "seq", bit) for bit in (sbits[2], sbits[1], sbits[1] + sbits[2])]
    kv_bits = sbits

    up_bits, dn_bits = sbits[:2], [sbits[1], sbits[0]]
    seq_orders = (shard_order(up_bits), shard_order(dn_bits))

    def others(bits):
        return sorted((b for b in sbits if b not in bits), key=lambda b: (b > sbits[2], -b))

    chunk_out = shape((2, rows, width), BF)
    n1c_out = shape((2, rows, part), BF)
    sums_out = shape((8, max(hidden, width)), F32)
    mlp_scratch = [
        pltpu.VMEM((2 * rows, width), F32),
        pltpu.VMEM((2 * rows, width), BF),
        pltpu.VMEM((2 * rows, width), BF),
    ]
    most = min(slots, slots // 2 + 1)
    chunk_blocks = 2
    most_chunks = -(-most // chunk_blocks)
    chunk = chunk_blocks * BLOCK
    per_group = HEADS
    while most_chunks * chunk * per_group * BLOCK * 8 > 20 * MIB and per_group > 2:
        per_group = {12: 6, 6: 4, 4: 2}[per_group]
    lanes = per_group * BLOCK
    span = per_group * HDIM
    def attend(side, early, outs):
        return run(
            functools.partial(attend_kernel, kv_bits, sbits, side, per_group, chunk_blocks, most),
            outs,
            (block_order, doc_lengths, qt, do_t, *kv_parts, cs, *early),
            [
                pltpu.VMEM((most_chunks, chunk, lanes), F32),
                pltpu.VMEM((most_chunks, chunk, lanes), F32),
                pltpu.VMEM((chunk, lanes), BF),
                pltpu.VMEM((chunk, lanes), BF),
                pltpu.VMEM((most_chunks, chunk, BLOCK), F32),
                pltpu.VMEM((most_chunks * chunk, 2 * HDIM), BF),
                pltpu.VMEM((most_chunks, 2 * HDIM, chunk), BF),
                pltpu.VMEM((slots * BLOCK, 2 * HDIM), F32),
                pltpu.VMEM((HDIM, lanes), BF),
                pltpu.VMEM((HDIM, lanes), BF),
                pltpu.VMEM((HDIM, lanes), F32),
                pltpu.VMEM((HDIM, lanes), F32),
                pltpu.SMEM((2, slots), jnp.int32),
            ],
            limit=36 if slots <= 16 else 60,
            name="attend",
            time=(2, 10)[side],
            grid=(HEADS // per_group,),
            in_specs=[
                SMEM,
                SMEM,
                pl.BlockSpec((span, BLOCK), lambda g: (g, side)),
                pl.BlockSpec((span, BLOCK), lambda g: (g, side)),
                VMEM,
                VMEM,
                pl.BlockSpec((ROT, BLOCK), lambda g: (0, side)),
            ]
            + [VMEM] * len(early),
        )

    far_out = shape((BLOCK, width + 2 * part), BF)
    keep_a, send_a, n1a, early_up, early_dn, early_sums = run(
        functools.partial(mlp_kernel, None, False),
        (
            chunk_out,
            chunk_out,
            n1c_out,
            shape((hidden, width), F32),
            shape((hidden, width), F32),
            sums_out,
        ),
        (both_0, bulk_1, up_weight, down_weight, up_bias, vec),
        mlp_scratch,
        limit=24,
        name="mlp_near",
        time=0,
    )
    back_a = swap(send_a, "fsdp", 1)
    kv_near = join_all(sequence, *kv_parts)
    kv_parts = [kv_near, swap(kv_near, "seq", sbits[0])]
    task = (join_step, [View(qo_2, 0, part)], 1), (join_step, [View(qo_2, part, part)], 1)
    views = sequence.stage(task)
    qo_3 = [swap(views[t, 0].array, "fsdp", 1) for t in range(2)]
    qt, do_t, wq, wo = run(
        functools.partial(query_kernel, rels),
        (
            shape((width, rows), BF),
            shape((width, rows), BF),
            shape((width, width), BF),
            shape((width, width), BF),
        ),
        (n1, both_0, vec, cs, qo_0, qo_2, bulk_1, *qo_3),
        name="query",
    )

    own, far_0, near, dkv = attend(
        0,
        (),
        (
            shape((BLOCK, width), BF),
            far_out,
            shape((BLOCK, width + part), BF),
            shape((slots * BLOCK, 2 * HDIM), F32),
        ),
    )
    z2 = [swap(far_0, "fsdp", 2)]
    both_3 = swap(join_all(sequence, both_2), "fsdp", 1)
    keep_b, send_b, n1b, upk, ups, dnk, dns, sums = run(
        functools.partial(mlp_kernel, seq_orders, True),
        (chunk_out, chunk_out, n1c_out)
        + (shape((hidden // 2, width), BF),) * 4
        + (sums_out,),
        (both_2, both_3, up_weight, down_weight, up_bias, vec, early_up, early_dn, early_sums),
        mlp_scratch + [pltpu.VMEM((hidden, width), F32)] * 2,
        limit=28,
        name="mlp_far",
        time=8,
        after=(back_a,),
    )
    up = Sum(upk, ups, up_bits, others(up_bits))
    dn = Sum(dnk, dns, dn_bits, others(dn_bits))
    own, far_1, z_near, dkv_near, dkv_far = attend(
        1,
        (own, near, dkv),
        (shape((rows, width), BF), far_out, shape((rows, width + part), BF))
        + (shape((seqs * BLOCK, 2 * HDIM), BF),) * 2,
    )
    z2.append(swap(far_1, "fsdp", 2))
    dkv = Reduce(dkv_near, dkv_far, sbits)
    z1 = swap(z_near, "fsdp", 1)
    flow(sequence, up, dn)
    z2, relay_z = run(
        functools.partial(relay_kernel, part),
        (shape((rows, width + part), BF),) * 2,
        z2,
        name="relay",
    )
    z3 = swap(relay_z, "fsdp", 1)
    flow(sequence, up)
    qo_bits = sbits[:2]
    qo_order = shard_order(qo_bits)
    qok, qos = run(
        functools.partial(weight_kernel, qo_order),
        (shape((part, width), BF),) * 2,
        (n1a, n1b, own, z_near, z1, z2, z3, both_0, bulk_1, both_2, both_3),
        [pltpu.VMEM((2 * part, width), F32)],
        name="weight",
    )
    qo = Sum(qok, qos, qo_bits, others(qo_bits), small=True)
    flow(sequence, dkv)
    while dkv.left():
        flow(sequence, dkv)
    mixed = shape((48 * fsdp // 2, width), BF)
    dn1, near_t, far_t = run(
        functools.partial(tail_kernel, rels),
        (shape((rows, width), F32), mixed, mixed),
        (both_0, n1, z_near, wq, wkv, vec, cs, *[v.array for v in dkv.pair()], sums),
        [pltpu.VMEM((fsdp, 2 * HDIM + 8, part), F32)],
        name="tail",
    )
    mix = Mix(near_t, far_t, fbits, [sbits[1], sbits[0], sbits[2]] + sbits[3:])
    flow(sequence, qo)
    flow(sequence, dn)
    while up.left() > 2:
        flow(sequence, up)
    flow(sequence, up)
    flow(sequence, mix)
    flow(sequence, qo)
    flow(sequence, up)
    flow(sequence, mix)
    back_b = swap(send_b, "fsdp", 1)
    back = sequence.stage([(merge_step, [View(keep_b), View(back_b)], 1)])[0, 0].array
    back = swap(back, "fsdp", 2)
    flow(sequence, mix)
    while dn.left() > 2:
        flow(sequence, dn)
    flow(sequence, dn)
    flow(sequence, qo)
    flow(sequence, mix)
    flow(sequence, qo)
    flow(sequence, dn)
    layer_out, grad_tokens = run(
        output_kernel,
        (shape((rows, width), BF),) * 2,
        (both_0, own, wo, vec, dn1, keep_a, back_a, back),
        name="output",
        token=False,
    )
    while up.left() + dn.left() + qo.left() + mix.left():
        flow(sequence, *[item for item in (qo, mix, up, dn) if item.left()])

    def matrix(item, order, count):
        near, far = item.pair()
        each = 2 * near.rows // len(order)
        views = [(view.start, view.rows) for view in (near, far)]
        return run(
            functools.partial(matrix_kernel, order, *views),
            (shape((2 * near.rows // count, width), F32),) * count,
            (near.array, far.array),
            [
                pltpu.VMEM((len(order), each, width), F32),
                pltpu.SemaphoreType.DMA((len(order),)),
            ],
            name="matrix",
            token=False,
            out_specs=(HBM,) * count,
        )

    vector = shape((part,), F32)
    g1, b1, qb, kb, vb, ob, g2, b2, ub, db, wk, wv = run(
        functools.partial(vector_kernel, *[v.start for v in mix.pair()]),
        (
            vector,
            vector,
            vector,
            shape(key_bias.shape, F32),
            shape(value_bias.shape, F32),
            vector,
            vector,
            vector,
            shape((hidden,), F32),
            vector,
            shape((HDIM, part), F32),
            shape((HDIM, part), F32),
        ),
        tuple(v.array for v in mix.pair()),
        limit=16,
        token=False,
        name="vector",
    )
    grad_query, grad_out = matrix(qo, qo_order, 2)
    (grad_up,) = matrix(up, seq_orders[0], 1)
    (grad_down,) = matrix(dn, seq_orders[1], 1)
    return (
        layer_out.reshape(1, rows, width),
        grad_tokens.reshape(1, rows, width),
        g1,
        b1,
        grad_query,
        qb,
        wk.T,
        kb,
        wv.T,
        vb,
        grad_out,
        ob,
        g2,
        b2,
        grad_up,
        ub,
        grad_down,
        db,
    )


def solution(mesh):
    split = P("fsdp")
    matrix = P("fsdp", None)
    stream = P("fsdp", "seq", None)
    return jax.shard_map(
        on_device,
        mesh=mesh,
        in_specs=(
            stream,
            P(),
            matrix,
            split,
            split,
            matrix,
            split,
            matrix,
            split,
            matrix,
            split,
            matrix,
            split,
            split,
            split,
            matrix,
            split,
            matrix,
            split,
            stream,
        ),
        out_specs=(
            stream,
            stream,
            split,
            split,
            matrix,
            split,
            matrix,
            split,
            matrix,
            split,
            matrix,
            split,
            split,
            split,
            matrix,
            split,
            matrix,
            split,
        ),
        check_vma=False,
    )
```

time: 164 us -> 162 us (0.988)
  local copies, waits for them, and re-layouts: 5.31 us -> 1.54 us
  Pallas kernels: 38.6 us -> 36.3 us
  starting transfers between devices: 52.3 us -> 54.4 us
  waiting for transfers between devices: 66.7 us -> 68.5 us
    unnamed x30 -> x18, local copies, waits for them, and re-layouts: 5.31 us -> 1.54 us
    pallas_call x24 -> x37, Pallas kernels: 38.6 us -> 36.3 us  [run(): pl.pallas_call(body, out_shape=outs, in_specs=list(specs.get('in_specs',...]
    ppermute x45 -> x43, starting transfers between devices: 52.3 us -> 54.4 us  [swap(): return lax.ppermute(value, axis, [(i, i ^ bit) for i in range(size)])]
    ppermute x45 -> x43, waiting for transfers between devices: 66.7 us -> 68.5 us  [swap(): return lax.ppermute(value, axis, [(i, i ^ bit) for i in range(size)])]
  transfers between devices with their start and end apart: 45 -> 43, of which waited for: 24 -> 18; matrix products, arithmetic and copies ran while one was open for 0% -> 0% of each run, Pallas kernels for 21% -> 19%
where the time goes in v3:
time: 162 us
  waiting for transfers between devices  68.5 us (42%)
  starting transfers between devices  54.4 us (34%)
  Pallas kernels  36.3 us (22%)
    ppermute x43, waiting for transfers between devices, swap(): return lax.ppermute(value, axis, [(i, i ^ bit) for i in range(size)])  68.5 us
    ppermute x43, starting transfers between devices, swap(): return lax.ppermute(value, axis, [(i, i ^ bit) for i in range(size)])  54.4 us
    pallas_call x37, Pallas kernels, run(): pl.pallas_call(body, out_shape=outs, in_specs=list(specs.get('in_specs',...  36.3 us
  transfers between devices with their start and end apart: 43, of which 18 were waited for; matrix products, arithmetic and copies ran while one was open for 0% of the time, Pallas kernels for 19%

profile of v3, /device:TPU:0, one launch (start us, length us, event | category | flops | bytes accessed | tf_op | source)
XLA Modules:
  0.0 162.3 jit_solution(1139086437481229649)
XLA Ops:
  0.7 3.6 %pack.1 = (bf16[144,192]{1,0:T(8,128)(2,1)}, bf16[512,768]{1,0:T(8,128)(2,1)}, bf16[384,768]{1,0:T(8,128)(2,1)}, bf16[896,768]{1,0:T(8,128)(2,1)}) custom-call(bf16[256,768]{1,0:T(8,128)(2,1)} %bitcast.10, bf16[256,768]{1,0:T(8,128)(2,1)} %bitcast.12, bf16[192,768]{1,0:T(8,128)(2,1)} %refs_2_.3, bf16[192,768]{1,0:T(8,128)(2,1)} %refs_3_.3, ...), custom_call_target="tpu_custom_call" | custom-call | flops 2000000000 | bytes 1000 | tf_op jit(solution)/shard_map/pack/pallas_call | solution.py:62
  4.3 0.5 collective-permute-start.4
  4.9 2.9 %collective-permute-start = (bf16[144,192]{1,0:T(8,128)(2,1)}, bf16[144,192]{1,0:T(8,128)(2,1)S(1)}, u32[]{:S(2)}, u32[]{:S(2)}) collective-permute-start(bf16[144,192]{1,0:T(8,128)(2,1)} %get-tuple-element.91.refs_2_.refs_1_), channel_id=1, source_target_pairs={{0,2},{1,3},{2,0},{3,1},{4,6},{5,7},{6,4},{7,5},{8,10},{9,11},{10,... | collective-permute-start | bytes 165896 | tf_op jit(solution)/shard_map/ppermute | solution.py:184
  7.9 2.0 %collective-permute-start.11 = (bf16[512,768]{1,0:T(8,128)(2,1)}, bf16[512,768]{1,0:T(8,128)(2,1)S(1)}, u32[]{:S(2)}, u32[]{:S(2)}) collective-permute-start(bf16[512,768]{1,0:T(8,128)(2,1)} %get-tuple-element.90.refs_0_.refs_1_.refs_7_), channel_id=1, source_target_pairs={{0,2},{1,3},{2,0},{3,1},{4,6},{5,7},{6,4},{7,5},{8,10},{9,11},{10,... | collective-permute-start | bytes 2359304 | tf_op jit(solution)/shard_map/ppermute | solution.py:184
  10.1 0.6 collective-permute-done.refs_2_
  10.8 0.9 copy-done.6
  11.7 0.3 collective-permute-done.2.refs_4_
  12.0 0.6 copy-done.5
  12.7 0.9 front.1
  13.6 4.3 %collective-permute-start.7 = (bf16[256,128]{1,0:T(8,128)(2,1)S(1)}, bf16[256,128]{1,0:T(8,128)(2,1)S(1)}, u32[]{:S(2)}, u32[]{:S(2)}) collective-permute-start(bf16[256,128]{1,0:T(8,128)(2,1)S(1)} %get-tuple-element.96.refs_0_), channel_id=1, source_target_pairs={{0,24},{4,28},{8,16},{12,20},{16,8},{20,12},{24,0},{28,4},{1,25},{... | collective-permute-start | bytes 196616 | tf_op jit(solution)/shard_map/ppermute | solution.py:184
  17.9 0.6 collective-permute-start.5
  18.5 4.9 %mlp_near.1 = (bf16[2,256,768]{2,1,0:T(8,128)(2,1)S(1)}, bf16[2,256,768]{2,1,0:T(8,128)(2,1)S(1)}, bf16[2,256,192]{2,1,0:T(8,128)(2,1)S(1)}, f32[768,768]{1,0:T(...) custom-call(bf16[512,768]{1,0:T(8,128)(2,1)S(1)} %copy-done, ...), custom_call_target="tpu_custom_call" | custom-call | flops 1 | bytes 1000 | tf_op jit(solution)/shard_map/mlp_near/pallas_call | solution.py:62
  23.5 0.3 collective-permute-done.5.refs_1_
  23.8 0.5 collective-permute-done.3.refs_0_.refs_5_
  24.4 0.5 collective-permute-start.8
  24.9 1.5 collective-permute-start.10
  26.4 1.0 query.1
  27.4 5.8 %collective-permute-done.10.refs_5_ = bf16[1024,128]{1,0:T(8,128)(2,1)S(1)} collective-permute-done((bf16[1024,128]{1,0:T(8,128)(2,1)S(1)}, bf16[1024,128]{1,0:T(8,128)(2,1)S(1)}, u32[]{:S(2)}, u32[]{:S(2)}) %collective-permute-start.10) | collective-permute-done | bytes 262176 | tf_op jit(solution)/shard_map/ppermute | solution.py:184
  33.2 4.0 %attend.2 = (bf16[128,768]{1,0:T(8,128)(2,1)S(1)}, bf16[128,1152]{1,0:T(8,128)(2,1)S(1)}, bf16[128,960]{1,0:T(8,128)(2,1)S(1)}, f32[2048,128]{1,0:T(8,128)S(1)}) custom-call(s32[16]{0:T(128)S(1)} %copy-done.7, s32[1,4]{1,0:T(1,128)S(1)} %copy-done.8, bf16[768,256]{1,0:T(8,128)(2,1)S(1)} %get-tuple-element.100.refs_2_.refs_7_, ...), custom_call_target="tpu_custom_call" | custom-call | flops 2000000000 | bytes 1000 | tf_op jit(solution)/shard_map/attend/pallas_call | solution.py:62
  37.2 2.9 %collective-permute-done.11.refs_0_.refs_9_ = bf16[512,768]{1,0:T(8,128)(2,1)S(1)} collective-permute-done((bf16[512,768]{1,0:T(8,128)(2,1)}, bf16[512,768]{1,0:T(8,128)(2,1)S(1)}, u32[]{:S(2)}, u32[]{:S(2)}) %collective-permute-start.11) | collective-permute-done | bytes 786464 | tf_op jit(solution)/shard_map/ppermute | solution.py:184
  40.2 1.8 %collective-permute-start.16 = (bf16[128,1152]{1,0:T(8,128)(2,1)S(1)}, bf16[128,1152]{1,0:T(8,128)(2,1)S(1)}, u32[]{:S(2)}, u32[]{:S(2)}) collective-permute-start(bf16[128,1152]{1,0:T(8,128)(2,1)S(1)} %get-tuple-element.118), channel_id=1, source_target_pairs={{0,2},{1,3},{2,0},{3,1},{4,6},{5,7},{6,4},{7,5},{8,10},{9,11},{10,... | collective-permute-start | bytes 884744 | tf_op jit(solution)/shard_map/ppermute | solution.py:184
  42.0 0.5 collective-permute-done.12.refs_1_.refs_10_
  42.4 5.3 %mlp_far.1 = (bf16[2,256,768]{2,1,0:T(8,128)(2,1)S(1)}, bf16[2,256,768]{2,1,0:T(8,128)(2,1)S(1)}, bf16[2,256,192]{2,1,0:T(8,128)(2,1)S(1)}, bf16[384,768]{1,0:T(...) custom-call(bf16[512,768]{1,0:T(8,128)(2,1)S(1)} %collective-permute, ...), custom_call_target="tpu_custom_call" | custom-call | flops 8000000000 | bytes 1000 | tf_op jit(solution)/shard_map/mlp_far/pallas_call | solution.py:62
  47.8 4.3 %collective-permute-start.18 = (bf16[384,768]{1,0:T(8,128)(2,1)S(1)}, bf16[384,768]{1,0:T(8,128)(2,1)S(1)}, u32[]{:S(2)}, u32[]{:S(2)}) collective-permute-start(bf16[384,768]{1,0:T(8,128)(2,1)S(1)} %get-tuple-element.121), channel_id=1, source_target_pairs={{0,4},{4,0},{8,12},{12,8},{16,20},{20,16},{24,28},{28,24},{1,5},{5... | collective-permute-start | bytes 1769480 | tf_op jit(solution)/shard_map/ppermute | solution.py:184
  52.1 6.1 %attend.3 = (bf16[256,768]{1,0:T(8,128)(2,1)S(1)}, bf16[128,1152]{1,0:T(8,128)(2,1)S(1)}, bf16[256,960]{1,0:T(8,128)(2,1)S(1)}, bf16[1024,128]{1,0:T(8,128)(2,1)S(1)}, bf16[1024,128]{1,0:T(8,128)(2,1)S(1)}) custom-call(s32[16]{0:T(128)S(1)} %copy-done.7, s32[1,4]{1,0:T(1,128)S(1)} %copy-done.8, bf16[768,256]{1,0:T(8,128)(2,1)S(1)} %get-tuple-element.100.refs_2_.refs_7_, ...), custom_call_target="tpu_custom_call" | custom-call | flops 10000000000 | bytes 1000 | tf_op jit(solution)/shard_map/attend/pallas_call | solution.py:62
  58.2 2.3 %collective-permute-start.17 = (bf16[128,1152]{1,0:T(8,128)(2,1)S(1)}, bf16[128,1152]{1,0:T(8,128)(2,1)S(1)}, u32[]{:S(2)}, u32[]{:S(2)}) collective-permute-start(bf16[128,1152]{1,0:T(8,128)(2,1)S(1)} %get-tuple-element.119), channel_id=1, source_target_pairs={{0,2},{1,3},{2,0},{3,1},{4,6},{5,7},{6,4},{7,5},{8,10},{9,11},{10,... | collective-permute-start | bytes 884744 | tf_op jit(solution)/shard_map/ppermute | solution.py:184
  60.5 5.2 %collective-permute-done.18.refs_1_ = bf16[384,768]{1,0:T(8,128)(2,1)S(1)} collective-permute-done((bf16[384,768]{1,0:T(8,128)(2,1)S(1)}, bf16[384,768]{1,0:T(8,128)(2,1)S(1)}, u32[]{:S(2)}, u32[]{:S(2)}) %collective-permute-start.18) | collective-permute-done | bytes 589856 | tf_op jit(solution)/shard_map/ppermute | solution.py:184
  65.7 1.5 collective-permute-done.19.refs_3_
  67.2 0.3 stage.24
  67.7 6.0 %collective-permute-start.21 = (bf16[192,768]{1,0:T(8,128)(2,1)S(1)}, bf16[192,768]{1,0:T(8,128)(2,1)S(1)}, u32[]{:S(2)}, u32[]{:S(2)}) collective-permute-start(bf16[192,768]{1,0:T(8,128)(2,1)S(1)} %get-tuple-element.124.refs_2_), channel_id=1, source_target_pairs={{0,8},{4,12},{8,0},{12,4},{16,24},{20,28},{24,16},{28,20},{1,9},{5... | collective-permute-start | bytes 884744 | tf_op jit(solution)/shard_map/ppermute | solution.py:184
  73.7 0.2 collective-permute-start.24
  73.9 7.4 %collective-permute-done.21.refs_1_ = bf16[192,768]{1,0:T(8,128)(2,1)S(1)} collective-permute-done((bf16[192,768]{1,0:T(8,128)(2,1)S(1)}, bf16[192,768]{1,0:T(8,128)(2,1)S(1)}, u32[]{:S(2)}, u32[]{:S(2)}) %collective-permute-start.21) | collective-permute-done | bytes 294944 | tf_op jit(solution)/shard_map/ppermute | solution.py:184
  81.4 1.1 weight.1
  82.5 0.5 collective-permute-start.28
  83.0 1.6 %collective-permute-start.27 = (bf16[192,768]{1,0:T(8,128)(2,1)S(1)}, bf16[192,768]{1,0:T(8,128)(2,1)S(1)}, u32[]{:S(2)}, u32[]{:S(2)}) collective-permute-start(bf16[192,768]{1,0:T(8,128)(2,1)S(1)} %get-tuple-element.140), channel_id=1, source_target_pairs={{0,4},{4,0},{8,12},{12,8},{16,20},{20,16},{24,28},{28,24},{1,5},{5... | collective-permute-start | bytes 884744 | tf_op jit(solution)/shard_map/ppermute | solution.py:184
  84.6 5.0 %collective-permute-start.26 = (bf16[192,768]{1,0:T(8,128)(2,1)S(1)}, bf16[192,768]{1,0:T(8,128)(2,1)S(1)}, u32[]{:S(2)}, u32[]{:S(2)}) collective-permute-start(bf16[192,768]{1,0:T(8,128)(2,1)S(1)} %stage.25.refs_11_.refs_0_), channel_id=1, source_target_pairs={{0,16},{4,20},{8,24},{12,28},{16,0},{20,4},{24,8},{28,12},{1,17},{... | collective-permute-start | bytes 884744 | tf_op jit(solution)/shard_map/ppermute | solution.py:184
  89.7 0.3 collective-permute-start.22
  90.0 8.3 %collective-permute-done.22.refs_1_ = bf16[512,128]{1,0:T(8,128)(2,1)S(1)} collective-permute-done((bf16[512,128]{1,0:T(8,128)(2,1)S(1)}, bf16[512,128]{1,0:T(8,128)(2,1)S(1)}, u32[]{:S(2)}, u32[]{:S(2)}) %collective-permute-start.22) | collective-permute-done | bytes 131104 | tf_op jit(solution)/shard_map/ppermute | solution.py:184
  98.3 1.3 collective-permute-start.23
  99.5 4.9 %collective-permute-done.23.refs_8_ = bf16[256,128]{1,0:T(8,128)(2,1)S(1)} collective-permute-done((bf16[256,128]{1,0:T(8,128)(2,1)S(1)}, bf16[256,128]{1,0:T(8,128)(2,1)S(1)}, u32[]{:S(2)}, u32[]{:S(2)}) %collective-permute-start.23) | collective-permute-done | bytes 65568 | tf_op jit(solution)/shard_map/ppermute | solution.py:184
  104.5 1.1 tail.1
  105.8 1.6 collective-permute-start.30
  107.4 2.4 %collective-permute-start.33 = (bf16[192,768]{1,0:T(8,128)(2,1)S(1)}, bf16[192,768]{1,0:T(8,128)(2,1)S(1)}, u32[]{:S(2)}, u32[]{:S(2)}) collective-permute-start(bf16[192,768]{1,0:T(8,128)(2,1)S(1)} %stage.29.refs_2_.refs_0_), channel_id=1, source_target_pairs={{0,16},{4,20},{8,24},{12,28},{16,0},{20,4},{24,8},{28,12},{1,17},{... | collective-permute-start | bytes 884744 | tf_op jit(solution)/shard_map/ppermute | solution.py:184
  110.0 0.6 collective-permute-start.29
  110.7 13.6 %collective-permute-done.31.refs_1_ = bf16[96,768]{1,0:T(8,128)(2,1)S(1)} collective-permute-done((bf16[96,768]{1,0:T(8,128)(2,1)S(1)}, bf16[96,768]{1,0:T(8,128)(2,1)S(1)}, u32[]{:S(2)}, u32[]{:S(2)}) %collective-permute-start.31) | collective-permute-done | bytes 147488 | tf_op jit(solution)/shard_map/ppermute | solution.py:184
  124.4 0.4 collective-permute-start.34
  124.8 2.8 %collective-permute-start.36 = (bf16[96,768]{1,0:T(8,128)(2,1)S(1)}, bf16[96,768]{1,0:T(8,128)(2,1)S(1)}, u32[]{:S(2)}, u32[]{:S(2)}) collective-permute-start(bf16[96,768]{1,0:T(8,128)(2,1)S(1)} %stage.32.refs_2_.refs_0_), channel_id=1, source_target_pairs={{0,16},{4,20},{8,24},{12,28},{16,0},{20,4},{24,8},{28,12},{1,17},{... | collective-permute-start | bytes 442376 | tf_op jit(solution)/shard_map/ppermute | solution.py:184
  127.6 0.2 stage.35.refs_2_
  127.8 1.8 %collective-permute-done.34.refs_1_ = bf16[48,768]{1,0:T(8,128)(2,1)S(1)} collective-permute-done((bf16[48,768]{1,0:T(8,128)(2,1)S(1)}, bf16[48,768]{1,0:T(8,128)(2,1)S(1)}, u32[]{:S(2)}, u32[]{:S(2)}) %collective-permute-start.34) | collective-permute-done | bytes 73760 | tf_op jit(solution)/shard_map/ppermute | solution.py:184
  129.7 1.7 %collective-permute-start.35 = (bf16[192,768]{1,0:T(8,128)(2,1)S(1)}, bf16[192,768]{1,0:T(8,128)(2,1)S(1)}, u32[]{:S(2)}, u32[]{:S(2)}) collective-permute-start(bf16[192,768]{1,0:T(8,128)(2,1)S(1)} %stage.37.refs_2_.refs_0_), channel_id=1, source_target_pairs={{0,4},{4,0},{8,12},{12,8},{16,20},{20,16},{24,28},{28,24},{1,5},{5... | collective-permute-start | bytes 884744 | tf_op jit(solution)/shard_map/ppermute | solution.py:184
  131.4 1.1 collective-permute-done.36.refs_1_
  132.6 0.2 collective-permute-start.37
  132.8 1.7 %collective-permute-start.38 = (bf16[48,768]{1,0:T(8,128)(2,1)S(1)}, bf16[48,768]{1,0:T(8,128)(2,1)S(1)}, u32[]{:S(2)}, u32[]{:S(2)}) collective-permute-start(bf16[48,768]{1,0:T(8,128)(2,1)S(1)} %stage.36.refs_2_.refs_0_), channel_id=1, source_target_pairs={{0,4},{4,0},{8,12},{12,8},{16,20},{20,16},{24,28},{28,24},{1,5},{5... | collective-permute-start | bytes 221192 | tf_op jit(solution)/shard_map/ppermute | solution.py:184
  134.4 0.4 collective-permute-start.41
  134.8 6.4 %collective-permute-done.38.refs_1_ = bf16[48,768]{1,0:T(8,128)(2,1)S(1)} collective-permute-done((bf16[48,768]{1,0:T(8,128)(2,1)S(1)}, bf16[48,768]{1,0:T(8,128)(2,1)S(1)}, u32[]{:S(2)}, u32[]{:S(2)}) %collective-permute-start.38) | collective-permute-done | bytes 73760 | tf_op jit(solution)/shard_map/ppermute | solution.py:184
  141.4 1.8 %collective-permute-start.40 = (bf16[192,768]{1,0:T(8,128)(2,1)S(1)}, bf16[192,768]{1,0:T(8,128)(2,1)S(1)}, u32[]{:S(2)}, u32[]{:S(2)}) collective-permute-start(bf16[192,768]{1,0:T(8,128)(2,1)S(1)} %stage.40.refs_2_.refs_0_), channel_id=1, source_target_pairs={{0,4},{4,0},{8,12},{12,8},{16,20},{20,16},{24,28},{28,24},{1,5},{5... | collective-permute-start | bytes 884744 | tf_op jit(solution)/shard_map/ppermute | solution.py:184
  143.2 4.7 %collective-permute-start.39 = (bf16[48,768]{1,0:T(8,128)(2,1)S(1)}, bf16[48,768]{1,0:T(8,128)(2,1)S(1)}, u32[]{:S(2)}, u32[]{:S(2)}) collective-permute-start(bf16[48,768]{1,0:T(8,128)(2,1)S(1)} %stage.39.refs_2_.refs_0_), channel_id=1, source_target_pairs={{0,16},{4,20},{8,24},{12,28},{16,0},{20,4},{24,8},{28,12},{1,17},{... | collective-permute-start | bytes 221192 | tf_op jit(solution)/shard_map/ppermute | solution.py:184
  148.0 2.4 %collective-permute-done.39.refs_1_ = bf16[48,768]{1,0:T(8,128)(2,1)S(1)} collective-permute-done((bf16[48,768]{1,0:T(8,128)(2,1)S(1)}, bf16[48,768]{1,0:T(8,128)(2,1)S(1)}, u32[]{:S(2)}, u32[]{:S(2)}) %collective-permute-start.39) | collective-permute-done | bytes 73760 | tf_op jit(solution)/shard_map/ppermute | solution.py:184
  150.4 1.0 vector.1
  151.3 4.9 %collective-permute-done.40.refs_1_ = bf16[192,768]{1,0:T(8,128)(2,1)S(1)} collective-permute-done((bf16[192,768]{1,0:T(8,128)(2,1)S(1)}, bf16[192,768]{1,0:T(8,128)(2,1)S(1)}, u32[]{:S(2)}, u32[]{:S(2)}) %collective-permute-start.40) | collective-permute-done | bytes 294944 | tf_op jit(solution)/shard_map/ppermute | solution.py:184
  156.2 1.1 matrix.3
  157.3 1.5 matrix.4
  158.8 1.8 %output.1 = (bf16[256,768]{1,0:T(8,128)(2,1)}, bf16[256,768]{1,0:T(8,128)(2,1)}) custom-call(bf16[512,768]{1,0:T(8,128)(2,1)S(1)} %copy-done, bf16[256,768]{1,0:T(8,128)(2,1)S(1)} %get-tuple-element.109.refs_2_.refs_1_, bf16[768,768]{1,0:T(8,128)(2,1)S(1)} %get-tuple-element.110.refs_2_, f32[16,768]{1,0:T(8,128)S(1)} %get-tuple-element.93.refs_5_.refs_6_.refs_2_.refs_3_, ...), custom_call_target="tpu_custom_call" | custom-call | flops 1 | bytes 1000 | tf_op jit(solution)/shard_map/output/pallas_call | solution.py:62
  160.7 1.5 matrix.5
  (81 shorter events, 2.0 us)
Async XLA Ops:
  0.7 9.2 %copy-start.7 = (s32[16]{0:T(128)S(1)}, s32[16]{0:T(128)}, u32[]{:S(2)}) copy-start(s32[16]{0:T(128)} %refs_0_.3) | copy-start | bytes 196
  4.3 13.6 %collective-permute-start.4 = (bf16[896,768]{1,0:T(8,128)(2,1)}, bf16[896,768]{1,0:T(8,128)(2,1)S(1)}, u32[]{:S(2)}, u32[]{:S(2)}) collective-permute-start(bf16[896,768]{1,0:T(8,128)(2,1)} %get-tuple-element.95), channel_id=1, source_target_pairs={{0,1},{1,0},{2,3},{3,2},{4,5},{5,4},{6,7},{7,6},{8,9},{9,8},{10,11... | collective-permute-start | bytes 4128776 | tf_op jit(solution)/shard_map/ppermute | solution.py:184
  4.8 6.9 %collective-permute-start.1 = (bf16[144,192]{1,0:T(8,128)(2,1)}, bf16[144,192]{1,0:T(8,128)(2,1)S(1)}, u32[]{:S(2)}, u32[]{:S(2)}) collective-permute-start(bf16[144,192]{1,0:T(8,128)(2,1)} %get-tuple-element.91.refs_2_.refs_1_), channel_id=1, source_target_pairs={{0,1},{1,0},{2,3},{3,2},{4,5},{5,4},{6,7},{7,6},{8,9},{9,8},{10,11... | collective-permute-start | bytes 165896 | tf_op jit(solution)/shard_map/ppermute | solution.py:184
  4.9 5.9 %collective-permute-start = (bf16[144,192]{1,0:T(8,128)(2,1)}, bf16[144,192]{1,0:T(8,128)(2,1)S(1)}, u32[]{:S(2)}, u32[]{:S(2)}) collective-permute-start(bf16[144,192]{1,0:T(8,128)(2,1)} %get-tuple-element.91.refs_2_.refs_1_), channel_id=1, source_target_pairs={{0,2},{1,3},{2,0},{3,1},{4,6},{5,7},{6,4},{7,5},{8,10},{9,11},{10,... | collective-permute-start | bytes 165896 | tf_op jit(solution)/shard_map/ppermute | solution.py:184
  7.8 16.4 %collective-permute-start.3 = (bf16[384,768]{1,0:T(8,128)(2,1)}, bf16[384,768]{1,0:T(8,128)(2,1)S(1)}, u32[]{:S(2)}, u32[]{:S(2)}) collective-permute-start(bf16[384,768]{1,0:T(8,128)(2,1)} %get-tuple-element.94.refs_4_), channel_id=1, source_target_pairs={{0,2},{1,3},{2,0},{3,1},{4,6},{5,7},{6,4},{7,5},{8,10},{9,11},{10,... | collective-permute-start | bytes 1769480 | tf_op jit(solution)/shard_map/ppermute | solution.py:184
  7.9 32.2 %collective-permute-start.11 = (bf16[512,768]{1,0:T(8,128)(2,1)}, bf16[512,768]{1,0:T(8,128)(2,1)S(1)}, u32[]{:S(2)}, u32[]{:S(2)}) collective-permute-start(bf16[512,768]{1,0:T(8,128)(2,1)} %get-tuple-element.90.refs_0_.refs_1_.refs_7_), channel_id=1, source_target_pairs={{0,2},{1,3},{2,0},{3,1},{4,6},{5,7},{6,4},{7,5},{8,10},{9,11},{10,... | collective-permute-start | bytes 2359304 | tf_op jit(solution)/shard_map/ppermute | solution.py:184
  10.8 1.3 collective-permute-start.2
  10.8 0.9 copy-start.6
  11.7 1.0 copy-start.5
  11.7 6.8 %copy-start = (bf16[512,768]{1,0:T(8,128)(2,1)S(1)}, bf16[512,768]{1,0:T(8,128)(2,1)}, u32[]{:S(2)}) copy-start(bf16[512,768]{1,0:T(8,128)(2,1)} %get-tuple-element.90.refs_0_.refs_1_.refs_7_) | copy-start | bytes 2359300
  11.7 6.8 %copy-start.1 = (bf16[768,768]{1,0:T(8,128)(2,1)S(1)}, bf16[768,768]{1,0:T(8,128)(2,1)}, u32[]{:S(2)}) copy-start(bf16[768,768]{1,0:T(8,128)(2,1)} %refs_2_.5) | copy-start | bytes 3538948
  11.7 6.8 %copy-start.2 = (bf16[768,768]{1,0:T(8,128)(2,1)S(1)}, bf16[768,768]{1,0:T(8,128)(2,1)}, u32[]{:S(2)}) copy-start(bf16[768,768]{1,0:T(8,128)(2,1)} %refs_3_.5) | copy-start | bytes 3538948
  11.7 6.8 %copy-start.4 = (bf16[768]{0:T(1024)(128)(2,1)S(1)}, bf16[768]{0:T(1024)(128)(2,1)}, u32[]{:S(2)}) copy-start(bf16[768]{0:T(1024)(128)(2,1)} %refs_4_.5) | copy-start | bytes 4612
  13.6 9.9 %collective-permute-start.7 = (bf16[256,128]{1,0:T(8,128)(2,1)S(1)}, bf16[256,128]{1,0:T(8,128)(2,1)S(1)}, u32[]{:S(2)}, u32[]{:S(2)}) collective-permute-start(bf16[256,128]{1,0:T(8,128)(2,1)S(1)} %get-tuple-element.96.refs_0_), channel_id=1, source_target_pairs={{0,24},{4,28},{8,16},{12,20},{16,8},{20,12},{24,0},{28,4},{1,25},{... | collective-permute-start | bytes 196616 | tf_op jit(solution)/shard_map/ppermute | solution.py:184
  17.8 5.6 %collective-permute-start.6 = (bf16[256,128]{1,0:T(8,128)(2,1)S(1)}, bf16[256,128]{1,0:T(8,128)(2,1)S(1)}, u32[]{:S(2)}, u32[]{:S(2)}) collective-permute-start(bf16[256,128]{1,0:T(8,128)(2,1)S(1)} %get-tuple-element.96.refs_0_), channel_id=1, source_target_pairs={{0,8},{4,12},{8,0},{12,4},{16,24},{20,28},{24,16},{28,20},{1,9},{5... | collective-permute-start | bytes 196616 | tf_op jit(solution)/shard_map/ppermute | solution.py:184
  17.9 5.9 %collective-permute-start.5 = (bf16[256,128]{1,0:T(8,128)(2,1)S(1)}, bf16[256,128]{1,0:T(8,128)(2,1)S(1)}, u32[]{:S(2)}, u32[]{:S(2)}) collective-permute-start(bf16[256,128]{1,0:T(8,128)(2,1)S(1)} %get-tuple-element.96.refs_0_), channel_id=1, source_target_pairs={{0,16},{4,20},{8,24},{12,28},{16,0},{20,4},{24,8},{28,12},{1,17},{... | collective-permute-start | bytes 196616 | tf_op jit(solution)/shard_map/ppermute | solution.py:184
  23.4 3.0 %copy-start.3 = (bf16[384,768]{1,0:T(8,128)(2,1)S(1)}, bf16[384,768]{1,0:T(8,128)(2,1)}, u32[]{:S(2)}) copy-start(bf16[384,768]{1,0:T(8,128)(2,1)} %get-tuple-element.94.refs_4_) | copy-start | bytes 1769476
  24.3 2.1 %collective-permute-start.9 = (bf16[192,768]{1,0:T(8,128)(2,1)S(1)}, bf16[192,768]{1,0:T(8,128)(2,1)S(1)}, u32[]{:S(2)}, u32[]{:S(2)}) collective-permute-start(bf16[192,768]{1,0:T(8,128)(2,1)S(1)} %get-tuple-element.99), channel_id=1, source_target_pairs={{0,1},{1,0},{2,3},{3,2},{4,5},{5,4},{6,7},{7,6},{8,9},{9,8},{10,11... | collective-permute-start | bytes 884744 | tf_op jit(solution)/shard_map/ppermute | solution.py:184
  24.4 2.0 %collective-permute-start.8 = (bf16[192,768]{1,0:T(8,128)(2,1)S(1)}, bf16[192,768]{1,0:T(8,128)(2,1)S(1)}, u32[]{:S(2)}, u32[]{:S(2)}) collective-permute-start(bf16[192,768]{1,0:T(8,128)(2,1)S(1)} %get-tuple-element.98.refs_9_), channel_id=1, source_target_pairs={{0,1},{1,0},{2,3},{3,2},{4,5},{5,4},{6,7},{7,6},{8,9},{9,8},{10,11... | collective-permute-start | bytes 884744 | tf_op jit(solution)/shard_map/ppermute | solution.py:184
  24.9 8.3 %collective-permute-start.10 = (bf16[1024,128]{1,0:T(8,128)(2,1)S(1)}, bf16[1024,128]{1,0:T(8,128)(2,1)S(1)}, u32[]{:S(2)}, u32[]{:S(2)}) collective-permute-start(bf16[1024,128]{1,0:T(8,128)(2,1)S(1)} %stage.21.refs_1_.refs_4_), channel_id=1, source_target_pairs={{0,4},{4,0},{8,12},{12,8},{16,20},{20,16},{24,28},{28,24},{1,5},{5... | collective-permute-start | bytes 786440 | tf_op jit(solution)/shard_map/ppermute | solution.py:184
  26.4 15.6 %collective-permute-start.13 = (bf16[2,256,768]{2,1,0:T(8,128)(2,1)S(1)}, bf16[2,256,768]{2,1,0:T(8,128)(2,1)S(1)}, u32[]{:S(2)}, u32[]{:S(2)}) collective-permute-start(bf16[2,256,768]{2,1,0:T(8,128)(2,1)S(1)} %get-tuple-element.107), channel_id=1, source_target_pairs={{0,1},{1,0},{2,3},{3,2},{4,5},{5,4},{6,7},{7,6},{8,9},{9,8},{10,11... | collective-permute-start | bytes 2359304 | tf_op jit(solution)/shard_map/ppermute | solution.py:184
  26.4 6.8 %copy-start.8 = (s32[1,4]{1,0:T(1,128)S(1)}, s32[1,4]{1,0:T(1,128)}, u32[]{:S(2)}) copy-start(s32[1,4]{1,0:T(1,128)} %refs_1_.3) | copy-start | bytes 52
  40.1 2.4 %collective-permute-start.12 = (bf16[512,768]{1,0:T(8,128)(2,1)S(1)}, bf16[512,768]{1,0:T(8,128)(2,1)S(1)}, u32[]{:S(2)}, u32[]{:S(2)}) collective-permute-start(bf16[512,768]{1,0:T(8,128)(2,1)S(1)} %stage.23.refs_9_), channel_id=1, source_target_pairs={{0,1},{1,0},{2,3},{3,2},{4,5},{5,4},{6,7},{7,6},{8,9},{9,8},{10,11... | collective-permute-start | bytes 2359304 | tf_op jit(solution)/shard_map/ppermute | solution.py:184
  40.2 27.3 %collective-permute-start.16 = (bf16[128,1152]{1,0:T(8,128)(2,1)S(1)}, bf16[128,1152]{1,0:T(8,128)(2,1)S(1)}, u32[]{:S(2)}, u32[]{:S(2)}) collective-permute-start(bf16[128,1152]{1,0:T(8,128)(2,1)S(1)} %get-tuple-element.118), channel_id=1, source_target_pairs={{0,2},{1,3},{2,0},{3,1},{4,6},{5,7},{6,4},{7,5},{8,10},{9,11},{10,... | collective-permute-start | bytes 884744 | tf_op jit(solution)/shard_map/ppermute | solution.py:184
  47.8 18.0 %collective-permute-start.18 = (bf16[384,768]{1,0:T(8,128)(2,1)S(1)}, bf16[384,768]{1,0:T(8,128)(2,1)S(1)}, u32[]{:S(2)}, u32[]{:S(2)}) collective-permute-start(bf16[384,768]{1,0:T(8,128)(2,1)S(1)} %get-tuple-element.121), channel_id=1, source_target_pairs={{0,4},{4,0},{8,12},{12,8},{16,20},{20,16},{24,28},{28,24},{1,5},{5... | collective-permute-start | bytes 1769480 | tf_op jit(solution)/shard_map/ppermute | solution.py:184
  52.1 15.1 %collective-permute-start.19 = (bf16[384,768]{1,0:T(8,128)(2,1)S(1)}, bf16[384,768]{1,0:T(8,128)(2,1)S(1)}, u32[]{:S(2)}, u32[]{:S(2)}) collective-permute-start(bf16[384,768]{1,0:T(8,128)(2,1)S(1)} %get-tuple-element.123), channel_id=1, source_target_pairs={{0,8},{4,12},{8,0},{12,4},{16,24},{20,28},{24,16},{28,20},{1,9},{5... | collective-permute-start | bytes 1769480 | tf_op jit(solution)/shard_map/ppermute | solution.py:184
  58.2 9.3 %collective-permute-start.17 = (bf16[128,1152]{1,0:T(8,128)(2,1)S(1)}, bf16[128,1152]{1,0:T(8,128)(2,1)S(1)}, u32[]{:S(2)}, u32[]{:S(2)}) collective-permute-start(bf16[128,1152]{1,0:T(8,128)(2,1)S(1)} %get-tuple-element.119), channel_id=1, source_target_pairs={{0,2},{1,3},{2,0},{3,1},{4,6},{5,7},{6,4},{7,5},{8,10},{9,11},{10,... | collective-permute-start | bytes 884744 | tf_op jit(solution)/shard_map/ppermute | solution.py:184
  60.5 20.9 %collective-permute-start.15 = (bf16[256,960]{1,0:T(8,128)(2,1)S(1)}, bf16[256,960]{1,0:T(8,128)(2,1)S(1)}, u32[]{:S(2)}, u32[]{:S(2)}) collective-permute-start(bf16[256,960]{1,0:T(8,128)(2,1)S(1)} %get-tuple-element.111.refs_3_.refs_2_), channel_id=1, source_target_pairs={{0,1},{1,0},{2,3},{3,2},{4,5},{5,4},{6,7},{7,6},{8,9},{9,8},{10,11... | collective-permute-start | bytes 1474568 | tf_op jit(solution)/shard_map/ppermute | solution.py:184
  67.6 13.7 %collective-permute-start.20 = (bf16[256,960]{1,0:T(8,128)(2,1)S(1)}, bf16[256,960]{1,0:T(8,128)(2,1)S(1)}, u32[]{:S(2)}, u32[]{:S(2)}) collective-permute-start(bf16[256,960]{1,0:T(8,128)(2,1)S(1)} %get-tuple-element.126), channel_id=1, source_target_pairs={{0,1},{1,0},{2,3},{3,2},{4,5},{5,4},{6,7},{7,6},{8,9},{9,8},{10,11... | collective-permute-start | bytes 1474568 | tf_op jit(solution)/shard_map/ppermute | solution.py:184
  67.7 13.6 %collective-permute-start.21 = (bf16[192,768]{1,0:T(8,128)(2,1)S(1)}, bf16[192,768]{1,0:T(8,128)(2,1)S(1)}, u32[]{:S(2)}, u32[]{:S(2)}) collective-permute-start(bf16[192,768]{1,0:T(8,128)(2,1)S(1)} %get-tuple-element.124.refs_2_), channel_id=1, source_target_pairs={{0,8},{4,12},{8,0},{12,4},{16,24},{20,28},{24,16},{28,20},{1,9},{5... | collective-permute-start | bytes 884744 | tf_op jit(solution)/shard_map/ppermute | solution.py:184
  73.7 15.9 %collective-permute-start.14 = (bf16[1024,128]{1,0:T(8,128)(2,1)S(1)}, bf16[1024,128]{1,0:T(8,128)(2,1)S(1)}, u32[]{:S(2)}, u32[]{:S(2)}) collective-permute-start(bf16[1024,128]{1,0:T(8,128)(2,1)S(1)} %get-tuple-element.115), channel_id=1, source_target_pairs={{0,4},{4,0},{8,12},{12,8},{16,20},{20,16},{24,28},{28,24},{1,5},{5... | collective-permute-start | bytes 786440 | tf_op jit(solution)/shard_map/ppermute | solution.py:184
  73.7 53.9 %collective-permute-start.24 = (bf16[2,256,768]{2,1,0:T(8,128)(2,1)S(1)}, bf16[2,256,768]{2,1,0:T(8,128)(2,1)S(1)}, u32[]{:S(2)}, u32[]{:S(2)}) collective-permute-start(bf16[2,256,768]{2,1,0:T(8,128)(2,1)S(1)} %get-tuple-element.136), channel_id=1, source_target_pairs={{0,1},{1,0},{2,3},{3,2},{4,5},{5,4},{6,7},{7,6},{8,9},{9,8},{10,11... | collective-permute-start | bytes 2359304 | tf_op jit(solution)/shard_map/ppermute | solution.py:184
  82.5 23.0 %collective-permute-start.28 = (bf16[192,768]{1,0:T(8,128)(2,1)S(1)}, bf16[192,768]{1,0:T(8,128)(2,1)S(1)}, u32[]{:S(2)}, u32[]{:S(2)}) collective-permute-start(bf16[192,768]{1,0:T(8,128)(2,1)S(1)} %get-tuple-element.141), channel_id=1, source_target_pairs={{0,4},{4,0},{8,12},{12,8},{16,20},{20,16},{24,28},{28,24},{1,5},{5... | collective-permute-start | bytes 884744 | tf_op jit(solution)/shard_map/ppermute | solution.py:184
  83.0 22.7 %collective-permute-start.27 = (bf16[192,768]{1,0:T(8,128)(2,1)S(1)}, bf16[192,768]{1,0:T(8,128)(2,1)S(1)}, u32[]{:S(2)}, u32[]{:S(2)}) collective-permute-start(bf16[192,768]{1,0:T(8,128)(2,1)S(1)} %get-tuple-element.140), channel_id=1, source_target_pairs={{0,4},{4,0},{8,12},{12,8},{16,20},{20,16},{24,28},{28,24},{1,5},{5... | collective-permute-start | bytes 884744 | tf_op jit(solution)/shard_map/ppermute | solution.py:184
  84.6 21.1 %collective-permute-start.26 = (bf16[192,768]{1,0:T(8,128)(2,1)S(1)}, bf16[192,768]{1,0:T(8,128)(2,1)S(1)}, u32[]{:S(2)}, u32[]{:S(2)}) collective-permute-start(bf16[192,768]{1,0:T(8,128)(2,1)S(1)} %stage.25.refs_11_.refs_0_), channel_id=1, source_target_pairs={{0,16},{4,20},{8,24},{12,28},{16,0},{20,4},{24,8},{28,12},{1,17},{... | collective-permute-start | bytes 884744 | tf_op jit(solution)/shard_map/ppermute | solution.py:184
  89.7 8.6 %collective-permute-start.22 = (bf16[512,128]{1,0:T(8,128)(2,1)S(1)}, bf16[512,128]{1,0:T(8,128)(2,1)S(1)}, u32[]{:S(2)}, u32[]{:S(2)}) collective-permute-start(bf16[512,128]{1,0:T(8,128)(2,1)S(1)} %get-tuple-element.130.refs_2_), channel_id=1, source_target_pairs={{0,8},{4,12},{8,0},{12,4},{16,24},{20,28},{24,16},{28,20},{1,9},{5... | collective-permute-start | bytes 393224 | tf_op jit(solution)/shard_map/ppermute | solution.py:184
  98.3 6.2 %collective-permute-start.23 = (bf16[256,128]{1,0:T(8,128)(2,1)S(1)}, bf16[256,128]{1,0:T(8,128)(2,1)S(1)}, u32[]{:S(2)}, u32[]{:S(2)}) collective-permute-start(bf16[256,128]{1,0:T(8,128)(2,1)S(1)} %get-tuple-element.132.refs_10_), channel_id=1, source_target_pairs={{0,16},{4,20},{8,24},{12,28},{16,0},{20,4},{24,8},{28,12},{1,17},{... | collective-permute-start | bytes 196616 | tf_op jit(solution)/shard_map/ppermute | solution.py:184
  105.8 18.5 %collective-permute-start.30 = (bf16[192,768]{1,0:T(8,128)(2,1)S(1)}, bf16[192,768]{1,0:T(8,128)(2,1)S(1)}, u32[]{:S(2)}, u32[]{:S(2)}) collective-permute-start(bf16[192,768]{1,0:T(8,128)(2,1)S(1)} %stage.30.refs_2_.refs_0_), channel_id=1, source_target_pairs={{0,8},{4,12},{8,0},{12,4},{16,24},{20,28},{24,16},{28,20},{1,9},{5... | collective-permute-start | bytes 884744 | tf_op jit(solution)/shard_map/ppermute | solution.py:184
  107.4 2.6 %collective-permute-start.25 = (bf16[96,768]{1,0:T(8,128)(2,1)S(1)}, bf16[96,768]{1,0:T(8,128)(2,1)S(1)}, u32[]{:S(2)}, u32[]{:S(2)}) collective-permute-start(bf16[96,768]{1,0:T(8,128)(2,1)S(1)} %get-tuple-element.138), channel_id=1, source_target_pairs={{0,1},{1,0},{2,3},{3,2},{4,5},{5,4},{6,7},{7,6},{8,9},{9,8},{10,11... | collective-permute-start | bytes 442376 | tf_op jit(solution)/shard_map/ppermute | solution.py:184
  107.4 22.2 %collective-permute-start.33 = (bf16[192,768]{1,0:T(8,128)(2,1)S(1)}, bf16[192,768]{1,0:T(8,128)(2,1)S(1)}, u32[]{:S(2)}, u32[]{:S(2)}) collective-permute-start(bf16[192,768]{1,0:T(8,128)(2,1)S(1)} %stage.29.refs_2_.refs_0_), channel_id=1, source_target_pairs={{0,16},{4,20},{8,24},{12,28},{16,0},{20,4},{24,8},{28,12},{1,17},{... | collective-permute-start | bytes 884744 | tf_op jit(solution)/shard_map/ppermute | solution.py:184
  109.8 14.5 %collective-permute-start.31 = (bf16[96,768]{1,0:T(8,128)(2,1)S(1)}, bf16[96,768]{1,0:T(8,128)(2,1)S(1)}, u32[]{:S(2)}, u32[]{:S(2)}) collective-permute-start(bf16[96,768]{1,0:T(8,128)(2,1)S(1)} %get-tuple-element.142.refs_2_), channel_id=1, source_target_pairs={{0,8},{4,12},{8,0},{12,4},{16,24},{20,28},{24,16},{28,20},{1,9},{5... | collective-permute-start | bytes 442376 | tf_op jit(solution)/shard_map/ppermute | solution.py:184
  110.0 14.4 %collective-permute-start.29 = (bf16[48,768]{1,0:T(8,128)(2,1)S(1)}, bf16[48,768]{1,0:T(8,128)(2,1)S(1)}, u32[]{:S(2)}, u32[]{:S(2)}) collective-permute-start(bf16[48,768]{1,0:T(8,128)(2,1)S(1)} %get-tuple-element.144.refs_2_), channel_id=1, source_target_pairs={{0,2},{1,3},{2,0},{3,1},{4,6},{5,7},{6,4},{7,5},{8,10},{9,11},{10,... | collective-permute-start | bytes 221192 | tf_op jit(solution)/shard_map/ppermute | solution.py:184
  124.4 5.1 %collective-permute-start.34 = (bf16[48,768]{1,0:T(8,128)(2,1)S(1)}, bf16[48,768]{1,0:T(8,128)(2,1)S(1)}, u32[]{:S(2)}, u32[]{:S(2)}) collective-permute-start(bf16[48,768]{1,0:T(8,128)(2,1)S(1)} %stage.34.refs_2_.refs_0_), channel_id=1, source_target_pairs={{0,8},{4,12},{8,0},{12,4},{16,24},{20,28},{24,16},{28,20},{1,9},{5... | collective-permute-start | bytes 221192 | tf_op jit(solution)/shard_map/ppermute | solution.py:184
  124.8 7.7 %collective-permute-start.36 = (bf16[96,768]{1,0:T(8,128)(2,1)S(1)}, bf16[96,768]{1,0:T(8,128)(2,1)S(1)}, u32[]{:S(2)}, u32[]{:S(2)}) collective-permute-start(bf16[96,768]{1,0:T(8,128)(2,1)S(1)} %stage.32.refs_2_.refs_0_), channel_id=1, source_target_pairs={{0,16},{4,20},{8,24},{12,28},{16,0},{20,4},{24,8},{28,12},{1,17},{... | collective-permute-start | bytes 442376 | tf_op jit(solution)/shard_map/ppermute | solution.py:184
  129.7 11.6 %collective-permute-start.35 = (bf16[192,768]{1,0:T(8,128)(2,1)S(1)}, bf16[192,768]{1,0:T(8,128)(2,1)S(1)}, u32[]{:S(2)}, u32[]{:S(2)}) collective-permute-start(bf16[192,768]{1,0:T(8,128)(2,1)S(1)} %stage.37.refs_2_.refs_0_), channel_id=1, source_target_pairs={{0,4},{4,0},{8,12},{12,8},{16,20},{20,16},{24,28},{28,24},{1,5},{5... | collective-permute-start | bytes 884744 | tf_op jit(solution)/shard_map/ppermute | solution.py:184
  131.4 27.4 %collective-permute-start.32 = (bf16[2,256,768]{2,1,0:T(8,128)(2,1)S(1)}, bf16[2,256,768]{2,1,0:T(8,128)(2,1)S(1)}, u32[]{:S(2)}, u32[]{:S(2)}) collective-permute-start(bf16[2,256,768]{2,1,0:T(8,128)(2,1)S(1)} %stage.35.refs_2_), channel_id=1, source_target_pairs={{0,2},{1,3},{2,0},{3,1},{4,6},{5,7},{6,4},{7,5},{8,10},{9,11},{10,... | collective-permute-start | bytes 2359304 | tf_op jit(solution)/shard_map/ppermute | solution.py:184
  132.6 8.7 %collective-permute-start.37 = (bf16[96,768]{1,0:T(8,128)(2,1)S(1)}, bf16[96,768]{1,0:T(8,128)(2,1)S(1)}, u32[]{:S(2)}, u32[]{:S(2)}) collective-permute-start(bf16[96,768]{1,0:T(8,128)(2,1)S(1)} %stage.38.refs_2_.refs_0_), channel_id=1, source_target_pairs={{0,8},{4,12},{8,0},{12,4},{16,24},{20,28},{24,16},{28,20},{1,9},{5... | collective-permute-start | bytes 442376 | tf_op jit(solution)/shard_map/ppermute | solution.py:184
  132.8 8.5 %collective-permute-start.38 = (bf16[48,768]{1,0:T(8,128)(2,1)S(1)}, bf16[48,768]{1,0:T(8,128)(2,1)S(1)}, u32[]{:S(2)}, u32[]{:S(2)}) collective-permute-start(bf16[48,768]{1,0:T(8,128)(2,1)S(1)} %stage.36.refs_2_.refs_0_), channel_id=1, source_target_pairs={{0,4},{4,0},{8,12},{12,8},{16,20},{20,16},{24,28},{28,24},{1,5},{5... | collective-permute-start | bytes 221192 | tf_op jit(solution)/shard_map/ppermute | solution.py:184
  134.4 22.8 %collective-permute-start.41 = (bf16[384,768]{1,0:T(8,128)(2,1)S(1)}, bf16[384,768]{1,0:T(8,128)(2,1)S(1)}, u32[]{:S(2)}, u32[]{:S(2)}) collective-permute-start(bf16[384,768]{1,0:T(8,128)(2,1)S(1)} %stage.33.refs_2_.refs_0_), channel_id=1, source_target_pairs={{0,4},{4,0},{8,12},{12,8},{16,20},{20,16},{24,28},{28,24},{1,5},{5... | collective-permute-start | bytes 1769480 | tf_op jit(solution)/shard_map/ppermute | solution.py:184
  141.4 19.3 %collective-permute-start.42 = (bf16[384,768]{1,0:T(8,128)(2,1)S(1)}, bf16[384,768]{1,0:T(8,128)(2,1)S(1)}, u32[]{:S(2)}, u32[]{:S(2)}) collective-permute-start(bf16[384,768]{1,0:T(8,128)(2,1)S(1)} %stage.41.refs_8_.refs_2_.refs_0_), channel_id=1, source_target_pairs={{0,8},{4,12},{8,0},{12,4},{16,24},{20,28},{24,16},{28,20},{1,9},{5... | collective-permute-start | bytes 1769480 | tf_op jit(solution)/shard_map/ppermute | solution.py:184
  141.4 14.8 %collective-permute-start.40 = (bf16[192,768]{1,0:T(8,128)(2,1)S(1)}, bf16[192,768]{1,0:T(8,128)(2,1)S(1)}, u32[]{:S(2)}, u32[]{:S(2)}) collective-permute-start(bf16[192,768]{1,0:T(8,128)(2,1)S(1)} %stage.40.refs_2_.refs_0_), channel_id=1, source_target_pairs={{0,4},{4,0},{8,12},{12,8},{16,20},{20,16},{24,28},{28,24},{1,5},{5... | collective-permute-start | bytes 884744 | tf_op jit(solution)/shard_map/ppermute | solution.py:184
  143.2 7.2 %collective-permute-start.39 = (bf16[48,768]{1,0:T(8,128)(2,1)S(1)}, bf16[48,768]{1,0:T(8,128)(2,1)S(1)}, u32[]{:S(2)}, u32[]{:S(2)}) collective-permute-start(bf16[48,768]{1,0:T(8,128)(2,1)S(1)} %stage.39.refs_2_.refs_0_), channel_id=1, source_target_pairs={{0,16},{4,20},{8,24},{12,28},{16,0},{20,4},{24,8},{28,12},{1,17},{... | collective-permute-start | bytes 221192 | tf_op jit(solution)/shard_map/ppermute | solution.py:184

commit v4 on v3

--- a/solution.py
+++ b/solution.py
@@ -611,7 +611,8 @@
 
 
 def output_kernel(both_ref, o_ref, wo_ref, vec_ref, dn1_ref, a_ref, b_ref, c_ref, *outs):
-    layer_ref, grad_ref = outs
+    layer_ref, grad_ref, mark = outs
+    mark[...] = jnp.zeros_like(mark)
     rows = o_ref.shape[0]
     x, dy = both_ref[:rows].astype(F32), both_ref[rows:].astype(F32)
     mlp = a_ref[0].astype(F32) + b_ref[0].astype(F32) + c_ref[0].astype(F32)
@@ -800,7 +801,8 @@
 
 
 def matrix_kernel(order, near_view, far_view, near_ref, far_ref, *refs):
-    outs, (held, sems) = refs[:-2], refs[-2:]
+    outs, (mark, held, sems) = refs[:-3], refs[-3:]
+    mark[...] = jnp.zeros_like(mark)
     seq_me = lax.axis_index("seq")
     shards = len(order)
     half = shards // 2
@@ -1030,7 +1032,7 @@
             ],
             limit=36 if slots <= 16 else 60,
             name="attend",
-            time=(2, 10)[side],
+            time=(2, 14)[side],
             grid=(HEADS // per_group,),
             in_specs=[
                 SMEM,
@@ -1045,6 +1047,22 @@
         )
 
     far_out = shape((BLOCK, width + 2 * part), BF)
+    def matrix(item, order, count):
+        near, far = item.pair()
+        each = 2 * near.rows // len(order)
+        views = [(view.start, view.rows) for view in (near, far)]
+        return run(
+            functools.partial(matrix_kernel, order, *views),
+            (shape((2 * near.rows // count, width), F32),) * count + (shape((8, 128), F32),),
+            (near.array, far.array),
+            [
+                pltpu.VMEM((len(order), each, width), F32),
+                pltpu.SemaphoreType.DMA((len(order),)),
+            ],
+            name="matrix",
+            out_specs=(HBM,) * count + (VMEM,),
+        )[:count]
+
     keep_a, send_a, n1a, early_up, early_dn, early_sums = run(
         functools.partial(mlp_kernel, None, False),
         (
@@ -1100,7 +1118,7 @@
         mlp_scratch + [pltpu.VMEM((hidden, width), F32)] * 2,
         limit=28,
         name="mlp_far",
-        time=8,
+        time=14,
         after=(back_a,),
     )
     up = Sum(upk, ups, up_bits, others(up_bits))
@@ -1122,6 +1140,7 @@
         name="relay",
     )
     z3 = swap(relay_z, "fsdp", 1)
+    flow(sequence, dkv)
     flow(sequence, up)
     qo_bits = sbits[:2]
     qo_order = shard_order(qo_bits)
@@ -1133,9 +1152,9 @@
         name="weight",
     )
     qo = Sum(qok, qos, qo_bits, others(qo_bits), small=True)
-    flow(sequence, dkv)
     while dkv.left():
         flow(sequence, dkv)
+    flow(sequence, dn)
     mixed = shape((48 * fsdp // 2, width), BF)
     dn1, near_t, far_t = run(
         functools.partial(tail_kernel, rels),
@@ -1145,14 +1164,12 @@
         name="tail",
     )
     mix = Mix(near_t, far_t, fbits, [sbits[1], sbits[0], sbits[2]] + sbits[3:])
-    flow(sequence, qo)
-    flow(sequence, dn)
     while up.left() > 2:
         flow(sequence, up)
     flow(sequence, up)
+    flow(sequence, qo)
     flow(sequence, mix)
-    flow(sequence, qo)
-    flow(sequence, up)
+    flow(sequence, qo, up)
     flow(sequence, mix)
     back_b = swap(send_b, "fsdp", 1)
     back = sequence.stage([(merge_step, [View(keep_b), View(back_b)], 1)])[0, 0].array
@@ -1162,36 +1179,20 @@
         flow(sequence, dn)
     flow(sequence, dn)
     flow(sequence, qo)
+    while mix.left() > 1:
+        flow(sequence, mix)
     flow(sequence, mix)
+    while qo.left() > 1:
+        flow(sequence, qo)
     flow(sequence, qo)
     flow(sequence, dn)
-    layer_out, grad_tokens = run(
+    layer_out, grad_tokens, _ = run(
         output_kernel,
-        (shape((rows, width), BF),) * 2,
+        (shape((rows, width), BF),) * 2 + (shape((8, 128), F32),),
         (both_0, own, wo, vec, dn1, keep_a, back_a, back),
         name="output",
-        token=False,
-    )
-    while up.left() + dn.left() + qo.left() + mix.left():
-        flow(sequence, *[item for item in (qo, mix, up, dn) if item.left()])
-
-    def matrix(item, order, count):
-        near, far = item.pair()
-        each = 2 * near.rows // len(order)
-        views = [(view.start, view.rows) for view in (near, far)]
-        return run(
-            functools.partial(matrix_kernel, order, *views),
-            (shape((2 * near.rows // count, width), F32),) * count,
-            (near.array, far.array),
-            [
-                pltpu.VMEM((len(order), each, width), F32),
-                pltpu.SemaphoreType.DMA((len(order),)),
-            ],
-            name="matrix",
-            token=False,
-            out_specs=(HBM,) * count,
-        )
-
+    )
+    (grad_up,) = matrix(up, seq_orders[0], 1)
     vector = shape((part,), F32)
     g1, b1, qb, kb, vb, ob, g2, b2, ub, db, wk, wv = run(
         functools.partial(vector_kernel, *[v.start for v in mix.pair()]),
@@ -1211,11 +1212,9 @@
         ),
         tuple(v.array for v in mix.pair()),
         limit=16,
-        token=False,
         name="vector",
     )
     grad_query, grad_out = matrix(qo, qo_order, 2)
-    (grad_up,) = matrix(up, seq_orders[0], 1)
     (grad_down,) = matrix(dn, seq_orders[1], 1)
     return (
         layer_out.reshape(1, rows, width),

time: 162 us -> 155 us (0.957)
  waiting for transfers between devices: 68.5 us -> 57.8 us
  Pallas kernels: 36.3 us -> 38.9 us
    ppermute x43, waiting for transfers between devices: 68.5 us -> 57.8 us  [swap(): return lax.ppermute(value, axis, [(i, i ^ bit) for i in range(size)])]
    pallas_call x37 -> x36, Pallas kernels: 36.3 us -> 38.9 us  [run(): pl.pallas_call(body, out_shape=outs, in_specs=list(specs.get('in_specs',...]
  transfers between devices with their start and end apart: 43 -> 43, of which waited for: 18 -> 19; matrix products, arithmetic and copies ran while one was open for 0% -> 0% of each run, Pallas kernels for 19% -> 21%
where the time goes in v4:
time: 155 us
  waiting for transfers between devices  57.8 us (37%)
  starting transfers between devices  54.5 us (35%)
  Pallas kernels  38.9 us (25%)
  local copies, waits for them, and re-layouts  2.2 us (1%)
    ppermute x43, waiting for transfers between devices, swap(): return lax.ppermute(value, axis, [(i, i ^ bit) for i in range(size)])  57.8 us
    ppermute x43, starting transfers between devices, swap(): return lax.ppermute(value, axis, [(i, i ^ bit) for i in range(size)])  54.5 us
    pallas_call x36, Pallas kernels, run(): pl.pallas_call(body, out_shape=outs, in_specs=list(specs.get('in_specs',...  38.9 us
  transfers between devices with their start and end apart: 43, of which 19 were waited for; matrix products, arithmetic and copies ran while one was open for 0% of the time, Pallas kernels for 21%

profile of v4, /device:TPU:0, one launch (start us, length us, event | category | flops | bytes accessed | tf_op | source)
XLA Modules:
  0.0 155.0 jit_solution(5138087072223827229)
XLA Ops:
  0.7 3.5 %pack.1 = (bf16[144,192]{1,0:T(8,128)(2,1)}, bf16[512,768]{1,0:T(8,128)(2,1)}, bf16[384,768]{1,0:T(8,128)(2,1)}, bf16[896,768]{1,0:T(8,128)(2,1)}) custom-call(bf16[256,768]{1,0:T(8,128)(2,1)} %bitcast.10, bf16[256,768]{1,0:T(8,128)(2,1)} %bitcast.12, bf16[192,768]{1,0:T(8,128)(2,1)} %refs_2_.3, bf16[192,768]{1,0:T(8,128)(2,1)} %refs_3_.3, ...), custom_call_target="tpu_custom_call" | custom-call | flops 2000000000 | bytes 1000 | tf_op jit(solution)/shard_map/pack/pallas_call | solution.py:62
  4.2 0.5 collective-permute-start.4
  4.8 2.9 %collective-permute-start = (bf16[144,192]{1,0:T(8,128)(2,1)}, bf16[144,192]{1,0:T(8,128)(2,1)S(1)}, u32[]{:S(2)}, u32[]{:S(2)}) collective-permute-start(bf16[144,192]{1,0:T(8,128)(2,1)} %get-tuple-element.98.refs_2_.refs_1_), channel_id=1, source_target_pairs={{0,2},{1,3},{2,0},{3,1},{4,6},{5,7},{6,4},{7,5},{8,10},{9,11},{10,... | collective-permute-start | bytes 165896 | tf_op jit(solution)/shard_map/ppermute | solution.py:184
  7.8 2.0 %collective-permute-start.11 = (bf16[512,768]{1,0:T(8,128)(2,1)}, bf16[512,768]{1,0:T(8,128)(2,1)S(1)}, u32[]{:S(2)}, u32[]{:S(2)}) collective-permute-start(bf16[512,768]{1,0:T(8,128)(2,1)} %get-tuple-element.97.refs_0_.refs_1_.refs_7_), channel_id=1, source_target_pairs={{0,2},{1,3},{2,0},{3,1},{4,6},{5,7},{6,4},{7,5},{8,10},{9,11},{10,... | collective-permute-start | bytes 2359304 | tf_op jit(solution)/shard_map/ppermute | solution.py:184
  10.1 0.6 collective-permute-done.refs_2_
  10.7 0.9 copy-done.7
  12.0 0.6 copy-done.6
  12.6 0.9 front.1
  13.5 4.3 %collective-permute-start.7 = (bf16[256,128]{1,0:T(8,128)(2,1)S(1)}, bf16[256,128]{1,0:T(8,128)(2,1)S(1)}, u32[]{:S(2)}, u32[]{:S(2)}) collective-permute-start(bf16[256,128]{1,0:T(8,128)(2,1)S(1)} %get-tuple-element.103.refs_0_), channel_id=1, source_target_pairs={{0,24},{4,28},{8,16},{12,20},{16,8},{20,12},{24,0},{28,4},{1,25},{... | collective-permute-start | bytes 196616 | tf_op jit(solution)/shard_map/ppermute | solution.py:184
  17.8 0.6 collective-permute-start.5
  18.4 4.9 %mlp_near.1 = (bf16[2,256,768]{2,1,0:T(8,128)(2,1)S(1)}, bf16[2,256,768]{2,1,0:T(8,128)(2,1)S(1)}, bf16[2,256,192]{2,1,0:T(8,128)(2,1)S(1)}, f32[768,768]{1,0:T(...) custom-call(bf16[512,768]{1,0:T(8,128)(2,1)S(1)} %copy-done, ...), custom_call_target="tpu_custom_call" | custom-call | flops 1 | bytes 1000 | tf_op jit(solution)/shard_map/mlp_near/pallas_call | solution.py:62
  23.7 0.5 collective-permute-done.3.refs_0_.refs_5_
  24.3 0.5 collective-permute-start.8
  24.8 1.5 collective-permute-start.10
  26.3 1.0 query.1
  27.3 5.8 %collective-permute-done.10.refs_5_ = bf16[1024,128]{1,0:T(8,128)(2,1)S(1)} collective-permute-done((bf16[1024,128]{1,0:T(8,128)(2,1)S(1)}, bf16[1024,128]{1,0:T(8,128)(2,1)S(1)}, u32[]{:S(2)}, u32[]{:S(2)}) %collective-permute-start.10) | collective-permute-done | bytes 262176 | tf_op jit(solution)/shard_map/ppermute | solution.py:184
  33.1 6.1 %attend.2 = (bf16[128,768]{1,0:T(8,128)(2,1)S(1)}, bf16[128,1152]{1,0:T(8,128)(2,1)S(1)}, bf16[128,960]{1,0:T(8,128)(2,1)S(1)}, f32[2048,128]{1,0:T(8,128)S(1)}) custom-call(s32[16]{0:T(128)S(1)} %copy-done.8, s32[1,4]{1,0:T(1,128)S(1)} %copy-done.9, bf16[768,256]{1,0:T(8,128)(2,1)S(1)} %get-tuple-element.107.refs_2_.refs_7_, ...), custom_call_target="tpu_custom_call" | custom-call | flops 2000000000 | bytes 1000 | tf_op jit(solution)/shard_map/attend/pallas_call | solution.py:62
  39.2 0.8 collective-permute-done.11.refs_0_.refs_9_
  40.0 0.6 collective-permute-start.12
  40.6 2.4 %collective-permute-start.15 = (bf16[128,1152]{1,0:T(8,128)(2,1)S(1)}, bf16[128,1152]{1,0:T(8,128)(2,1)S(1)}, u32[]{:S(2)}, u32[]{:S(2)}) collective-permute-start(bf16[128,1152]{1,0:T(8,128)(2,1)S(1)} %get-tuple-element.123), channel_id=1, source_target_pairs={{0,2},{1,3},{2,0},{3,1},{4,6},{5,7},{6,4},{7,5},{8,10},{9,11},{10,... | collective-permute-start | bytes 884744 | tf_op jit(solution)/shard_map/ppermute | solution.py:184
  43.0 5.3 %mlp_far.1 = (bf16[2,256,768]{2,1,0:T(8,128)(2,1)S(1)}, bf16[2,256,768]{2,1,0:T(8,128)(2,1)S(1)}, bf16[2,256,192]{2,1,0:T(8,128)(2,1)S(1)}, bf16[384,768]{1,0:T(...) custom-call(bf16[512,768]{1,0:T(8,128)(2,1)S(1)} %collective-permute, ...), custom_call_target="tpu_custom_call" | custom-call | flops 14000000000 | bytes 1000 | tf_op jit(solution)/shard_map/mlp_far/pallas_call | solution.py:62
  48.4 2.2 %collective-permute-start.17 = (bf16[384,768]{1,0:T(8,128)(2,1)S(1)}, bf16[384,768]{1,0:T(8,128)(2,1)S(1)}, u32[]{:S(2)}, u32[]{:S(2)}) collective-permute-start(bf16[384,768]{1,0:T(8,128)(2,1)S(1)} %get-tuple-element.126), channel_id=1, source_target_pairs={{0,4},{4,0},{8,12},{12,8},{16,20},{20,16},{24,28},{28,24},{1,5},{5... | collective-permute-start | bytes 1769480 | tf_op jit(solution)/shard_map/ppermute | solution.py:184
  50.6 3.7 %collective-permute-start.18 = (bf16[384,768]{1,0:T(8,128)(2,1)S(1)}, bf16[384,768]{1,0:T(8,128)(2,1)S(1)}, u32[]{:S(2)}, u32[]{:S(2)}) collective-permute-start(bf16[384,768]{1,0:T(8,128)(2,1)S(1)} %get-tuple-element.128), channel_id=1, source_target_pairs={{0,8},{4,12},{8,0},{12,4},{16,24},{20,28},{24,16},{28,20},{1,9},{5... | collective-permute-start | bytes 1769480 | tf_op jit(solution)/shard_map/ppermute | solution.py:184
  54.2 6.1 %attend.3 = (bf16[256,768]{1,0:T(8,128)(2,1)S(1)}, bf16[128,1152]{1,0:T(8,128)(2,1)S(1)}, bf16[256,960]{1,0:T(8,128)(2,1)S(1)}, bf16[1024,128]{1,0:T(8,128)(2,1)S(1)}, bf16[1024,128]{1,0:T(8,128)(2,1)S(1)}) custom-call(s32[16]{0:T(128)S(1)} %copy-done.8, s32[1,4]{1,0:T(1,128)S(1)} %copy-done.9, bf16[768,256]{1,0:T(8,128)(2,1)S(1)} %get-tuple-element.107.refs_2_.refs_7_, ...), custom_call_target="tpu_custom_call" | custom-call | flops 14000000000 | bytes 1000 | tf_op jit(solution)/shard_map/attend/pallas_call | solution.py:62
  60.6 3.6 %collective-permute-done.17.refs_1_ = bf16[384,768]{1,0:T(8,128)(2,1)S(1)} collective-permute-done((bf16[384,768]{1,0:T(8,128)(2,1)S(1)}, bf16[384,768]{1,0:T(8,128)(2,1)S(1)}, u32[]{:S(2)}, u32[]{:S(2)}) %collective-permute-start.17) | collective-permute-done | bytes 589856 | tf_op jit(solution)/shard_map/ppermute | solution.py:184
  64.2 3.4 %collective-permute-done.18.refs_3_ = bf16[384,768]{1,0:T(8,128)(2,1)S(1)} collective-permute-done((bf16[384,768]{1,0:T(8,128)(2,1)S(1)}, bf16[384,768]{1,0:T(8,128)(2,1)S(1)}, u32[]{:S(2)}, u32[]{:S(2)}) %collective-permute-start.18) | collective-permute-done | bytes 589856 | tf_op jit(solution)/shard_map/ppermute | solution.py:184
  67.9 1.1 collective-permute-done.16.refs_1_
  69.1 0.8 collective-permute-start.22
  69.9 0.4 collective-permute-start.14
  70.3 8.0 %collective-permute-done.14.refs_1_ = bf16[1024,128]{1,0:T(8,128)(2,1)S(1)} collective-permute-done((bf16[1024,128]{1,0:T(8,128)(2,1)S(1)}, bf16[1024,128]{1,0:T(8,128)(2,1)S(1)}, u32[]{:S(2)}, u32[]{:S(2)}) %collective-permute-start.14) | collective-permute-done | bytes 262176 | tf_op jit(solution)/shard_map/ppermute | solution.py:184
  78.3 0.4 collective-permute-start.24
  78.8 5.7 %collective-permute-start.28 = (bf16[192,768]{1,0:T(8,128)(2,1)S(1)}, bf16[192,768]{1,0:T(8,128)(2,1)S(1)}, u32[]{:S(2)}, u32[]{:S(2)}) collective-permute-start(bf16[192,768]{1,0:T(8,128)(2,1)S(1)} %stage.25.refs_11_.refs_0_), channel_id=1, source_target_pairs={{0,16},{4,20},{8,24},{12,28},{16,0},{20,4},{24,8},{28,12},{1,17},{... | collective-permute-start | bytes 884744 | tf_op jit(solution)/shard_map/ppermute | solution.py:184
  84.5 0.6 collective-permute-start.19
  85.1 1.1 weight.1
  86.2 1.5 collective-permute-start.27
  87.7 5.5 %collective-permute-done.19.refs_1_ = bf16[512,128]{1,0:T(8,128)(2,1)S(1)} collective-permute-done((bf16[512,128]{1,0:T(8,128)(2,1)S(1)}, bf16[512,128]{1,0:T(8,128)(2,1)S(1)}, u32[]{:S(2)}, u32[]{:S(2)}) %collective-permute-start.19) | collective-permute-done | bytes 131104 | tf_op jit(solution)/shard_map/ppermute | solution.py:184
  93.2 1.7 %collective-permute-start.23 = (bf16[256,128]{1,0:T(8,128)(2,1)S(1)}, bf16[256,128]{1,0:T(8,128)(2,1)S(1)}, u32[]{:S(2)}, u32[]{:S(2)}) collective-permute-start(bf16[256,128]{1,0:T(8,128)(2,1)S(1)} %get-tuple-element.139.refs_2_), channel_id=1, source_target_pairs={{0,16},{4,20},{8,24},{12,28},{16,0},{20,4},{24,8},{28,12},{1,17},{... | collective-permute-start | bytes 196616 | tf_op jit(solution)/shard_map/ppermute | solution.py:184
  95.0 4.5 %collective-permute-done.23.refs_8_ = bf16[256,128]{1,0:T(8,128)(2,1)S(1)} collective-permute-done((bf16[256,128]{1,0:T(8,128)(2,1)S(1)}, bf16[256,128]{1,0:T(8,128)(2,1)S(1)}, u32[]{:S(2)}, u32[]{:S(2)}) %collective-permute-start.23) | collective-permute-done | bytes 65568 | tf_op jit(solution)/shard_map/ppermute | solution.py:184
  99.5 1.1 tail.1
  100.7 1.5 collective-permute-start.31
  102.2 2.8 %collective-permute-start.33 = (bf16[192,768]{1,0:T(8,128)(2,1)S(1)}, bf16[192,768]{1,0:T(8,128)(2,1)S(1)}, u32[]{:S(2)}, u32[]{:S(2)}) collective-permute-start(bf16[192,768]{1,0:T(8,128)(2,1)S(1)} %stage.27.refs_10_.refs_0_), channel_id=1, source_target_pairs={{0,16},{4,20},{8,24},{12,28},{16,0},{20,4},{24,8},{28,12},{1,17},{... | collective-permute-start | bytes 884744 | tf_op jit(solution)/shard_map/ppermute | solution.py:184
  105.3 0.4 collective-permute-start.29
  105.7 9.7 %collective-permute-done.31.refs_3_ = bf16[192,768]{1,0:T(8,128)(2,1)S(1)} collective-permute-done((bf16[192,768]{1,0:T(8,128)(2,1)S(1)}, bf16[192,768]{1,0:T(8,128)(2,1)S(1)}, u32[]{:S(2)}, u32[]{:S(2)}) %collective-permute-start.31) | collective-permute-done | bytes 294944 | tf_op jit(solution)/shard_map/ppermute | solution.py:184
  115.4 2.8 %collective-permute-done.30.refs_1_ = bf16[96,768]{1,0:T(8,128)(2,1)S(1)} collective-permute-done((bf16[96,768]{1,0:T(8,128)(2,1)S(1)}, bf16[96,768]{1,0:T(8,128)(2,1)S(1)}, u32[]{:S(2)}, u32[]{:S(2)}) %collective-permute-start.30) | collective-permute-done | bytes 147488 | tf_op jit(solution)/shard_map/ppermute | solution.py:184
  118.3 1.3 collective-permute-start.34
  119.6 3.3 %collective-permute-start.36 = (bf16[96,768]{1,0:T(8,128)(2,1)S(1)}, bf16[96,768]{1,0:T(8,128)(2,1)S(1)}, u32[]{:S(2)}, u32[]{:S(2)}) collective-permute-start(bf16[96,768]{1,0:T(8,128)(2,1)S(1)} %get-tuple-element.153.refs_2_.refs_0_), channel_id=1, source_target_pairs={{0,16},{4,20},{8,24},{12,28},{16,0},{20,4},{24,8},{28,12},{1,17},{... | collective-permute-start | bytes 442376 | tf_op jit(solution)/shard_map/ppermute | solution.py:184
  123.1 0.4 collective-permute-done.34.refs_1_
  123.7 2.0 %collective-permute-start.35 = (bf16[192,768]{1,0:T(8,128)(2,1)S(1)}, bf16[192,768]{1,0:T(8,128)(2,1)S(1)}, u32[]{:S(2)}, u32[]{:S(2)}) collective-permute-start(bf16[192,768]{1,0:T(8,128)(2,1)S(1)} %stage.35.refs_2_.refs_0_), channel_id=1, source_target_pairs={{0,4},{4,0},{8,12},{12,8},{16,20},{20,16},{24,28},{28,24},{1,5},{5... | collective-permute-start | bytes 884744 | tf_op jit(solution)/shard_map/ppermute | solution.py:184
  125.6 0.5 collective-permute-start.32
  126.1 1.7 %collective-permute-done.36.refs_1_ = bf16[96,768]{1,0:T(8,128)(2,1)S(1)} collective-permute-done((bf16[96,768]{1,0:T(8,128)(2,1)S(1)}, bf16[96,768]{1,0:T(8,128)(2,1)S(1)}, u32[]{:S(2)}, u32[]{:S(2)}) %collective-permute-start.36) | collective-permute-done | bytes 147488 | tf_op jit(solution)/shard_map/ppermute | solution.py:184
  128.2 0.8 collective-permute-start.38
  128.9 1.2 collective-permute-start.40
  130.2 4.5 %collective-permute-done.38.refs_1_ = bf16[48,768]{1,0:T(8,128)(2,1)S(1)} collective-permute-done((bf16[48,768]{1,0:T(8,128)(2,1)S(1)}, bf16[48,768]{1,0:T(8,128)(2,1)S(1)}, u32[]{:S(2)}, u32[]{:S(2)}) %collective-permute-start.38) | collective-permute-done | bytes 73760 | tf_op jit(solution)/shard_map/ppermute | solution.py:184
  134.8 1.7 %collective-permute-start.42 = (bf16[384,768]{1,0:T(8,128)(2,1)S(1)}, bf16[384,768]{1,0:T(8,128)(2,1)S(1)}, u32[]{:S(2)}, u32[]{:S(2)}) collective-permute-start(bf16[384,768]{1,0:T(8,128)(2,1)S(1)} %stage.39.refs_8_.refs_0_), channel_id=1, source_target_pairs={{0,8},{4,12},{8,0},{12,4},{16,24},{20,28},{24,16},{28,20},{1,9},{5... | collective-permute-start | bytes 1769480 | tf_op jit(solution)/shard_map/ppermute | solution.py:184
  136.5 0.5 collective-permute-start.41
  137.0 5.3 %collective-permute-start.39 = (bf16[48,768]{1,0:T(8,128)(2,1)S(1)}, bf16[48,768]{1,0:T(8,128)(2,1)S(1)}, u32[]{:S(2)}, u32[]{:S(2)}) collective-permute-start(bf16[48,768]{1,0:T(8,128)(2,1)S(1)} %stage.37.refs_2_.refs_0_), channel_id=1, source_target_pairs={{0,16},{4,20},{8,24},{12,28},{16,0},{20,4},{24,8},{28,12},{1,17},{... | collective-permute-start | bytes 221192 | tf_op jit(solution)/shard_map/ppermute | solution.py:184
  142.4 1.9 %output.1 = (bf16[256,768]{1,0:T(8,128)(2,1)}, bf16[256,768]{1,0:T(8,128)(2,1)}, f32[8,128]{1,0:T(8,128)S(1)}) custom-call(bf16[512,768]{1,0:T(8,128)(2,1)S(1)} %copy-done, bf16[256,768]{1,0:T(8,128)(2,1)S(1)} %get-tuple-element.116.refs_2_.refs_1_, bf16[768,768]{1,0:T(8,128)(2,1)S(1)} %get-tuple-element.117.refs_2_, ...), custom_call_target="tpu_custom_call" | custom-call | flops 1 | bytes 1000 | tf_op jit(solution)/shard_map/output/pallas_call | solution.py:62
  144.2 3.1 %collective-permute-done.40.refs_1_ = bf16[384,768]{1,0:T(8,128)(2,1)S(1)} collective-permute-done((bf16[384,768]{1,0:T(8,128)(2,1)S(1)}, bf16[384,768]{1,0:T(8,128)(2,1)S(1)}, u32[]{:S(2)}, u32[]{:S(2)}) %collective-permute-start.40) | collective-permute-done | bytes 589856 | tf_op jit(solution)/shard_map/ppermute | solution.py:184
  147.3 1.5 matrix.3
  148.8 1.0 vector.1
  149.8 1.2 collective-permute-done.41.refs_1_
  151.0 0.7 copy-done.5
  151.6 1.1 matrix.4
  152.7 2.1 %matrix.5 = (f32[768,768]{1,0:T(8,128)}, f32[8,128]{1,0:T(8,128)}) custom-call(bf16[384,768]{1,0:T(8,128)(2,1)S(1)} %stage.39.refs_8_.refs_0_, bf16[384,768]{1,0:T(8,128)(2,1)S(1)} %collective-permute-done.42.refs_1_, f32[8,128]{1,0:T(8,128)S(1)} %get-tuple-element.173.refs_2_), custom_call_target="tpu_custom_call" | custom-call | flops 1 | bytes 1000 | tf_op jit(solution)/shard_map/matrix/pallas_call | solution.py:62
  (82 shorter events, 3.5 us)
Async XLA Ops:
  0.7 9.1 %copy-start.8 = (s32[16]{0:T(128)S(1)}, s32[16]{0:T(128)}, u32[]{:S(2)}) copy-start(s32[16]{0:T(128)} %refs_0_.3) | copy-start | bytes 196
  4.2 13.6 %collective-permute-start.4 = (bf16[896,768]{1,0:T(8,128)(2,1)}, bf16[896,768]{1,0:T(8,128)(2,1)S(1)}, u32[]{:S(2)}, u32[]{:S(2)}) collective-permute-start(bf16[896,768]{1,0:T(8,128)(2,1)} %get-tuple-element.102), channel_id=1, source_target_pairs={{0,1},{1,0},{2,3},{3,2},{4,5},{5,4},{6,7},{7,6},{8,9},{9,8},{10,11... | collective-permute-start | bytes 4128776 | tf_op jit(solution)/shard_map/ppermute | solution.py:184
  4.7 6.9 %collective-permute-start.1 = (bf16[144,192]{1,0:T(8,128)(2,1)}, bf16[144,192]{1,0:T(8,128)(2,1)S(1)}, u32[]{:S(2)}, u32[]{:S(2)}) collective-permute-start(bf16[144,192]{1,0:T(8,128)(2,1)} %get-tuple-element.98.refs_2_.refs_1_), channel_id=1, source_target_pairs={{0,1},{1,0},{2,3},{3,2},{4,5},{5,4},{6,7},{7,6},{8,9},{9,8},{10,11... | collective-permute-start | bytes 165896 | tf_op jit(solution)/shard_map/ppermute | solution.py:184
  4.8 5.9 %collective-permute-start = (bf16[144,192]{1,0:T(8,128)(2,1)}, bf16[144,192]{1,0:T(8,128)(2,1)S(1)}, u32[]{:S(2)}, u32[]{:S(2)}) collective-permute-start(bf16[144,192]{1,0:T(8,128)(2,1)} %get-tuple-element.98.refs_2_.refs_1_), channel_id=1, source_target_pairs={{0,2},{1,3},{2,0},{3,1},{4,6},{5,7},{6,4},{7,5},{8,10},{9,11},{10,... | collective-permute-start | bytes 165896 | tf_op jit(solution)/shard_map/ppermute | solution.py:184
  7.8 16.4 %collective-permute-start.3 = (bf16[384,768]{1,0:T(8,128)(2,1)}, bf16[384,768]{1,0:T(8,128)(2,1)S(1)}, u32[]{:S(2)}, u32[]{:S(2)}) collective-permute-start(bf16[384,768]{1,0:T(8,128)(2,1)} %get-tuple-element.101.refs_4_), channel_id=1, source_target_pairs={{0,2},{1,3},{2,0},{3,1},{4,6},{5,7},{6,4},{7,5},{8,10},{9,11},{10,... | collective-permute-start | bytes 1769480 | tf_op jit(solution)/shard_map/ppermute | solution.py:184
  7.8 32.2 %collective-permute-start.11 = (bf16[512,768]{1,0:T(8,128)(2,1)}, bf16[512,768]{1,0:T(8,128)(2,1)S(1)}, u32[]{:S(2)}, u32[]{:S(2)}) collective-permute-start(bf16[512,768]{1,0:T(8,128)(2,1)} %get-tuple-element.97.refs_0_.refs_1_.refs_7_), channel_id=1, source_target_pairs={{0,2},{1,3},{2,0},{3,1},{4,6},{5,7},{6,4},{7,5},{8,10},{9,11},{10,... | collective-permute-start | bytes 2359304 | tf_op jit(solution)/shard_map/ppermute | solution.py:184
  10.7 1.3 collective-permute-start.2
  10.7 0.9 copy-start.7
  11.6 1.0 copy-start.6
  11.6 6.8 %copy-start = (bf16[512,768]{1,0:T(8,128)(2,1)S(1)}, bf16[512,768]{1,0:T(8,128)(2,1)}, u32[]{:S(2)}) copy-start(bf16[512,768]{1,0:T(8,128)(2,1)} %get-tuple-element.97.refs_0_.refs_1_.refs_7_) | copy-start | bytes 2359300
  11.6 6.8 %copy-start.1 = (bf16[768,768]{1,0:T(8,128)(2,1)S(1)}, bf16[768,768]{1,0:T(8,128)(2,1)}, u32[]{:S(2)}) copy-start(bf16[768,768]{1,0:T(8,128)(2,1)} %refs_2_.5) | copy-start | bytes 3538948
  11.6 6.8 %copy-start.2 = (bf16[768,768]{1,0:T(8,128)(2,1)S(1)}, bf16[768,768]{1,0:T(8,128)(2,1)}, u32[]{:S(2)}) copy-start(bf16[768,768]{1,0:T(8,128)(2,1)} %refs_3_.5) | copy-start | bytes 3538948
  11.6 6.8 %copy-start.4 = (bf16[768]{0:T(1024)(128)(2,1)S(1)}, bf16[768]{0:T(1024)(128)(2,1)}, u32[]{:S(2)}) copy-start(bf16[768]{0:T(1024)(128)(2,1)} %refs_4_.5) | copy-start | bytes 4612
  13.5 9.9 %collective-permute-start.7 = (bf16[256,128]{1,0:T(8,128)(2,1)S(1)}, bf16[256,128]{1,0:T(8,128)(2,1)S(1)}, u32[]{:S(2)}, u32[]{:S(2)}) collective-permute-start(bf16[256,128]{1,0:T(8,128)(2,1)S(1)} %get-tuple-element.103.refs_0_), channel_id=1, source_target_pairs={{0,24},{4,28},{8,16},{12,20},{16,8},{20,12},{24,0},{28,4},{1,25},{... | collective-permute-start | bytes 196616 | tf_op jit(solution)/shard_map/ppermute | solution.py:184
  17.8 5.6 %collective-permute-start.6 = (bf16[256,128]{1,0:T(8,128)(2,1)S(1)}, bf16[256,128]{1,0:T(8,128)(2,1)S(1)}, u32[]{:S(2)}, u32[]{:S(2)}) collective-permute-start(bf16[256,128]{1,0:T(8,128)(2,1)S(1)} %get-tuple-element.103.refs_0_), channel_id=1, source_target_pairs={{0,8},{4,12},{8,0},{12,4},{16,24},{20,28},{24,16},{28,20},{1,9},{5... | collective-permute-start | bytes 196616 | tf_op jit(solution)/shard_map/ppermute | solution.py:184
  17.8 5.9 %collective-permute-start.5 = (bf16[256,128]{1,0:T(8,128)(2,1)S(1)}, bf16[256,128]{1,0:T(8,128)(2,1)S(1)}, u32[]{:S(2)}, u32[]{:S(2)}) collective-permute-start(bf16[256,128]{1,0:T(8,128)(2,1)S(1)} %get-tuple-element.103.refs_0_), channel_id=1, source_target_pairs={{0,16},{4,20},{8,24},{12,28},{16,0},{20,4},{24,8},{28,12},{1,17},{... | collective-permute-start | bytes 196616 | tf_op jit(solution)/shard_map/ppermute | solution.py:184
  23.3 3.0 %copy-start.3 = (bf16[384,768]{1,0:T(8,128)(2,1)S(1)}, bf16[384,768]{1,0:T(8,128)(2,1)}, u32[]{:S(2)}) copy-start(bf16[384,768]{1,0:T(8,128)(2,1)} %get-tuple-element.101.refs_4_) | copy-start | bytes 1769476
  24.2 2.1 %collective-permute-start.9 = (bf16[192,768]{1,0:T(8,128)(2,1)S(1)}, bf16[192,768]{1,0:T(8,128)(2,1)S(1)}, u32[]{:S(2)}, u32[]{:S(2)}) collective-permute-start(bf16[192,768]{1,0:T(8,128)(2,1)S(1)} %get-tuple-element.106), channel_id=1, source_target_pairs={{0,1},{1,0},{2,3},{3,2},{4,5},{5,4},{6,7},{7,6},{8,9},{9,8},{10,11... | collective-permute-start | bytes 884744 | tf_op jit(solution)/shard_map/ppermute | solution.py:184
  24.3 2.0 %collective-permute-start.8 = (bf16[192,768]{1,0:T(8,128)(2,1)S(1)}, bf16[192,768]{1,0:T(8,128)(2,1)S(1)}, u32[]{:S(2)}, u32[]{:S(2)}) collective-permute-start(bf16[192,768]{1,0:T(8,128)(2,1)S(1)} %get-tuple-element.105.refs_9_), channel_id=1, source_target_pairs={{0,1},{1,0},{2,3},{3,2},{4,5},{5,4},{6,7},{7,6},{8,9},{9,8},{10,11... | collective-permute-start | bytes 884744 | tf_op jit(solution)/shard_map/ppermute | solution.py:184
  24.8 8.3 %collective-permute-start.10 = (bf16[1024,128]{1,0:T(8,128)(2,1)S(1)}, bf16[1024,128]{1,0:T(8,128)(2,1)S(1)}, u32[]{:S(2)}, u32[]{:S(2)}) collective-permute-start(bf16[1024,128]{1,0:T(8,128)(2,1)S(1)} %stage.20.refs_1_.refs_4_), channel_id=1, source_target_pairs={{0,4},{4,0},{8,12},{12,8},{16,20},{20,16},{24,28},{28,24},{1,5},{5... | collective-permute-start | bytes 786440 | tf_op jit(solution)/shard_map/ppermute | solution.py:184
  26.3 16.7 %collective-permute-start.13 = (bf16[2,256,768]{2,1,0:T(8,128)(2,1)S(1)}, bf16[2,256,768]{2,1,0:T(8,128)(2,1)S(1)}, u32[]{:S(2)}, u32[]{:S(2)}) collective-permute-start(bf16[2,256,768]{2,1,0:T(8,128)(2,1)S(1)} %get-tuple-element.114), channel_id=1, source_target_pairs={{0,1},{1,0},{2,3},{3,2},{4,5},{5,4},{6,7},{7,6},{8,9},{9,8},{10,11... | collective-permute-start | bytes 2359304 | tf_op jit(solution)/shard_map/ppermute | solution.py:184
  26.3 6.8 %copy-start.9 = (s32[1,4]{1,0:T(1,128)S(1)}, s32[1,4]{1,0:T(1,128)}, u32[]{:S(2)}) copy-start(s32[1,4]{1,0:T(1,128)} %refs_1_.3) | copy-start | bytes 52
  40.0 3.0 %collective-permute-start.12 = (bf16[512,768]{1,0:T(8,128)(2,1)S(1)}, bf16[512,768]{1,0:T(8,128)(2,1)S(1)}, u32[]{:S(2)}, u32[]{:S(2)}) collective-permute-start(bf16[512,768]{1,0:T(8,128)(2,1)S(1)} %stage.22.refs_9_), channel_id=1, source_target_pairs={{0,1},{1,0},{2,3},{3,2},{4,5},{5,4},{6,7},{7,6},{8,9},{9,8},{10,11... | collective-permute-start | bytes 2359304 | tf_op jit(solution)/shard_map/ppermute | solution.py:184
  40.6 27.2 %collective-permute-start.15 = (bf16[128,1152]{1,0:T(8,128)(2,1)S(1)}, bf16[128,1152]{1,0:T(8,128)(2,1)S(1)}, u32[]{:S(2)}, u32[]{:S(2)}) collective-permute-start(bf16[128,1152]{1,0:T(8,128)(2,1)S(1)} %get-tuple-element.123), channel_id=1, source_target_pairs={{0,2},{1,3},{2,0},{3,1},{4,6},{5,7},{6,4},{7,5},{8,10},{9,11},{10,... | collective-permute-start | bytes 884744 | tf_op jit(solution)/shard_map/ppermute | solution.py:184
  48.4 15.9 %collective-permute-start.17 = (bf16[384,768]{1,0:T(8,128)(2,1)S(1)}, bf16[384,768]{1,0:T(8,128)(2,1)S(1)}, u32[]{:S(2)}, u32[]{:S(2)}) collective-permute-start(bf16[384,768]{1,0:T(8,128)(2,1)S(1)} %get-tuple-element.126), channel_id=1, source_target_pairs={{0,4},{4,0},{8,12},{12,8},{16,20},{20,16},{24,28},{28,24},{1,5},{5... | collective-permute-start | bytes 1769480 | tf_op jit(solution)/shard_map/ppermute | solution.py:184
  50.6 17.0 %collective-permute-start.18 = (bf16[384,768]{1,0:T(8,128)(2,1)S(1)}, bf16[384,768]{1,0:T(8,128)(2,1)S(1)}, u32[]{:S(2)}, u32[]{:S(2)}) collective-permute-start(bf16[384,768]{1,0:T(8,128)(2,1)S(1)} %get-tuple-element.128), channel_id=1, source_target_pairs={{0,8},{4,12},{8,0},{12,4},{16,24},{20,28},{24,16},{28,20},{1,9},{5... | collective-permute-start | bytes 1769480 | tf_op jit(solution)/shard_map/ppermute | solution.py:184
  60.4 8.5 %collective-permute-start.16 = (bf16[128,1152]{1,0:T(8,128)(2,1)S(1)}, bf16[128,1152]{1,0:T(8,128)(2,1)S(1)}, u32[]{:S(2)}, u32[]{:S(2)}) collective-permute-start(bf16[128,1152]{1,0:T(8,128)(2,1)S(1)} %get-tuple-element.124), channel_id=1, source_target_pairs={{0,2},{1,3},{2,0},{3,1},{4,6},{5,7},{6,4},{7,5},{8,10},{9,11},{10,... | collective-permute-start | bytes 884744 | tf_op jit(solution)/shard_map/ppermute | solution.py:184
  60.6 23.9 %collective-permute-start.20 = (bf16[256,960]{1,0:T(8,128)(2,1)S(1)}, bf16[256,960]{1,0:T(8,128)(2,1)S(1)}, u32[]{:S(2)}, u32[]{:S(2)}) collective-permute-start(bf16[256,960]{1,0:T(8,128)(2,1)S(1)} %get-tuple-element.118.refs_3_.refs_2_), channel_id=1, source_target_pairs={{0,1},{1,0},{2,3},{3,2},{4,5},{5,4},{6,7},{7,6},{8,9},{9,8},{10,11... | collective-permute-start | bytes 1474568 | tf_op jit(solution)/shard_map/ppermute | solution.py:184
  69.1 16.1 %collective-permute-start.21 = (bf16[256,960]{1,0:T(8,128)(2,1)S(1)}, bf16[256,960]{1,0:T(8,128)(2,1)S(1)}, u32[]{:S(2)}, u32[]{:S(2)}) collective-permute-start(bf16[256,960]{1,0:T(8,128)(2,1)S(1)} %get-tuple-element.135), channel_id=1, source_target_pairs={{0,1},{1,0},{2,3},{3,2},{4,5},{5,4},{6,7},{7,6},{8,9},{9,8},{10,11... | collective-permute-start | bytes 1474568 | tf_op jit(solution)/shard_map/ppermute | solution.py:184
  69.1 9.6 %collective-permute-start.22 = (bf16[192,768]{1,0:T(8,128)(2,1)S(1)}, bf16[192,768]{1,0:T(8,128)(2,1)S(1)}, u32[]{:S(2)}, u32[]{:S(2)}) collective-permute-start(bf16[192,768]{1,0:T(8,128)(2,1)S(1)} %get-tuple-element.129.refs_2_), channel_id=1, source_target_pairs={{0,8},{4,12},{8,0},{12,4},{16,24},{20,28},{24,16},{28,20},{1,9},{5... | collective-permute-start | bytes 884744 | tf_op jit(solution)/shard_map/ppermute | solution.py:184
  69.9 8.4 %collective-permute-start.14 = (bf16[1024,128]{1,0:T(8,128)(2,1)S(1)}, bf16[1024,128]{1,0:T(8,128)(2,1)S(1)}, u32[]{:S(2)}, u32[]{:S(2)}) collective-permute-start(bf16[1024,128]{1,0:T(8,128)(2,1)S(1)} %get-tuple-element.122), channel_id=1, source_target_pairs={{0,4},{4,0},{8,12},{12,8},{16,20},{20,16},{24,28},{28,24},{1,5},{5... | collective-permute-start | bytes 786440 | tf_op jit(solution)/shard_map/ppermute | solution.py:184
  70.3 52.7 %collective-permute-start.25 = (bf16[2,256,768]{2,1,0:T(8,128)(2,1)S(1)}, bf16[2,256,768]{2,1,0:T(8,128)(2,1)S(1)}, u32[]{:S(2)}, u32[]{:S(2)}) collective-permute-start(bf16[2,256,768]{2,1,0:T(8,128)(2,1)S(1)} %get-tuple-element.145), channel_id=1, source_target_pairs={{0,1},{1,0},{2,3},{3,2},{4,5},{5,4},{6,7},{7,6},{8,9},{9,8},{10,11... | collective-permute-start | bytes 2359304 | tf_op jit(solution)/shard_map/ppermute | solution.py:184
  78.3 16.6 %collective-permute-start.24 = (bf16[192,768]{1,0:T(8,128)(2,1)S(1)}, bf16[192,768]{1,0:T(8,128)(2,1)S(1)}, u32[]{:S(2)}, u32[]{:S(2)}) collective-permute-start(bf16[192,768]{1,0:T(8,128)(2,1)S(1)} %get-tuple-element.141), channel_id=1, source_target_pairs={{0,4},{4,0},{8,12},{12,8},{16,20},{20,16},{24,28},{28,24},{1,5},{5... | collective-permute-start | bytes 884744 | tf_op jit(solution)/shard_map/ppermute | solution.py:184
  78.8 21.8 %collective-permute-start.28 = (bf16[192,768]{1,0:T(8,128)(2,1)S(1)}, bf16[192,768]{1,0:T(8,128)(2,1)S(1)}, u32[]{:S(2)}, u32[]{:S(2)}) collective-permute-start(bf16[192,768]{1,0:T(8,128)(2,1)S(1)} %stage.25.refs_11_.refs_0_), channel_id=1, source_target_pairs={{0,16},{4,20},{8,24},{12,28},{16,0},{20,4},{24,8},{28,12},{1,17},{... | collective-permute-start | bytes 884744 | tf_op jit(solution)/shard_map/ppermute | solution.py:184
  84.5 8.7 %collective-permute-start.19 = (bf16[512,128]{1,0:T(8,128)(2,1)S(1)}, bf16[512,128]{1,0:T(8,128)(2,1)S(1)}, u32[]{:S(2)}, u32[]{:S(2)}) collective-permute-start(bf16[512,128]{1,0:T(8,128)(2,1)S(1)} %get-tuple-element.132.refs_2_), channel_id=1, source_target_pairs={{0,8},{4,12},{8,0},{12,4},{16,24},{20,28},{24,16},{28,20},{1,9},{5... | collective-permute-start | bytes 393224 | tf_op jit(solution)/shard_map/ppermute | solution.py:184
  86.2 18.7 %collective-permute-start.27 = (bf16[192,768]{1,0:T(8,128)(2,1)S(1)}, bf16[192,768]{1,0:T(8,128)(2,1)S(1)}, u32[]{:S(2)}, u32[]{:S(2)}) collective-permute-start(bf16[192,768]{1,0:T(8,128)(2,1)S(1)} %get-tuple-element.148), channel_id=1, source_target_pairs={{0,4},{4,0},{8,12},{12,8},{16,20},{20,16},{24,28},{28,24},{1,5},{5... | collective-permute-start | bytes 884744 | tf_op jit(solution)/shard_map/ppermute | solution.py:184
  93.2 6.3 %collective-permute-start.23 = (bf16[256,128]{1,0:T(8,128)(2,1)S(1)}, bf16[256,128]{1,0:T(8,128)(2,1)S(1)}, u32[]{:S(2)}, u32[]{:S(2)}) collective-permute-start(bf16[256,128]{1,0:T(8,128)(2,1)S(1)} %get-tuple-element.139.refs_2_), channel_id=1, source_target_pairs={{0,16},{4,20},{8,24},{12,28},{16,0},{20,4},{24,8},{28,12},{1,17},{... | collective-permute-start | bytes 196616 | tf_op jit(solution)/shard_map/ppermute | solution.py:184
  100.7 14.7 %collective-permute-start.31 = (bf16[192,768]{1,0:T(8,128)(2,1)S(1)}, bf16[192,768]{1,0:T(8,128)(2,1)S(1)}, u32[]{:S(2)}, u32[]{:S(2)}) collective-permute-start(bf16[192,768]{1,0:T(8,128)(2,1)S(1)} %stage.28.refs_2_), channel_id=1, source_target_pairs={{0,8},{4,12},{8,0},{12,4},{16,24},{20,28},{24,16},{28,20},{1,9},{5... | collective-permute-start | bytes 884744 | tf_op jit(solution)/shard_map/ppermute | solution.py:184
  102.2 3.1 %collective-permute-start.26 = (bf16[96,768]{1,0:T(8,128)(2,1)S(1)}, bf16[96,768]{1,0:T(8,128)(2,1)S(1)}, u32[]{:S(2)}, u32[]{:S(2)}) collective-permute-start(bf16[96,768]{1,0:T(8,128)(2,1)S(1)} %get-tuple-element.147), channel_id=1, source_target_pairs={{0,1},{1,0},{2,3},{3,2},{4,5},{5,4},{6,7},{7,6},{8,9},{9,8},{10,11... | collective-permute-start | bytes 442376 | tf_op jit(solution)/shard_map/ppermute | solution.py:184
  102.2 21.4 %collective-permute-start.33 = (bf16[192,768]{1,0:T(8,128)(2,1)S(1)}, bf16[192,768]{1,0:T(8,128)(2,1)S(1)}, u32[]{:S(2)}, u32[]{:S(2)}) collective-permute-start(bf16[192,768]{1,0:T(8,128)(2,1)S(1)} %stage.27.refs_10_.refs_0_), channel_id=1, source_target_pairs={{0,16},{4,20},{8,24},{12,28},{16,0},{20,4},{24,8},{28,12},{1,17},{... | collective-permute-start | bytes 884744 | tf_op jit(solution)/shard_map/ppermute | solution.py:184
  105.0 13.1 %collective-permute-start.30 = (bf16[96,768]{1,0:T(8,128)(2,1)S(1)}, bf16[96,768]{1,0:T(8,128)(2,1)S(1)}, u32[]{:S(2)}, u32[]{:S(2)}) collective-permute-start(bf16[96,768]{1,0:T(8,128)(2,1)S(1)} %get-tuple-element.149.refs_2_), channel_id=1, source_target_pairs={{0,8},{4,12},{8,0},{12,4},{16,24},{20,28},{24,16},{28,20},{1,9},{5... | collective-permute-start | bytes 442376 | tf_op jit(solution)/shard_map/ppermute | solution.py:184
  105.3 12.9 %collective-permute-start.29 = (bf16[48,768]{1,0:T(8,128)(2,1)S(1)}, bf16[48,768]{1,0:T(8,128)(2,1)S(1)}, u32[]{:S(2)}, u32[]{:S(2)}) collective-permute-start(bf16[48,768]{1,0:T(8,128)(2,1)S(1)} %get-tuple-element.151.refs_4_), channel_id=1, source_target_pairs={{0,2},{1,3},{2,0},{3,1},{4,6},{5,7},{6,4},{7,5},{8,10},{9,11},{10,... | collective-permute-start | bytes 221192 | tf_op jit(solution)/shard_map/ppermute | solution.py:184
  118.3 5.2 %collective-permute-start.34 = (bf16[48,768]{1,0:T(8,128)(2,1)S(1)}, bf16[48,768]{1,0:T(8,128)(2,1)S(1)}, u32[]{:S(2)}, u32[]{:S(2)}) collective-permute-start(bf16[48,768]{1,0:T(8,128)(2,1)S(1)} %stage.32.refs_2_.refs_0_), channel_id=1, source_target_pairs={{0,8},{4,12},{8,0},{12,4},{16,24},{20,28},{24,16},{28,20},{1,9},{5... | collective-permute-start | bytes 221192 | tf_op jit(solution)/shard_map/ppermute | solution.py:184
  119.6 8.2 %collective-permute-start.36 = (bf16[96,768]{1,0:T(8,128)(2,1)S(1)}, bf16[96,768]{1,0:T(8,128)(2,1)S(1)}, u32[]{:S(2)}, u32[]{:S(2)}) collective-permute-start(bf16[96,768]{1,0:T(8,128)(2,1)S(1)} %get-tuple-element.153.refs_2_.refs_0_), channel_id=1, source_target_pairs={{0,16},{4,20},{8,24},{12,28},{16,0},{20,4},{24,8},{28,12},{1,17},{... | collective-permute-start | bytes 442376 | tf_op jit(solution)/shard_map/ppermute | solution.py:184
  123.7 11.1 %collective-permute-start.35 = (bf16[192,768]{1,0:T(8,128)(2,1)S(1)}, bf16[192,768]{1,0:T(8,128)(2,1)S(1)}, u32[]{:S(2)}, u32[]{:S(2)}) collective-permute-start(bf16[192,768]{1,0:T(8,128)(2,1)S(1)} %stage.35.refs_2_.refs_0_), channel_id=1, source_target_pairs={{0,4},{4,0},{8,12},{12,8},{16,20},{20,16},{24,28},{28,24},{1,5},{5... | collective-permute-start | bytes 884744 | tf_op jit(solution)/shard_map/ppermute | solution.py:184
  125.6 16.7 %collective-permute-start.32 = (bf16[2,256,768]{2,1,0:T(8,128)(2,1)S(1)}, bf16[2,256,768]{2,1,0:T(8,128)(2,1)S(1)}, u32[]{:S(2)}, u32[]{:S(2)}) collective-permute-start(bf16[2,256,768]{2,1,0:T(8,128)(2,1)S(1)} %stage.33.refs_2_), channel_id=1, source_target_pairs={{0,2},{1,3},{2,0},{3,1},{4,6},{5,7},{6,4},{7,5},{8,10},{9,11},{10,... | collective-permute-start | bytes 2359304 | tf_op jit(solution)/shard_map/ppermute | solution.py:184
  127.8 6.9 %collective-permute-start.37 = (bf16[96,768]{1,0:T(8,128)(2,1)S(1)}, bf16[96,768]{1,0:T(8,128)(2,1)S(1)}, u32[]{:S(2)}, u32[]{:S(2)}) collective-permute-start(bf16[96,768]{1,0:T(8,128)(2,1)S(1)} %stage.36.refs_2_.refs_0_), channel_id=1, source_target_pairs={{0,8},{4,12},{8,0},{12,4},{16,24},{20,28},{24,16},{28,20},{1,9},{5... | collective-permute-start | bytes 442376 | tf_op jit(solution)/shard_map/ppermute | solution.py:184
  128.2 6.5 %collective-permute-start.38 = (bf16[48,768]{1,0:T(8,128)(2,1)S(1)}, bf16[48,768]{1,0:T(8,128)(2,1)S(1)}, u32[]{:S(2)}, u32[]{:S(2)}) collective-permute-start(bf16[48,768]{1,0:T(8,128)(2,1)S(1)} %stage.34.refs_2_.refs_0_), channel_id=1, source_target_pairs={{0,4},{4,0},{8,12},{12,8},{16,20},{20,16},{24,28},{28,24},{1,5},{5... | collective-permute-start | bytes 221192 | tf_op jit(solution)/shard_map/ppermute | solution.py:184
  128.9 18.4 %collective-permute-start.40 = (bf16[384,768]{1,0:T(8,128)(2,1)S(1)}, bf16[384,768]{1,0:T(8,128)(2,1)S(1)}, u32[]{:S(2)}, u32[]{:S(2)}) collective-permute-start(bf16[384,768]{1,0:T(8,128)(2,1)S(1)} %get-tuple-element.156.refs_0_), channel_id=1, source_target_pairs={{0,4},{4,0},{8,12},{12,8},{16,20},{20,16},{24,28},{28,24},{1,5},{5... | collective-permute-start | bytes 1769480 | tf_op jit(solution)/shard_map/ppermute | solution.py:184
  134.8 17.9 %collective-permute-start.42 = (bf16[384,768]{1,0:T(8,128)(2,1)S(1)}, bf16[384,768]{1,0:T(8,128)(2,1)S(1)}, u32[]{:S(2)}, u32[]{:S(2)}) collective-permute-start(bf16[384,768]{1,0:T(8,128)(2,1)S(1)} %stage.39.refs_8_.refs_0_), channel_id=1, source_target_pairs={{0,8},{4,12},{8,0},{12,4},{16,24},{20,28},{24,16},{28,20},{1,9},{5... | collective-permute-start | bytes 1769480 | tf_op jit(solution)/shard_map/ppermute | solution.py:184
  136.5 14.5 %collective-permute-start.41 = (bf16[192,768]{1,0:T(8,128)(2,1)S(1)}, bf16[192,768]{1,0:T(8,128)(2,1)S(1)}, u32[]{:S(2)}, u32[]{:S(2)}) collective-permute-start(bf16[192,768]{1,0:T(8,128)(2,1)S(1)} %stage.38.refs_2_.refs_0_), channel_id=1, source_target_pairs={{0,4},{4,0},{8,12},{12,8},{16,20},{20,16},{24,28},{28,24},{1,5},{5... | collective-permute-start | bytes 884744 | tf_op jit(solution)/shard_map/ppermute | solution.py:184
  137.0 11.7 %collective-permute-start.39 = (bf16[48,768]{1,0:T(8,128)(2,1)S(1)}, bf16[48,768]{1,0:T(8,128)(2,1)S(1)}, u32[]{:S(2)}, u32[]{:S(2)}) collective-permute-start(bf16[48,768]{1,0:T(8,128)(2,1)S(1)} %stage.37.refs_2_.refs_0_), channel_id=1, source_target_pairs={{0,16},{4,20},{8,24},{12,28},{16,0},{20,4},{24,8},{28,12},{1,17},{... | collective-permute-start | bytes 221192 | tf_op jit(solution)/shard_map/ppermute | solution.py:184
  151.0 0.7 copy-start.5

commit v5 on v4

--- a/solution.py
+++ b/solution.py
@@ -1002,7 +1002,7 @@
         pltpu.VMEM((2 * rows, width), BF),
     ]
     most = min(slots, slots // 2 + 1)
-    chunk_blocks = 2
+    chunk_blocks = 3
     most_chunks = -(-most // chunk_blocks)
     chunk = chunk_blocks * BLOCK
     per_group = HEADS
@@ -1171,13 +1171,13 @@
     flow(sequence, mix)
     flow(sequence, qo, up)
     flow(sequence, mix)
-    back_b = swap(send_b, "fsdp", 1)
-    back = sequence.stage([(merge_step, [View(keep_b), View(back_b)], 1)])[0, 0].array
-    back = swap(back, "fsdp", 2)
     flow(sequence, mix)
     while dn.left() > 2:
         flow(sequence, dn)
     flow(sequence, dn)
+    back_b = swap(send_b, "fsdp", 1)
+    back = sequence.stage([(merge_step, [View(keep_b), View(back_b)], 1)])[0, 0].array
+    back = swap(back, "fsdp", 2)
     flow(sequence, qo)
     while mix.left() > 1:
         flow(sequence, mix)

time: 155 us -> 154 us (level)
  starting transfers between devices: 54.5 us -> 60.3 us
  waiting for transfers between devices: 57.8 us -> 53.9 us
  Pallas kernels: 38.9 us -> 36.1 us
    ppermute x43, starting transfers between devices: 54.5 us -> 60.3 us  [swap(): return lax.ppermute(value, axis, [(i, i ^ bit) for i in range(size)])]
    ppermute x43, waiting for transfers between devices: 57.8 us -> 53.9 us  [swap(): return lax.ppermute(value, axis, [(i, i ^ bit) for i in range(size)])]
    pallas_call x36, Pallas kernels: 38.9 us -> 36.1 us  [run(): pl.pallas_call(body, out_shape=outs, in_specs=list(specs.get('in_specs',...]
  transfers between devices with their start and end apart: 43 -> 43, of which waited for: 19 -> 18; matrix products, arithmetic and copies ran while one was open for 0% -> 0% of each run, Pallas kernels for 21% -> 20%
where the time goes in v5:
time: 154 us
  starting transfers between devices  60.3 us (39%)
  waiting for transfers between devices  53.9 us (35%)
  Pallas kernels  36.1 us (23%)
  local copies, waits for them, and re-layouts  2.2 us (1%)
    ppermute x43, starting transfers between devices, swap(): return lax.ppermute(value, axis, [(i, i ^ bit) for i in range(size)])  60.3 us
    ppermute x43, waiting for transfers between devices, swap(): return lax.ppermute(value, axis, [(i, i ^ bit) for i in range(size)])  53.9 us
    pallas_call x36, Pallas kernels, run(): pl.pallas_call(body, out_shape=outs, in_specs=list(specs.get('in_specs',...  36.1 us
  transfers between devices with their start and end apart: 43, of which 18 were waited for; matrix products, arithmetic and copies ran while one was open for 0% of the time, Pallas kernels for 20%

profile of v5, /device:TPU:0, one launch (start us, length us, event | category | flops | bytes accessed | tf_op | source)
XLA Modules:
  0.0 154.0 jit_solution(13541178621286660057)
XLA Ops:
  0.7 3.5 %pack.1 = (bf16[144,192]{1,0:T(8,128)(2,1)}, bf16[512,768]{1,0:T(8,128)(2,1)}, bf16[384,768]{1,0:T(8,128)(2,1)}, bf16[896,768]{1,0:T(8,128)(2,1)}) custom-call(bf16[256,768]{1,0:T(8,128)(2,1)} %bitcast.10, bf16[256,768]{1,0:T(8,128)(2,1)} %bitcast.12, bf16[192,768]{1,0:T(8,128)(2,1)} %refs_2_.3, bf16[192,768]{1,0:T(8,128)(2,1)} %refs_3_.3, ...), custom_call_target="tpu_custom_call" | custom-call | flops 2000000000 | bytes 1000 | tf_op jit(solution)/shard_map/pack/pallas_call | solution.py:62
  4.2 0.5 collective-permute-start.4
  4.8 2.9 %collective-permute-start = (bf16[144,192]{1,0:T(8,128)(2,1)}, bf16[144,192]{1,0:T(8,128)(2,1)S(1)}, u32[]{:S(2)}, u32[]{:S(2)}) collective-permute-start(bf16[144,192]{1,0:T(8,128)(2,1)} %get-tuple-element.98.refs_2_.refs_1_), channel_id=1, source_target_pairs={{0,2},{1,3},{2,0},{3,1},{4,6},{5,7},{6,4},{7,5},{8,10},{9,11},{10,... | collective-permute-start | bytes 165896 | tf_op jit(solution)/shard_map/ppermute | solution.py:184
  7.8 2.0 %collective-permute-start.11 = (bf16[512,768]{1,0:T(8,128)(2,1)}, bf16[512,768]{1,0:T(8,128)(2,1)S(1)}, u32[]{:S(2)}, u32[]{:S(2)}) collective-permute-start(bf16[512,768]{1,0:T(8,128)(2,1)} %get-tuple-element.97.refs_0_.refs_1_.refs_7_), channel_id=1, source_target_pairs={{0,2},{1,3},{2,0},{3,1},{4,6},{5,7},{6,4},{7,5},{8,10},{9,11},{10,... | collective-permute-start | bytes 2359304 | tf_op jit(solution)/shard_map/ppermute | solution.py:184
  10.1 0.6 collective-permute-done.refs_2_
  10.7 0.9 copy-done.7
  11.6 0.3 collective-permute-done.2.refs_4_
  12.0 0.6 copy-done.6
  12.6 0.9 front.1
  13.5 4.3 %collective-permute-start.7 = (bf16[256,128]{1,0:T(8,128)(2,1)S(1)}, bf16[256,128]{1,0:T(8,128)(2,1)S(1)}, u32[]{:S(2)}, u32[]{:S(2)}) collective-permute-start(bf16[256,128]{1,0:T(8,128)(2,1)S(1)} %get-tuple-element.103.refs_0_), channel_id=1, source_target_pairs={{0,24},{4,28},{8,16},{12,20},{16,8},{20,12},{24,0},{28,4},{1,25},{... | collective-permute-start | bytes 196616 | tf_op jit(solution)/shard_map/ppermute | solution.py:184
  17.8 0.6 collective-permute-start.5
  18.4 4.9 %mlp_near.1 = (bf16[2,256,768]{2,1,0:T(8,128)(2,1)S(1)}, bf16[2,256,768]{2,1,0:T(8,128)(2,1)S(1)}, bf16[2,256,192]{2,1,0:T(8,128)(2,1)S(1)}, f32[768,768]{1,0:T(...) custom-call(bf16[512,768]{1,0:T(8,128)(2,1)S(1)} %copy-done, ...), custom_call_target="tpu_custom_call" | custom-call | flops 1 | bytes 1000 | tf_op jit(solution)/shard_map/mlp_near/pallas_call | solution.py:62
  23.7 0.5 collective-permute-done.3.refs_0_.refs_5_
  24.3 0.5 collective-permute-start.8
  24.8 1.5 collective-permute-start.10
  26.3 1.0 query.1
  27.3 5.8 %collective-permute-done.10.refs_5_ = bf16[1024,128]{1,0:T(8,128)(2,1)S(1)} collective-permute-done((bf16[1024,128]{1,0:T(8,128)(2,1)S(1)}, bf16[1024,128]{1,0:T(8,128)(2,1)S(1)}, u32[]{:S(2)}, u32[]{:S(2)}) %collective-permute-start.10) | collective-permute-done | bytes 262176 | tf_op jit(solution)/shard_map/ppermute | solution.py:184
  33.1 4.7 %attend.2 = (bf16[128,768]{1,0:T(8,128)(2,1)S(1)}, bf16[128,1152]{1,0:T(8,128)(2,1)S(1)}, bf16[128,960]{1,0:T(8,128)(2,1)S(1)}, f32[2048,128]{1,0:T(8,128)S(1)}) custom-call(s32[16]{0:T(128)S(1)} %copy-done.8, s32[1,4]{1,0:T(1,128)S(1)} %copy-done.9, bf16[768,256]{1,0:T(8,128)(2,1)S(1)} %get-tuple-element.107.refs_2_.refs_7_, ...), custom_call_target="tpu_custom_call" | custom-call | flops 2000000000 | bytes 1000 | tf_op jit(solution)/shard_map/attend/pallas_call | solution.py:62
  37.8 2.2 %collective-permute-done.11.refs_0_.refs_9_ = bf16[512,768]{1,0:T(8,128)(2,1)S(1)} collective-permute-done((bf16[512,768]{1,0:T(8,128)(2,1)}, bf16[512,768]{1,0:T(8,128)(2,1)S(1)}, u32[]{:S(2)}, u32[]{:S(2)}) %collective-permute-start.11) | collective-permute-done | bytes 786464 | tf_op jit(solution)/shard_map/ppermute | solution.py:184
  40.1 1.8 %collective-permute-start.15 = (bf16[128,1152]{1,0:T(8,128)(2,1)S(1)}, bf16[128,1152]{1,0:T(8,128)(2,1)S(1)}, u32[]{:S(2)}, u32[]{:S(2)}) collective-permute-start(bf16[128,1152]{1,0:T(8,128)(2,1)S(1)} %get-tuple-element.123), channel_id=1, source_target_pairs={{0,2},{1,3},{2,0},{3,1},{4,6},{5,7},{6,4},{7,5},{8,10},{9,11},{10,... | collective-permute-start | bytes 884744 | tf_op jit(solution)/shard_map/ppermute | solution.py:184
  41.9 0.5 collective-permute-done.12.refs_1_.refs_10_
  42.4 5.3 %mlp_far.1 = (bf16[2,256,768]{2,1,0:T(8,128)(2,1)S(1)}, bf16[2,256,768]{2,1,0:T(8,128)(2,1)S(1)}, bf16[2,256,192]{2,1,0:T(8,128)(2,1)S(1)}, bf16[384,768]{1,0:T(...) custom-call(bf16[512,768]{1,0:T(8,128)(2,1)S(1)} %collective-permute, ...), custom_call_target="tpu_custom_call" | custom-call | flops 14000000000 | bytes 1000 | tf_op jit(solution)/shard_map/mlp_far/pallas_call | solution.py:62
  47.7 2.2 %collective-permute-start.17 = (bf16[384,768]{1,0:T(8,128)(2,1)S(1)}, bf16[384,768]{1,0:T(8,128)(2,1)S(1)}, u32[]{:S(2)}, u32[]{:S(2)}) collective-permute-start(bf16[384,768]{1,0:T(8,128)(2,1)S(1)} %get-tuple-element.126), channel_id=1, source_target_pairs={{0,4},{4,0},{8,12},{12,8},{16,20},{20,16},{24,28},{28,24},{1,5},{5... | collective-permute-start | bytes 1769480 | tf_op jit(solution)/shard_map/ppermute | solution.py:184
  49.9 3.0 %collective-permute-start.18 = (bf16[384,768]{1,0:T(8,128)(2,1)S(1)}, bf16[384,768]{1,0:T(8,128)(2,1)S(1)}, u32[]{:S(2)}, u32[]{:S(2)}) collective-permute-start(bf16[384,768]{1,0:T(8,128)(2,1)S(1)} %get-tuple-element.128), channel_id=1, source_target_pairs={{0,8},{4,12},{8,0},{12,4},{16,24},{20,28},{24,16},{28,20},{1,9},{5... | collective-permute-start | bytes 1769480 | tf_op jit(solution)/shard_map/ppermute | solution.py:184
  52.9 4.8 %attend.3 = (bf16[256,768]{1,0:T(8,128)(2,1)S(1)}, bf16[128,1152]{1,0:T(8,128)(2,1)S(1)}, bf16[256,960]{1,0:T(8,128)(2,1)S(1)}, bf16[1024,128]{1,0:T(8,128)(2,1)S(1)}, bf16[1024,128]{1,0:T(8,128)(2,1)S(1)}) custom-call(s32[16]{0:T(128)S(1)} %copy-done.8, s32[1,4]{1,0:T(1,128)S(1)} %copy-done.9, bf16[768,256]{1,0:T(8,128)(2,1)S(1)} %get-tuple-element.107.refs_2_.refs_7_, ...), custom_call_target="tpu_custom_call" | custom-call | flops 14000000000 | bytes 1000 | tf_op jit(solution)/shard_map/attend/pallas_call | solution.py:62
  57.7 1.6 %collective-permute-start.16 = (bf16[128,1152]{1,0:T(8,128)(2,1)S(1)}, bf16[128,1152]{1,0:T(8,128)(2,1)S(1)}, u32[]{:S(2)}, u32[]{:S(2)}) collective-permute-start(bf16[128,1152]{1,0:T(8,128)(2,1)S(1)} %get-tuple-element.124), channel_id=1, source_target_pairs={{0,2},{1,3},{2,0},{3,1},{4,6},{5,7},{6,4},{7,5},{8,10},{9,11},{10,... | collective-permute-start | bytes 884744 | tf_op jit(solution)/shard_map/ppermute | solution.py:184
  59.2 4.3 %collective-permute-done.17.refs_1_ = bf16[384,768]{1,0:T(8,128)(2,1)S(1)} collective-permute-done((bf16[384,768]{1,0:T(8,128)(2,1)S(1)}, bf16[384,768]{1,0:T(8,128)(2,1)S(1)}, u32[]{:S(2)}, u32[]{:S(2)}) %collective-permute-start.17) | collective-permute-done | bytes 589856 | tf_op jit(solution)/shard_map/ppermute | solution.py:184
  63.5 3.0 %collective-permute-done.18.refs_3_ = bf16[384,768]{1,0:T(8,128)(2,1)S(1)} collective-permute-done((bf16[384,768]{1,0:T(8,128)(2,1)S(1)}, bf16[384,768]{1,0:T(8,128)(2,1)S(1)}, u32[]{:S(2)}, u32[]{:S(2)}) %collective-permute-start.18) | collective-permute-done | bytes 589856 | tf_op jit(solution)/shard_map/ppermute | solution.py:184
  67.0 1.8 %collective-permute-start.22 = (bf16[192,768]{1,0:T(8,128)(2,1)S(1)}, bf16[192,768]{1,0:T(8,128)(2,1)S(1)}, u32[]{:S(2)}, u32[]{:S(2)}) collective-permute-start(bf16[192,768]{1,0:T(8,128)(2,1)S(1)} %get-tuple-element.129.refs_2_), channel_id=1, source_target_pairs={{0,8},{4,12},{8,0},{12,4},{16,24},{20,28},{24,16},{28,20},{1,9},{5... | collective-permute-start | bytes 884744 | tf_op jit(solution)/shard_map/ppermute | solution.py:184
  68.8 2.5 %collective-permute-start.14 = (bf16[1024,128]{1,0:T(8,128)(2,1)S(1)}, bf16[1024,128]{1,0:T(8,128)(2,1)S(1)}, u32[]{:S(2)}, u32[]{:S(2)}) collective-permute-start(bf16[1024,128]{1,0:T(8,128)(2,1)S(1)} %get-tuple-element.122), channel_id=1, source_target_pairs={{0,4},{4,0},{8,12},{12,8},{16,20},{20,16},{24,28},{28,24},{1,5},{5... | collective-permute-start | bytes 786440 | tf_op jit(solution)/shard_map/ppermute | solution.py:184
  71.4 6.7 %collective-permute-done.14.refs_1_ = bf16[1024,128]{1,0:T(8,128)(2,1)S(1)} collective-permute-done((bf16[1024,128]{1,0:T(8,128)(2,1)S(1)}, bf16[1024,128]{1,0:T(8,128)(2,1)S(1)}, u32[]{:S(2)}, u32[]{:S(2)}) %collective-permute-start.14) | collective-permute-done | bytes 262176 | tf_op jit(solution)/shard_map/ppermute | solution.py:184
  78.2 1.7 %collective-permute-start.24 = (bf16[192,768]{1,0:T(8,128)(2,1)S(1)}, bf16[192,768]{1,0:T(8,128)(2,1)S(1)}, u32[]{:S(2)}, u32[]{:S(2)}) collective-permute-start(bf16[192,768]{1,0:T(8,128)(2,1)S(1)} %get-tuple-element.141), channel_id=1, source_target_pairs={{0,4},{4,0},{8,12},{12,8},{16,20},{20,16},{24,28},{28,24},{1,5},{5... | collective-permute-start | bytes 884744 | tf_op jit(solution)/shard_map/ppermute | solution.py:184
  80.1 3.9 %collective-permute-start.29 = (bf16[192,768]{1,0:T(8,128)(2,1)S(1)}, bf16[192,768]{1,0:T(8,128)(2,1)S(1)}, u32[]{:S(2)}, u32[]{:S(2)}) collective-permute-start(bf16[192,768]{1,0:T(8,128)(2,1)S(1)} %stage.25.refs_11_.refs_0_), channel_id=1, source_target_pairs={{0,16},{4,20},{8,24},{12,28},{16,0},{20,4},{24,8},{28,12},{1,17},{... | collective-permute-start | bytes 884744 | tf_op jit(solution)/shard_map/ppermute | solution.py:184
  84.0 0.6 collective-permute-start.19
  84.6 1.1 weight.1
  85.7 1.6 %collective-permute-start.28 = (bf16[192,768]{1,0:T(8,128)(2,1)S(1)}, bf16[192,768]{1,0:T(8,128)(2,1)S(1)}, u32[]{:S(2)}, u32[]{:S(2)}) collective-permute-start(bf16[192,768]{1,0:T(8,128)(2,1)S(1)} %get-tuple-element.148), channel_id=1, source_target_pairs={{0,4},{4,0},{8,12},{12,8},{16,20},{20,16},{24,28},{28,24},{1,5},{5... | collective-permute-start | bytes 884744 | tf_op jit(solution)/shard_map/ppermute | solution.py:184
  87.2 5.0 %collective-permute-done.19.refs_1_ = bf16[512,128]{1,0:T(8,128)(2,1)S(1)} collective-permute-done((bf16[512,128]{1,0:T(8,128)(2,1)S(1)}, bf16[512,128]{1,0:T(8,128)(2,1)S(1)}, u32[]{:S(2)}, u32[]{:S(2)}) %collective-permute-start.19) | collective-permute-done | bytes 131104 | tf_op jit(solution)/shard_map/ppermute | solution.py:184
  92.3 1.7 %collective-permute-start.23 = (bf16[256,128]{1,0:T(8,128)(2,1)S(1)}, bf16[256,128]{1,0:T(8,128)(2,1)S(1)}, u32[]{:S(2)}, u32[]{:S(2)}) collective-permute-start(bf16[256,128]{1,0:T(8,128)(2,1)S(1)} %get-tuple-element.139.refs_2_), channel_id=1, source_target_pairs={{0,16},{4,20},{8,24},{12,28},{16,0},{20,4},{24,8},{28,12},{1,17},{... | collective-permute-start | bytes 196616 | tf_op jit(solution)/shard_map/ppermute | solution.py:184
  94.0 4.5 %collective-permute-done.23.refs_8_ = bf16[256,128]{1,0:T(8,128)(2,1)S(1)} collective-permute-done((bf16[256,128]{1,0:T(8,128)(2,1)S(1)}, bf16[256,128]{1,0:T(8,128)(2,1)S(1)}, u32[]{:S(2)}, u32[]{:S(2)}) %collective-permute-start.23) | collective-permute-done | bytes 65568 | tf_op jit(solution)/shard_map/ppermute | solution.py:184
  98.5 1.1 tail.1
  99.7 1.5 collective-permute-start.32
  101.2 2.8 %collective-permute-start.26 = (bf16[192,768]{1,0:T(8,128)(2,1)S(1)}, bf16[192,768]{1,0:T(8,128)(2,1)S(1)}, u32[]{:S(2)}, u32[]{:S(2)}) collective-permute-start(bf16[192,768]{1,0:T(8,128)(2,1)S(1)} %stage.27.refs_10_.refs_0_), channel_id=1, source_target_pairs={{0,16},{4,20},{8,24},{12,28},{16,0},{20,4},{24,8},{28,12},{1,17},{... | collective-permute-start | bytes 884744 | tf_op jit(solution)/shard_map/ppermute | solution.py:184
  104.4 2.2 %collective-permute-start.30 = (bf16[48,768]{1,0:T(8,128)(2,1)S(1)}, bf16[48,768]{1,0:T(8,128)(2,1)S(1)}, u32[]{:S(2)}, u32[]{:S(2)}) collective-permute-start(bf16[48,768]{1,0:T(8,128)(2,1)S(1)} %get-tuple-element.151.refs_4_), channel_id=1, source_target_pairs={{0,2},{1,3},{2,0},{3,1},{4,6},{5,7},{6,4},{7,5},{8,10},{9,11},{10,... | collective-permute-start | bytes 221192 | tf_op jit(solution)/shard_map/ppermute | solution.py:184
  106.6 7.8 %collective-permute-done.32.refs_3_ = bf16[192,768]{1,0:T(8,128)(2,1)S(1)} collective-permute-done((bf16[192,768]{1,0:T(8,128)(2,1)S(1)}, bf16[192,768]{1,0:T(8,128)(2,1)S(1)}, u32[]{:S(2)}, u32[]{:S(2)}) %collective-permute-start.32) | collective-permute-done | bytes 294944 | tf_op jit(solution)/shard_map/ppermute | solution.py:184
  114.4 2.8 %collective-permute-done.31.refs_1_ = bf16[96,768]{1,0:T(8,128)(2,1)S(1)} collective-permute-done((bf16[96,768]{1,0:T(8,128)(2,1)S(1)}, bf16[96,768]{1,0:T(8,128)(2,1)S(1)}, u32[]{:S(2)}, u32[]{:S(2)}) %collective-permute-start.31) | collective-permute-done | bytes 147488 | tf_op jit(solution)/shard_map/ppermute | solution.py:184
  117.3 1.3 collective-permute-start.33
  118.6 3.3 %collective-permute-start.36 = (bf16[96,768]{1,0:T(8,128)(2,1)S(1)}, bf16[96,768]{1,0:T(8,128)(2,1)S(1)}, u32[]{:S(2)}, u32[]{:S(2)}) collective-permute-start(bf16[96,768]{1,0:T(8,128)(2,1)S(1)} %get-tuple-element.153.refs_2_.refs_0_), channel_id=1, source_target_pairs={{0,16},{4,20},{8,24},{12,28},{16,0},{20,4},{24,8},{28,12},{1,17},{... | collective-permute-start | bytes 442376 | tf_op jit(solution)/shard_map/ppermute | solution.py:184
  122.0 0.6 collective-permute-done.33.refs_1_
  122.7 1.2 collective-permute-start.35
  124.1 3.0 %collective-permute-start.34 = (bf16[2,256,768]{2,1,0:T(8,128)(2,1)S(1)}, bf16[2,256,768]{2,1,0:T(8,128)(2,1)S(1)}, u32[]{:S(2)}, u32[]{:S(2)}) collective-permute-start(bf16[2,256,768]{2,1,0:T(8,128)(2,1)S(1)} %stage.35.refs_2_), channel_id=1, source_target_pairs={{0,2},{1,3},{2,0},{3,1},{4,6},{5,7},{6,4},{7,5},{8,10},{9,11},{10,... | collective-permute-start | bytes 2359304 | tf_op jit(solution)/shard_map/ppermute | solution.py:184
  127.2 1.2 collective-permute-start.38
  128.5 0.9 collective-permute-start.40
  129.3 4.5 %collective-permute-done.38.refs_1_ = bf16[48,768]{1,0:T(8,128)(2,1)S(1)} collective-permute-done((bf16[48,768]{1,0:T(8,128)(2,1)S(1)}, bf16[48,768]{1,0:T(8,128)(2,1)S(1)}, u32[]{:S(2)}, u32[]{:S(2)}) %collective-permute-start.38) | collective-permute-done | bytes 73760 | tf_op jit(solution)/shard_map/ppermute | solution.py:184
  134.0 1.6 %collective-permute-start.42 = (bf16[384,768]{1,0:T(8,128)(2,1)S(1)}, bf16[384,768]{1,0:T(8,128)(2,1)S(1)}, u32[]{:S(2)}, u32[]{:S(2)}) collective-permute-start(bf16[384,768]{1,0:T(8,128)(2,1)S(1)} %stage.39.refs_8_.refs_0_), channel_id=1, source_target_pairs={{0,8},{4,12},{8,0},{12,4},{16,24},{20,28},{24,16},{28,20},{1,9},{5... | collective-permute-start | bytes 1769480 | tf_op jit(solution)/shard_map/ppermute | solution.py:184
  135.5 1.2 collective-permute-start.41
  136.7 4.6 %collective-permute-start.39 = (bf16[48,768]{1,0:T(8,128)(2,1)S(1)}, bf16[48,768]{1,0:T(8,128)(2,1)S(1)}, u32[]{:S(2)}, u32[]{:S(2)}) collective-permute-start(bf16[48,768]{1,0:T(8,128)(2,1)S(1)} %stage.37.refs_2_.refs_0_), channel_id=1, source_target_pairs={{0,16},{4,20},{8,24},{12,28},{16,0},{20,4},{24,8},{28,12},{1,17},{... | collective-permute-start | bytes 221192 | tf_op jit(solution)/shard_map/ppermute | solution.py:184
  141.3 1.8 %output.1 = (bf16[256,768]{1,0:T(8,128)(2,1)}, bf16[256,768]{1,0:T(8,128)(2,1)}, f32[8,128]{1,0:T(8,128)S(1)}) custom-call(bf16[512,768]{1,0:T(8,128)(2,1)S(1)} %copy-done, bf16[256,768]{1,0:T(8,128)(2,1)S(1)} %get-tuple-element.116.refs_2_.refs_1_, bf16[768,768]{1,0:T(8,128)(2,1)S(1)} %get-tuple-element.117.refs_2_, ...), custom_call_target="tpu_custom_call" | custom-call | flops 1 | bytes 1000 | tf_op jit(solution)/shard_map/output/pallas_call | solution.py:62
  143.2 3.3 %collective-permute-done.40.refs_1_ = bf16[384,768]{1,0:T(8,128)(2,1)S(1)} collective-permute-done((bf16[384,768]{1,0:T(8,128)(2,1)S(1)}, bf16[384,768]{1,0:T(8,128)(2,1)S(1)}, u32[]{:S(2)}, u32[]{:S(2)}) %collective-permute-start.40) | collective-permute-done | bytes 589856 | tf_op jit(solution)/shard_map/ppermute | solution.py:184
  146.5 1.5 matrix.3
  148.0 1.0 vector.1
  148.9 1.1 collective-permute-done.41.refs_1_
  150.0 0.7 copy-done.5
  150.7 1.1 matrix.4
  151.8 2.1 %matrix.5 = (f32[768,768]{1,0:T(8,128)}, f32[8,128]{1,0:T(8,128)}) custom-call(bf16[384,768]{1,0:T(8,128)(2,1)S(1)} %stage.39.refs_8_.refs_0_, bf16[384,768]{1,0:T(8,128)(2,1)S(1)} %collective-permute-done.42.refs_1_, f32[8,128]{1,0:T(8,128)S(1)} %get-tuple-element.173.refs_2_), custom_call_target="tpu_custom_call" | custom-call | flops 1 | bytes 1000 | tf_op jit(solution)/shard_map/matrix/pallas_call | solution.py:62
  (82 shorter events, 2.8 us)
Async XLA Ops:
  0.7 9.1 %copy-start.8 = (s32[16]{0:T(128)S(1)}, s32[16]{0:T(128)}, u32[]{:S(2)}) copy-start(s32[16]{0:T(128)} %refs_0_.3) | copy-start | bytes 196
  4.2 13.6 %collective-permute-start.4 = (bf16[896,768]{1,0:T(8,128)(2,1)}, bf16[896,768]{1,0:T(8,128)(2,1)S(1)}, u32[]{:S(2)}, u32[]{:S(2)}) collective-permute-start(bf16[896,768]{1,0:T(8,128)(2,1)} %get-tuple-element.102), channel_id=1, source_target_pairs={{0,1},{1,0},{2,3},{3,2},{4,5},{5,4},{6,7},{7,6},{8,9},{9,8},{10,11... | collective-permute-start | bytes 4128776 | tf_op jit(solution)/shard_map/ppermute | solution.py:184
  4.7 6.9 %collective-permute-start.1 = (bf16[144,192]{1,0:T(8,128)(2,1)}, bf16[144,192]{1,0:T(8,128)(2,1)S(1)}, u32[]{:S(2)}, u32[]{:S(2)}) collective-permute-start(bf16[144,192]{1,0:T(8,128)(2,1)} %get-tuple-element.98.refs_2_.refs_1_), channel_id=1, source_target_pairs={{0,1},{1,0},{2,3},{3,2},{4,5},{5,4},{6,7},{7,6},{8,9},{9,8},{10,11... | collective-permute-start | bytes 165896 | tf_op jit(solution)/shard_map/ppermute | solution.py:184
  4.8 5.9 %collective-permute-start = (bf16[144,192]{1,0:T(8,128)(2,1)}, bf16[144,192]{1,0:T(8,128)(2,1)S(1)}, u32[]{:S(2)}, u32[]{:S(2)}) collective-permute-start(bf16[144,192]{1,0:T(8,128)(2,1)} %get-tuple-element.98.refs_2_.refs_1_), channel_id=1, source_target_pairs={{0,2},{1,3},{2,0},{3,1},{4,6},{5,7},{6,4},{7,5},{8,10},{9,11},{10,... | collective-permute-start | bytes 165896 | tf_op jit(solution)/shard_map/ppermute | solution.py:184
  7.8 16.4 %collective-permute-start.3 = (bf16[384,768]{1,0:T(8,128)(2,1)}, bf16[384,768]{1,0:T(8,128)(2,1)S(1)}, u32[]{:S(2)}, u32[]{:S(2)}) collective-permute-start(bf16[384,768]{1,0:T(8,128)(2,1)} %get-tuple-element.101.refs_4_), channel_id=1, source_target_pairs={{0,2},{1,3},{2,0},{3,1},{4,6},{5,7},{6,4},{7,5},{8,10},{9,11},{10,... | collective-permute-start | bytes 1769480 | tf_op jit(solution)/shard_map/ppermute | solution.py:184
  7.8 32.2 %collective-permute-start.11 = (bf16[512,768]{1,0:T(8,128)(2,1)}, bf16[512,768]{1,0:T(8,128)(2,1)S(1)}, u32[]{:S(2)}, u32[]{:S(2)}) collective-permute-start(bf16[512,768]{1,0:T(8,128)(2,1)} %get-tuple-element.97.refs_0_.refs_1_.refs_7_), channel_id=1, source_target_pairs={{0,2},{1,3},{2,0},{3,1},{4,6},{5,7},{6,4},{7,5},{8,10},{9,11},{10,... | collective-permute-start | bytes 2359304 | tf_op jit(solution)/shard_map/ppermute | solution.py:184
  10.7 1.3 collective-permute-start.2
  10.7 0.9 copy-start.7
  11.6 1.0 copy-start.6
  11.6 6.8 %copy-start = (bf16[512,768]{1,0:T(8,128)(2,1)S(1)}, bf16[512,768]{1,0:T(8,128)(2,1)}, u32[]{:S(2)}) copy-start(bf16[512,768]{1,0:T(8,128)(2,1)} %get-tuple-element.97.refs_0_.refs_1_.refs_7_) | copy-start | bytes 2359300
  11.6 6.8 %copy-start.1 = (bf16[768,768]{1,0:T(8,128)(2,1)S(1)}, bf16[768,768]{1,0:T(8,128)(2,1)}, u32[]{:S(2)}) copy-start(bf16[768,768]{1,0:T(8,128)(2,1)} %refs_2_.5) | copy-start | bytes 3538948
  11.6 6.8 %copy-start.2 = (bf16[768,768]{1,0:T(8,128)(2,1)S(1)}, bf16[768,768]{1,0:T(8,128)(2,1)}, u32[]{:S(2)}) copy-start(bf16[768,768]{1,0:T(8,128)(2,1)} %refs_3_.5) | copy-start | bytes 3538948
  11.6 6.8 %copy-start.4 = (bf16[768]{0:T(1024)(128)(2,1)S(1)}, bf16[768]{0:T(1024)(128)(2,1)}, u32[]{:S(2)}) copy-start(bf16[768]{0:T(1024)(128)(2,1)} %refs_4_.5) | copy-start | bytes 4612
  13.5 9.9 %collective-permute-start.7 = (bf16[256,128]{1,0:T(8,128)(2,1)S(1)}, bf16[256,128]{1,0:T(8,128)(2,1)S(1)}, u32[]{:S(2)}, u32[]{:S(2)}) collective-permute-start(bf16[256,128]{1,0:T(8,128)(2,1)S(1)} %get-tuple-element.103.refs_0_), channel_id=1, source_target_pairs={{0,24},{4,28},{8,16},{12,20},{16,8},{20,12},{24,0},{28,4},{1,25},{... | collective-permute-start | bytes 196616 | tf_op jit(solution)/shard_map/ppermute | solution.py:184
  17.8 5.6 %collective-permute-start.6 = (bf16[256,128]{1,0:T(8,128)(2,1)S(1)}, bf16[256,128]{1,0:T(8,128)(2,1)S(1)}, u32[]{:S(2)}, u32[]{:S(2)}) collective-permute-start(bf16[256,128]{1,0:T(8,128)(2,1)S(1)} %get-tuple-element.103.refs_0_), channel_id=1, source_target_pairs={{0,8},{4,12},{8,0},{12,4},{16,24},{20,28},{24,16},{28,20},{1,9},{5... | collective-permute-start | bytes 196616 | tf_op jit(solution)/shard_map/ppermute | solution.py:184
  17.8 5.9 %collective-permute-start.5 = (bf16[256,128]{1,0:T(8,128)(2,1)S(1)}, bf16[256,128]{1,0:T(8,128)(2,1)S(1)}, u32[]{:S(2)}, u32[]{:S(2)}) collective-permute-start(bf16[256,128]{1,0:T(8,128)(2,1)S(1)} %get-tuple-element.103.refs_0_), channel_id=1, source_target_pairs={{0,16},{4,20},{8,24},{12,28},{16,0},{20,4},{24,8},{28,12},{1,17},{... | collective-permute-start | bytes 196616 | tf_op jit(solution)/shard_map/ppermute | solution.py:184
  23.3 3.0 %copy-start.3 = (bf16[384,768]{1,0:T(8,128)(2,1)S(1)}, bf16[384,768]{1,0:T(8,128)(2,1)}, u32[]{:S(2)}) copy-start(bf16[384,768]{1,0:T(8,128)(2,1)} %get-tuple-element.101.refs_4_) | copy-start | bytes 1769476
  24.2 2.1 %collective-permute-start.9 = (bf16[192,768]{1,0:T(8,128)(2,1)S(1)}, bf16[192,768]{1,0:T(8,128)(2,1)S(1)}, u32[]{:S(2)}, u32[]{:S(2)}) collective-permute-start(bf16[192,768]{1,0:T(8,128)(2,1)S(1)} %get-tuple-element.106), channel_id=1, source_target_pairs={{0,1},{1,0},{2,3},{3,2},{4,5},{5,4},{6,7},{7,6},{8,9},{9,8},{10,11... | collective-permute-start | bytes 884744 | tf_op jit(solution)/shard_map/ppermute | solution.py:184
  24.3 2.0 %collective-permute-start.8 = (bf16[192,768]{1,0:T(8,128)(2,1)S(1)}, bf16[192,768]{1,0:T(8,128)(2,1)S(1)}, u32[]{:S(2)}, u32[]{:S(2)}) collective-permute-start(bf16[192,768]{1,0:T(8,128)(2,1)S(1)} %get-tuple-element.105.refs_9_), channel_id=1, source_target_pairs={{0,1},{1,0},{2,3},{3,2},{4,5},{5,4},{6,7},{7,6},{8,9},{9,8},{10,11... | collective-permute-start | bytes 884744 | tf_op jit(solution)/shard_map/ppermute | solution.py:184
  24.8 8.3 %collective-permute-start.10 = (bf16[1024,128]{1,0:T(8,128)(2,1)S(1)}, bf16[1024,128]{1,0:T(8,128)(2,1)S(1)}, u32[]{:S(2)}, u32[]{:S(2)}) collective-permute-start(bf16[1024,128]{1,0:T(8,128)(2,1)S(1)} %stage.20.refs_1_.refs_4_), channel_id=1, source_target_pairs={{0,4},{4,0},{8,12},{12,8},{16,20},{20,16},{24,28},{28,24},{1,5},{5... | collective-permute-start | bytes 786440 | tf_op jit(solution)/shard_map/ppermute | solution.py:184
  26.3 15.6 %collective-permute-start.13 = (bf16[2,256,768]{2,1,0:T(8,128)(2,1)S(1)}, bf16[2,256,768]{2,1,0:T(8,128)(2,1)S(1)}, u32[]{:S(2)}, u32[]{:S(2)}) collective-permute-start(bf16[2,256,768]{2,1,0:T(8,128)(2,1)S(1)} %get-tuple-element.114), channel_id=1, source_target_pairs={{0,1},{1,0},{2,3},{3,2},{4,5},{5,4},{6,7},{7,6},{8,9},{9,8},{10,11... | collective-permute-start | bytes 2359304 | tf_op jit(solution)/shard_map/ppermute | solution.py:184
  26.3 6.8 %copy-start.9 = (s32[1,4]{1,0:T(1,128)S(1)}, s32[1,4]{1,0:T(1,128)}, u32[]{:S(2)}) copy-start(s32[1,4]{1,0:T(1,128)} %refs_1_.3) | copy-start | bytes 52
  40.0 2.4 %collective-permute-start.12 = (bf16[512,768]{1,0:T(8,128)(2,1)S(1)}, bf16[512,768]{1,0:T(8,128)(2,1)S(1)}, u32[]{:S(2)}, u32[]{:S(2)}) collective-permute-start(bf16[512,768]{1,0:T(8,128)(2,1)S(1)} %stage.22.refs_9_), channel_id=1, source_target_pairs={{0,1},{1,0},{2,3},{3,2},{4,5},{5,4},{6,7},{7,6},{8,9},{9,8},{10,11... | collective-permute-start | bytes 2359304 | tf_op jit(solution)/shard_map/ppermute | solution.py:184
  40.1 26.7 %collective-permute-start.15 = (bf16[128,1152]{1,0:T(8,128)(2,1)S(1)}, bf16[128,1152]{1,0:T(8,128)(2,1)S(1)}, u32[]{:S(2)}, u32[]{:S(2)}) collective-permute-start(bf16[128,1152]{1,0:T(8,128)(2,1)S(1)} %get-tuple-element.123), channel_id=1, source_target_pairs={{0,2},{1,3},{2,0},{3,1},{4,6},{5,7},{6,4},{7,5},{8,10},{9,11},{10,... | collective-permute-start | bytes 884744 | tf_op jit(solution)/shard_map/ppermute | solution.py:184
  47.7 15.8 %collective-permute-start.17 = (bf16[384,768]{1,0:T(8,128)(2,1)S(1)}, bf16[384,768]{1,0:T(8,128)(2,1)S(1)}, u32[]{:S(2)}, u32[]{:S(2)}) collective-permute-start(bf16[384,768]{1,0:T(8,128)(2,1)S(1)} %get-tuple-element.126), channel_id=1, source_target_pairs={{0,4},{4,0},{8,12},{12,8},{16,20},{20,16},{24,28},{28,24},{1,5},{5... | collective-permute-start | bytes 1769480 | tf_op jit(solution)/shard_map/ppermute | solution.py:184
  49.9 16.6 %collective-permute-start.18 = (bf16[384,768]{1,0:T(8,128)(2,1)S(1)}, bf16[384,768]{1,0:T(8,128)(2,1)S(1)}, u32[]{:S(2)}, u32[]{:S(2)}) collective-permute-start(bf16[384,768]{1,0:T(8,128)(2,1)S(1)} %get-tuple-element.128), channel_id=1, source_target_pairs={{0,8},{4,12},{8,0},{12,4},{16,24},{20,28},{24,16},{28,20},{1,9},{5... | collective-permute-start | bytes 1769480 | tf_op jit(solution)/shard_map/ppermute | solution.py:184
  57.7 9.1 %collective-permute-start.16 = (bf16[128,1152]{1,0:T(8,128)(2,1)S(1)}, bf16[128,1152]{1,0:T(8,128)(2,1)S(1)}, u32[]{:S(2)}, u32[]{:S(2)}) collective-permute-start(bf16[128,1152]{1,0:T(8,128)(2,1)S(1)} %get-tuple-element.124), channel_id=1, source_target_pairs={{0,2},{1,3},{2,0},{3,1},{4,6},{5,7},{6,4},{7,5},{8,10},{9,11},{10,... | collective-permute-start | bytes 884744 | tf_op jit(solution)/shard_map/ppermute | solution.py:184
  59.2 24.7 %collective-permute-start.20 = (bf16[256,960]{1,0:T(8,128)(2,1)S(1)}, bf16[256,960]{1,0:T(8,128)(2,1)S(1)}, u32[]{:S(2)}, u32[]{:S(2)}) collective-permute-start(bf16[256,960]{1,0:T(8,128)(2,1)S(1)} %get-tuple-element.118.refs_3_.refs_2_), channel_id=1, source_target_pairs={{0,1},{1,0},{2,3},{3,2},{4,5},{5,4},{6,7},{7,6},{8,9},{9,8},{10,11... | collective-permute-start | bytes 1474568 | tf_op jit(solution)/shard_map/ppermute | solution.py:184
  67.0 17.6 %collective-permute-start.21 = (bf16[256,960]{1,0:T(8,128)(2,1)S(1)}, bf16[256,960]{1,0:T(8,128)(2,1)S(1)}, u32[]{:S(2)}, u32[]{:S(2)}) collective-permute-start(bf16[256,960]{1,0:T(8,128)(2,1)S(1)} %get-tuple-element.135), channel_id=1, source_target_pairs={{0,1},{1,0},{2,3},{3,2},{4,5},{5,4},{6,7},{7,6},{8,9},{9,8},{10,11... | collective-permute-start | bytes 1474568 | tf_op jit(solution)/shard_map/ppermute | solution.py:184
  67.0 12.9 %collective-permute-start.22 = (bf16[192,768]{1,0:T(8,128)(2,1)S(1)}, bf16[192,768]{1,0:T(8,128)(2,1)S(1)}, u32[]{:S(2)}, u32[]{:S(2)}) collective-permute-start(bf16[192,768]{1,0:T(8,128)(2,1)S(1)} %get-tuple-element.129.refs_2_), channel_id=1, source_target_pairs={{0,8},{4,12},{8,0},{12,4},{16,24},{20,28},{24,16},{28,20},{1,9},{5... | collective-permute-start | bytes 884744 | tf_op jit(solution)/shard_map/ppermute | solution.py:184
  68.8 9.3 %collective-permute-start.14 = (bf16[1024,128]{1,0:T(8,128)(2,1)S(1)}, bf16[1024,128]{1,0:T(8,128)(2,1)S(1)}, u32[]{:S(2)}, u32[]{:S(2)}) collective-permute-start(bf16[1024,128]{1,0:T(8,128)(2,1)S(1)} %get-tuple-element.122), channel_id=1, source_target_pairs={{0,4},{4,0},{8,12},{12,8},{16,20},{20,16},{24,28},{28,24},{1,5},{5... | collective-permute-start | bytes 786440 | tf_op jit(solution)/shard_map/ppermute | solution.py:184
  71.3 52.6 %collective-permute-start.25 = (bf16[2,256,768]{2,1,0:T(8,128)(2,1)S(1)}, bf16[2,256,768]{2,1,0:T(8,128)(2,1)S(1)}, u32[]{:S(2)}, u32[]{:S(2)}) collective-permute-start(bf16[2,256,768]{2,1,0:T(8,128)(2,1)S(1)} %get-tuple-element.145), channel_id=1, source_target_pairs={{0,1},{1,0},{2,3},{3,2},{4,5},{5,4},{6,7},{7,6},{8,9},{9,8},{10,11... | collective-permute-start | bytes 2359304 | tf_op jit(solution)/shard_map/ppermute | solution.py:184
  78.2 15.8 %collective-permute-start.24 = (bf16[192,768]{1,0:T(8,128)(2,1)S(1)}, bf16[192,768]{1,0:T(8,128)(2,1)S(1)}, u32[]{:S(2)}, u32[]{:S(2)}) collective-permute-start(bf16[192,768]{1,0:T(8,128)(2,1)S(1)} %get-tuple-element.141), channel_id=1, source_target_pairs={{0,4},{4,0},{8,12},{12,8},{16,20},{20,16},{24,28},{28,24},{1,5},{5... | collective-permute-start | bytes 884744 | tf_op jit(solution)/shard_map/ppermute | solution.py:184
  80.1 19.6 %collective-permute-start.29 = (bf16[192,768]{1,0:T(8,128)(2,1)S(1)}, bf16[192,768]{1,0:T(8,128)(2,1)S(1)}, u32[]{:S(2)}, u32[]{:S(2)}) collective-permute-start(bf16[192,768]{1,0:T(8,128)(2,1)S(1)} %stage.25.refs_11_.refs_0_), channel_id=1, source_target_pairs={{0,16},{4,20},{8,24},{12,28},{16,0},{20,4},{24,8},{28,12},{1,17},{... | collective-permute-start | bytes 884744 | tf_op jit(solution)/shard_map/ppermute | solution.py:184
  84.0 8.2 %collective-permute-start.19 = (bf16[512,128]{1,0:T(8,128)(2,1)S(1)}, bf16[512,128]{1,0:T(8,128)(2,1)S(1)}, u32[]{:S(2)}, u32[]{:S(2)}) collective-permute-start(bf16[512,128]{1,0:T(8,128)(2,1)S(1)} %get-tuple-element.132.refs_2_), channel_id=1, source_target_pairs={{0,8},{4,12},{8,0},{12,4},{16,24},{20,28},{24,16},{28,20},{1,9},{5... | collective-permute-start | bytes 393224 | tf_op jit(solution)/shard_map/ppermute | solution.py:184
  85.7 18.3 %collective-permute-start.28 = (bf16[192,768]{1,0:T(8,128)(2,1)S(1)}, bf16[192,768]{1,0:T(8,128)(2,1)S(1)}, u32[]{:S(2)}, u32[]{:S(2)}) collective-permute-start(bf16[192,768]{1,0:T(8,128)(2,1)S(1)} %get-tuple-element.148), channel_id=1, source_target_pairs={{0,4},{4,0},{8,12},{12,8},{16,20},{20,16},{24,28},{28,24},{1,5},{5... | collective-permute-start | bytes 884744 | tf_op jit(solution)/shard_map/ppermute | solution.py:184
  92.3 6.3 %collective-permute-start.23 = (bf16[256,128]{1,0:T(8,128)(2,1)S(1)}, bf16[256,128]{1,0:T(8,128)(2,1)S(1)}, u32[]{:S(2)}, u32[]{:S(2)}) collective-permute-start(bf16[256,128]{1,0:T(8,128)(2,1)S(1)} %get-tuple-element.139.refs_2_), channel_id=1, source_target_pairs={{0,16},{4,20},{8,24},{12,28},{16,0},{20,4},{24,8},{28,12},{1,17},{... | collective-permute-start | bytes 196616 | tf_op jit(solution)/shard_map/ppermute | solution.py:184
  99.7 14.7 %collective-permute-start.32 = (bf16[192,768]{1,0:T(8,128)(2,1)S(1)}, bf16[192,768]{1,0:T(8,128)(2,1)S(1)}, u32[]{:S(2)}, u32[]{:S(2)}) collective-permute-start(bf16[192,768]{1,0:T(8,128)(2,1)S(1)} %stage.28.refs_2_), channel_id=1, source_target_pairs={{0,8},{4,12},{8,0},{12,4},{16,24},{20,28},{24,16},{28,20},{1,9},{5... | collective-permute-start | bytes 884744 | tf_op jit(solution)/shard_map/ppermute | solution.py:184
  101.2 3.1 %collective-permute-start.27 = (bf16[96,768]{1,0:T(8,128)(2,1)S(1)}, bf16[96,768]{1,0:T(8,128)(2,1)S(1)}, u32[]{:S(2)}, u32[]{:S(2)}) collective-permute-start(bf16[96,768]{1,0:T(8,128)(2,1)S(1)} %get-tuple-element.147), channel_id=1, source_target_pairs={{0,1},{1,0},{2,3},{3,2},{4,5},{5,4},{6,7},{7,6},{8,9},{9,8},{10,11... | collective-permute-start | bytes 442376 | tf_op jit(solution)/shard_map/ppermute | solution.py:184
  101.2 21.4 %collective-permute-start.26 = (bf16[192,768]{1,0:T(8,128)(2,1)S(1)}, bf16[192,768]{1,0:T(8,128)(2,1)S(1)}, u32[]{:S(2)}, u32[]{:S(2)}) collective-permute-start(bf16[192,768]{1,0:T(8,128)(2,1)S(1)} %stage.27.refs_10_.refs_0_), channel_id=1, source_target_pairs={{0,16},{4,20},{8,24},{12,28},{16,0},{20,4},{24,8},{28,12},{1,17},{... | collective-permute-start | bytes 884744 | tf_op jit(solution)/shard_map/ppermute | solution.py:184
  104.1 13.1 %collective-permute-start.31 = (bf16[96,768]{1,0:T(8,128)(2,1)S(1)}, bf16[96,768]{1,0:T(8,128)(2,1)S(1)}, u32[]{:S(2)}, u32[]{:S(2)}) collective-permute-start(bf16[96,768]{1,0:T(8,128)(2,1)S(1)} %get-tuple-element.149.refs_2_), channel_id=1, source_target_pairs={{0,8},{4,12},{8,0},{12,4},{16,24},{20,28},{24,16},{28,20},{1,9},{5... | collective-permute-start | bytes 442376 | tf_op jit(solution)/shard_map/ppermute | solution.py:184
  104.4 12.9 %collective-permute-start.30 = (bf16[48,768]{1,0:T(8,128)(2,1)S(1)}, bf16[48,768]{1,0:T(8,128)(2,1)S(1)}, u32[]{:S(2)}, u32[]{:S(2)}) collective-permute-start(bf16[48,768]{1,0:T(8,128)(2,1)S(1)} %get-tuple-element.151.refs_4_), channel_id=1, source_target_pairs={{0,2},{1,3},{2,0},{3,1},{4,6},{5,7},{6,4},{7,5},{8,10},{9,11},{10,... | collective-permute-start | bytes 221192 | tf_op jit(solution)/shard_map/ppermute | solution.py:184
  117.3 5.3 %collective-permute-start.33 = (bf16[48,768]{1,0:T(8,128)(2,1)S(1)}, bf16[48,768]{1,0:T(8,128)(2,1)S(1)}, u32[]{:S(2)}, u32[]{:S(2)}) collective-permute-start(bf16[48,768]{1,0:T(8,128)(2,1)S(1)} %stage.32.refs_0_.refs_2_), channel_id=1, source_target_pairs={{0,8},{4,12},{8,0},{12,4},{16,24},{20,28},{24,16},{28,20},{1,9},{5... | collective-permute-start | bytes 221192 | tf_op jit(solution)/shard_map/ppermute | solution.py:184
  118.6 8.5 %collective-permute-start.36 = (bf16[96,768]{1,0:T(8,128)(2,1)S(1)}, bf16[96,768]{1,0:T(8,128)(2,1)S(1)}, u32[]{:S(2)}, u32[]{:S(2)}) collective-permute-start(bf16[96,768]{1,0:T(8,128)(2,1)S(1)} %get-tuple-element.153.refs_2_.refs_0_), channel_id=1, source_target_pairs={{0,16},{4,20},{8,24},{12,28},{16,0},{20,4},{24,8},{28,12},{1,17},{... | collective-permute-start | bytes 442376 | tf_op jit(solution)/shard_map/ppermute | solution.py:184
  122.7 11.2 %collective-permute-start.35 = (bf16[192,768]{1,0:T(8,128)(2,1)S(1)}, bf16[192,768]{1,0:T(8,128)(2,1)S(1)}, u32[]{:S(2)}, u32[]{:S(2)}) collective-permute-start(bf16[192,768]{1,0:T(8,128)(2,1)S(1)} %stage.34.refs_2_.refs_0_), channel_id=1, source_target_pairs={{0,4},{4,0},{8,12},{12,8},{16,20},{20,16},{24,28},{28,24},{1,5},{5... | collective-permute-start | bytes 884744 | tf_op jit(solution)/shard_map/ppermute | solution.py:184
  124.1 17.2 %collective-permute-start.34 = (bf16[2,256,768]{2,1,0:T(8,128)(2,1)S(1)}, bf16[2,256,768]{2,1,0:T(8,128)(2,1)S(1)}, u32[]{:S(2)}, u32[]{:S(2)}) collective-permute-start(bf16[2,256,768]{2,1,0:T(8,128)(2,1)S(1)} %stage.35.refs_2_), channel_id=1, source_target_pairs={{0,2},{1,3},{2,0},{3,1},{4,6},{5,7},{6,4},{7,5},{8,10},{9,11},{10,... | collective-permute-start | bytes 2359304 | tf_op jit(solution)/shard_map/ppermute | solution.py:184
  127.2 6.7 %collective-permute-start.37 = (bf16[96,768]{1,0:T(8,128)(2,1)S(1)}, bf16[96,768]{1,0:T(8,128)(2,1)S(1)}, u32[]{:S(2)}, u32[]{:S(2)}) collective-permute-start(bf16[96,768]{1,0:T(8,128)(2,1)S(1)} %stage.36.refs_2_.refs_0_), channel_id=1, source_target_pairs={{0,8},{4,12},{8,0},{12,4},{16,24},{20,28},{24,16},{28,20},{1,9},{5... | collective-permute-start | bytes 442376 | tf_op jit(solution)/shard_map/ppermute | solution.py:184
  127.2 6.6 %collective-permute-start.38 = (bf16[48,768]{1,0:T(8,128)(2,1)S(1)}, bf16[48,768]{1,0:T(8,128)(2,1)S(1)}, u32[]{:S(2)}, u32[]{:S(2)}) collective-permute-start(bf16[48,768]{1,0:T(8,128)(2,1)S(1)} %stage.33.refs_2_.refs_0_), channel_id=1, source_target_pairs={{0,4},{4,0},{8,12},{12,8},{16,20},{20,16},{24,28},{28,24},{1,5},{5... | collective-permute-start | bytes 221192 | tf_op jit(solution)/shard_map/ppermute | solution.py:184
  128.5 18.0 %collective-permute-start.40 = (bf16[384,768]{1,0:T(8,128)(2,1)S(1)}, bf16[384,768]{1,0:T(8,128)(2,1)S(1)}, u32[]{:S(2)}, u32[]{:S(2)}) collective-permute-start(bf16[384,768]{1,0:T(8,128)(2,1)S(1)} %get-tuple-element.156.refs_0_), channel_id=1, source_target_pairs={{0,4},{4,0},{8,12},{12,8},{16,20},{20,16},{24,28},{28,24},{1,5},{5... | collective-permute-start | bytes 1769480 | tf_op jit(solution)/shard_map/ppermute | solution.py:184
  134.0 17.8 %collective-permute-start.42 = (bf16[384,768]{1,0:T(8,128)(2,1)S(1)}, bf16[384,768]{1,0:T(8,128)(2,1)S(1)}, u32[]{:S(2)}, u32[]{:S(2)}) collective-permute-start(bf16[384,768]{1,0:T(8,128)(2,1)S(1)} %stage.39.refs_8_.refs_0_), channel_id=1, source_target_pairs={{0,8},{4,12},{8,0},{12,4},{16,24},{20,28},{24,16},{28,20},{1,9},{5... | collective-permute-start | bytes 1769480 | tf_op jit(solution)/shard_map/ppermute | solution.py:184
  135.5 14.5 %collective-permute-start.41 = (bf16[192,768]{1,0:T(8,128)(2,1)S(1)}, bf16[192,768]{1,0:T(8,128)(2,1)S(1)}, u32[]{:S(2)}, u32[]{:S(2)}) collective-permute-start(bf16[192,768]{1,0:T(8,128)(2,1)S(1)} %stage.38.refs_2_.refs_0_), channel_id=1, source_target_pairs={{0,4},{4,0},{8,12},{12,8},{16,20},{20,16},{24,28},{28,24},{1,5},{5... | collective-permute-start | bytes 884744 | tf_op jit(solution)/shard_map/ppermute | solution.py:184
  136.7 11.3 %collective-permute-start.39 = (bf16[48,768]{1,0:T(8,128)(2,1)S(1)}, bf16[48,768]{1,0:T(8,128)(2,1)S(1)}, u32[]{:S(2)}, u32[]{:S(2)}) collective-permute-start(bf16[48,768]{1,0:T(8,128)(2,1)S(1)} %stage.37.refs_2_.refs_0_), channel_id=1, source_target_pairs={{0,16},{4,20},{8,24},{12,28},{16,0},{20,4},{24,8},{28,12},{1,17},{... | collective-permute-start | bytes 221192 | tf_op jit(solution)/shard_map/ppermute | solution.py:184
  150.0 0.7 copy-start.5

commit v6 on v5

--- a/solution.py
+++ b/solution.py
@@ -1186,13 +1186,13 @@
         flow(sequence, qo)
     flow(sequence, qo)
     flow(sequence, dn)
+    (grad_up,) = matrix(up, seq_orders[0], 1)
     layer_out, grad_tokens, _ = run(
         output_kernel,
         (shape((rows, width), BF),) * 2 + (shape((8, 128), F32),),
         (both_0, own, wo, vec, dn1, keep_a, back_a, back),
         name="output",
     )
-    (grad_up,) = matrix(up, seq_orders[0], 1)
     vector = shape((part,), F32)
     g1, b1, qb, kb, vb, ob, g2, b2, ub, db, wk, wv = run(
         functools.partial(vector_kernel, *[v.start for v in mix.pair()]),

time: 154 us -> 155 us (level); the launches traced: 154 us -> 153 us
  starting transfers between devices: 60.3 us -> 51.5 us
  Pallas kernels: 36.1 us -> 41.7 us
  waiting for transfers between devices: 53.9 us -> 56.2 us
    ppermute x43, starting transfers between devices: 60.3 us -> 51.5 us  [swap(): return lax.ppermute(value, axis, [(i, i ^ bit) for i in range(size)])]
    pallas_call x36, Pallas kernels: 36.1 us -> 41.7 us  [run(): pl.pallas_call(body, out_shape=outs, in_specs=list(specs.get('in_specs',...]
    ppermute x43, waiting for transfers between devices: 53.9 us -> 56.2 us  [swap(): return lax.ppermute(value, axis, [(i, i ^ bit) for i in range(size)])]
  transfers between devices with their start and end apart: 43 -> 43, of which waited for: 18 -> 16; matrix products, arithmetic and copies ran while one was open for 0% -> 0% of each run, Pallas kernels for 20% -> 24%
where the time goes in v6:
time: 155 us; the launch traced here: 153 us
  waiting for transfers between devices  56.2 us (36%)
  starting transfers between devices  51.5 us (33%)
  Pallas kernels  41.7 us (27%)
  local copies, waits for them, and re-layouts  2.19 us (1%)
    ppermute x43, waiting for transfers between devices, swap(): return lax.ppermute(value, axis, [(i, i ^ bit) for i in range(size)])  56.2 us
    ppermute x43, starting transfers between devices, swap(): return lax.ppermute(value, axis, [(i, i ^ bit) for i in range(size)])  51.5 us
    pallas_call x36, Pallas kernels, run(): pl.pallas_call(body, out_shape=outs, in_specs=list(specs.get('in_specs',...  41.7 us
  transfers between devices with their start and end apart: 43, of which 16 were waited for; matrix products, arithmetic and copies ran while one was open for 0% of the time, Pallas kernels for 24%

profile of v6, /device:TPU:0, one launch (start us, length us, event | category | flops | bytes accessed | tf_op | source)
XLA Modules:
  0.0 153.2 jit_solution(3554407904566492891)
XLA Ops:
  0.7 3.5 %pack.1 = (bf16[144,192]{1,0:T(8,128)(2,1)}, bf16[512,768]{1,0:T(8,128)(2,1)}, bf16[384,768]{1,0:T(8,128)(2,1)}, bf16[896,768]{1,0:T(8,128)(2,1)}) custom-call(bf16[256,768]{1,0:T(8,128)(2,1)} %bitcast.10, bf16[256,768]{1,0:T(8,128)(2,1)} %bitcast.12, bf16[192,768]{1,0:T(8,128)(2,1)} %refs_2_.3, bf16[192,768]{1,0:T(8,128)(2,1)} %refs_3_.3, ...), custom_call_target="tpu_custom_call" | custom-call | flops 2000000000 | bytes 1000 | tf_op jit(solution)/shard_map/pack/pallas_call | solution.py:62
  4.2 0.5 collective-permute-start.4
  4.8 2.9 %collective-permute-start = (bf16[144,192]{1,0:T(8,128)(2,1)}, bf16[144,192]{1,0:T(8,128)(2,1)S(1)}, u32[]{:S(2)}, u32[]{:S(2)}) collective-permute-start(bf16[144,192]{1,0:T(8,128)(2,1)} %get-tuple-element.98.refs_2_.refs_1_), channel_id=1, source_target_pairs={{0,2},{1,3},{2,0},{3,1},{4,6},{5,7},{6,4},{7,5},{8,10},{9,11},{10,... | collective-permute-start | bytes 165896 | tf_op jit(solution)/shard_map/ppermute | solution.py:184
  7.8 2.0 %collective-permute-start.11 = (bf16[512,768]{1,0:T(8,128)(2,1)}, bf16[512,768]{1,0:T(8,128)(2,1)S(1)}, u32[]{:S(2)}, u32[]{:S(2)}) collective-permute-start(bf16[512,768]{1,0:T(8,128)(2,1)} %get-tuple-element.97.refs_0_.refs_1_.refs_7_), channel_id=1, source_target_pairs={{0,2},{1,3},{2,0},{3,1},{4,6},{5,7},{6,4},{7,5},{8,10},{9,11},{10,... | collective-permute-start | bytes 2359304 | tf_op jit(solution)/shard_map/ppermute | solution.py:184
  9.9 0.1 multiply_sine_fusion
  10.1 0.6 collective-permute-done.refs_2_
  10.7 0.9 copy-done.7
  11.6 0.3 collective-permute-done.2.refs_4_
  12.0 0.6 copy-done.6
  12.6 0.9 front.1
  13.5 4.3 %collective-permute-start.7 = (bf16[256,128]{1,0:T(8,128)(2,1)S(1)}, bf16[256,128]{1,0:T(8,128)(2,1)S(1)}, u32[]{:S(2)}, u32[]{:S(2)}) collective-permute-start(bf16[256,128]{1,0:T(8,128)(2,1)S(1)} %get-tuple-element.103.refs_0_), channel_id=1, source_target_pairs={{0,24},{4,28},{8,16},{12,20},{16,8},{20,12},{24,0},{28,4},{1,25},{... | collective-permute-start | bytes 196616 | tf_op jit(solution)/shard_map/ppermute | solution.py:184
  17.8 0.6 collective-permute-start.5
  18.4 4.9 %mlp_near.1 = (bf16[2,256,768]{2,1,0:T(8,128)(2,1)S(1)}, bf16[2,256,768]{2,1,0:T(8,128)(2,1)S(1)}, bf16[2,256,192]{2,1,0:T(8,128)(2,1)S(1)}, f32[768,768]{1,0:T(...) custom-call(bf16[512,768]{1,0:T(8,128)(2,1)S(1)} %copy-done, ...), custom_call_target="tpu_custom_call" | custom-call | flops 1 | bytes 1000 | tf_op jit(solution)/shard_map/mlp_near/pallas_call | solution.py:62
  23.4 0.3 collective-permute-done.5.refs_1_
  23.7 0.5 collective-permute-done.3.refs_0_.refs_5_
  24.3 0.5 collective-permute-start.8
  24.8 1.5 collective-permute-start.10
  26.3 1.0 query.1
  27.3 5.8 %collective-permute-done.10.refs_5_ = bf16[1024,128]{1,0:T(8,128)(2,1)S(1)} collective-permute-done((bf16[1024,128]{1,0:T(8,128)(2,1)S(1)}, bf16[1024,128]{1,0:T(8,128)(2,1)S(1)}, u32[]{:S(2)}, u32[]{:S(2)}) %collective-permute-start.10) | collective-permute-done | bytes 262176 | tf_op jit(solution)/shard_map/ppermute | solution.py:184
  33.1 10.3 %attend.2 = (bf16[128,768]{1,0:T(8,128)(2,1)S(1)}, bf16[128,1152]{1,0:T(8,128)(2,1)S(1)}, bf16[128,960]{1,0:T(8,128)(2,1)S(1)}, f32[2048,128]{1,0:T(8,128)S(1)}) custom-call(s32[16]{0:T(128)S(1)} %copy-done.8, s32[1,4]{1,0:T(1,128)S(1)} %copy-done.9, bf16[768,256]{1,0:T(8,128)(2,1)S(1)} %get-tuple-element.107.refs_2_.refs_7_, ...), custom_call_target="tpu_custom_call" | custom-call | flops 2000000000 | bytes 1000 | tf_op jit(solution)/shard_map/attend/pallas_call | solution.py:62
  43.6 1.6 %collective-permute-start.15 = (bf16[128,1152]{1,0:T(8,128)(2,1)S(1)}, bf16[128,1152]{1,0:T(8,128)(2,1)S(1)}, u32[]{:S(2)}, u32[]{:S(2)}) collective-permute-start(bf16[128,1152]{1,0:T(8,128)(2,1)S(1)} %get-tuple-element.123), channel_id=1, source_target_pairs={{0,2},{1,3},{2,0},{3,1},{4,6},{5,7},{6,4},{7,5},{8,10},{9,11},{10,... | collective-permute-start | bytes 884744 | tf_op jit(solution)/shard_map/ppermute | solution.py:184
  45.2 0.7 collective-permute-done.12.refs_1_.refs_10_
  45.9 5.3 %mlp_far.1 = (bf16[2,256,768]{2,1,0:T(8,128)(2,1)S(1)}, bf16[2,256,768]{2,1,0:T(8,128)(2,1)S(1)}, bf16[2,256,192]{2,1,0:T(8,128)(2,1)S(1)}, bf16[384,768]{1,0:T(...) custom-call(bf16[512,768]{1,0:T(8,128)(2,1)S(1)} %collective-permute, ...), custom_call_target="tpu_custom_call" | custom-call | flops 14000000000 | bytes 1000 | tf_op jit(solution)/shard_map/mlp_far/pallas_call | solution.py:62
  51.4 4.7 %attend.3 = (bf16[256,768]{1,0:T(8,128)(2,1)S(1)}, bf16[128,1152]{1,0:T(8,128)(2,1)S(1)}, bf16[256,960]{1,0:T(8,128)(2,1)S(1)}, bf16[1024,128]{1,0:T(8,128)(2,1)S(1)}, bf16[1024,128]{1,0:T(8,128)(2,1)S(1)}) custom-call(s32[16]{0:T(128)S(1)} %copy-done.8, s32[1,4]{1,0:T(1,128)S(1)} %copy-done.9, bf16[768,256]{1,0:T(8,128)(2,1)S(1)} %get-tuple-element.107.refs_2_.refs_7_, ...), custom_call_target="tpu_custom_call" | custom-call | flops 14000000000 | bytes 1000 | tf_op jit(solution)/shard_map/attend/pallas_call | solution.py:62
  56.1 1.6 %collective-permute-start.16 = (bf16[128,1152]{1,0:T(8,128)(2,1)S(1)}, bf16[128,1152]{1,0:T(8,128)(2,1)S(1)}, u32[]{:S(2)}, u32[]{:S(2)}) collective-permute-start(bf16[128,1152]{1,0:T(8,128)(2,1)S(1)} %get-tuple-element.124), channel_id=1, source_target_pairs={{0,2},{1,3},{2,0},{3,1},{4,6},{5,7},{6,4},{7,5},{8,10},{9,11},{10,... | collective-permute-start | bytes 884744 | tf_op jit(solution)/shard_map/ppermute | solution.py:184
  57.7 8.9 %collective-permute-done.17.refs_1_ = bf16[384,768]{1,0:T(8,128)(2,1)S(1)} collective-permute-done((bf16[384,768]{1,0:T(8,128)(2,1)S(1)}, bf16[384,768]{1,0:T(8,128)(2,1)S(1)}, u32[]{:S(2)}, u32[]{:S(2)}) %collective-permute-start.17) | collective-permute-done | bytes 589856 | tf_op jit(solution)/shard_map/ppermute | solution.py:184
  66.7 0.3 stage.23
  67.0 0.1 relay.1
  67.2 2.9 %collective-permute-start.22 = (bf16[192,768]{1,0:T(8,128)(2,1)S(1)}, bf16[192,768]{1,0:T(8,128)(2,1)S(1)}, u32[]{:S(2)}, u32[]{:S(2)}) collective-permute-start(bf16[192,768]{1,0:T(8,128)(2,1)S(1)} %get-tuple-element.129.refs_2_), channel_id=1, source_target_pairs={{0,8},{4,12},{8,0},{12,4},{16,24},{20,28},{24,16},{28,20},{1,9},{5... | collective-permute-start | bytes 884744 | tf_op jit(solution)/shard_map/ppermute | solution.py:184
  70.1 0.2 collective-permute-start.25
  70.2 8.2 %collective-permute-done.14.refs_1_ = bf16[1024,128]{1,0:T(8,128)(2,1)S(1)} collective-permute-done((bf16[1024,128]{1,0:T(8,128)(2,1)S(1)}, bf16[1024,128]{1,0:T(8,128)(2,1)S(1)}, u32[]{:S(2)}, u32[]{:S(2)}) %collective-permute-start.14) | collective-permute-done | bytes 262176 | tf_op jit(solution)/shard_map/ppermute | solution.py:184
  78.4 0.3 collective-permute-start.24
  78.9 5.0 %collective-permute-start.29 = (bf16[192,768]{1,0:T(8,128)(2,1)S(1)}, bf16[192,768]{1,0:T(8,128)(2,1)S(1)}, u32[]{:S(2)}, u32[]{:S(2)}) collective-permute-start(bf16[192,768]{1,0:T(8,128)(2,1)S(1)} %stage.25.refs_11_.refs_0_), channel_id=1, source_target_pairs={{0,16},{4,20},{8,24},{12,28},{16,0},{20,4},{24,8},{28,12},{1,17},{... | collective-permute-start | bytes 884744 | tf_op jit(solution)/shard_map/ppermute | solution.py:184
  83.9 0.3 collective-permute-start.19
  84.2 1.1 weight.1
  85.3 0.7 collective-permute-start.28
  86.0 6.5 %collective-permute-done.19.refs_1_ = bf16[512,128]{1,0:T(8,128)(2,1)S(1)} collective-permute-done((bf16[512,128]{1,0:T(8,128)(2,1)S(1)}, bf16[512,128]{1,0:T(8,128)(2,1)S(1)}, u32[]{:S(2)}, u32[]{:S(2)}) %collective-permute-start.19) | collective-permute-done | bytes 131104 | tf_op jit(solution)/shard_map/ppermute | solution.py:184
  92.5 0.9 collective-permute-start.23
  93.5 4.8 %collective-permute-done.23.refs_8_ = bf16[256,128]{1,0:T(8,128)(2,1)S(1)} collective-permute-done((bf16[256,128]{1,0:T(8,128)(2,1)S(1)}, bf16[256,128]{1,0:T(8,128)(2,1)S(1)}, u32[]{:S(2)}, u32[]{:S(2)}) %collective-permute-start.23) | collective-permute-done | bytes 65568 | tf_op jit(solution)/shard_map/ppermute | solution.py:184
  98.3 1.1 tail.1
  99.5 2.0 %collective-permute-start.32 = (bf16[192,768]{1,0:T(8,128)(2,1)S(1)}, bf16[192,768]{1,0:T(8,128)(2,1)S(1)}, u32[]{:S(2)}, u32[]{:S(2)}) collective-permute-start(bf16[192,768]{1,0:T(8,128)(2,1)S(1)} %stage.28.refs_2_), channel_id=1, source_target_pairs={{0,8},{4,12},{8,0},{12,4},{16,24},{20,28},{24,16},{28,20},{1,9},{5... | collective-permute-start | bytes 884744 | tf_op jit(solution)/shard_map/ppermute | solution.py:184
  101.5 2.0 %collective-permute-start.26 = (bf16[192,768]{1,0:T(8,128)(2,1)S(1)}, bf16[192,768]{1,0:T(8,128)(2,1)S(1)}, u32[]{:S(2)}, u32[]{:S(2)}) collective-permute-start(bf16[192,768]{1,0:T(8,128)(2,1)S(1)} %stage.27.refs_10_.refs_0_), channel_id=1, source_target_pairs={{0,16},{4,20},{8,24},{12,28},{16,0},{20,4},{24,8},{28,12},{1,17},{... | collective-permute-start | bytes 884744 | tf_op jit(solution)/shard_map/ppermute | solution.py:184
  103.6 0.2 collective-permute-start.31
  103.9 1.8 %collective-permute-start.30 = (bf16[48,768]{1,0:T(8,128)(2,1)S(1)}, bf16[48,768]{1,0:T(8,128)(2,1)S(1)}, u32[]{:S(2)}, u32[]{:S(2)}) collective-permute-start(bf16[48,768]{1,0:T(8,128)(2,1)S(1)} %get-tuple-element.151.refs_4_), channel_id=1, source_target_pairs={{0,2},{1,3},{2,0},{3,1},{4,6},{5,7},{6,4},{7,5},{8,10},{9,11},{10,... | collective-permute-start | bytes 221192 | tf_op jit(solution)/shard_map/ppermute | solution.py:184
  105.6 7.3 %collective-permute-done.32.refs_3_ = bf16[192,768]{1,0:T(8,128)(2,1)S(1)} collective-permute-done((bf16[192,768]{1,0:T(8,128)(2,1)S(1)}, bf16[192,768]{1,0:T(8,128)(2,1)S(1)}, u32[]{:S(2)}, u32[]{:S(2)}) %collective-permute-start.32) | collective-permute-done | bytes 294944 | tf_op jit(solution)/shard_map/ppermute | solution.py:184
  112.9 3.5 %collective-permute-done.31.refs_1_ = bf16[96,768]{1,0:T(8,128)(2,1)S(1)} collective-permute-done((bf16[96,768]{1,0:T(8,128)(2,1)S(1)}, bf16[96,768]{1,0:T(8,128)(2,1)S(1)}, u32[]{:S(2)}, u32[]{:S(2)}) %collective-permute-start.31) | collective-permute-done | bytes 147488 | tf_op jit(solution)/shard_map/ppermute | solution.py:184
  116.6 1.7 %collective-permute-start.33 = (bf16[48,768]{1,0:T(8,128)(2,1)S(1)}, bf16[48,768]{1,0:T(8,128)(2,1)S(1)}, u32[]{:S(2)}, u32[]{:S(2)}) collective-permute-start(bf16[48,768]{1,0:T(8,128)(2,1)S(1)} %stage.32.refs_0_.refs_2_), channel_id=1, source_target_pairs={{0,8},{4,12},{8,0},{12,4},{16,24},{20,28},{24,16},{28,20},{1,9},{5... | collective-permute-start | bytes 221192 | tf_op jit(solution)/shard_map/ppermute | solution.py:184
  118.3 2.9 %collective-permute-start.37 = (bf16[96,768]{1,0:T(8,128)(2,1)S(1)}, bf16[96,768]{1,0:T(8,128)(2,1)S(1)}, u32[]{:S(2)}, u32[]{:S(2)}) collective-permute-start(bf16[96,768]{1,0:T(8,128)(2,1)S(1)} %get-tuple-element.153.refs_2_.refs_0_), channel_id=1, source_target_pairs={{0,16},{4,20},{8,24},{12,28},{16,0},{20,4},{24,8},{28,12},{1,17},{... | collective-permute-start | bytes 442376 | tf_op jit(solution)/shard_map/ppermute | solution.py:184
  121.3 2.1 %collective-permute-start.36 = (bf16[192,768]{1,0:T(8,128)(2,1)S(1)}, bf16[192,768]{1,0:T(8,128)(2,1)S(1)}, u32[]{:S(2)}, u32[]{:S(2)}) collective-permute-start(bf16[192,768]{1,0:T(8,128)(2,1)S(1)} %stage.34.refs_2_.refs_0_), channel_id=1, source_target_pairs={{0,4},{4,0},{8,12},{12,8},{16,20},{20,16},{24,28},{28,24},{1,5},{5... | collective-permute-start | bytes 884744 | tf_op jit(solution)/shard_map/ppermute | solution.py:184
  123.4 0.2 stage.35.refs_2_
  123.6 2.9 %collective-permute-start.34 = (bf16[2,256,768]{2,1,0:T(8,128)(2,1)S(1)}, bf16[2,256,768]{2,1,0:T(8,128)(2,1)S(1)}, u32[]{:S(2)}, u32[]{:S(2)}) collective-permute-start(bf16[2,256,768]{2,1,0:T(8,128)(2,1)S(1)} %stage.35.refs_2_), channel_id=1, source_target_pairs={{0,2},{1,3},{2,0},{3,1},{4,6},{5,7},{6,4},{7,5},{8,10},{9,11},{10,... | collective-permute-start | bytes 2359304 | tf_op jit(solution)/shard_map/ppermute | solution.py:184
  126.6 2.1 %collective-permute-start.39 = (bf16[48,768]{1,0:T(8,128)(2,1)S(1)}, bf16[48,768]{1,0:T(8,128)(2,1)S(1)}, u32[]{:S(2)}, u32[]{:S(2)}) collective-permute-start(bf16[48,768]{1,0:T(8,128)(2,1)S(1)} %stage.33.refs_2_.refs_0_), channel_id=1, source_target_pairs={{0,4},{4,0},{8,12},{12,8},{16,20},{20,16},{24,28},{28,24},{1,5},{5... | collective-permute-start | bytes 221192 | tf_op jit(solution)/shard_map/ppermute | solution.py:184
  128.8 3.3 %collective-permute-done.39.refs_1_ = bf16[48,768]{1,0:T(8,128)(2,1)S(1)} collective-permute-done((bf16[48,768]{1,0:T(8,128)(2,1)S(1)}, bf16[48,768]{1,0:T(8,128)(2,1)S(1)}, u32[]{:S(2)}, u32[]{:S(2)}) %collective-permute-start.39) | collective-permute-done | bytes 73760 | tf_op jit(solution)/shard_map/ppermute | solution.py:184
  132.1 0.9 collective-permute-done.38.refs_1_
  133.1 0.9 collective-permute-start.42
  134.0 2.3 %collective-permute-start.41 = (bf16[192,768]{1,0:T(8,128)(2,1)S(1)}, bf16[192,768]{1,0:T(8,128)(2,1)S(1)}, u32[]{:S(2)}, u32[]{:S(2)}) collective-permute-start(bf16[192,768]{1,0:T(8,128)(2,1)S(1)} %stage.38.refs_2_.refs_0_), channel_id=1, source_target_pairs={{0,4},{4,0},{8,12},{12,8},{16,20},{20,16},{24,28},{28,24},{1,5},{5... | collective-permute-start | bytes 884744 | tf_op jit(solution)/shard_map/ppermute | solution.py:184
  136.3 4.3 %collective-permute-start.40 = (bf16[48,768]{1,0:T(8,128)(2,1)S(1)}, bf16[48,768]{1,0:T(8,128)(2,1)S(1)}, u32[]{:S(2)}, u32[]{:S(2)}) collective-permute-start(bf16[48,768]{1,0:T(8,128)(2,1)S(1)} %stage.37.refs_2_.refs_0_), channel_id=1, source_target_pairs={{0,16},{4,20},{8,24},{12,28},{16,0},{20,4},{24,8},{28,12},{1,17},{... | collective-permute-start | bytes 221192 | tf_op jit(solution)/shard_map/ppermute | solution.py:184
  140.6 4.3 %collective-permute-done.35.refs_1_ = bf16[384,768]{1,0:T(8,128)(2,1)S(1)} collective-permute-done((bf16[384,768]{1,0:T(8,128)(2,1)S(1)}, bf16[384,768]{1,0:T(8,128)(2,1)S(1)}, u32[]{:S(2)}, u32[]{:S(2)}) %collective-permute-start.35) | collective-permute-done | bytes 589856 | tf_op jit(solution)/shard_map/ppermute | solution.py:184
  144.9 1.5 matrix.3
  146.4 1.8 %output.1 = (bf16[256,768]{1,0:T(8,128)(2,1)}, bf16[256,768]{1,0:T(8,128)(2,1)}, f32[8,128]{1,0:T(8,128)S(1)}) custom-call(bf16[512,768]{1,0:T(8,128)(2,1)S(1)} %copy-done, bf16[256,768]{1,0:T(8,128)(2,1)S(1)} %get-tuple-element.116.refs_2_.refs_1_, bf16[768,768]{1,0:T(8,128)(2,1)S(1)} %get-tuple-element.117.refs_2_, ...), custom_call_target="tpu_custom_call" | custom-call | flops 1 | bytes 1000 | tf_op jit(solution)/shard_map/output/pallas_call | solution.py:62
  148.3 1.0 vector.1
  149.2 0.7 copy-done.5
  149.9 1.1 matrix.4
  151.0 2.1 %matrix.5 = (f32[768,768]{1,0:T(8,128)}, f32[8,128]{1,0:T(8,128)}) custom-call(bf16[384,768]{1,0:T(8,128)(2,1)S(1)} %stage.39.refs_2_.refs_0_, bf16[384,768]{1,0:T(8,128)(2,1)S(1)} %collective-permute-done.42.refs_1_, f32[8,128]{1,0:T(8,128)S(1)} %get-tuple-element.173.refs_2_), custom_call_target="tpu_custom_call" | custom-call | flops 1 | bytes 1000 | tf_op jit(solution)/shard_map/matrix/pallas_call | solution.py:62
  (82 shorter events, 1.9 us)
Async XLA Ops:
  0.7 9.1 %copy-start.8 = (s32[16]{0:T(128)S(1)}, s32[16]{0:T(128)}, u32[]{:S(2)}) copy-start(s32[16]{0:T(128)} %refs_0_.3) | copy-start | bytes 196
  4.2 13.6 %collective-permute-start.4 = (bf16[896,768]{1,0:T(8,128)(2,1)}, bf16[896,768]{1,0:T(8,128)(2,1)S(1)}, u32[]{:S(2)}, u32[]{:S(2)}) collective-permute-start(bf16[896,768]{1,0:T(8,128)(2,1)} %get-tuple-element.102), channel_id=1, source_target_pairs={{0,1},{1,0},{2,3},{3,2},{4,5},{5,4},{6,7},{7,6},{8,9},{9,8},{10,11... | collective-permute-start | bytes 4128776 | tf_op jit(solution)/shard_map/ppermute | solution.py:184
  4.7 6.9 %collective-permute-start.1 = (bf16[144,192]{1,0:T(8,128)(2,1)}, bf16[144,192]{1,0:T(8,128)(2,1)S(1)}, u32[]{:S(2)}, u32[]{:S(2)}) collective-permute-start(bf16[144,192]{1,0:T(8,128)(2,1)} %get-tuple-element.98.refs_2_.refs_1_), channel_id=1, source_target_pairs={{0,1},{1,0},{2,3},{3,2},{4,5},{5,4},{6,7},{7,6},{8,9},{9,8},{10,11... | collective-permute-start | bytes 165896 | tf_op jit(solution)/shard_map/ppermute | solution.py:184
  4.8 5.9 %collective-permute-start = (bf16[144,192]{1,0:T(8,128)(2,1)}, bf16[144,192]{1,0:T(8,128)(2,1)S(1)}, u32[]{:S(2)}, u32[]{:S(2)}) collective-permute-start(bf16[144,192]{1,0:T(8,128)(2,1)} %get-tuple-element.98.refs_2_.refs_1_), channel_id=1, source_target_pairs={{0,2},{1,3},{2,0},{3,1},{4,6},{5,7},{6,4},{7,5},{8,10},{9,11},{10,... | collective-permute-start | bytes 165896 | tf_op jit(solution)/shard_map/ppermute | solution.py:184
  7.8 16.4 %collective-permute-start.3 = (bf16[384,768]{1,0:T(8,128)(2,1)}, bf16[384,768]{1,0:T(8,128)(2,1)S(1)}, u32[]{:S(2)}, u32[]{:S(2)}) collective-permute-start(bf16[384,768]{1,0:T(8,128)(2,1)} %get-tuple-element.101.refs_4_), channel_id=1, source_target_pairs={{0,2},{1,3},{2,0},{3,1},{4,6},{5,7},{6,4},{7,5},{8,10},{9,11},{10,... | collective-permute-start | bytes 1769480 | tf_op jit(solution)/shard_map/ppermute | solution.py:184
  7.8 35.7 %collective-permute-start.11 = (bf16[512,768]{1,0:T(8,128)(2,1)}, bf16[512,768]{1,0:T(8,128)(2,1)S(1)}, u32[]{:S(2)}, u32[]{:S(2)}) collective-permute-start(bf16[512,768]{1,0:T(8,128)(2,1)} %get-tuple-element.97.refs_0_.refs_1_.refs_7_), channel_id=1, source_target_pairs={{0,2},{1,3},{2,0},{3,1},{4,6},{5,7},{6,4},{7,5},{8,10},{9,11},{10,... | collective-permute-start | bytes 2359304 | tf_op jit(solution)/shard_map/ppermute | solution.py:184
  10.7 1.3 collective-permute-start.2
  10.7 0.9 copy-start.7
  11.6 1.0 copy-start.6
  11.6 6.8 %copy-start = (bf16[512,768]{1,0:T(8,128)(2,1)S(1)}, bf16[512,768]{1,0:T(8,128)(2,1)}, u32[]{:S(2)}) copy-start(bf16[512,768]{1,0:T(8,128)(2,1)} %get-tuple-element.97.refs_0_.refs_1_.refs_7_) | copy-start | bytes 2359300
  11.6 6.8 %copy-start.1 = (bf16[768,768]{1,0:T(8,128)(2,1)S(1)}, bf16[768,768]{1,0:T(8,128)(2,1)}, u32[]{:S(2)}) copy-start(bf16[768,768]{1,0:T(8,128)(2,1)} %refs_2_.5) | copy-start | bytes 3538948
  11.6 6.8 %copy-start.2 = (bf16[768,768]{1,0:T(8,128)(2,1)S(1)}, bf16[768,768]{1,0:T(8,128)(2,1)}, u32[]{:S(2)}) copy-start(bf16[768,768]{1,0:T(8,128)(2,1)} %refs_3_.5) | copy-start | bytes 3538948
  11.6 6.8 %copy-start.4 = (bf16[768]{0:T(1024)(128)(2,1)S(1)}, bf16[768]{0:T(1024)(128)(2,1)}, u32[]{:S(2)}) copy-start(bf16[768]{0:T(1024)(128)(2,1)} %refs_4_.5) | copy-start | bytes 4612
  13.5 9.9 %collective-permute-start.7 = (bf16[256,128]{1,0:T(8,128)(2,1)S(1)}, bf16[256,128]{1,0:T(8,128)(2,1)S(1)}, u32[]{:S(2)}, u32[]{:S(2)}) collective-permute-start(bf16[256,128]{1,0:T(8,128)(2,1)S(1)} %get-tuple-element.103.refs_0_), channel_id=1, source_target_pairs={{0,24},{4,28},{8,16},{12,20},{16,8},{20,12},{24,0},{28,4},{1,25},{... | collective-permute-start | bytes 196616 | tf_op jit(solution)/shard_map/ppermute | solution.py:184
  17.8 5.6 %collective-permute-start.6 = (bf16[256,128]{1,0:T(8,128)(2,1)S(1)}, bf16[256,128]{1,0:T(8,128)(2,1)S(1)}, u32[]{:S(2)}, u32[]{:S(2)}) collective-permute-start(bf16[256,128]{1,0:T(8,128)(2,1)S(1)} %get-tuple-element.103.refs_0_), channel_id=1, source_target_pairs={{0,8},{4,12},{8,0},{12,4},{16,24},{20,28},{24,16},{28,20},{1,9},{5... | collective-permute-start | bytes 196616 | tf_op jit(solution)/shard_map/ppermute | solution.py:184
  17.8 5.9 %collective-permute-start.5 = (bf16[256,128]{1,0:T(8,128)(2,1)S(1)}, bf16[256,128]{1,0:T(8,128)(2,1)S(1)}, u32[]{:S(2)}, u32[]{:S(2)}) collective-permute-start(bf16[256,128]{1,0:T(8,128)(2,1)S(1)} %get-tuple-element.103.refs_0_), channel_id=1, source_target_pairs={{0,16},{4,20},{8,24},{12,28},{16,0},{20,4},{24,8},{28,12},{1,17},{... | collective-permute-start | bytes 196616 | tf_op jit(solution)/shard_map/ppermute | solution.py:184
  23.3 3.0 %copy-start.3 = (bf16[384,768]{1,0:T(8,128)(2,1)S(1)}, bf16[384,768]{1,0:T(8,128)(2,1)}, u32[]{:S(2)}) copy-start(bf16[384,768]{1,0:T(8,128)(2,1)} %get-tuple-element.101.refs_4_) | copy-start | bytes 1769476
  24.2 2.1 %collective-permute-start.9 = (bf16[192,768]{1,0:T(8,128)(2,1)S(1)}, bf16[192,768]{1,0:T(8,128)(2,1)S(1)}, u32[]{:S(2)}, u32[]{:S(2)}) collective-permute-start(bf16[192,768]{1,0:T(8,128)(2,1)S(1)} %get-tuple-element.106), channel_id=1, source_target_pairs={{0,1},{1,0},{2,3},{3,2},{4,5},{5,4},{6,7},{7,6},{8,9},{9,8},{10,11... | collective-permute-start | bytes 884744 | tf_op jit(solution)/shard_map/ppermute | solution.py:184
  24.3 2.0 %collective-permute-start.8 = (bf16[192,768]{1,0:T(8,128)(2,1)S(1)}, bf16[192,768]{1,0:T(8,128)(2,1)S(1)}, u32[]{:S(2)}, u32[]{:S(2)}) collective-permute-start(bf16[192,768]{1,0:T(8,128)(2,1)S(1)} %get-tuple-element.105.refs_9_), channel_id=1, source_target_pairs={{0,1},{1,0},{2,3},{3,2},{4,5},{5,4},{6,7},{7,6},{8,9},{9,8},{10,11... | collective-permute-start | bytes 884744 | tf_op jit(solution)/shard_map/ppermute | solution.py:184
  24.8 8.3 %collective-permute-start.10 = (bf16[1024,128]{1,0:T(8,128)(2,1)S(1)}, bf16[1024,128]{1,0:T(8,128)(2,1)S(1)}, u32[]{:S(2)}, u32[]{:S(2)}) collective-permute-start(bf16[1024,128]{1,0:T(8,128)(2,1)S(1)} %stage.20.refs_1_.refs_4_), channel_id=1, source_target_pairs={{0,4},{4,0},{8,12},{12,8},{16,20},{20,16},{24,28},{28,24},{1,5},{5... | collective-permute-start | bytes 786440 | tf_op jit(solution)/shard_map/ppermute | solution.py:184
  26.3 18.9 %collective-permute-start.13 = (bf16[2,256,768]{2,1,0:T(8,128)(2,1)S(1)}, bf16[2,256,768]{2,1,0:T(8,128)(2,1)S(1)}, u32[]{:S(2)}, u32[]{:S(2)}) collective-permute-start(bf16[2,256,768]{2,1,0:T(8,128)(2,1)S(1)} %get-tuple-element.114), channel_id=1, source_target_pairs={{0,1},{1,0},{2,3},{3,2},{4,5},{5,4},{6,7},{7,6},{8,9},{9,8},{10,11... | collective-permute-start | bytes 2359304 | tf_op jit(solution)/shard_map/ppermute | solution.py:184
  26.3 6.8 %copy-start.9 = (s32[1,4]{1,0:T(1,128)S(1)}, s32[1,4]{1,0:T(1,128)}, u32[]{:S(2)}) copy-start(s32[1,4]{1,0:T(1,128)} %refs_1_.3) | copy-start | bytes 52
  43.5 2.4 %collective-permute-start.12 = (bf16[512,768]{1,0:T(8,128)(2,1)S(1)}, bf16[512,768]{1,0:T(8,128)(2,1)S(1)}, u32[]{:S(2)}, u32[]{:S(2)}) collective-permute-start(bf16[512,768]{1,0:T(8,128)(2,1)S(1)} %stage.22.refs_9_), channel_id=1, source_target_pairs={{0,1},{1,0},{2,3},{3,2},{4,5},{5,4},{6,7},{7,6},{8,9},{9,8},{10,11... | collective-permute-start | bytes 2359304 | tf_op jit(solution)/shard_map/ppermute | solution.py:184
  43.6 23.4 %collective-permute-start.15 = (bf16[128,1152]{1,0:T(8,128)(2,1)S(1)}, bf16[128,1152]{1,0:T(8,128)(2,1)S(1)}, u32[]{:S(2)}, u32[]{:S(2)}) collective-permute-start(bf16[128,1152]{1,0:T(8,128)(2,1)S(1)} %get-tuple-element.123), channel_id=1, source_target_pairs={{0,2},{1,3},{2,0},{3,1},{4,6},{5,7},{6,4},{7,5},{8,10},{9,11},{10,... | collective-permute-start | bytes 884744 | tf_op jit(solution)/shard_map/ppermute | solution.py:184
  51.2 15.4 %collective-permute-start.17 = (bf16[384,768]{1,0:T(8,128)(2,1)S(1)}, bf16[384,768]{1,0:T(8,128)(2,1)S(1)}, u32[]{:S(2)}, u32[]{:S(2)}) collective-permute-start(bf16[384,768]{1,0:T(8,128)(2,1)S(1)} %get-tuple-element.126), channel_id=1, source_target_pairs={{0,4},{4,0},{8,12},{12,8},{16,20},{20,16},{24,28},{28,24},{1,5},{5... | collective-permute-start | bytes 1769480 | tf_op jit(solution)/shard_map/ppermute | solution.py:184
  51.3 15.4 %collective-permute-start.18 = (bf16[384,768]{1,0:T(8,128)(2,1)S(1)}, bf16[384,768]{1,0:T(8,128)(2,1)S(1)}, u32[]{:S(2)}, u32[]{:S(2)}) collective-permute-start(bf16[384,768]{1,0:T(8,128)(2,1)S(1)} %get-tuple-element.128), channel_id=1, source_target_pairs={{0,8},{4,12},{8,0},{12,4},{16,24},{20,28},{24,16},{28,20},{1,9},{5... | collective-permute-start | bytes 1769480 | tf_op jit(solution)/shard_map/ppermute | solution.py:184
  56.1 10.9 %collective-permute-start.16 = (bf16[128,1152]{1,0:T(8,128)(2,1)S(1)}, bf16[128,1152]{1,0:T(8,128)(2,1)S(1)}, u32[]{:S(2)}, u32[]{:S(2)}) collective-permute-start(bf16[128,1152]{1,0:T(8,128)(2,1)S(1)} %get-tuple-element.124), channel_id=1, source_target_pairs={{0,2},{1,3},{2,0},{3,1},{4,6},{5,7},{6,4},{7,5},{8,10},{9,11},{10,... | collective-permute-start | bytes 884744 | tf_op jit(solution)/shard_map/ppermute | solution.py:184
  57.7 26.2 %collective-permute-start.20 = (bf16[256,960]{1,0:T(8,128)(2,1)S(1)}, bf16[256,960]{1,0:T(8,128)(2,1)S(1)}, u32[]{:S(2)}, u32[]{:S(2)}) collective-permute-start(bf16[256,960]{1,0:T(8,128)(2,1)S(1)} %get-tuple-element.118.refs_3_.refs_2_), channel_id=1, source_target_pairs={{0,1},{1,0},{2,3},{3,2},{4,5},{5,4},{6,7},{7,6},{8,9},{9,8},{10,11... | collective-permute-start | bytes 1474568 | tf_op jit(solution)/shard_map/ppermute | solution.py:184
  67.1 17.1 %collective-permute-start.21 = (bf16[256,960]{1,0:T(8,128)(2,1)S(1)}, bf16[256,960]{1,0:T(8,128)(2,1)S(1)}, u32[]{:S(2)}, u32[]{:S(2)}) collective-permute-start(bf16[256,960]{1,0:T(8,128)(2,1)S(1)} %get-tuple-element.135), channel_id=1, source_target_pairs={{0,1},{1,0},{2,3},{3,2},{4,5},{5,4},{6,7},{7,6},{8,9},{9,8},{10,11... | collective-permute-start | bytes 1474568 | tf_op jit(solution)/shard_map/ppermute | solution.py:184
  67.2 11.6 %collective-permute-start.22 = (bf16[192,768]{1,0:T(8,128)(2,1)S(1)}, bf16[192,768]{1,0:T(8,128)(2,1)S(1)}, u32[]{:S(2)}, u32[]{:S(2)}) collective-permute-start(bf16[192,768]{1,0:T(8,128)(2,1)S(1)} %get-tuple-element.129.refs_2_), channel_id=1, source_target_pairs={{0,8},{4,12},{8,0},{12,4},{16,24},{20,28},{24,16},{28,20},{1,9},{5... | collective-permute-start | bytes 884744 | tf_op jit(solution)/shard_map/ppermute | solution.py:184
  70.1 8.4 %collective-permute-start.14 = (bf16[1024,128]{1,0:T(8,128)(2,1)S(1)}, bf16[1024,128]{1,0:T(8,128)(2,1)S(1)}, u32[]{:S(2)}, u32[]{:S(2)}) collective-permute-start(bf16[1024,128]{1,0:T(8,128)(2,1)S(1)} %get-tuple-element.122), channel_id=1, source_target_pairs={{0,4},{4,0},{8,12},{12,8},{16,20},{20,16},{24,28},{28,24},{1,5},{5... | collective-permute-start | bytes 786440 | tf_op jit(solution)/shard_map/ppermute | solution.py:184
  70.1 53.3 %collective-permute-start.25 = (bf16[2,256,768]{2,1,0:T(8,128)(2,1)S(1)}, bf16[2,256,768]{2,1,0:T(8,128)(2,1)S(1)}, u32[]{:S(2)}, u32[]{:S(2)}) collective-permute-start(bf16[2,256,768]{2,1,0:T(8,128)(2,1)S(1)} %get-tuple-element.145), channel_id=1, source_target_pairs={{0,1},{1,0},{2,3},{3,2},{4,5},{5,4},{6,7},{7,6},{8,9},{9,8},{10,11... | collective-permute-start | bytes 2359304 | tf_op jit(solution)/shard_map/ppermute | solution.py:184
  78.4 14.9 %collective-permute-start.24 = (bf16[192,768]{1,0:T(8,128)(2,1)S(1)}, bf16[192,768]{1,0:T(8,128)(2,1)S(1)}, u32[]{:S(2)}, u32[]{:S(2)}) collective-permute-start(bf16[192,768]{1,0:T(8,128)(2,1)S(1)} %get-tuple-element.141), channel_id=1, source_target_pairs={{0,4},{4,0},{8,12},{12,8},{16,20},{20,16},{24,28},{28,24},{1,5},{5... | collective-permute-start | bytes 884744 | tf_op jit(solution)/shard_map/ppermute | solution.py:184
  78.9 20.5 %collective-permute-start.29 = (bf16[192,768]{1,0:T(8,128)(2,1)S(1)}, bf16[192,768]{1,0:T(8,128)(2,1)S(1)}, u32[]{:S(2)}, u32[]{:S(2)}) collective-permute-start(bf16[192,768]{1,0:T(8,128)(2,1)S(1)} %stage.25.refs_11_.refs_0_), channel_id=1, source_target_pairs={{0,16},{4,20},{8,24},{12,28},{16,0},{20,4},{24,8},{28,12},{1,17},{... | collective-permute-start | bytes 884744 | tf_op jit(solution)/shard_map/ppermute | solution.py:184
  83.9 8.6 %collective-permute-start.19 = (bf16[512,128]{1,0:T(8,128)(2,1)S(1)}, bf16[512,128]{1,0:T(8,128)(2,1)S(1)}, u32[]{:S(2)}, u32[]{:S(2)}) collective-permute-start(bf16[512,128]{1,0:T(8,128)(2,1)S(1)} %get-tuple-element.132.refs_2_), channel_id=1, source_target_pairs={{0,8},{4,12},{8,0},{12,4},{16,24},{20,28},{24,16},{28,20},{1,9},{5... | collective-permute-start | bytes 393224 | tf_op jit(solution)/shard_map/ppermute | solution.py:184
  85.3 18.2 %collective-permute-start.28 = (bf16[192,768]{1,0:T(8,128)(2,1)S(1)}, bf16[192,768]{1,0:T(8,128)(2,1)S(1)}, u32[]{:S(2)}, u32[]{:S(2)}) collective-permute-start(bf16[192,768]{1,0:T(8,128)(2,1)S(1)} %get-tuple-element.148), channel_id=1, source_target_pairs={{0,4},{4,0},{8,12},{12,8},{16,20},{20,16},{24,28},{28,24},{1,5},{5... | collective-permute-start | bytes 884744 | tf_op jit(solution)/shard_map/ppermute | solution.py:184
  92.5 5.8 %collective-permute-start.23 = (bf16[256,128]{1,0:T(8,128)(2,1)S(1)}, bf16[256,128]{1,0:T(8,128)(2,1)S(1)}, u32[]{:S(2)}, u32[]{:S(2)}) collective-permute-start(bf16[256,128]{1,0:T(8,128)(2,1)S(1)} %get-tuple-element.139.refs_2_), channel_id=1, source_target_pairs={{0,16},{4,20},{8,24},{12,28},{16,0},{20,4},{24,8},{28,12},{1,17},{... | collective-permute-start | bytes 196616 | tf_op jit(solution)/shard_map/ppermute | solution.py:184
  99.5 13.5 %collective-permute-start.32 = (bf16[192,768]{1,0:T(8,128)(2,1)S(1)}, bf16[192,768]{1,0:T(8,128)(2,1)S(1)}, u32[]{:S(2)}, u32[]{:S(2)}) collective-permute-start(bf16[192,768]{1,0:T(8,128)(2,1)S(1)} %stage.28.refs_2_), channel_id=1, source_target_pairs={{0,8},{4,12},{8,0},{12,4},{16,24},{20,28},{24,16},{28,20},{1,9},{5... | collective-permute-start | bytes 884744 | tf_op jit(solution)/shard_map/ppermute | solution.py:184
  101.5 2.3 %collective-permute-start.27 = (bf16[96,768]{1,0:T(8,128)(2,1)S(1)}, bf16[96,768]{1,0:T(8,128)(2,1)S(1)}, u32[]{:S(2)}, u32[]{:S(2)}) collective-permute-start(bf16[96,768]{1,0:T(8,128)(2,1)S(1)} %get-tuple-element.147), channel_id=1, source_target_pairs={{0,1},{1,0},{2,3},{3,2},{4,5},{5,4},{6,7},{7,6},{8,9},{9,8},{10,11... | collective-permute-start | bytes 442376 | tf_op jit(solution)/shard_map/ppermute | solution.py:184
  101.5 19.7 %collective-permute-start.26 = (bf16[192,768]{1,0:T(8,128)(2,1)S(1)}, bf16[192,768]{1,0:T(8,128)(2,1)S(1)}, u32[]{:S(2)}, u32[]{:S(2)}) collective-permute-start(bf16[192,768]{1,0:T(8,128)(2,1)S(1)} %stage.27.refs_10_.refs_0_), channel_id=1, source_target_pairs={{0,16},{4,20},{8,24},{12,28},{16,0},{20,4},{24,8},{28,12},{1,17},{... | collective-permute-start | bytes 884744 | tf_op jit(solution)/shard_map/ppermute | solution.py:184
  103.6 12.9 %collective-permute-start.31 = (bf16[96,768]{1,0:T(8,128)(2,1)S(1)}, bf16[96,768]{1,0:T(8,128)(2,1)S(1)}, u32[]{:S(2)}, u32[]{:S(2)}) collective-permute-start(bf16[96,768]{1,0:T(8,128)(2,1)S(1)} %get-tuple-element.149.refs_2_), channel_id=1, source_target_pairs={{0,8},{4,12},{8,0},{12,4},{16,24},{20,28},{24,16},{28,20},{1,9},{5... | collective-permute-start | bytes 442376 | tf_op jit(solution)/shard_map/ppermute | solution.py:184
  103.9 12.7 %collective-permute-start.30 = (bf16[48,768]{1,0:T(8,128)(2,1)S(1)}, bf16[48,768]{1,0:T(8,128)(2,1)S(1)}, u32[]{:S(2)}, u32[]{:S(2)}) collective-permute-start(bf16[48,768]{1,0:T(8,128)(2,1)S(1)} %get-tuple-element.151.refs_4_), channel_id=1, source_target_pairs={{0,2},{1,3},{2,0},{3,1},{4,6},{5,7},{6,4},{7,5},{8,10},{9,11},{10,... | collective-permute-start | bytes 221192 | tf_op jit(solution)/shard_map/ppermute | solution.py:184
  116.6 4.6 %collective-permute-start.33 = (bf16[48,768]{1,0:T(8,128)(2,1)S(1)}, bf16[48,768]{1,0:T(8,128)(2,1)S(1)}, u32[]{:S(2)}, u32[]{:S(2)}) collective-permute-start(bf16[48,768]{1,0:T(8,128)(2,1)S(1)} %stage.32.refs_0_.refs_2_), channel_id=1, source_target_pairs={{0,8},{4,12},{8,0},{12,4},{16,24},{20,28},{24,16},{28,20},{1,9},{5... | collective-permute-start | bytes 221192 | tf_op jit(solution)/shard_map/ppermute | solution.py:184
  118.3 8.2 %collective-permute-start.37 = (bf16[96,768]{1,0:T(8,128)(2,1)S(1)}, bf16[96,768]{1,0:T(8,128)(2,1)S(1)}, u32[]{:S(2)}, u32[]{:S(2)}) collective-permute-start(bf16[96,768]{1,0:T(8,128)(2,1)S(1)} %get-tuple-element.153.refs_2_.refs_0_), channel_id=1, source_target_pairs={{0,16},{4,20},{8,24},{12,28},{16,0},{20,4},{24,8},{28,12},{1,17},{... | collective-permute-start | bytes 442376 | tf_op jit(solution)/shard_map/ppermute | solution.py:184
  121.3 11.7 %collective-permute-start.36 = (bf16[192,768]{1,0:T(8,128)(2,1)S(1)}, bf16[192,768]{1,0:T(8,128)(2,1)S(1)}, u32[]{:S(2)}, u32[]{:S(2)}) collective-permute-start(bf16[192,768]{1,0:T(8,128)(2,1)S(1)} %stage.34.refs_2_.refs_0_), channel_id=1, source_target_pairs={{0,4},{4,0},{8,12},{12,8},{16,20},{20,16},{24,28},{28,24},{1,5},{5... | collective-permute-start | bytes 884744 | tf_op jit(solution)/shard_map/ppermute | solution.py:184
  123.6 22.8 %collective-permute-start.34 = (bf16[2,256,768]{2,1,0:T(8,128)(2,1)S(1)}, bf16[2,256,768]{2,1,0:T(8,128)(2,1)S(1)}, u32[]{:S(2)}, u32[]{:S(2)}) collective-permute-start(bf16[2,256,768]{2,1,0:T(8,128)(2,1)S(1)} %stage.35.refs_2_), channel_id=1, source_target_pairs={{0,2},{1,3},{2,0},{3,1},{4,6},{5,7},{6,4},{7,5},{8,10},{9,11},{10,... | collective-permute-start | bytes 2359304 | tf_op jit(solution)/shard_map/ppermute | solution.py:184
  126.5 6.5 %collective-permute-start.38 = (bf16[96,768]{1,0:T(8,128)(2,1)S(1)}, bf16[96,768]{1,0:T(8,128)(2,1)S(1)}, u32[]{:S(2)}, u32[]{:S(2)}) collective-permute-start(bf16[96,768]{1,0:T(8,128)(2,1)S(1)} %stage.36.refs_2_.refs_0_), channel_id=1, source_target_pairs={{0,8},{4,12},{8,0},{12,4},{16,24},{20,28},{24,16},{28,20},{1,9},{5... | collective-permute-start | bytes 442376 | tf_op jit(solution)/shard_map/ppermute | solution.py:184
  126.6 5.4 %collective-permute-start.39 = (bf16[48,768]{1,0:T(8,128)(2,1)S(1)}, bf16[48,768]{1,0:T(8,128)(2,1)S(1)}, u32[]{:S(2)}, u32[]{:S(2)}) collective-permute-start(bf16[48,768]{1,0:T(8,128)(2,1)S(1)} %stage.33.refs_2_.refs_0_), channel_id=1, source_target_pairs={{0,4},{4,0},{8,12},{12,8},{16,20},{20,16},{24,28},{28,24},{1,5},{5... | collective-permute-start | bytes 221192 | tf_op jit(solution)/shard_map/ppermute | solution.py:184
  128.7 16.3 %collective-permute-start.35 = (bf16[384,768]{1,0:T(8,128)(2,1)S(1)}, bf16[384,768]{1,0:T(8,128)(2,1)S(1)}, u32[]{:S(2)}, u32[]{:S(2)}) collective-permute-start(bf16[384,768]{1,0:T(8,128)(2,1)S(1)} %get-tuple-element.154.refs_0_), channel_id=1, source_target_pairs={{0,4},{4,0},{8,12},{12,8},{16,20},{20,16},{24,28},{28,24},{1,5},{5... | collective-permute-start | bytes 1769480 | tf_op jit(solution)/shard_map/ppermute | solution.py:184
  133.1 17.9 %collective-permute-start.42 = (bf16[384,768]{1,0:T(8,128)(2,1)S(1)}, bf16[384,768]{1,0:T(8,128)(2,1)S(1)}, u32[]{:S(2)}, u32[]{:S(2)}) collective-permute-start(bf16[384,768]{1,0:T(8,128)(2,1)S(1)} %stage.39.refs_2_.refs_0_), channel_id=1, source_target_pairs={{0,8},{4,12},{8,0},{12,4},{16,24},{20,28},{24,16},{28,20},{1,9},{5... | collective-permute-start | bytes 1769480 | tf_op jit(solution)/shard_map/ppermute | solution.py:184
  134.0 15.2 %collective-permute-start.41 = (bf16[192,768]{1,0:T(8,128)(2,1)S(1)}, bf16[192,768]{1,0:T(8,128)(2,1)S(1)}, u32[]{:S(2)}, u32[]{:S(2)}) collective-permute-start(bf16[192,768]{1,0:T(8,128)(2,1)S(1)} %stage.38.refs_2_.refs_0_), channel_id=1, source_target_pairs={{0,4},{4,0},{8,12},{12,8},{16,20},{20,16},{24,28},{28,24},{1,5},{5... | collective-permute-start | bytes 884744 | tf_op jit(solution)/shard_map/ppermute | solution.py:184
  136.3 11.9 %collective-permute-start.40 = (bf16[48,768]{1,0:T(8,128)(2,1)S(1)}, bf16[48,768]{1,0:T(8,128)(2,1)S(1)}, u32[]{:S(2)}, u32[]{:S(2)}) collective-permute-start(bf16[48,768]{1,0:T(8,128)(2,1)S(1)} %stage.37.refs_2_.refs_0_), channel_id=1, source_target_pairs={{0,16},{4,20},{8,24},{12,28},{16,0},{20,4},{24,8},{28,12},{1,17},{... | collective-permute-start | bytes 221192 | tf_op jit(solution)/shard_map/ppermute | solution.py:184
  149.2 0.7 copy-start.5
